TPU v7x, 256 devices: a whole 4x4x8 slice. The times are simulated.
256 devices in a mesh: region: 8 (over y, core), gy: 8 (over z), gz: 4 (over x).
Axes of the slice: x: 4, y: 4, z: 8, core: 2. Of those that a mesh axis runs over, the one named last changes fastest.
Arguments:
- loads: float32 [256, 32, 768], P(('region', 'gy', 'gz')), may hold values from -62 to 62
- schur: bfloat16 [256, 768, 768], P(('region', 'gy', 'gz')), may hold values from -1 to 3.5, as said below
- dirichlet: bfloat16 [256, 768, 768], P(('region', 'gy', 'gz')), may hold values from -1 to 1.75, as said below
- coupling: bfloat16 [256, 768, 128], P(('region', 'gy', 'gz')), may hold values from -0.21875 to 0.21875
- coarse_inverse: float32 [512, 512], replicated, may hold values from -1 to 1, as said below
- pairing: int32 [256, 6, 128], P(('region', 'gy', 'gz')), may hold values from 0 to 127, as said below
- corner_map: int32 [256, 128], P(('region', 'gy', 'gz')), may hold values from 0 to 511, as said below
- counts: int32 [256], P(('region', 'gy', 'gz')), may hold values from 1 to 1, as said below
Outputs:
- solution: float32 [256, 32, 768], P(('region', 'gy', 'gz'))
- residual: float32 [256, 32, 768], P(('region', 'gy', 'gz'))
Inputs may be any that keep to these rules, and one draw needn't show every extreme that they name: `schur`: symmetric and positive definite for every subdomain. `dirichlet`: symmetric and positive definite for every subdomain. `coarse_inverse`: symmetric and positive definite. `counts`: some device has all 1 slots live. `pairing`: within each face block a permutation; the two slots that hold one multiplier name each other. `corner_map`: device d owns coarse degrees of freedom d * 2 to d * 2 + 1; every corner of a subdomain on device d maps to one owned by d or by a device one step away along one of the three directions; slot 0 of device d maps its first 2 corners to d's own in order.
All inputs are finite; a program needn't handle non-finite values.
Results may differ from a plain program's by a relative error of at most 0.0065.
The roundings to bfloat16 on the way count: a program that leaves them out, or rounds other values in their place, can miss the bound.
Values sent between devices are 32-bit elements; how exact they have to be, the bound alone decides.
No kernel may reach another device: no remote copies, remote signals or barrier semaphores. Data moves between devices by JAX's collectives and lax.ppermute only.
A program may use at most 64 MiB of HBM per device.

v0:
```python
import jax
import jax.numpy as jnp
from jax import lax
from jax.sharding import PartitionSpec as P

ITERS = 2


HIGHEST_PREC = lax.Precision.HIGHEST


def padded(cells, sides, width):
    for axis, dim in sides:
        count = lax.axis_size(axis)
        ends = count - 1
        head = lax.slice_in_dim(cells, 0, width, axis=dim)
        tail = lax.slice_in_dim(cells, cells.shape[dim] - width, cells.shape[dim], axis=dim)
        cells = jnp.concatenate(
            [
                lax.ppermute(tail, axis, [(i, (i + 1) % count) for i in range(ends)]),
                cells,
                lax.ppermute(head, axis, [((i + 1) % count, i) for i in range(ends)]),
            ],
            axis=dim,
        )
    return cells


def partner_terms(values, perm_table):
    number, columns, width = values.shape
    face_size = width // 6
    face_view = values.reshape(number, columns, 6, face_size)
    region_ext = padded(face_view[:, :, 0:2], (("region", 2),), 1)
    tiles_y = padded(face_view[:, :, 2:4], (("gy", 2),), 1)
    zrow = jnp.swapaxes(face_view[:, :, 4:6], 1, 2).reshape(2 * number, columns, face_size)
    tiles_z = padded(zrow, (("gz", 0),), 1)
    lower_z = tiles_z[0 : 2 * number : 2]
    upper_z = tiles_z[3 : 2 * number + 2 : 2]
    received = jnp.stack(
        [
            region_ext[:, :, 0],
            region_ext[:, :, 3],
            tiles_y[:, :, 0],
            tiles_y[:, :, 3],
            lower_z,
            upper_z,
        ],
        axis=2,
    )
    permuted = jnp.einsum("scfk,sfkj->scfj", received, perm_table, precision=HIGHEST_PREC)
    return permuted.reshape(number, columns, width)


def assemble(values, living, perm_table):
    return living[:, None, None] * (values + partner_terms(values, perm_table))


def weighted_inner(weight, left, right_vec):
    return jnp.sum(weight * left * right_vec, axis=(0, 2))


def residual_product(weight, left, right_vec):
    return lax.psum(weighted_inner(weight, left, right_vec), ("region", "gy", "gz"))


def local(loads, schur, dirichlet, coupling, coarse_inverse, pairing, corner_map, counts):
    subs_here = schur.shape[0]
    slots = schur.shape[1]
    coarse_size = coarse_inverse.shape[0]
    face_size = pairing.shape[2]
    perm_table = (
        jnp.arange(face_size, dtype=jnp.int32)[None, None, :, None] == pairing[:, :, None, :]
    ).astype(jnp.float32)
    living = (jnp.arange(subs_here, dtype=jnp.int32) < counts[0]).astype(jnp.float32)
    live_col = living[:, None, None]
    live_ones = jnp.broadcast_to(live_col, (subs_here, 1, slots))
    multiplicity = assemble(live_ones, living, perm_table)
    weight = live_col / jnp.maximum(multiplicity, 1.0)
    right_side = assemble(loads * live_col, living, perm_table)
    onehot_f = (
        corner_map[:, :, None] == jnp.arange(coarse_size, dtype=jnp.int32)[None, None, :]
    ).astype(jnp.float32)
    onehot_bf = onehot_f.astype(jnp.bfloat16)

    def precondition(residual):
        scaled = (weight * residual).astype(jnp.bfloat16)
        applied = jnp.einsum("srm,smn->srn", scaled, dirichlet, preferred_element_type=jnp.float32)
        return assemble(weight * applied, living, perm_table)

    residual = right_side
    solution = jnp.zeros_like(right_side)
    precond = precondition(residual)
    resid_dot = residual_product(weight, residual, precond)
    direction = precond
    for iteration in range(ITERS):
        dir_bf = direction.astype(jnp.bfloat16)
        local_terms = (
            jnp.einsum("srm,smn->srn", dir_bf, schur, preferred_element_type=jnp.float32) * live_col
        )
        corner_terms = (
            jnp.einsum("srm,smj->srj", dir_bf, coupling, preferred_element_type=jnp.float32)
            * live_col
        )
        partial_sum = jnp.einsum("sjc,srj->cr", onehot_f, corner_terms, precision=HIGHEST_PREC)
        gathered = lax.psum(partial_sum, ("region", "gy", "gz"))
        solved = jnp.dot(coarse_inverse, gathered, precision=HIGHEST_PREC).astype(jnp.bfloat16)
        picked = jnp.einsum(
            "sjc,cr->sjr", onehot_bf, solved, preferred_element_type=jnp.float32
        ).astype(jnp.bfloat16)
        own_coarse = (
            jnp.einsum("sjr,smj->srm", picked, coupling, preferred_element_type=jnp.float32)
            * live_col
        )
        image_vec = assemble(local_terms + own_coarse, living, perm_table)
        curvature = lax.psum(weighted_inner(weight, direction, image_vec), ("region", "gy", "gz"))
        image_vec, curvature = (image_vec, curvature)
        step_size = (resid_dot / curvature)[None, :, None]
        solution = solution + step_size * direction
        residual = residual - step_size * image_vec
        if iteration + 1 < ITERS:
            precond = precondition(residual)
            new_dot = residual_product(weight, residual, precond)
            direction = precond + (new_dot / resid_dot)[None, :, None] * direction
            resid_dot = new_dot
    return (solution, residual)


def solution(mesh):
    in_specs = (
        P(("region", "gy", "gz"), None, None),
        P(("region", "gy", "gz"), None, None),
        P(("region", "gy", "gz"), None, None),
        P(("region", "gy", "gz"), None, None),
        P(),
        P(("region", "gy", "gz"), None, None),
        P(("region", "gy", "gz"), None),
        P(("region", "gy", "gz")),
    )
    out_specs = (P(("region", "gy", "gz"), None, None), P(("region", "gy", "gz"), None, None))
    return jax.shard_map(local, mesh=mesh, in_specs=in_specs, out_specs=out_specs, check_vma=False)
```

profile of v0, /device:TPU:2, one launch (start us, length us, event | category | flops | bytes accessed | tf_op | source)
XLA Modules:
  0.0 888.2 jit_solution(8641405572129003994)
XLA Ops:
  8.0 1.7 collective-permute-start
  9.7 1.3 collective-permute-start.1
  11.0 3.8 collective-permute-start.2
  14.9 1.3 collective-permute-start.3
  16.2 3.4 collective-permute-start.4
  21.3 2.4 collective-permute-start.5
  23.8 3.6 collective-permute-start.6
  27.3 1.3 collective-permute-start.7
  28.6 4.5 collective-permute-start.8
  33.1 1.3 collective-permute-start.9
  34.4 3.4 collective-permute-start.10
  38.2 2.4 collective-permute-start.11
  40.7 3.1 collective-permute-done.11
  44.6 3.6 collective-permute-start.12
  48.2 1.3 collective-permute-start.13
  49.5 4.5 collective-permute-start.14
  54.0 1.3 collective-permute-start.15
  55.3 3.1 collective-permute-start.16
  58.4 2.7 collective-permute-start.17
  61.3 2.8 collective-permute-done.17
  64.6 1.2 convolution_multiply_fusion.1
  65.8 1.1 fusion.30
  66.9 1.0 fusion.2
  67.9 259.5 %all-reduce.4.cloned.1.call-done = f32[512,32]{1,0:T(8,128)} async-done(((f32[512,32]{1,0:T(8,128)}), f32[512,32]{1,0:T(8,128)}) %all-reduce.4.cloned.1.call-update) | async-done | bytes 65552 | tf_op jit(solution)/shard_map/psum | solution.py:105
  327.4 2.0 convolution_convert_fusion.3
  329.5 2.1 fusion.8
  331.6 1.6 reshape.290
  333.1 1.2 fusion.68
  335.2 1.3 collective-permute-start.18
  336.5 1.3 collective-permute-start.19
  337.8 2.4 collective-permute-start.20
  340.2 1.3 collective-permute-start.21
  341.5 3.3 collective-permute-start.22
  344.9 2.5 collective-permute-start.23
  347.5 3.1 collective-permute-done.23
  351.6 1.0 multiply_reduce_fusion.1
  352.7 77.0 %all-reduce = (f32[32]{0:T(128)S(1)}, f32[32]{0:T(128)S(1)}) all-reduce(f32[32]{0:T(128)S(1)} %get-tuple-element.4, f32[32]{0:T(128)S(1)} %multiply_reduce_fusion.1), channel_id=1, replica_groups=mesh['region'=8,'gy'=8,'gz'=4] {'region','gy','gz'}, use_global_device_ids=true, to_apply=%region_1.0 | all-reduce | flops 64 | bytes 512 | tf_op jit(solution)/shard_map/psum | solution.py:63
  429.7 1.1 bitcast_subtract_fusion.1
  431.4 1.0 fusion.13
  432.4 1.6 reshape.294
  433.9 1.2 fusion.67
  436.0 1.7 collective-permute-start.24
  437.8 1.3 collective-permute-start.25
  439.1 3.9 collective-permute-start.26
  443.0 1.3 collective-permute-start.27
  444.3 3.2 collective-permute-start.28
  447.6 2.6 collective-permute-start.29
  450.3 2.9 collective-permute-done.29
  454.2 1.1 fusion.44
  455.3 75.7 %psum.45 = f32[32]{0:T(128)S(1)} all-reduce(f32[32]{0:T(128)S(1)} %fusion.44), channel_id=1, replica_groups=mesh['region'=8,'gy'=8,'gz'=4] {'region','gy','gz'}, use_global_device_ids=true, to_apply=%region_6.0 | all-reduce | flops 32 | bytes 256 | tf_op jit(solution)/shard_map/psum | solution.py:63
  531.0 1.0 multiply_add_fusion
  532.7 1.1 convolution_multiply_fusion
  533.8 1.1 fusion.28
  534.9 1.9 fusion
  536.8 247.5 %all-reduce.6.cloned.1.call-done = f32[512,32]{1,0:T(8,128)} async-done(((f32[512,32]{1,0:T(8,128)}), f32[512,32]{1,0:T(8,128)}) %all-reduce.6.cloned.1.call-update) | async-done | bytes 65552 | tf_op jit(solution)/shard_map/psum | solution.py:105
  784.3 2.0 convolution_convert_fusion.1
  786.9 1.3 collective-permute-start.30
  788.2 1.3 collective-permute-start.31
  789.5 2.4 collective-permute-start.32
  791.9 1.3 collective-permute-start.33
  793.3 3.3 collective-permute-start.34
  796.6 2.5 collective-permute-start.35
  799.2 3.1 collective-permute-done.35
  802.8 77.0 %psum.47 = f32[32]{0:T(128)S(1)} all-reduce(f32[32]{0:T(128)S(1)} %multiply_reduce_fusion), channel_id=1, replica_groups=mesh['region'=8,'gy'=8,'gz'=4] {'region','gy','gz'}, use_global_device_ids=true, to_apply=%region_9.0 | all-reduce | flops 32 | bytes 256 | tf_op jit(solution)/shard_map/psum | solution.py:115
  (140 shorter events, 11.2 us)
Async XLA Ops:
  7.2 37.0 %copy-start = (bf16[1,768,768]{2,1,0:T(8,128)(2,1)S(1)}, bf16[1,768,768]{2,1,0:T(8,128)(2,1)}, u32[]{:S(2)}) copy-start(bf16[1,768,768]{2,1,0:T(8,128)(2,1)} %param.10) | copy-start | bytes 3538948
  7.2 36.9 %copy-start.11 = (f32[1,32,768]{2,1,0:T(8,128)S(1)}, f32[1,32,768]{2,1,0:T(8,128)}, u32[]{:S(2)}) copy-start(f32[1,32,768]{2,1,0:T(8,128)} %param.8) | copy-start | bytes 294916
  7.2 320.2 %all-reduce.4.cloned.1.call-start = ((), (), s32[]{:S(2)}) async-start(), calls=%async_computation | async-start | bytes 524288 | tf_op jit(solution)/shard_map/psum | solution.py:105
  8.0 13.3 %collective-permute-start = (f32[1,1,1,128]{3,2,1,0:T(1,128)S(1)}, f32[1,1,1,128]{3,2,1,0:T(1,128)S(1)}, u32[]{:S(2)}, u32[]{:S(2)}) collective-permute-start(f32[1,1,1,128]{3,2,1,0:T(1,128)S(1)} %slice.190), channel_id=1, source_target_pairs={{0,32},{32,64},{64,96},{96,128},{128,160},{160,192},{192,224},{1,3... | collective-permute-start | bytes 1544 | tf_op jit(solution)/shard_map/ppermute | solution.py:20
  9.7 14.0 %collective-permute-start.1 = (f32[1,1,1,128]{3,2,1,0:T(1,128)S(1)}, f32[1,1,1,128]{3,2,1,0:T(1,128)S(1)}, u32[]{:S(2)}, u32[]{:S(2)}) collective-permute-start(f32[1,1,1,128]{3,2,1,0:T(1,128)S(1)} %slice.190), channel_id=1, source_target_pairs={{32,0},{64,32},{96,64},{128,96},{160,128},{192,160},{224,192},{33,... | collective-permute-start | bytes 1544 | tf_op jit(solution)/shard_map/ppermute | solution.py:22
  11.0 16.3 %collective-permute-start.2 = (f32[1,1,1,128]{3,2,1,0:T(1,128)S(1)}, f32[1,1,1,128]{3,2,1,0:T(1,128)S(1)}, u32[]{:S(2)}, u32[]{:S(2)}) collective-permute-start(f32[1,1,1,128]{3,2,1,0:T(1,128)S(1)} %slice.190), channel_id=1, source_target_pairs={{0,4},{4,8},{8,12},{12,16},{16,20},{20,24},{24,28},{1,5},{5,9},{9,... | collective-permute-start | bytes 1544 | tf_op jit(solution)/shard_map/ppermute | solution.py:20
  14.9 13.8 %collective-permute-start.3 = (f32[1,1,1,128]{3,2,1,0:T(1,128)S(1)}, f32[1,1,1,128]{3,2,1,0:T(1,128)S(1)}, u32[]{:S(2)}, u32[]{:S(2)}) collective-permute-start(f32[1,1,1,128]{3,2,1,0:T(1,128)S(1)} %slice.190), channel_id=1, source_target_pairs={{4,0},{8,4},{12,8},{16,12},{20,16},{24,20},{28,24},{5,1},{9,5},{13... | collective-permute-start | bytes 1544 | tf_op jit(solution)/shard_map/ppermute | solution.py:22
  16.2 16.9 %collective-permute-start.4 = (f32[1,1,128]{2,1,0:T(1,128)S(1)}, f32[1,1,128]{2,1,0:T(1,128)S(1)}, u32[]{:S(2)}, u32[]{:S(2)}) collective-permute-start(f32[1,1,128]{2,1,0:T(1,128)S(1)} %slice.191), channel_id=1, source_target_pairs={{0,1},{1,2},{2,3},{4,5},{5,6},{6,7},{8,9},{9,10},{10,11},{12,13},{... | collective-permute-start | bytes 1544 | tf_op jit(solution)/shard_map/ppermute | solution.py:20
  21.3 13.1 %collective-permute-start.5 = (f32[1,1,128]{2,1,0:T(1,128)S(1)}, f32[1,1,128]{2,1,0:T(1,128)S(1)}, u32[]{:S(2)}, u32[]{:S(2)}) collective-permute-start(f32[1,1,128]{2,1,0:T(1,128)S(1)} %slice.191), channel_id=1, source_target_pairs={{1,0},{2,1},{3,2},{5,4},{6,5},{7,6},{9,8},{10,9},{11,10},{13,12},{... | collective-permute-start | bytes 1544 | tf_op jit(solution)/shard_map/ppermute | solution.py:22
  23.8 14.4 %collective-permute-start.6 = (f32[1,32,1,128]{3,1,2,0:T(8,128)S(1)}, f32[1,32,1,128]{3,1,2,0:T(8,128)S(1)}, u32[]{:S(2)}, u32[]{:S(2)}) collective-permute-start(f32[1,32,1,128]{3,1,2,0:T(8,128)S(1)} %bitcast.246), channel_id=1, source_target_pairs={{0,32},{32,64},{64,96},{96,128},{128,160},{160,192},{192,224},{1,3... | collective-permute-start | bytes 49160 | tf_op jit(solution)/shard_map/ppermute | solution.py:20
  27.3 13.3 %collective-permute-start.7 = (f32[1,32,1,128]{3,1,2,0:T(8,128)S(1)}, f32[1,32,1,128]{3,1,2,0:T(8,128)S(1)}, u32[]{:S(2)}, u32[]{:S(2)}) collective-permute-start(f32[1,32,1,128]{3,1,2,0:T(8,128)S(1)} %bitcast.245), channel_id=1, source_target_pairs={{32,0},{64,32},{96,64},{128,96},{160,128},{192,160},{224,192},{33,... | collective-permute-start | bytes 49160 | tf_op jit(solution)/shard_map/ppermute | solution.py:22
  28.6 12.0 %collective-permute-start.8 = (f32[1,32,1,128]{3,1,2,0:T(8,128)S(1)}, f32[1,32,1,128]{3,1,2,0:T(8,128)S(1)}, u32[]{:S(2)}, u32[]{:S(2)}) collective-permute-start(f32[1,32,1,128]{3,1,2,0:T(8,128)S(1)} %bitcast.244), channel_id=1, source_target_pairs={{0,4},{4,8},{8,12},{12,16},{16,20},{20,24},{24,28},{1,5},{5,9},{9,... | collective-permute-start | bytes 49160 | tf_op jit(solution)/shard_map/ppermute | solution.py:20
  33.1 7.5 collective-permute-start.9
  34.4 6.3 collective-permute-start.10
  38.2 5.6 collective-permute-start.11
  44.1 20.3 %copy-start.6 = (f32[1,32,768]{2,1,0:T(8,128)}, f32[1,32,768]{2,1,0:T(8,128)S(1)}, u32[]{:S(2)}) copy-start(f32[1,32,768]{2,1,0:T(8,128)S(1)} %fusion.42) | copy-start | bytes 294916
  44.5 21.3 %copy-start.13 = (s32[1,128]{1,0:T(1,128)S(1)}, s32[1,128]{1,0:T(1,128)}, u32[]{:S(2)}) copy-start(s32[1,128]{1,0:T(1,128)} %param.14) | copy-start | bytes 1540
  44.5 22.4 %copy-start.1 = (bf16[1,768,768]{2,1,0:T(8,128)(2,1)S(1)}, bf16[1,768,768]{2,1,0:T(8,128)(2,1)}, u32[]{:S(2)}) copy-start(bf16[1,768,768]{2,1,0:T(8,128)(2,1)} %param.9) | copy-start | bytes 3538948
  44.6 13.8 %collective-permute-start.12 = (f32[1,32,1,128]{3,1,2,0:T(8,128)S(1)}, f32[1,32,1,128]{3,1,2,0:T(8,128)S(1)}, u32[]{:S(2)}, u32[]{:S(2)}) collective-permute-start(f32[1,32,1,128]{3,1,2,0:T(8,128)S(1)} %bitcast.259), channel_id=1, source_target_pairs={{0,32},{32,64},{64,96},{96,128},{128,160},{160,192},{192,224},{1,3... | collective-permute-start | bytes 49160 | tf_op jit(solution)/shard_map/ppermute | solution.py:20
  48.2 13.0 %collective-permute-start.13 = (f32[1,32,1,128]{3,1,2,0:T(8,128)S(1)}, f32[1,32,1,128]{3,1,2,0:T(8,128)S(1)}, u32[]{:S(2)}, u32[]{:S(2)}) collective-permute-start(f32[1,32,1,128]{3,1,2,0:T(8,128)S(1)} %bitcast.255), channel_id=1, source_target_pairs={{32,0},{64,32},{96,64},{128,96},{160,128},{192,160},{224,192},{33,... | collective-permute-start | bytes 49160 | tf_op jit(solution)/shard_map/ppermute | solution.py:22
  49.5 11.7 %collective-permute-start.14 = (f32[1,32,1,128]{3,1,2,0:T(8,128)S(1)}, f32[1,32,1,128]{3,1,2,0:T(8,128)S(1)}, u32[]{:S(2)}, u32[]{:S(2)}) collective-permute-start(f32[1,32,1,128]{3,1,2,0:T(8,128)S(1)} %bitcast.251), channel_id=1, source_target_pairs={{0,4},{4,8},{8,12},{12,16},{16,20},{20,24},{24,28},{1,5},{5,9},{9,... | collective-permute-start | bytes 49160 | tf_op jit(solution)/shard_map/ppermute | solution.py:20
  54.0 7.2 collective-permute-start.15
  55.3 5.9 collective-permute-start.16
  58.4 5.6 collective-permute-start.17
  64.6 262.8 %copy-start.2 = (f32[512,512]{1,0:T(8,128)S(1)}, f32[512,512]{1,0:T(8,128)}, u32[]{:S(2)}) copy-start(f32[512,512]{1,0:T(8,128)} %param.12) | copy-start | bytes 3145732
  66.9 717.4 %all-reduce.6.cloned.1.call-start = ((), (), s32[]{:S(2)}) async-start(), calls=%async_computation.1 | async-start | bytes 524288 | tf_op jit(solution)/shard_map/psum | solution.py:105
  335.2 9.7 %collective-permute-start.18 = (f32[1,32,1,128]{3,1,2,0:T(8,128)S(1)}, f32[1,32,1,128]{3,1,2,0:T(8,128)S(1)}, u32[]{:S(2)}, u32[]{:S(2)}) collective-permute-start(f32[1,32,1,128]{3,1,2,0:T(8,128)S(1)} %bitcast.260), channel_id=1, source_target_pairs={{0,32},{32,64},{64,96},{96,128},{128,160},{160,192},{192,224},{1,3... | collective-permute-start | bytes 49160 | tf_op jit(solution)/shard_map/ppermute | solution.py:20
  336.5 10.9 %collective-permute-start.19 = (f32[1,32,1,128]{3,1,2,0:T(8,128)S(1)}, f32[1,32,1,128]{3,1,2,0:T(8,128)S(1)}, u32[]{:S(2)}, u32[]{:S(2)}) collective-permute-start(f32[1,32,1,128]{3,1,2,0:T(8,128)S(1)} %bitcast.256), channel_id=1, source_target_pairs={{32,0},{64,32},{96,64},{128,96},{160,128},{192,160},{224,192},{33,... | collective-permute-start | bytes 49160 | tf_op jit(solution)/shard_map/ppermute | solution.py:22
  337.8 9.6 %collective-permute-start.20 = (f32[1,32,1,128]{3,1,2,0:T(8,128)S(1)}, f32[1,32,1,128]{3,1,2,0:T(8,128)S(1)}, u32[]{:S(2)}, u32[]{:S(2)}) collective-permute-start(f32[1,32,1,128]{3,1,2,0:T(8,128)S(1)} %bitcast.252), channel_id=1, source_target_pairs={{0,4},{4,8},{8,12},{12,16},{16,20},{20,24},{24,28},{1,5},{5,9},{9,... | collective-permute-start | bytes 49160 | tf_op jit(solution)/shard_map/ppermute | solution.py:20
  340.2 7.2 collective-permute-start.21
  341.5 5.9 collective-permute-start.22
  344.9 5.7 collective-permute-start.23
  351.0 0.6 copy-start.9
  430.8 0.6 copy-start.7
  436.0 11.5 %collective-permute-start.24 = (f32[1,32,1,128]{3,1,2,0:T(8,128)S(1)}, f32[1,32,1,128]{3,1,2,0:T(8,128)S(1)}, u32[]{:S(2)}, u32[]{:S(2)}) collective-permute-start(f32[1,32,1,128]{3,1,2,0:T(8,128)S(1)} %bitcast.261), channel_id=1, source_target_pairs={{0,32},{32,64},{64,96},{96,128},{128,160},{160,192},{192,224},{1,3... | collective-permute-start | bytes 49160 | tf_op jit(solution)/shard_map/ppermute | solution.py:20
  437.8 12.4 %collective-permute-start.25 = (f32[1,32,1,128]{3,1,2,0:T(8,128)S(1)}, f32[1,32,1,128]{3,1,2,0:T(8,128)S(1)}, u32[]{:S(2)}, u32[]{:S(2)}) collective-permute-start(f32[1,32,1,128]{3,1,2,0:T(8,128)S(1)} %bitcast.257), channel_id=1, source_target_pairs={{32,0},{64,32},{96,64},{128,96},{160,128},{192,160},{224,192},{33,... | collective-permute-start | bytes 49160 | tf_op jit(solution)/shard_map/ppermute | solution.py:22
  439.1 11.1 %collective-permute-start.26 = (f32[1,32,1,128]{3,1,2,0:T(8,128)S(1)}, f32[1,32,1,128]{3,1,2,0:T(8,128)S(1)}, u32[]{:S(2)}, u32[]{:S(2)}) collective-permute-start(f32[1,32,1,128]{3,1,2,0:T(8,128)S(1)} %bitcast.253), channel_id=1, source_target_pairs={{0,4},{4,8},{8,12},{12,16},{16,20},{20,24},{24,28},{1,5},{5,9},{9,... | collective-permute-start | bytes 49160 | tf_op jit(solution)/shard_map/ppermute | solution.py:20
  443.0 7.2 collective-permute-start.27
  444.3 5.9 collective-permute-start.28
  447.6 5.6 collective-permute-start.29
  453.6 0.6 copy-start.10
  532.1 0.6 copy-start.4
  536.8 249.6 %copy-start.3 = (bf16[1,768,128]{2,1,0:T(8,128)(2,1)S(1)}, bf16[1,768,128]{2,1,0:T(8,128)(2,1)}, u32[]{:S(2)}) copy-start(bf16[1,768,128]{2,1,0:T(8,128)(2,1)} %param.11) | copy-start | bytes 589828
  536.8 249.6 %copy-start.12 = (f32[32,768]{1,0:T(8,128)S(1)}, f32[32,768]{1,0:T(8,128)}, u32[]{:S(2)}) copy-start(f32[32,768]{1,0:T(8,128)} %fusion) | copy-start | bytes 294916
  536.8 265.9 %copy-start.5 = (f32[32,768]{1,0:T(8,128)S(1)}, f32[32,768]{1,0:T(8,128)}, u32[]{:S(2)}) copy-start(f32[32,768]{1,0:T(8,128)} %copy-done.4) | copy-start | bytes 294916
  786.4 93.5 %copy-start.8 = (f32[1,32,768]{2,1,0:T(8,128)S(1)}, f32[1,32,768]{2,1,0:T(8,128)}, u32[]{:S(2)}) copy-start(f32[1,32,768]{2,1,0:T(8,128)} %copy-done.7) | copy-start | bytes 294916
  786.9 9.7 %collective-permute-start.30 = (f32[1,32,1,128]{3,1,2,0:T(8,128)S(1)}, f32[1,32,1,128]{3,1,2,0:T(8,128)S(1)}, u32[]{:S(2)}, u32[]{:S(2)}) collective-permute-start(f32[1,32,1,128]{3,1,2,0:T(8,128)S(1)} %bitcast.262), channel_id=1, source_target_pairs={{0,32},{32,64},{64,96},{96,128},{128,160},{160,192},{192,224},{1,3... | collective-permute-start | bytes 49160 | tf_op jit(solution)/shard_map/ppermute | solution.py:20
  788.2 10.9 %collective-permute-start.31 = (f32[1,32,1,128]{3,1,2,0:T(8,128)S(1)}, f32[1,32,1,128]{3,1,2,0:T(8,128)S(1)}, u32[]{:S(2)}, u32[]{:S(2)}) collective-permute-start(f32[1,32,1,128]{3,1,2,0:T(8,128)S(1)} %bitcast.258), channel_id=1, source_target_pairs={{32,0},{64,32},{96,64},{128,96},{160,128},{192,160},{224,192},{33,... | collective-permute-start | bytes 49160 | tf_op jit(solution)/shard_map/ppermute | solution.py:22
  789.5 9.6 %collective-permute-start.32 = (f32[1,32,1,128]{3,1,2,0:T(8,128)S(1)}, f32[1,32,1,128]{3,1,2,0:T(8,128)S(1)}, u32[]{:S(2)}, u32[]{:S(2)}) collective-permute-start(f32[1,32,1,128]{3,1,2,0:T(8,128)S(1)} %bitcast.254), channel_id=1, source_target_pairs={{0,4},{4,8},{8,12},{12,16},{16,20},{20,24},{24,28},{1,5},{5,9},{9,... | collective-permute-start | bytes 49160 | tf_op jit(solution)/shard_map/ppermute | solution.py:20
  791.9 7.2 collective-permute-start.33
  793.3 5.9 collective-permute-start.34
  796.6 5.7 collective-permute-start.35
Sparse Core Ops, SparseCore 0:
  67.0 260.3 all-reduce.3
  535.0 249.2 all-reduce.5
where the time goes:
time: 892 us; the launch traced here: 888 us
  waiting for transfers between devices  522 us (59%)
  blocking collectives  230 us (26%)
  starting transfers between devices  85.3 us (10%)
  matrix products  16.9 us (2%)
  between operations  15.9 us (2%)
  local copies, waits for them, and re-layouts  11.3 us (1%)
    psum x2, waiting for transfers between devices, local(): gathered = lax.psum(partial_sum, ('region', 'gy', 'gz'))  507 us
    psum x2, blocking collectives, residual_product(): lax.psum(weighted_inner(weight, left, right_vec), ('region', 'gy', 'gz'))  153 us
    psum x1, blocking collectives, local(): lax.psum(weighted_inner(weight, direction, image_vec), ('region', 'gy', '...  77 us
    ppermute x18, starting transfers between devices, padded(): lax.ppermute(tail, axis, [(i, (i + 1) % count) for i in range(ends)])  54.5 us
    ppermute x18, starting transfers between devices, padded(): lax.ppermute(head, axis, [((i + 1) % count, i) for i in range(ends)])  30.7 us
  transfers between devices with their start and end apart: 38, of which 7 were waited for; matrix products, arithmetic and copies ran while one was open for 1% of the time, Pallas kernels for 0%

commit v1 on v0

v1 whole, which is shorter than its diff:
```python
import jax
import jax.numpy as jnp
from jax import lax
from jax.experimental import pallas as pl
from jax.experimental.pallas import tpu as pltpu
from jax.sharding import PartitionSpec as P

AXES = ("region", "gy", "gz")
SIZES = (8, 8, 4)
F32 = jnp.float32
BF16 = jnp.bfloat16
LOADS = 32
FACE = 128
MULT = 768
COARSE = 512
SIDE = 32
HIGHEST = lax.Precision.HIGHEST
VM = pl.BlockSpec(memory_space=pltpu.VMEM)
SM = pl.BlockSpec(memory_space=pltpu.SMEM)


def matmul(left, right):
    return jnp.dot(left, right, preferred_element_type=F32)


def matmul_nt(left, right, precision=None):
    return lax.dot_general(
        left, right, (((1,), (1,)), ((), ())), precision=precision, preferred_element_type=F32
    )


def live_of(counts):
    return (counts[0] > 0).astype(F32)


def coords():
    return [lax.axis_index(axis) for axis in AXES]


def store_sends(sends, faces):
    for e, place in enumerate(coords()):
        odd = place % 2 == 1
        sends[2 * e][...] = jnp.where(odd, faces[2 * e], faces[2 * e + 1])
        sends[2 * e + 1][...] = jnp.where(odd, faces[2 * e + 1], faces[2 * e])


def received_faces(recvs, rows):
    out = []
    for e, place in enumerate(coords()):
        odd = place % 2 == 1
        first, second = recvs[2 * e][rows, :], recvs[2 * e + 1][rows, :]
        lower = jnp.where(odd, first, second)
        upper = jnp.where(odd, second, first)
        out.append(jnp.where(place > 0, lower, 0.0))
        out.append(jnp.where(place < SIZES[e] - 1, upper, 0.0))
    return out


def partner(recvs, pairing, rows=slice(0, LOADS)):
    faces = received_faces(recvs, rows)
    parts = []
    for f in range(6):
        index = jnp.broadcast_to(pairing[0, f : f + 1, :], faces[f].shape)
        parts.append(jnp.take_along_axis(faces[f], index, axis=1))
    return jnp.concatenate(parts, axis=1)


def split_faces(value):
    return [value[:, f * FACE : (f + 1) * FACE] for f in range(6)]


def load_sums(left, right):
    return matmul_nt(jnp.ones((8, MULT), F32), left * right, HIGHEST)


def column(row):
    r = lax.broadcasted_iota(jnp.int32, (LOADS, LOADS), 0)
    c = lax.broadcasted_iota(jnp.int32, (LOADS, LOADS), 1)
    return jnp.sum(jnp.where(r == c, row, 0.0), axis=1, keepdims=True)


def prepare_kernel(counts, loads, *sends):
    live = live_of(counts)
    value = loads[0] * live
    mark = jnp.full((8, FACE), live, F32)
    faces = [jnp.concatenate([face, mark], axis=0) for face in split_faces(value)]
    store_sends(sends, faces)


def precondition(weight, residual, dirichlet):
    scaled = (weight * residual).astype(BF16)
    return weight * matmul(scaled, dirichlet[0])


def first_kernel(counts, loads, pairing, dirichlet, *refs):
    recvs, (resid, weight_ref, terms, dots), sends = refs[:6], refs[6:10], refs[10:]
    live = live_of(counts)
    residual = live * (loads[0] * live + partner(recvs, pairing))
    multiplicity = live * (live + partner(recvs, pairing, slice(LOADS, LOADS + 8)))
    weight = live / jnp.maximum(multiplicity, 1.0)
    weight_ref[...] = weight
    resid[...] = residual
    applied = precondition(weight[0:1], residual, dirichlet)
    terms[...] = applied
    dots[...] = load_sums(residual, applied)
    store_sends(sends, split_faces(applied))


def corner_message(corner_map, corner_terms, scalars):
    place = coords()
    devices = []
    for step in ((0, 0, 0), (1, 0, 0), (-1, 0, 0), None, (0, 1, 0), (0, -1, 0), (0, 0, 1), (0, 0, -1)):
        if step is None:
            devices.append(None)
            continue
        a, b, c = [(p + s + n) % n for p, s, n in zip(place, step, SIZES)]
        devices.append((a * SIZES[1] + b) * SIZES[2] + c)
    row = lax.broadcasted_iota(jnp.int32, (16, FACE), 0)
    target = jnp.full((16, FACE), -1, jnp.int32)
    for index, device in enumerate(devices):
        for which in range(2):
            at = which * 8 + (index % 2) * 4 + index // 2
            if device is not None:
                target = jnp.where(row == at, device * 2 + which, target)
    chosen = (target == corner_map[0:1, :]).astype(F32)
    sums = matmul_nt(chosen, corner_terms, HIGHEST)
    body = jnp.concatenate([sums[0:4], sums[8:12], sums[4:8], sums[12:16]], axis=1)
    zero = jnp.zeros((1, LOADS), F32)
    tail = jnp.concatenate(list(scalars) + [zero] * (4 - len(scalars)), axis=1)
    return jnp.concatenate([body, jnp.broadcast_to(tail, (4, FACE))], axis=0)


def send_message(out, message):
    for peer in range(out.shape[0]):
        out[peer] = message


def second_kernel(counts, pairing, corner_map, schur, coupling, terms, dots, *refs):
    recvs, (z_ref, local_ref, out) = refs[:6], refs[6:]
    live = live_of(counts)
    direction = live * (terms[...] + partner(recvs, pairing))
    dir_bf = direction.astype(BF16)
    local_terms = live * matmul(dir_bf, schur[0])
    corner_terms = live * matmul(dir_bf, coupling[0])
    z_ref[...] = direction
    local_ref[...] = local_terms
    curve = load_sums(direction, local_terms)
    send_message(out, corner_message(corner_map, corner_terms, (dots[0:1], curve[0:1])))


def plane_kernel(got, out):
    rows = lax.broadcasted_iota(jnp.int32, (SIDE, FACE), 0) % SIZES[2]
    lane = lax.broadcasted_iota(jnp.int32, (SIDE, FACE), 1)
    along_b = got[:, 2, :]
    along_c = got[:, 3, :]
    b_up = pltpu.roll(along_b, SIZES[2], 0)
    b_down = pltpu.roll(pltpu.roll(along_b, SIDE - SIZES[2], 0), 64, 1)
    c_up = jnp.where(rows == 0, pltpu.roll(along_c, SIDE - 3, 0), pltpu.roll(along_c, 1, 0))
    c_down = jnp.where(rows == 3, pltpu.roll(along_c, 3, 0), pltpu.roll(along_c, SIDE - 1, 0))
    c_down = pltpu.roll(c_down, 64, 1)
    own = got[:, 0, :] + jnp.where(lane < 64, (b_up + b_down) + (c_up + c_down), 0.0)
    down = got[:, 1, :]
    scalars = jnp.broadcast_to(jnp.sum(got[:, 4, :], axis=0, keepdims=True), (8, FACE))
    for peer in range(SIZES[0]):
        out[peer, 0:32, :] = own
        out[peer, 32:64, :] = down
        out[peer, 64:72, :] = scalars


def coarse_sums(got, scratch):
    pieces = []
    for a in range(SIZES[0]):
        below, above = (a + 7) % 8, (a + 1) % 8
        pieces.append(
            got[a, 0:32, :] + pltpu.roll(got[below, 0:32, :], 64, 1) + got[above, 32:64, :]
        )
    whole = jnp.concatenate(pieces, axis=0)
    scratch[pl.Slice(0, COARSE // 2, 2), :] = whole[:, 0:32]
    scratch[pl.Slice(1, COARSE // 2, 2), :] = whole[:, 32:64]
    scalars = got[0, 64:72, :]
    for a in range(1, SIZES[0]):
        scalars = scalars + got[a, 64:72, :]
    return scratch[...], [scalars[0:1, i * 32 : i * 32 + 32] for i in range(4)]


def coarse_solve(inverse, gathered, corner_map, coupling):
    solved = jnp.dot(
        inverse[...], gathered, precision=HIGHEST, preferred_element_type=F32
    ).astype(BF16)
    row = lax.broadcasted_iota(jnp.int32, (COARSE, FACE), 0)
    chosen = (row == corner_map[0:1, :]).astype(F32).astype(BF16)
    picked = lax.dot_general(
        solved, chosen, (((0,), (0,)), ((), ())), preferred_element_type=F32
    ).astype(BF16)
    energy = jnp.sum(solved.astype(F32) * gathered, axis=0, keepdims=True)
    return matmul_nt(picked, coupling[0]), energy


def third_kernel(counts, corner_map, coupling, inverse, got, local_ref, *refs):
    image_ref, gathered_ref, scalar_ref = refs[:3]
    sends, scratch = refs[3:9], refs[9]
    live = live_of(counts)
    gathered, (resid_dot, local_curve, _, _) = coarse_sums(got, scratch)
    coarse_terms, energy = coarse_solve(inverse, gathered, corner_map, coupling)
    image = live * (local_ref[...] + coarse_terms)
    step_size = resid_dot / (local_curve + energy)
    image_ref[...] = image
    gathered_ref[...] = gathered
    scalar_ref[...] = jnp.concatenate(
        [resid_dot, local_curve, step_size, jnp.zeros((5, LOADS), F32)], axis=0
    )
    store_sends(sends, split_faces(image))


def fourth_kernel(counts, pairing, dirichlet, resid, weight_ref, image_ref, scalar_ref, *refs):
    recvs, (resid_out, terms, dots), sends = refs[:6], refs[6:9], refs[9:]
    live = live_of(counts)
    step_size = column(scalar_ref[2:3, :])
    residual = resid[...] - step_size * (live * (image_ref[...] + partner(recvs, pairing)))
    resid_out[...] = residual
    applied = precondition(weight_ref[0:1, :], residual, dirichlet)
    terms[...] = applied
    dots[...] = load_sums(residual, applied)
    store_sends(sends, split_faces(applied))


def fifth_kernel(counts, pairing, corner_map, schur, coupling, terms, dots, local_ref, *refs):
    recvs, (precond_ref, out) = refs[:6], refs[6:]
    live = live_of(counts)
    precond = live * (terms[...] + partner(recvs, pairing))
    precond_ref[...] = precond
    high = precond.astype(BF16)
    low = (precond - high.astype(F32)).astype(BF16)
    local_terms = live * matmul(high, schur[0])
    both = matmul(jnp.concatenate([high, low], axis=0), coupling[0])
    corner_terms = live * (both[:LOADS] + both[LOADS:])
    square = load_sums(precond, local_terms)
    cross = load_sums(precond, local_ref[...])
    scalars = (dots[0:1], square[0:1], cross[0:1])
    send_message(out, corner_message(corner_map, corner_terms, scalars))


def sixth_kernel(
    counts, corner_map, schur, coupling, inverse, got, gathered_ref, scalar_ref, z_ref, precond_ref, *refs
):
    solution_ref, image_ref, step_ref = refs[:3]
    sends, scratch = refs[3:9], refs[9]
    live = live_of(counts)
    gathered, (new_dot, square, cross, _) = coarse_sums(got, scratch)
    beta = new_dot / scalar_ref[0:1, :]
    gathered = gathered + beta * gathered_ref[...]
    coarse_terms, energy = coarse_solve(inverse, gathered, corner_map, coupling)
    local_curve = square + 2.0 * beta * cross + beta * beta * scalar_ref[1:2, :]
    step_size = new_dot / (local_curve + energy)
    first = z_ref[...]
    direction = precond_ref[...] + column(beta) * first
    local_terms = matmul(direction.astype(BF16), schur[0])
    image = live * (local_terms + coarse_terms)
    image_ref[...] = image
    store_sends(sends, split_faces(image))
    step_ref[...] = jnp.broadcast_to(step_size, (8, LOADS))
    solution_ref[0] = column(scalar_ref[2:3, :]) * first + column(step_size) * direction


def seventh_kernel(counts, pairing, resid, image_ref, step_ref, *refs):
    recvs, (out,) = refs[:6], refs[6:]
    live = live_of(counts)
    image = live * (image_ref[...] + partner(recvs, pairing))
    out[0] = resid[...] - column(step_ref[0:1, :]) * image


def call(kernel, shapes, *operands, scratch=()):
    specs = [SM if operand.shape == (1,) else VM for operand in operands]
    return pl.pallas_call(
        kernel,
        out_shape=[jax.ShapeDtypeStruct(shape, F32) for shape in shapes],
        in_specs=specs,
        out_specs=[VM] * len(shapes),
        scratch_shapes=list(scratch),
        compiler_params=pltpu.CompilerParams(vmem_limit_bytes=32 * 1024 * 1024),
    )(*operands)


def matched(count, start):
    pairs = []
    for low in range(start, count, 2):
        high = (low + 1) % count
        pairs += [(low, high), (high, low)]
    return pairs


def exchange(sends):
    return [
        lax.ppermute(value, AXES[k // 2], matched(SIZES[k // 2], k % 2))
        for k, value in enumerate(sends)
    ]


def spread(message, axes):
    return lax.all_to_all(message, axes, 0, 0)


def local(loads, schur, dirichlet, coupling, coarse_inverse, pairing, corner_map, counts):
    vector = (LOADS, MULT)
    faces = [(LOADS, FACE)] * 6
    small = (8, LOADS)
    solver_scratch = [pltpu.VMEM((COARSE, LOADS), F32)]

    sends = call(prepare_kernel, [(LOADS + 8, FACE)] * 6, counts, loads)
    resid, weight, terms, dots, *sends = call(
        first_kernel, [vector, (8, MULT), vector, small] + faces,
        counts, loads, pairing, dirichlet, *exchange(sends),
    )
    first, local_terms, message = call(
        second_kernel, [vector, vector, (SIDE, 8, FACE)],
        counts, pairing, corner_map, schur, coupling, terms, dots, *exchange(sends),
    )
    (message,) = call(plane_kernel, [(SIZES[0], 72, FACE)], spread(message, ("gy", "gz")))
    image, gathered, scalars, *sends = call(
        third_kernel, [vector, (COARSE, LOADS), small] + faces,
        counts, corner_map, coupling, coarse_inverse, spread(message, "region"), local_terms,
        scratch=solver_scratch,
    )
    resid, terms, dots, *sends = call(
        fourth_kernel, [vector, vector, small] + faces,
        counts, pairing, dirichlet, resid, weight, image, scalars, *exchange(sends),
    )
    precond, message = call(
        fifth_kernel, [vector, (SIDE, 8, FACE)],
        counts, pairing, corner_map, schur, coupling, terms, dots, local_terms, *exchange(sends),
    )
    (message,) = call(plane_kernel, [(SIZES[0], 72, FACE)], spread(message, ("gy", "gz")))
    solution_out, image, step, *sends = call(
        sixth_kernel, [(1,) + vector, vector, small] + faces,
        counts, corner_map, schur, coupling, coarse_inverse, spread(message, "region"),
        gathered, scalars, first, precond, scratch=solver_scratch,
    )
    (residual_out,) = call(
        seventh_kernel, [(1,) + vector],
        counts, pairing, resid, image, step, *exchange(sends),
    )
    return solution_out, residual_out


def solution(mesh):
    block = P(AXES, None, None)
    in_specs = (block, block, block, block, P(), block, P(AXES, None), P(AXES))
    return jax.shard_map(
        local, mesh=mesh, in_specs=in_specs, out_specs=(block, block), check_vma=False
    )
```

time: 892 us -> 115 us (0.13)
  waiting for transfers between devices: 522 us -> 12.6 us
  blocking collectives: 230 us -> 53.2 us
  starting transfers between devices: 85.3 us -> 36.1 us
  matrix products: 16.9 us -> 0 us
  between operations: 15.9 us -> 1.5 us
    psum x2 -> x0, waiting for transfers between devices: 507 us -> none  [local(): gathered = lax.psum(partial_sum, ('region', 'gy', 'gz'))]
    psum x3 -> x0, blocking collectives: 230 us -> none  [the longest x2 153 us: residual_product(): lax.psum(weighted_inner(weight, left, right_vec), ('region', 'gy', 'gz'))]
    all_to_all x0 -> x4, blocking collectives: none -> 53.2 us  [spread(): return lax.all_to_all(message, axes, 0, 0)]
    ppermute x36 -> x30, starting transfers between devices: 85.2 us -> 36.1 us  [exchange(): lax.ppermute(value, AXES[k // 2], matched(SIZES[k // 2], k % 2))]
    dot_general x18 -> x0, matrix products: 16.9 us -> none  [the longest x2 4.1 us: local(): jnp.dot(coarse_inverse, gathered, precision=HIGHEST_PREC)]
  transfers between devices with their start and end apart: 38 -> 30, of which waited for: 7 -> 11; matrix products, arithmetic and copies ran while one was open for 1% -> 1% of each run, Pallas kernels for 0% -> 0%
where the time goes in v1:
time: 115 us; the launch traced here: 114 us
  blocking collectives  53.2 us (46%)
  starting transfers between devices  36.1 us (31%)
  waiting for transfers between devices  12.6 us (11%)
  Pallas kernels  7.7 us (7%)
  local copies, waits for them, and re-layouts  2.87 us (2%)
  between operations  1.5 us (1%)
    all_to_all x4, blocking collectives, spread(): return lax.all_to_all(message, axes, 0, 0)  53.2 us
    ppermute x30, starting transfers between devices, exchange(): lax.ppermute(value, AXES[k // 2], matched(SIZES[k // 2], k % 2))  36.1 us
    ppermute x30, waiting for transfers between devices, exchange(): lax.ppermute(value, AXES[k // 2], matched(SIZES[k // 2], k % 2))  12.6 us
    pallas_call x10, Pallas kernels, call(): pl.pallas_call(kernel, out_shape=[jax.ShapeDtypeStruct(shape, F32) for sh...  7.7 us
    unnamed x15, local copies, waits for them, and re-layouts  2.87 us
  transfers between devices with their start and end apart: 30, of which 11 were waited for; matrix products, arithmetic and copies ran while one was open for 1% of the time, Pallas kernels for 0%

profile of v1, /device:TPU:2, one launch (start us, length us, event | category | flops | bytes accessed | tf_op | source)
XLA Modules:
  0.0 113.9 jit_solution(7134849985397874744)
XLA Ops:
  1.4 0.9 copy-done.5
  2.3 0.1 collective-permute-start
  2.4 3.1 %collective-permute-start.1 = (f32[40,128]{1,0:T(8,128)S(1)}, f32[40,128]{1,0:T(8,128)S(1)}, u32[]{:S(2)}, u32[]{:S(2)}) collective-permute-start(f32[40,128]{1,0:T(8,128)S(1)} %get-tuple-element.51), channel_id=1, source_target_pairs={{32,64},{64,32},{96,128},{128,96},{160,192},{192,160},{224,0},{0,2... | collective-permute-start | bytes 61448 | tf_op jit(solution)/shard_map/ppermute | solution.py:294
  5.5 1.9 %collective-permute-start.2 = (f32[40,128]{1,0:T(8,128)S(1)}, f32[40,128]{1,0:T(8,128)S(1)}, u32[]{:S(2)}, u32[]{:S(2)}) collective-permute-start(f32[40,128]{1,0:T(8,128)S(1)} %get-tuple-element.52), channel_id=1, source_target_pairs={{0,4},{4,0},{8,12},{12,8},{16,20},{20,16},{24,28},{28,24},{1,5},{5... | collective-permute-start | bytes 61448 | tf_op jit(solution)/shard_map/ppermute | solution.py:294
  7.4 4.9 %collective-permute-start.3 = (f32[40,128]{1,0:T(8,128)S(1)}, f32[40,128]{1,0:T(8,128)S(1)}, u32[]{:S(2)}, u32[]{:S(2)}) collective-permute-start(f32[40,128]{1,0:T(8,128)S(1)} %get-tuple-element.53), channel_id=1, source_target_pairs={{4,8},{8,4},{12,16},{16,12},{20,24},{24,20},{28,0},{0,28},{5,9},{9... | collective-permute-start | bytes 61448 | tf_op jit(solution)/shard_map/ppermute | solution.py:294
  12.4 0.5 collective-permute-start.4
  12.9 0.0 collective-permute-done.refs_0_
  12.9 2.2 %collective-permute-start.5 = (f32[40,128]{1,0:T(8,128)S(1)}, f32[40,128]{1,0:T(8,128)S(1)}, u32[]{:S(2)}, u32[]{:S(2)}) collective-permute-start(f32[40,128]{1,0:T(8,128)S(1)} %get-tuple-element.55), channel_id=1, source_target_pairs={{1,2},{2,1},{3,0},{0,3},{5,6},{6,5},{7,4},{4,7},{9,10},{10,9},{11,... | collective-permute-start | bytes 61448 | tf_op jit(solution)/shard_map/ppermute | solution.py:294
  15.1 0.7 copy.13.pairing
  15.8 0.0 collective-permute-done.1.refs_1_
  15.8 0.0 collective-permute-done.2.refs_2_
  15.8 0.4 collective-permute-done.4.refs_4_
  16.2 0.7 collective-permute-done.5.refs_5_
  16.8 1.3 %copy-done.1 = bf16[1,768,768]{2,1,0:T(8,128)(2,1)S(1)} copy-done((bf16[1,768,768]{2,1,0:T(8,128)(2,1)S(1)}, bf16[1,768,768]{2,1,0:T(8,128)(2,1)}, u32[]{:S(2)}) %copy-start.1) | copy-done | bytes 1179672
  18.1 0.6 shard_map.96
  18.7 0.9 collective-permute-start.7
  19.6 0.0 collective-permute-start.8
  19.6 2.0 %collective-permute-start.9 = (f32[32,128]{1,0:T(8,128)S(1)}, f32[32,128]{1,0:T(8,128)S(1)}, u32[]{:S(2)}, u32[]{:S(2)}) collective-permute-start(f32[32,128]{1,0:T(8,128)S(1)} %get-tuple-element.63), channel_id=1, source_target_pairs={{4,8},{8,4},{12,16},{16,12},{20,24},{24,20},{28,0},{0,28},{5,9},{9... | collective-permute-start | bytes 49160 | tf_op jit(solution)/shard_map/ppermute | solution.py:294
  21.6 2.6 %collective-permute-start.10 = (f32[32,128]{1,0:T(8,128)S(1)}, f32[32,128]{1,0:T(8,128)S(1)}, u32[]{:S(2)}, u32[]{:S(2)}) collective-permute-start(f32[32,128]{1,0:T(8,128)S(1)} %get-tuple-element.64), channel_id=1, source_target_pairs={{0,1},{1,0},{2,3},{3,2},{4,5},{5,4},{6,7},{7,6},{8,9},{9,8},{10,11... | collective-permute-start | bytes 49160 | tf_op jit(solution)/shard_map/ppermute | solution.py:294
  24.2 1.5 %collective-permute-start.11 = (f32[32,128]{1,0:T(8,128)S(1)}, f32[32,128]{1,0:T(8,128)S(1)}, u32[]{:S(2)}, u32[]{:S(2)}) collective-permute-start(f32[32,128]{1,0:T(8,128)S(1)} %get-tuple-element.65), channel_id=1, source_target_pairs={{1,2},{2,1},{3,0},{0,3},{5,6},{6,5},{7,4},{4,7},{9,10},{10,9},{11,... | collective-permute-start | bytes 49160 | tf_op jit(solution)/shard_map/ppermute | solution.py:294
  25.7 0.2 collective-permute-done.10.refs_4_
  25.9 2.0 %collective-permute-done.11.refs_5_ = f32[32,128]{1,0:T(8,128)S(1)} collective-permute-done((f32[32,128]{1,0:T(8,128)S(1)}, f32[32,128]{1,0:T(8,128)S(1)}, u32[]{:S(2)}, u32[]{:S(2)}) %collective-permute-start.11) | collective-permute-done | bytes 16416 | tf_op jit(solution)/shard_map/ppermute | solution.py:294
  27.9 0.0 copy-start.3
  27.9 0.7 shard_map.97
  28.6 15.6 %all_to_all.20.got = f32[32,8,128]{2,1,0:T(8,128)S(1)} all-to-all(f32[32,8,128]{2,1,0:T(8,128)S(1)} %get-tuple-element.66), channel_id=1, replica_groups=mesh['region'=8,'gy'=8,'gz'=4] {'gy','gz'}, dimensions={0} | all-to-all | bytes 262144 | tf_op jit(solution)/shard_map/all_to_all | solution.py:300
  44.2 0.1 shard_map.98
  44.3 0.0 copy-start.2
  44.4 10.4 %all_to_all.21.got = f32[8,72,128]{2,1,0:T(8,128)S(1)} all-to-all(f32[8,72,128]{2,1,0:T(8,128)S(1)} %shard_map.98), channel_id=1, replica_groups=mesh['region'=8,'gy'=8,'gz'=4] {'region'}, dimensions={0} | all-to-all | bytes 589824 | tf_op jit(solution)/shard_map/all_to_all | solution.py:300
  54.8 1.6 %shard_map.99 = (f32[32,768]{1,0:T(8,128)S(1)}, f32[512,32]{1,0:T(8,128)S(1)}, f32[8,32]{1,0:T(8,128)S(1)}, f32[32,128]{1,0:T(8,128)S(1)}, f32[32,128]{1,0:T(8,1...) custom-call(s32[1]{0:T(128)S(6)} %copy.15.counts, ...), custom_call_target="tpu_custom_call" | custom-call | tf_op jit(solution)/shard_map/pallas_call | solution.py:274
  56.4 0.1 collective-permute-start.12
  56.5 1.3 %collective-permute-start.13 = (f32[32,128]{1,0:T(8,128)S(1)}, f32[32,128]{1,0:T(8,128)S(1)}, u32[]{:S(2)}, u32[]{:S(2)}) collective-permute-start(f32[32,128]{1,0:T(8,128)S(1)} %get-tuple-element.71), channel_id=1, source_target_pairs={{32,64},{64,32},{96,128},{128,96},{160,192},{192,160},{224,0},{0,2... | collective-permute-start | bytes 49160 | tf_op jit(solution)/shard_map/ppermute | solution.py:294
  57.8 1.4 %collective-permute-start.14 = (f32[32,128]{1,0:T(8,128)S(1)}, f32[32,128]{1,0:T(8,128)S(1)}, u32[]{:S(2)}, u32[]{:S(2)}) collective-permute-start(f32[32,128]{1,0:T(8,128)S(1)} %get-tuple-element.72), channel_id=1, source_target_pairs={{0,4},{4,0},{8,12},{12,8},{16,20},{20,16},{24,28},{28,24},{1,5},{5... | collective-permute-start | bytes 49160 | tf_op jit(solution)/shard_map/ppermute | solution.py:294
  59.1 0.5 collective-permute-start.15
  59.7 1.3 %collective-permute-start.16 = (f32[32,128]{1,0:T(8,128)S(1)}, f32[32,128]{1,0:T(8,128)S(1)}, u32[]{:S(2)}, u32[]{:S(2)}) collective-permute-start(f32[32,128]{1,0:T(8,128)S(1)} %get-tuple-element.74), channel_id=1, source_target_pairs={{0,1},{1,0},{2,3},{3,2},{4,5},{5,4},{6,7},{7,6},{8,9},{9,8},{10,11... | collective-permute-start | bytes 49160 | tf_op jit(solution)/shard_map/ppermute | solution.py:294
  61.0 0.8 collective-permute-start.17
  61.8 0.0 collective-permute-done.14.refs_2_
  61.8 2.3 %collective-permute-done.15.refs_3_ = f32[32,128]{1,0:T(8,128)S(1)} collective-permute-done((f32[32,128]{1,0:T(8,128)S(1)}, f32[32,128]{1,0:T(8,128)S(1)}, u32[]{:S(2)}, u32[]{:S(2)}) %collective-permute-start.15) | collective-permute-done | bytes 16416 | tf_op jit(solution)/shard_map/ppermute | solution.py:294
  64.1 0.7 collective-permute-done.17.refs_5_
  64.8 0.6 shard_map.100
  65.4 0.7 collective-permute-start.19
  66.0 1.0 collective-permute-start.20
  67.0 1.8 %collective-permute-start.21 = (f32[32,128]{1,0:T(8,128)S(1)}, f32[32,128]{1,0:T(8,128)S(1)}, u32[]{:S(2)}, u32[]{:S(2)}) collective-permute-start(f32[32,128]{1,0:T(8,128)S(1)} %get-tuple-element.81), channel_id=1, source_target_pairs={{4,8},{8,4},{12,16},{16,12},{20,24},{24,20},{28,0},{0,28},{5,9},{9... | collective-permute-start | bytes 49160 | tf_op jit(solution)/shard_map/ppermute | solution.py:294
  68.8 1.9 %collective-permute-start.22 = (f32[32,128]{1,0:T(8,128)S(1)}, f32[32,128]{1,0:T(8,128)S(1)}, u32[]{:S(2)}, u32[]{:S(2)}) collective-permute-start(f32[32,128]{1,0:T(8,128)S(1)} %get-tuple-element.82), channel_id=1, source_target_pairs={{0,1},{1,0},{2,3},{3,2},{4,5},{5,4},{6,7},{7,6},{8,9},{9,8},{10,11... | collective-permute-start | bytes 49160 | tf_op jit(solution)/shard_map/ppermute | solution.py:294
  70.7 0.0 collective-permute-done.18.refs_0_
  70.7 0.3 collective-permute-start.23
  71.0 1.0 collective-permute-done.21.refs_3_
  72.0 0.6 collective-permute-done.22.refs_4_
  72.5 1.9 %collective-permute-done.23.refs_5_ = f32[32,128]{1,0:T(8,128)S(1)} collective-permute-done((f32[32,128]{1,0:T(8,128)S(1)}, f32[32,128]{1,0:T(8,128)S(1)}, u32[]{:S(2)}, u32[]{:S(2)}) %collective-permute-start.23) | collective-permute-done | bytes 16416 | tf_op jit(solution)/shard_map/ppermute | solution.py:294
  74.4 0.7 shard_map.101
  75.1 15.9 %all_to_all.22.got = f32[32,8,128]{2,1,0:T(8,128)S(1)} all-to-all(f32[32,8,128]{2,1,0:T(8,128)S(1)} %get-tuple-element.84), channel_id=1, replica_groups=mesh['region'=8,'gy'=8,'gz'=4] {'gy','gz'}, dimensions={0} | all-to-all | bytes 262144 | tf_op jit(solution)/shard_map/all_to_all | solution.py:300
  91.0 0.1 shard_map.102
  91.1 11.3 %all_to_all.23.got = f32[8,72,128]{2,1,0:T(8,128)S(1)} all-to-all(f32[8,72,128]{2,1,0:T(8,128)S(1)} %shard_map.102), channel_id=1, replica_groups=mesh['region'=8,'gy'=8,'gz'=4] {'region'}, dimensions={0} | all-to-all | bytes 589824 | tf_op jit(solution)/shard_map/all_to_all | solution.py:300
  102.4 2.5 %shard_map.103 = (f32[1,32,768]{2,1,0:T(8,128)}, f32[32,768]{1,0:T(8,128)S(1)}, f32[8,32]{1,0:T(8,128)S(1)}, f32[32,128]{1,0:T(8,128)S(1)}, f32[32,128]{1,0:T(8,...) custom-call(s32[1]{0:T(128)S(6)} %copy.15.counts, ...), custom_call_target="tpu_custom_call" | custom-call | tf_op jit(solution)/shard_map/pallas_call | solution.py:274
  104.9 0.0 collective-permute-start.24
  104.9 1.3 %collective-permute-start.25 = (f32[32,128]{1,0:T(8,128)S(1)}, f32[32,128]{1,0:T(8,128)S(1)}, u32[]{:S(2)}, u32[]{:S(2)}) collective-permute-start(f32[32,128]{1,0:T(8,128)S(1)} %get-tuple-element.93), channel_id=1, source_target_pairs={{32,64},{64,32},{96,128},{128,96},{160,192},{192,160},{224,0},{0,2... | collective-permute-start | bytes 49160 | tf_op jit(solution)/shard_map/ppermute | solution.py:294
  106.2 1.4 %collective-permute-start.26 = (f32[32,128]{1,0:T(8,128)S(1)}, f32[32,128]{1,0:T(8,128)S(1)}, u32[]{:S(2)}, u32[]{:S(2)}) collective-permute-start(f32[32,128]{1,0:T(8,128)S(1)} %get-tuple-element.94), channel_id=1, source_target_pairs={{0,4},{4,0},{8,12},{12,8},{16,20},{20,16},{24,28},{28,24},{1,5},{5... | collective-permute-start | bytes 49160 | tf_op jit(solution)/shard_map/ppermute | solution.py:294
  107.5 0.4 collective-permute-start.27
  107.9 1.5 %collective-permute-start.28 = (f32[32,128]{1,0:T(8,128)S(1)}, f32[32,128]{1,0:T(8,128)S(1)}, u32[]{:S(2)}, u32[]{:S(2)}) collective-permute-start(f32[32,128]{1,0:T(8,128)S(1)} %get-tuple-element.96), channel_id=1, source_target_pairs={{0,1},{1,0},{2,3},{3,2},{4,5},{5,4},{6,7},{7,6},{8,9},{9,8},{10,11... | collective-permute-start | bytes 49160 | tf_op jit(solution)/shard_map/ppermute | solution.py:294
  109.4 0.0 collective-permute-done.24.refs_0_
  109.4 0.8 collective-permute-start.29
  110.2 2.3 %collective-permute-done.27.refs_3_ = f32[32,128]{1,0:T(8,128)S(1)} collective-permute-done((f32[32,128]{1,0:T(8,128)S(1)}, f32[32,128]{1,0:T(8,128)S(1)}, u32[]{:S(2)}, u32[]{:S(2)}) %collective-permute-start.27) | collective-permute-done | bytes 16416 | tf_op jit(solution)/shard_map/ppermute | solution.py:294
  112.5 0.0 collective-permute-done.28.refs_4_
  112.5 0.7 collective-permute-done.29.refs_5_
  113.2 0.8 shard_map.104
  (25 shorter events, 0.1 us)
Async XLA Ops:
  0.6 27.3 %copy-start = (bf16[1,768,768]{2,1,0:T(8,128)(2,1)S(1)}, bf16[1,768,768]{2,1,0:T(8,128)(2,1)}, u32[]{:S(2)}) copy-start(bf16[1,768,768]{2,1,0:T(8,128)(2,1)} %schur.5) | copy-start | bytes 3538948
  1.4 0.9 copy-start.5
  2.3 10.6 %collective-permute-start = (f32[40,128]{1,0:T(8,128)S(1)}, f32[40,128]{1,0:T(8,128)S(1)}, u32[]{:S(2)}, u32[]{:S(2)}) collective-permute-start(f32[40,128]{1,0:T(8,128)S(1)} %get-tuple-element.50), channel_id=1, source_target_pairs={{0,32},{32,0},{64,96},{96,64},{128,160},{160,128},{192,224},{224,1... | collective-permute-start | bytes 61448 | tf_op jit(solution)/shard_map/ppermute | solution.py:294
  2.4 13.4 %collective-permute-start.1 = (f32[40,128]{1,0:T(8,128)S(1)}, f32[40,128]{1,0:T(8,128)S(1)}, u32[]{:S(2)}, u32[]{:S(2)}) collective-permute-start(f32[40,128]{1,0:T(8,128)S(1)} %get-tuple-element.51), channel_id=1, source_target_pairs={{32,64},{64,32},{96,128},{128,96},{160,192},{192,160},{224,0},{0,2... | collective-permute-start | bytes 61448 | tf_op jit(solution)/shard_map/ppermute | solution.py:294
  5.5 10.2 %collective-permute-start.2 = (f32[40,128]{1,0:T(8,128)S(1)}, f32[40,128]{1,0:T(8,128)S(1)}, u32[]{:S(2)}, u32[]{:S(2)}) collective-permute-start(f32[40,128]{1,0:T(8,128)S(1)} %get-tuple-element.52), channel_id=1, source_target_pairs={{0,4},{4,0},{8,12},{12,8},{16,20},{20,16},{24,28},{28,24},{1,5},{5... | collective-permute-start | bytes 61448 | tf_op jit(solution)/shard_map/ppermute | solution.py:294
  7.4 8.3 %collective-permute-start.3 = (f32[40,128]{1,0:T(8,128)S(1)}, f32[40,128]{1,0:T(8,128)S(1)}, u32[]{:S(2)}, u32[]{:S(2)}) collective-permute-start(f32[40,128]{1,0:T(8,128)S(1)} %get-tuple-element.53), channel_id=1, source_target_pairs={{4,8},{8,4},{12,16},{16,12},{20,24},{24,20},{28,0},{0,28},{5,9},{9... | collective-permute-start | bytes 61448 | tf_op jit(solution)/shard_map/ppermute | solution.py:294
  12.4 3.8 %collective-permute-start.4 = (f32[40,128]{1,0:T(8,128)S(1)}, f32[40,128]{1,0:T(8,128)S(1)}, u32[]{:S(2)}, u32[]{:S(2)}) collective-permute-start(f32[40,128]{1,0:T(8,128)S(1)} %get-tuple-element.54), channel_id=1, source_target_pairs={{0,1},{1,0},{2,3},{3,2},{4,5},{5,4},{6,7},{7,6},{8,9},{9,8},{10,11... | collective-permute-start | bytes 61448 | tf_op jit(solution)/shard_map/ppermute | solution.py:294
  12.9 3.9 %collective-permute-start.5 = (f32[40,128]{1,0:T(8,128)S(1)}, f32[40,128]{1,0:T(8,128)S(1)}, u32[]{:S(2)}, u32[]{:S(2)}) collective-permute-start(f32[40,128]{1,0:T(8,128)S(1)} %get-tuple-element.55), channel_id=1, source_target_pairs={{1,2},{2,1},{3,0},{0,3},{5,6},{6,5},{7,4},{4,7},{9,10},{10,9},{11,... | collective-permute-start | bytes 61448 | tf_op jit(solution)/shard_map/ppermute | solution.py:294
  16.8 1.3 %copy-start.1 = (bf16[1,768,768]{2,1,0:T(8,128)(2,1)S(1)}, bf16[1,768,768]{2,1,0:T(8,128)(2,1)}, u32[]{:S(2)}) copy-start(bf16[1,768,768]{2,1,0:T(8,128)(2,1)} %dirichlet.3) | copy-start | bytes 3538948
  18.1 9.8 %copy-start.4 = (bf16[1,768,128]{2,1,0:T(8,128)(2,1)S(1)}, bf16[1,768,128]{2,1,0:T(8,128)(2,1)}, u32[]{:S(2)}) copy-start(bf16[1,768,128]{2,1,0:T(8,128)(2,1)} %coupling.7) | copy-start | bytes 589828
  18.1 9.8 %copy-start.6 = (s32[1,128]{1,0:T(1,128)S(1)}, s32[1,128]{1,0:T(1,128)}, u32[]{:S(2)}) copy-start(s32[1,128]{1,0:T(1,128)} %corner_map.7) | copy-start | bytes 1540
  18.7 5.5 %collective-permute-start.6 = (f32[32,128]{1,0:T(8,128)S(1)}, f32[32,128]{1,0:T(8,128)S(1)}, u32[]{:S(2)}, u32[]{:S(2)}) collective-permute-start(f32[32,128]{1,0:T(8,128)S(1)} %get-tuple-element.60), channel_id=1, source_target_pairs={{0,32},{32,0},{64,96},{96,64},{128,160},{160,128},{192,224},{224,1... | collective-permute-start | bytes 49160 | tf_op jit(solution)/shard_map/ppermute | solution.py:294
  18.7 7.0 %collective-permute-start.7 = (f32[32,128]{1,0:T(8,128)S(1)}, f32[32,128]{1,0:T(8,128)S(1)}, u32[]{:S(2)}, u32[]{:S(2)}) collective-permute-start(f32[32,128]{1,0:T(8,128)S(1)} %get-tuple-element.61), channel_id=1, source_target_pairs={{32,64},{64,32},{96,128},{128,96},{160,192},{192,160},{224,0},{0,2... | collective-permute-start | bytes 49160 | tf_op jit(solution)/shard_map/ppermute | solution.py:294
  19.6 6.1 %collective-permute-start.8 = (f32[32,128]{1,0:T(8,128)S(1)}, f32[32,128]{1,0:T(8,128)S(1)}, u32[]{:S(2)}, u32[]{:S(2)}) collective-permute-start(f32[32,128]{1,0:T(8,128)S(1)} %get-tuple-element.62), channel_id=1, source_target_pairs={{0,4},{4,0},{8,12},{12,8},{16,20},{20,16},{24,28},{28,24},{1,5},{5... | collective-permute-start | bytes 49160 | tf_op jit(solution)/shard_map/ppermute | solution.py:294
  19.6 6.1 %collective-permute-start.9 = (f32[32,128]{1,0:T(8,128)S(1)}, f32[32,128]{1,0:T(8,128)S(1)}, u32[]{:S(2)}, u32[]{:S(2)}) collective-permute-start(f32[32,128]{1,0:T(8,128)S(1)} %get-tuple-element.63), channel_id=1, source_target_pairs={{4,8},{8,4},{12,16},{16,12},{20,24},{24,20},{28,0},{0,28},{5,9},{9... | collective-permute-start | bytes 49160 | tf_op jit(solution)/shard_map/ppermute | solution.py:294
  21.6 4.3 %collective-permute-start.10 = (f32[32,128]{1,0:T(8,128)S(1)}, f32[32,128]{1,0:T(8,128)S(1)}, u32[]{:S(2)}, u32[]{:S(2)}) collective-permute-start(f32[32,128]{1,0:T(8,128)S(1)} %get-tuple-element.64), channel_id=1, source_target_pairs={{0,1},{1,0},{2,3},{3,2},{4,5},{5,4},{6,7},{7,6},{8,9},{9,8},{10,11... | collective-permute-start | bytes 49160 | tf_op jit(solution)/shard_map/ppermute | solution.py:294
  24.2 3.7 %collective-permute-start.11 = (f32[32,128]{1,0:T(8,128)S(1)}, f32[32,128]{1,0:T(8,128)S(1)}, u32[]{:S(2)}, u32[]{:S(2)}) collective-permute-start(f32[32,128]{1,0:T(8,128)S(1)} %get-tuple-element.65), channel_id=1, source_target_pairs={{1,2},{2,1},{3,0},{0,3},{5,6},{6,5},{7,4},{4,7},{9,10},{10,9},{11,... | collective-permute-start | bytes 49160 | tf_op jit(solution)/shard_map/ppermute | solution.py:294
  27.9 26.9 %copy-start.3 = (f32[512,512]{1,0:T(8,128)S(1)}, f32[512,512]{1,0:T(8,128)}, u32[]{:S(2)}) copy-start(f32[512,512]{1,0:T(8,128)} %inverse.3) | copy-start | bytes 3145732
  44.3 20.4 %copy-start.2 = (bf16[1,768,768]{2,1,0:T(8,128)(2,1)S(1)}, bf16[1,768,768]{2,1,0:T(8,128)(2,1)}, u32[]{:S(2)}) copy-start(bf16[1,768,768]{2,1,0:T(8,128)(2,1)} %dirichlet.3) | copy-start | bytes 3538948
  56.4 4.6 %collective-permute-start.12 = (f32[32,128]{1,0:T(8,128)S(1)}, f32[32,128]{1,0:T(8,128)S(1)}, u32[]{:S(2)}, u32[]{:S(2)}) collective-permute-start(f32[32,128]{1,0:T(8,128)S(1)} %get-tuple-element.70), channel_id=1, source_target_pairs={{0,32},{32,0},{64,96},{96,64},{128,160},{160,128},{192,224},{224,1... | collective-permute-start | bytes 49160 | tf_op jit(solution)/shard_map/ppermute | solution.py:294
  56.5 5.3 %collective-permute-start.13 = (f32[32,128]{1,0:T(8,128)S(1)}, f32[32,128]{1,0:T(8,128)S(1)}, u32[]{:S(2)}, u32[]{:S(2)}) collective-permute-start(f32[32,128]{1,0:T(8,128)S(1)} %get-tuple-element.71), channel_id=1, source_target_pairs={{32,64},{64,32},{96,128},{128,96},{160,192},{192,160},{224,0},{0,2... | collective-permute-start | bytes 49160 | tf_op jit(solution)/shard_map/ppermute | solution.py:294
  57.8 4.1 %collective-permute-start.14 = (f32[32,128]{1,0:T(8,128)S(1)}, f32[32,128]{1,0:T(8,128)S(1)}, u32[]{:S(2)}, u32[]{:S(2)}) collective-permute-start(f32[32,128]{1,0:T(8,128)S(1)} %get-tuple-element.72), channel_id=1, source_target_pairs={{0,4},{4,0},{8,12},{12,8},{16,20},{20,16},{24,28},{28,24},{1,5},{5... | collective-permute-start | bytes 49160 | tf_op jit(solution)/shard_map/ppermute | solution.py:294
  59.1 4.9 %collective-permute-start.15 = (f32[32,128]{1,0:T(8,128)S(1)}, f32[32,128]{1,0:T(8,128)S(1)}, u32[]{:S(2)}, u32[]{:S(2)}) collective-permute-start(f32[32,128]{1,0:T(8,128)S(1)} %get-tuple-element.73), channel_id=1, source_target_pairs={{4,8},{8,4},{12,16},{16,12},{20,24},{24,20},{28,0},{0,28},{5,9},{9... | collective-permute-start | bytes 49160 | tf_op jit(solution)/shard_map/ppermute | solution.py:294
  59.7 4.4 %collective-permute-start.16 = (f32[32,128]{1,0:T(8,128)S(1)}, f32[32,128]{1,0:T(8,128)S(1)}, u32[]{:S(2)}, u32[]{:S(2)}) collective-permute-start(f32[32,128]{1,0:T(8,128)S(1)} %get-tuple-element.74), channel_id=1, source_target_pairs={{0,1},{1,0},{2,3},{3,2},{4,5},{5,4},{6,7},{7,6},{8,9},{9,8},{10,11... | collective-permute-start | bytes 49160 | tf_op jit(solution)/shard_map/ppermute | solution.py:294
  61.0 3.7 %collective-permute-start.17 = (f32[32,128]{1,0:T(8,128)S(1)}, f32[32,128]{1,0:T(8,128)S(1)}, u32[]{:S(2)}, u32[]{:S(2)}) collective-permute-start(f32[32,128]{1,0:T(8,128)S(1)} %get-tuple-element.75), channel_id=1, source_target_pairs={{1,2},{2,1},{3,0},{0,3},{5,6},{6,5},{7,4},{4,7},{9,10},{10,9},{11,... | collective-permute-start | bytes 49160 | tf_op jit(solution)/shard_map/ppermute | solution.py:294
  65.3 5.3 %collective-permute-start.18 = (f32[32,128]{1,0:T(8,128)S(1)}, f32[32,128]{1,0:T(8,128)S(1)}, u32[]{:S(2)}, u32[]{:S(2)}) collective-permute-start(f32[32,128]{1,0:T(8,128)S(1)} %get-tuple-element.78), channel_id=1, source_target_pairs={{0,32},{32,0},{64,96},{96,64},{128,160},{160,128},{192,224},{224,1... | collective-permute-start | bytes 49160 | tf_op jit(solution)/shard_map/ppermute | solution.py:294
  65.4 5.6 %collective-permute-start.19 = (f32[32,128]{1,0:T(8,128)S(1)}, f32[32,128]{1,0:T(8,128)S(1)}, u32[]{:S(2)}, u32[]{:S(2)}) collective-permute-start(f32[32,128]{1,0:T(8,128)S(1)} %get-tuple-element.79), channel_id=1, source_target_pairs={{32,64},{64,32},{96,128},{128,96},{160,192},{192,160},{224,0},{0,2... | collective-permute-start | bytes 49160 | tf_op jit(solution)/shard_map/ppermute | solution.py:294
  66.0 4.9 %collective-permute-start.20 = (f32[32,128]{1,0:T(8,128)S(1)}, f32[32,128]{1,0:T(8,128)S(1)}, u32[]{:S(2)}, u32[]{:S(2)}) collective-permute-start(f32[32,128]{1,0:T(8,128)S(1)} %get-tuple-element.80), channel_id=1, source_target_pairs={{0,4},{4,0},{8,12},{12,8},{16,20},{20,16},{24,28},{28,24},{1,5},{5... | collective-permute-start | bytes 49160 | tf_op jit(solution)/shard_map/ppermute | solution.py:294
  67.0 4.9 %collective-permute-start.21 = (f32[32,128]{1,0:T(8,128)S(1)}, f32[32,128]{1,0:T(8,128)S(1)}, u32[]{:S(2)}, u32[]{:S(2)}) collective-permute-start(f32[32,128]{1,0:T(8,128)S(1)} %get-tuple-element.81), channel_id=1, source_target_pairs={{4,8},{8,4},{12,16},{16,12},{20,24},{24,20},{28,0},{0,28},{5,9},{9... | collective-permute-start | bytes 49160 | tf_op jit(solution)/shard_map/ppermute | solution.py:294
  68.8 3.7 %collective-permute-start.22 = (f32[32,128]{1,0:T(8,128)S(1)}, f32[32,128]{1,0:T(8,128)S(1)}, u32[]{:S(2)}, u32[]{:S(2)}) collective-permute-start(f32[32,128]{1,0:T(8,128)S(1)} %get-tuple-element.82), channel_id=1, source_target_pairs={{0,1},{1,0},{2,3},{3,2},{4,5},{5,4},{6,7},{7,6},{8,9},{9,8},{10,11... | collective-permute-start | bytes 49160 | tf_op jit(solution)/shard_map/ppermute | solution.py:294
  70.7 3.7 %collective-permute-start.23 = (f32[32,128]{1,0:T(8,128)S(1)}, f32[32,128]{1,0:T(8,128)S(1)}, u32[]{:S(2)}, u32[]{:S(2)}) collective-permute-start(f32[32,128]{1,0:T(8,128)S(1)} %get-tuple-element.83), channel_id=1, source_target_pairs={{1,2},{2,1},{3,0},{0,3},{5,6},{6,5},{7,4},{4,7},{9,10},{10,9},{11,... | collective-permute-start | bytes 49160 | tf_op jit(solution)/shard_map/ppermute | solution.py:294
  104.9 4.5 %collective-permute-start.24 = (f32[32,128]{1,0:T(8,128)S(1)}, f32[32,128]{1,0:T(8,128)S(1)}, u32[]{:S(2)}, u32[]{:S(2)}) collective-permute-start(f32[32,128]{1,0:T(8,128)S(1)} %get-tuple-element.92), channel_id=1, source_target_pairs={{0,32},{32,0},{64,96},{96,64},{128,160},{160,128},{192,224},{224,1... | collective-permute-start | bytes 49160 | tf_op jit(solution)/shard_map/ppermute | solution.py:294
  104.9 5.3 %collective-permute-start.25 = (f32[32,128]{1,0:T(8,128)S(1)}, f32[32,128]{1,0:T(8,128)S(1)}, u32[]{:S(2)}, u32[]{:S(2)}) collective-permute-start(f32[32,128]{1,0:T(8,128)S(1)} %get-tuple-element.93), channel_id=1, source_target_pairs={{32,64},{64,32},{96,128},{128,96},{160,192},{192,160},{224,0},{0,2... | collective-permute-start | bytes 49160 | tf_op jit(solution)/shard_map/ppermute | solution.py:294
  106.2 4.0 %collective-permute-start.26 = (f32[32,128]{1,0:T(8,128)S(1)}, f32[32,128]{1,0:T(8,128)S(1)}, u32[]{:S(2)}, u32[]{:S(2)}) collective-permute-start(f32[32,128]{1,0:T(8,128)S(1)} %get-tuple-element.94), channel_id=1, source_target_pairs={{0,4},{4,0},{8,12},{12,8},{16,20},{20,16},{24,28},{28,24},{1,5},{5... | collective-permute-start | bytes 49160 | tf_op jit(solution)/shard_map/ppermute | solution.py:294
  107.5 4.9 %collective-permute-start.27 = (f32[32,128]{1,0:T(8,128)S(1)}, f32[32,128]{1,0:T(8,128)S(1)}, u32[]{:S(2)}, u32[]{:S(2)}) collective-permute-start(f32[32,128]{1,0:T(8,128)S(1)} %get-tuple-element.95), channel_id=1, source_target_pairs={{4,8},{8,4},{12,16},{16,12},{20,24},{24,20},{28,0},{0,28},{5,9},{9... | collective-permute-start | bytes 49160 | tf_op jit(solution)/shard_map/ppermute | solution.py:294
  107.9 4.6 %collective-permute-start.28 = (f32[32,128]{1,0:T(8,128)S(1)}, f32[32,128]{1,0:T(8,128)S(1)}, u32[]{:S(2)}, u32[]{:S(2)}) collective-permute-start(f32[32,128]{1,0:T(8,128)S(1)} %get-tuple-element.96), channel_id=1, source_target_pairs={{0,1},{1,0},{2,3},{3,2},{4,5},{5,4},{6,7},{7,6},{8,9},{9,8},{10,11... | collective-permute-start | bytes 49160 | tf_op jit(solution)/shard_map/ppermute | solution.py:294
  109.4 3.7 %collective-permute-start.29 = (f32[32,128]{1,0:T(8,128)S(1)}, f32[32,128]{1,0:T(8,128)S(1)}, u32[]{:S(2)}, u32[]{:S(2)}) collective-permute-start(f32[32,128]{1,0:T(8,128)S(1)} %get-tuple-element.97), channel_id=1, source_target_pairs={{1,2},{2,1},{3,0},{0,3},{5,6},{6,5},{7,4},{4,7},{9,10},{10,9},{11,... | collective-permute-start | bytes 49160 | tf_op jit(solution)/shard_map/ppermute | solution.py:294

commit v2 on v1

--- a/solution.py
+++ b/solution.py
@@ -16,7 +16,7 @@
 SIDE = 32
 HIGHEST = lax.Precision.HIGHEST
 VM = pl.BlockSpec(memory_space=pltpu.VMEM)
-SM = pl.BlockSpec(memory_space=pltpu.SMEM)
+SMEM = pl.BlockSpec(memory_space=pltpu.SMEM)
 
 
 def matmul(left, right):
@@ -27,10 +27,6 @@
     return lax.dot_general(
         left, right, (((1,), (1,)), ((), ())), precision=precision, preferred_element_type=F32
     )
-
-
-def live_of(counts):
-    return (counts[0] > 0).astype(F32)
 
 
 def coords():
@@ -60,7 +56,7 @@
     faces = received_faces(recvs, rows)
     parts = []
     for f in range(6):
-        index = jnp.broadcast_to(pairing[0, f : f + 1, :], faces[f].shape)
+        index = jnp.broadcast_to(pairing[f], faces[f].shape)
         parts.append(jnp.take_along_axis(faces[f], index, axis=1))
     return jnp.concatenate(parts, axis=1)
 
@@ -79,12 +75,19 @@
     return jnp.sum(jnp.where(r == c, row, 0.0), axis=1, keepdims=True)
 
 
-def prepare_kernel(counts, loads, *sends):
-    live = live_of(counts)
-    value = loads[0] * live
-    mark = jnp.full((8, FACE), live, F32)
+def living_kernel(counts, live_ref):
+    live_ref[...] = jnp.full((8, FACE), (counts[0] > 0).astype(F32), F32)
+
+
+def prepare_kernel(live_ref, loads, *sends):
+    mark = live_ref[...]
+    value = loads[0] * mark[0:1, 0:1]
     faces = [jnp.concatenate([face, mark], axis=0) for face in split_faces(value)]
     store_sends(sends, faces)
+
+
+def copy_kernel(source, out):
+    out[...] = source[...]
 
 
 def precondition(weight, residual, dirichlet):
@@ -92,9 +95,9 @@
     return weight * matmul(scaled, dirichlet[0])
 
 
-def first_kernel(counts, loads, pairing, dirichlet, *refs):
+def first_kernel(live_ref, loads, pairing, dirichlet, *refs):
     recvs, (resid, weight_ref, terms, dots), sends = refs[:6], refs[6:10], refs[10:]
-    live = live_of(counts)
+    live = live_ref[0:1, 0:1]
     residual = live * (loads[0] * live + partner(recvs, pairing))
     multiplicity = live * (live + partner(recvs, pairing, slice(LOADS, LOADS + 8)))
     weight = live / jnp.maximum(multiplicity, 1.0)
@@ -135,9 +138,9 @@
         out[peer] = message
 
 
-def second_kernel(counts, pairing, corner_map, schur, coupling, terms, dots, *refs):
+def second_kernel(live_ref, pairing, corner_map, schur, coupling, terms, dots, *refs):
     recvs, (z_ref, local_ref, out) = refs[:6], refs[6:]
-    live = live_of(counts)
+    live = live_ref[0:1, 0:1]
     direction = live * (terms[...] + partner(recvs, pairing))
     dir_bf = direction.astype(BF16)
     local_terms = live * matmul(dir_bf, schur[0])
@@ -161,32 +164,41 @@
     own = got[:, 0, :] + jnp.where(lane < 64, (b_up + b_down) + (c_up + c_down), 0.0)
     down = got[:, 1, :]
     scalars = jnp.broadcast_to(jnp.sum(got[:, 4, :], axis=0, keepdims=True), (8, FACE))
+    half = SIDE // 2
+    down = jnp.where(lane[:half] < 64, down[:half], pltpu.roll(down[half:], 64, 1))
     for peer in range(SIZES[0]):
         out[peer, 0:32, :] = own
-        out[peer, 32:64, :] = down
-        out[peer, 64:72, :] = scalars
+        out[peer, 32:48, :] = down
+        out[peer, 48:56, :] = scalars
 
 
 def coarse_sums(got, scratch):
     pieces = []
     for a in range(SIZES[0]):
         below, above = (a + 7) % 8, (a + 1) % 8
-        pieces.append(
-            got[a, 0:32, :] + pltpu.roll(got[below, 0:32, :], 64, 1) + got[above, 32:64, :]
-        )
+        down = got[above, 32:48, :]
+        down = jnp.concatenate([down, pltpu.roll(down, 64, 1)], axis=0)
+        pieces.append(got[a, 0:32, :] + pltpu.roll(got[below, 0:32, :], 64, 1) + down)
     whole = jnp.concatenate(pieces, axis=0)
     scratch[pl.Slice(0, COARSE // 2, 2), :] = whole[:, 0:32]
     scratch[pl.Slice(1, COARSE // 2, 2), :] = whole[:, 32:64]
-    scalars = got[0, 64:72, :]
+    scalars = got[0, 48:56, :]
     for a in range(1, SIZES[0]):
-        scalars = scalars + got[a, 64:72, :]
+        scalars = scalars + got[a, 48:56, :]
     return scratch[...], [scalars[0:1, i * 32 : i * 32 + 32] for i in range(4)]
 
 
+def halves(value):
+    high = value.astype(BF16)
+    return high, (value - high.astype(F32)).astype(BF16)
+
+
 def coarse_solve(inverse, gathered, corner_map, coupling):
-    solved = jnp.dot(
-        inverse[...], gathered, precision=HIGHEST, preferred_element_type=F32
-    ).astype(BF16)
+    mat_high, mat_low = halves(inverse[...])
+    vec_high, vec_low = halves(gathered)
+    both = matmul(mat_high, jnp.concatenate([vec_high, vec_low], axis=1))
+    solved = both[:, :LOADS] + (both[:, LOADS:] + matmul(mat_low, vec_high))
+    solved = solved.astype(BF16)
     row = lax.broadcasted_iota(jnp.int32, (COARSE, FACE), 0)
     chosen = (row == corner_map[0:1, :]).astype(F32).astype(BF16)
     picked = lax.dot_general(
@@ -196,10 +208,10 @@
     return matmul_nt(picked, coupling[0]), energy
 
 
-def third_kernel(counts, corner_map, coupling, inverse, got, local_ref, *refs):
+def third_kernel(live_ref, corner_map, coupling, inverse, got, local_ref, *refs):
     image_ref, gathered_ref, scalar_ref = refs[:3]
     sends, scratch = refs[3:9], refs[9]
-    live = live_of(counts)
+    live = live_ref[0:1, 0:1]
     gathered, (resid_dot, local_curve, _, _) = coarse_sums(got, scratch)
     coarse_terms, energy = coarse_solve(inverse, gathered, corner_map, coupling)
     image = live * (local_ref[...] + coarse_terms)
@@ -212,9 +224,9 @@
     store_sends(sends, split_faces(image))
 
 
-def fourth_kernel(counts, pairing, dirichlet, resid, weight_ref, image_ref, scalar_ref, *refs):
+def fourth_kernel(live_ref, pairing, dirichlet, resid, weight_ref, image_ref, scalar_ref, *refs):
     recvs, (resid_out, terms, dots), sends = refs[:6], refs[6:9], refs[9:]
-    live = live_of(counts)
+    live = live_ref[0:1, 0:1]
     step_size = column(scalar_ref[2:3, :])
     residual = resid[...] - step_size * (live * (image_ref[...] + partner(recvs, pairing)))
     resid_out[...] = residual
@@ -224,13 +236,12 @@
     store_sends(sends, split_faces(applied))
 
 
-def fifth_kernel(counts, pairing, corner_map, schur, coupling, terms, dots, local_ref, *refs):
+def fifth_kernel(live_ref, pairing, corner_map, schur, coupling, terms, dots, local_ref, *refs):
     recvs, (precond_ref, out) = refs[:6], refs[6:]
-    live = live_of(counts)
+    live = live_ref[0:1, 0:1]
     precond = live * (terms[...] + partner(recvs, pairing))
     precond_ref[...] = precond
-    high = precond.astype(BF16)
-    low = (precond - high.astype(F32)).astype(BF16)
+    high, low = halves(precond)
     local_terms = live * matmul(high, schur[0])
     both = matmul(jnp.concatenate([high, low], axis=0), coupling[0])
     corner_terms = live * (both[:LOADS] + both[LOADS:])
@@ -241,11 +252,11 @@
 
 
 def sixth_kernel(
-    counts, corner_map, schur, coupling, inverse, got, gathered_ref, scalar_ref, z_ref, precond_ref, *refs
+    live_ref, corner_map, schur, coupling, inverse, got, gathered_ref, scalar_ref, z_ref, precond_ref, *refs
 ):
     solution_ref, image_ref, step_ref = refs[:3]
     sends, scratch = refs[3:9], refs[9]
-    live = live_of(counts)
+    live = live_ref[0:1, 0:1]
     gathered, (new_dot, square, cross, _) = coarse_sums(got, scratch)
     beta = new_dot / scalar_ref[0:1, :]
     gathered = gathered + beta * gathered_ref[...]
@@ -262,22 +273,25 @@
     solution_ref[0] = column(scalar_ref[2:3, :]) * first + column(step_size) * direction
 
 
-def seventh_kernel(counts, pairing, resid, image_ref, step_ref, *refs):
+def seventh_kernel(live_ref, pairing, resid, image_ref, step_ref, *refs):
     recvs, (out,) = refs[:6], refs[6:]
-    live = live_of(counts)
+    live = live_ref[0:1, 0:1]
     image = live * (image_ref[...] + partner(recvs, pairing))
     out[0] = resid[...] - column(step_ref[0:1, :]) * image
 
 
-def call(kernel, shapes, *operands, scratch=()):
-    specs = [SM if operand.shape == (1,) else VM for operand in operands]
+def call(kernel, shapes, *operands, scratch=(), cost=None, spec=VM):
     return pl.pallas_call(
         kernel,
-        out_shape=[jax.ShapeDtypeStruct(shape, F32) for shape in shapes],
-        in_specs=specs,
+        out_shape=[
+            shape if hasattr(shape, "dtype") else jax.ShapeDtypeStruct(shape, F32)
+            for shape in shapes
+        ],
+        in_specs=[spec] * len(operands),
         out_specs=[VM] * len(shapes),
         scratch_shapes=list(scratch),
-        compiler_params=pltpu.CompilerParams(vmem_limit_bytes=32 * 1024 * 1024),
+        cost_estimate=cost,
+        compiler_params=pltpu.CompilerParams(vmem_limit_bytes=32 << 20),
     )(*operands)
 
 
@@ -306,38 +320,43 @@
     small = (8, LOADS)
     solver_scratch = [pltpu.VMEM((COARSE, LOADS), F32)]
 
-    sends = call(prepare_kernel, [(LOADS + 8, FACE)] * 6, counts, loads)
+    pairing = pairing.reshape(6, 1, FACE)
+    cost = pl.CostEstimate(flops=0, bytes_accessed=4 << 20, transcendentals=0)
+    (live,) = call(living_kernel, [(8, FACE)], counts, spec=SMEM, cost=cost)
+    sends = call(prepare_kernel, [(LOADS + 8, FACE)] * 6, live, loads)
+    (dirichlet,) = call(copy_kernel, [jax.ShapeDtypeStruct(dirichlet.shape, BF16)], dirichlet)
+    inverse = coarse_inverse
     resid, weight, terms, dots, *sends = call(
         first_kernel, [vector, (8, MULT), vector, small] + faces,
-        counts, loads, pairing, dirichlet, *exchange(sends),
+        live, loads, pairing, dirichlet, *exchange(sends),
     )
     first, local_terms, message = call(
         second_kernel, [vector, vector, (SIDE, 8, FACE)],
-        counts, pairing, corner_map, schur, coupling, terms, dots, *exchange(sends),
-    )
-    (message,) = call(plane_kernel, [(SIZES[0], 72, FACE)], spread(message, ("gy", "gz")))
+        live, pairing, corner_map, schur, coupling, terms, dots, *exchange(sends),
+    )
+    (message,) = call(plane_kernel, [(SIZES[0], 56, FACE)], spread(message, ("gy", "gz")))
     image, gathered, scalars, *sends = call(
         third_kernel, [vector, (COARSE, LOADS), small] + faces,
-        counts, corner_map, coupling, coarse_inverse, spread(message, "region"), local_terms,
+        live, corner_map, coupling, inverse, spread(message, "region"), local_terms,
         scratch=solver_scratch,
     )
     resid, terms, dots, *sends = call(
         fourth_kernel, [vector, vector, small] + faces,
-        counts, pairing, dirichlet, resid, weight, image, scalars, *exchange(sends),
+        live, pairing, dirichlet, resid, weight, image, scalars, *exchange(sends),
     )
     precond, message = call(
         fifth_kernel, [vector, (SIDE, 8, FACE)],
-        counts, pairing, corner_map, schur, coupling, terms, dots, local_terms, *exchange(sends),
-    )
-    (message,) = call(plane_kernel, [(SIZES[0], 72, FACE)], spread(message, ("gy", "gz")))
+        live, pairing, corner_map, schur, coupling, terms, dots, local_terms, *exchange(sends),
+    )
+    (message,) = call(plane_kernel, [(SIZES[0], 56, FACE)], spread(message, ("gy", "gz")))
     solution_out, image, step, *sends = call(
         sixth_kernel, [(1,) + vector, vector, small] + faces,
-        counts, corner_map, schur, coupling, coarse_inverse, spread(message, "region"),
+        live, corner_map, schur, coupling, inverse, spread(message, "region"),
         gathered, scalars, first, precond, scratch=solver_scratch,
     )
     (residual_out,) = call(
         seventh_kernel, [(1,) + vector],
-        counts, pairing, resid, image, step, *exchange(sends),
+        live, pairing, resid, image, step, *exchange(sends),
     )
     return solution_out, residual_out
 

time: 115 us -> 111 us (0.965)
    pallas_call x10 -> x12, Pallas kernels: 7.7 us -> 6.78 us  [call(): pl.pallas_call(kernel, out_shape=[shape if hasattr(shape, 'dtype') else j...]
    unnamed x15 -> x16, local copies, waits for them, and re-layouts: 2.87 us -> 2.59 us
  transfers between devices with their start and end apart: 30 -> 30, of which waited for: 11 -> 10; matrix products, arithmetic and copies ran while one was open for 1% -> 0% of each run, Pallas kernels for 0% -> 0%
where the time goes in v2:
time: 111 us; the launch traced here: 110 us
  blocking collectives  52.1 us (47%)
  starting transfers between devices  35.2 us (32%)
  waiting for transfers between devices  11.9 us (11%)
  Pallas kernels  6.78 us (6%)
  local copies, waits for them, and re-layouts  2.59 us (2%)
  between operations  1.46 us (1%)
    all_to_all x4, blocking collectives, spread(): return lax.all_to_all(message, axes, 0, 0)  52.1 us
    ppermute x30, starting transfers between devices, exchange(): lax.ppermute(value, AXES[k // 2], matched(SIZES[k // 2], k % 2))  35.2 us
    ppermute x30, waiting for transfers between devices, exchange(): lax.ppermute(value, AXES[k // 2], matched(SIZES[k // 2], k % 2))  11.9 us
    pallas_call x12, Pallas kernels, call(): pl.pallas_call(kernel, out_shape=[shape if hasattr(shape, 'dtype') else j...  6.78 us
    unnamed x16, local copies, waits for them, and re-layouts  2.59 us
  transfers between devices with their start and end apart: 30, of which 10 were waited for; matrix products, arithmetic and copies ran while one was open for 0% of the time, Pallas kernels for 0%

profile of v2, /device:TPU:2, one launch (start us, length us, event | category | flops | bytes accessed | tf_op | source)
XLA Modules:
  0.0 110.1 jit_solution(12547319070576095552)
XLA Ops:
  1.3 0.0 copy-start.4
  1.3 0.9 copy-done.4
  2.2 0.1 collective-permute-start
  2.3 3.1 %collective-permute-start.1 = (f32[40,128]{1,0:T(8,128)S(1)}, f32[40,128]{1,0:T(8,128)S(1)}, u32[]{:S(2)}, u32[]{:S(2)}) collective-permute-start(f32[40,128]{1,0:T(8,128)S(1)} %get-tuple-element.51), channel_id=1, source_target_pairs={{32,64},{64,32},{96,128},{128,96},{160,192},{192,160},{224,0},{0,2... | collective-permute-start | bytes 61448 | tf_op jit(solution)/shard_map/ppermute | solution.py:308
  5.5 1.9 %collective-permute-start.2 = (f32[40,128]{1,0:T(8,128)S(1)}, f32[40,128]{1,0:T(8,128)S(1)}, u32[]{:S(2)}, u32[]{:S(2)}) collective-permute-start(f32[40,128]{1,0:T(8,128)S(1)} %get-tuple-element.52), channel_id=1, source_target_pairs={{0,4},{4,0},{8,12},{12,8},{16,20},{20,16},{24,28},{28,24},{1,5},{5... | collective-permute-start | bytes 61448 | tf_op jit(solution)/shard_map/ppermute | solution.py:308
  7.4 4.9 %collective-permute-start.3 = (f32[40,128]{1,0:T(8,128)S(1)}, f32[40,128]{1,0:T(8,128)S(1)}, u32[]{:S(2)}, u32[]{:S(2)}) collective-permute-start(f32[40,128]{1,0:T(8,128)S(1)} %get-tuple-element.53), channel_id=1, source_target_pairs={{4,8},{8,4},{12,16},{16,12},{20,24},{24,20},{28,0},{0,28},{5,9},{9... | collective-permute-start | bytes 61448 | tf_op jit(solution)/shard_map/ppermute | solution.py:308
  12.3 0.5 collective-permute-start.4
  12.9 2.2 %collective-permute-start.5 = (f32[40,128]{1,0:T(8,128)S(1)}, f32[40,128]{1,0:T(8,128)S(1)}, u32[]{:S(2)}, u32[]{:S(2)}) collective-permute-start(f32[40,128]{1,0:T(8,128)S(1)} %get-tuple-element.55), channel_id=1, source_target_pairs={{1,2},{2,1},{3,0},{0,3},{5,6},{6,5},{7,4},{4,7},{9,10},{10,9},{11,... | collective-permute-start | bytes 61448 | tf_op jit(solution)/shard_map/ppermute | solution.py:308
  15.0 1.3 %copy-done.3 = bf16[1,768,768]{2,1,0:T(8,128)(2,1)S(1)} copy-done((bf16[1,768,768]{2,1,0:T(8,128)(2,1)S(1)}, bf16[1,768,768]{2,1,0:T(8,128)(2,1)}, u32[]{:S(2)}) %copy-start.3) | copy-done | bytes 1179672
  16.3 0.1 shard_map.96.dirichlet
  16.4 0.0 copy-start
  16.4 0.0 copy-start.2
  16.4 0.0 copy-start.7
  16.4 0.0 collective-permute-done.1.refs_1_
  16.4 0.0 collective-permute-done.4.refs_4_
  16.4 0.3 collective-permute-done.5.refs_5_
  16.8 0.4 copy-done.5
  17.2 0.6 shard_map.98
  17.8 0.0 collective-permute-start.6
  17.8 0.9 collective-permute-start.7
  18.6 2.0 %collective-permute-start.9 = (f32[32,128]{1,0:T(8,128)S(1)}, f32[32,128]{1,0:T(8,128)S(1)}, u32[]{:S(2)}, u32[]{:S(2)}) collective-permute-start(f32[32,128]{1,0:T(8,128)S(1)} %get-tuple-element.63), channel_id=1, source_target_pairs={{4,8},{8,4},{12,16},{16,12},{20,24},{24,20},{28,0},{0,28},{5,9},{9... | collective-permute-start | bytes 49160 | tf_op jit(solution)/shard_map/ppermute | solution.py:308
  20.7 2.2 %collective-permute-start.10 = (f32[32,128]{1,0:T(8,128)S(1)}, f32[32,128]{1,0:T(8,128)S(1)}, u32[]{:S(2)}, u32[]{:S(2)}) collective-permute-start(f32[32,128]{1,0:T(8,128)S(1)} %get-tuple-element.64), channel_id=1, source_target_pairs={{0,1},{1,0},{2,3},{3,2},{4,5},{5,4},{6,7},{7,6},{8,9},{9,8},{10,11... | collective-permute-start | bytes 49160 | tf_op jit(solution)/shard_map/ppermute | solution.py:308
  22.8 1.5 %collective-permute-start.11 = (f32[32,128]{1,0:T(8,128)S(1)}, f32[32,128]{1,0:T(8,128)S(1)}, u32[]{:S(2)}, u32[]{:S(2)}) collective-permute-start(f32[32,128]{1,0:T(8,128)S(1)} %get-tuple-element.65), channel_id=1, source_target_pairs={{1,2},{2,1},{3,0},{0,3},{5,6},{6,5},{7,4},{4,7},{9,10},{10,9},{11,... | collective-permute-start | bytes 49160 | tf_op jit(solution)/shard_map/ppermute | solution.py:308
  24.3 0.0 collective-permute-done.7.refs_1_
  24.3 0.2 collective-permute-done.10.refs_4_
  24.5 2.0 %collective-permute-done.11.refs_5_ = f32[32,128]{1,0:T(8,128)S(1)} collective-permute-done((f32[32,128]{1,0:T(8,128)S(1)}, f32[32,128]{1,0:T(8,128)S(1)}, u32[]{:S(2)}, u32[]{:S(2)}) %collective-permute-start.11) | collective-permute-done | bytes 16416 | tf_op jit(solution)/shard_map/ppermute | solution.py:308
  26.6 0.0 copy-start.1
  26.6 0.7 shard_map.99
  27.3 15.6 %all_to_all.20.got = f32[32,8,128]{2,1,0:T(8,128)S(1)} all-to-all(f32[32,8,128]{2,1,0:T(8,128)S(1)} %get-tuple-element.66), channel_id=1, replica_groups=mesh['region'=8,'gy'=8,'gz'=4] {'gy','gz'}, dimensions={0} | all-to-all | bytes 262144 | tf_op jit(solution)/shard_map/all_to_all | solution.py:314
  42.9 0.1 shard_map.100
  43.0 9.6 %all_to_all.21.got = f32[8,56,128]{2,1,0:T(8,128)S(1)} all-to-all(f32[8,56,128]{2,1,0:T(8,128)S(1)} %shard_map.100), channel_id=1, replica_groups=mesh['region'=8,'gy'=8,'gz'=4] {'region'}, dimensions={0} | all-to-all | bytes 458752 | tf_op jit(solution)/shard_map/all_to_all | solution.py:314
  52.6 1.1 shard_map.101
  53.7 0.1 collective-permute-start.12
  53.8 1.3 %collective-permute-start.13 = (f32[32,128]{1,0:T(8,128)S(1)}, f32[32,128]{1,0:T(8,128)S(1)}, u32[]{:S(2)}, u32[]{:S(2)}) collective-permute-start(f32[32,128]{1,0:T(8,128)S(1)} %get-tuple-element.71), channel_id=1, source_target_pairs={{32,64},{64,32},{96,128},{128,96},{160,192},{192,160},{224,0},{0,2... | collective-permute-start | bytes 49160 | tf_op jit(solution)/shard_map/ppermute | solution.py:308
  55.1 1.4 %collective-permute-start.14 = (f32[32,128]{1,0:T(8,128)S(1)}, f32[32,128]{1,0:T(8,128)S(1)}, u32[]{:S(2)}, u32[]{:S(2)}) collective-permute-start(f32[32,128]{1,0:T(8,128)S(1)} %get-tuple-element.72), channel_id=1, source_target_pairs={{0,4},{4,0},{8,12},{12,8},{16,20},{20,16},{24,28},{28,24},{1,5},{5... | collective-permute-start | bytes 49160 | tf_op jit(solution)/shard_map/ppermute | solution.py:308
  56.4 0.5 collective-permute-start.15
  57.0 1.3 %collective-permute-start.16 = (f32[32,128]{1,0:T(8,128)S(1)}, f32[32,128]{1,0:T(8,128)S(1)}, u32[]{:S(2)}, u32[]{:S(2)}) collective-permute-start(f32[32,128]{1,0:T(8,128)S(1)} %get-tuple-element.74), channel_id=1, source_target_pairs={{0,1},{1,0},{2,3},{3,2},{4,5},{5,4},{6,7},{7,6},{8,9},{9,8},{10,11... | collective-permute-start | bytes 49160 | tf_op jit(solution)/shard_map/ppermute | solution.py:308
  58.3 0.0 collective-permute-done.12.refs_0_
  58.3 0.8 collective-permute-start.17
  59.1 0.0 collective-permute-done.13.refs_1_
  59.1 2.3 %collective-permute-done.15.refs_3_ = f32[32,128]{1,0:T(8,128)S(1)} collective-permute-done((f32[32,128]{1,0:T(8,128)S(1)}, f32[32,128]{1,0:T(8,128)S(1)}, u32[]{:S(2)}, u32[]{:S(2)}) %collective-permute-start.15) | collective-permute-done | bytes 16416 | tf_op jit(solution)/shard_map/ppermute | solution.py:308
  61.4 0.7 collective-permute-done.17.refs_5_
  62.0 0.6 shard_map.102
  62.7 0.2 collective-permute-start.19
  62.9 0.9 collective-permute-start.20
  63.7 1.9 %collective-permute-start.21 = (f32[32,128]{1,0:T(8,128)S(1)}, f32[32,128]{1,0:T(8,128)S(1)}, u32[]{:S(2)}, u32[]{:S(2)}) collective-permute-start(f32[32,128]{1,0:T(8,128)S(1)} %get-tuple-element.81), channel_id=1, source_target_pairs={{4,8},{8,4},{12,16},{16,12},{20,24},{24,20},{28,0},{0,28},{5,9},{9... | collective-permute-start | bytes 49160 | tf_op jit(solution)/shard_map/ppermute | solution.py:308
  65.7 1.9 %collective-permute-start.22 = (f32[32,128]{1,0:T(8,128)S(1)}, f32[32,128]{1,0:T(8,128)S(1)}, u32[]{:S(2)}, u32[]{:S(2)}) collective-permute-start(f32[32,128]{1,0:T(8,128)S(1)} %get-tuple-element.82), channel_id=1, source_target_pairs={{0,1},{1,0},{2,3},{3,2},{4,5},{5,4},{6,7},{7,6},{8,9},{9,8},{10,11... | collective-permute-start | bytes 49160 | tf_op jit(solution)/shard_map/ppermute | solution.py:308
  67.5 0.3 collective-permute-start.23
  67.8 0.9 collective-permute-done.21.refs_3_
  68.7 0.7 collective-permute-done.22.refs_4_
  69.4 1.9 %collective-permute-done.23.refs_5_ = f32[32,128]{1,0:T(8,128)S(1)} collective-permute-done((f32[32,128]{1,0:T(8,128)S(1)}, f32[32,128]{1,0:T(8,128)S(1)}, u32[]{:S(2)}, u32[]{:S(2)}) %collective-permute-start.23) | collective-permute-done | bytes 16416 | tf_op jit(solution)/shard_map/ppermute | solution.py:308
  71.3 0.7 shard_map.103
  72.0 15.8 %all_to_all.22.got = f32[32,8,128]{2,1,0:T(8,128)S(1)} all-to-all(f32[32,8,128]{2,1,0:T(8,128)S(1)} %get-tuple-element.84), channel_id=1, replica_groups=mesh['region'=8,'gy'=8,'gz'=4] {'gy','gz'}, dimensions={0} | all-to-all | bytes 262144 | tf_op jit(solution)/shard_map/all_to_all | solution.py:314
  87.8 0.1 shard_map.104
  87.9 11.1 %all_to_all.23.got = f32[8,56,128]{2,1,0:T(8,128)S(1)} all-to-all(f32[8,56,128]{2,1,0:T(8,128)S(1)} %shard_map.104), channel_id=1, replica_groups=mesh['region'=8,'gy'=8,'gz'=4] {'region'}, dimensions={0} | all-to-all | bytes 458752 | tf_op jit(solution)/shard_map/all_to_all | solution.py:314
  99.0 2.0 %shard_map.105 = (f32[1,32,768]{2,1,0:T(8,128)}, f32[32,768]{1,0:T(8,128)S(1)}, f32[8,32]{1,0:T(8,128)S(1)}, f32[32,128]{1,0:T(8,128)S(1)}, f32[32,128]{1,0:T(8,...) custom-call(f32[8,128]{1,0:T(8,128)S(1)} %shard_map.95.live_ref, ...), custom_call_target="tpu_custom_call" | custom-call | tf_op jit(solution)/shard_map/pallas_call | solution.py:284
  101.0 1.3 %collective-permute-start.25 = (f32[32,128]{1,0:T(8,128)S(1)}, f32[32,128]{1,0:T(8,128)S(1)}, u32[]{:S(2)}, u32[]{:S(2)}) collective-permute-start(f32[32,128]{1,0:T(8,128)S(1)} %get-tuple-element.93), channel_id=1, source_target_pairs={{32,64},{64,32},{96,128},{128,96},{160,192},{192,160},{224,0},{0,2... | collective-permute-start | bytes 49160 | tf_op jit(solution)/shard_map/ppermute | solution.py:308
  102.3 1.4 %collective-permute-start.26 = (f32[32,128]{1,0:T(8,128)S(1)}, f32[32,128]{1,0:T(8,128)S(1)}, u32[]{:S(2)}, u32[]{:S(2)}) collective-permute-start(f32[32,128]{1,0:T(8,128)S(1)} %get-tuple-element.94), channel_id=1, source_target_pairs={{0,4},{4,0},{8,12},{12,8},{16,20},{20,16},{24,28},{28,24},{1,5},{5... | collective-permute-start | bytes 49160 | tf_op jit(solution)/shard_map/ppermute | solution.py:308
  103.7 0.4 collective-permute-start.27
  104.1 1.5 %collective-permute-start.28 = (f32[32,128]{1,0:T(8,128)S(1)}, f32[32,128]{1,0:T(8,128)S(1)}, u32[]{:S(2)}, u32[]{:S(2)}) collective-permute-start(f32[32,128]{1,0:T(8,128)S(1)} %get-tuple-element.96), channel_id=1, source_target_pairs={{0,1},{1,0},{2,3},{3,2},{4,5},{5,4},{6,7},{7,6},{8,9},{9,8},{10,11... | collective-permute-start | bytes 49160 | tf_op jit(solution)/shard_map/ppermute | solution.py:308
  105.5 0.8 collective-permute-start.29
  106.3 2.3 %collective-permute-done.27.refs_3_ = f32[32,128]{1,0:T(8,128)S(1)} collective-permute-done((f32[32,128]{1,0:T(8,128)S(1)}, f32[32,128]{1,0:T(8,128)S(1)}, u32[]{:S(2)}, u32[]{:S(2)}) %collective-permute-start.27) | collective-permute-done | bytes 16416 | tf_op jit(solution)/shard_map/ppermute | solution.py:308
  108.6 0.7 collective-permute-done.29.refs_5_
  109.3 0.8 shard_map.106
  (28 shorter events, 0.1 us)
Async XLA Ops:
  1.3 0.9 copy-start.4
  2.2 10.6 %collective-permute-start = (f32[40,128]{1,0:T(8,128)S(1)}, f32[40,128]{1,0:T(8,128)S(1)}, u32[]{:S(2)}, u32[]{:S(2)}) collective-permute-start(f32[40,128]{1,0:T(8,128)S(1)} %get-tuple-element.50), channel_id=1, source_target_pairs={{0,32},{32,0},{64,96},{96,64},{128,160},{160,128},{192,224},{224,1... | collective-permute-start | bytes 61448 | tf_op jit(solution)/shard_map/ppermute | solution.py:308
  2.3 14.1 %collective-permute-start.1 = (f32[40,128]{1,0:T(8,128)S(1)}, f32[40,128]{1,0:T(8,128)S(1)}, u32[]{:S(2)}, u32[]{:S(2)}) collective-permute-start(f32[40,128]{1,0:T(8,128)S(1)} %get-tuple-element.51), channel_id=1, source_target_pairs={{32,64},{64,32},{96,128},{128,96},{160,192},{192,160},{224,0},{0,2... | collective-permute-start | bytes 61448 | tf_op jit(solution)/shard_map/ppermute | solution.py:308
  5.5 11.0 %collective-permute-start.2 = (f32[40,128]{1,0:T(8,128)S(1)}, f32[40,128]{1,0:T(8,128)S(1)}, u32[]{:S(2)}, u32[]{:S(2)}) collective-permute-start(f32[40,128]{1,0:T(8,128)S(1)} %get-tuple-element.52), channel_id=1, source_target_pairs={{0,4},{4,0},{8,12},{12,8},{16,20},{20,16},{24,28},{28,24},{1,5},{5... | collective-permute-start | bytes 61448 | tf_op jit(solution)/shard_map/ppermute | solution.py:308
  7.4 9.1 %collective-permute-start.3 = (f32[40,128]{1,0:T(8,128)S(1)}, f32[40,128]{1,0:T(8,128)S(1)}, u32[]{:S(2)}, u32[]{:S(2)}) collective-permute-start(f32[40,128]{1,0:T(8,128)S(1)} %get-tuple-element.53), channel_id=1, source_target_pairs={{4,8},{8,4},{12,16},{16,12},{20,24},{24,20},{28,0},{0,28},{5,9},{9... | collective-permute-start | bytes 61448 | tf_op jit(solution)/shard_map/ppermute | solution.py:308
  12.3 4.1 %collective-permute-start.4 = (f32[40,128]{1,0:T(8,128)S(1)}, f32[40,128]{1,0:T(8,128)S(1)}, u32[]{:S(2)}, u32[]{:S(2)}) collective-permute-start(f32[40,128]{1,0:T(8,128)S(1)} %get-tuple-element.54), channel_id=1, source_target_pairs={{0,1},{1,0},{2,3},{3,2},{4,5},{5,4},{6,7},{7,6},{8,9},{9,8},{10,11... | collective-permute-start | bytes 61448 | tf_op jit(solution)/shard_map/ppermute | solution.py:308
  12.9 3.9 %collective-permute-start.5 = (f32[40,128]{1,0:T(8,128)S(1)}, f32[40,128]{1,0:T(8,128)S(1)}, u32[]{:S(2)}, u32[]{:S(2)}) collective-permute-start(f32[40,128]{1,0:T(8,128)S(1)} %get-tuple-element.55), channel_id=1, source_target_pairs={{1,2},{2,1},{3,0},{0,3},{5,6},{6,5},{7,4},{4,7},{9,10},{10,9},{11,... | collective-permute-start | bytes 61448 | tf_op jit(solution)/shard_map/ppermute | solution.py:308
  15.0 1.3 %copy-start.3 = (bf16[1,768,768]{2,1,0:T(8,128)(2,1)S(1)}, bf16[1,768,768]{2,1,0:T(8,128)(2,1)}, u32[]{:S(2)}) copy-start(bf16[1,768,768]{2,1,0:T(8,128)(2,1)} %source.1) | copy-start | bytes 3538948
  16.3 0.9 copy-start.5
  16.3 0.9 copy-start.6
  16.4 10.2 %copy-start = (bf16[1,768,768]{2,1,0:T(8,128)(2,1)S(1)}, bf16[1,768,768]{2,1,0:T(8,128)(2,1)}, u32[]{:S(2)}) copy-start(bf16[1,768,768]{2,1,0:T(8,128)(2,1)} %schur.5) | copy-start | bytes 3538948
  16.4 10.2 %copy-start.2 = (bf16[1,768,128]{2,1,0:T(8,128)(2,1)S(1)}, bf16[1,768,128]{2,1,0:T(8,128)(2,1)}, u32[]{:S(2)}) copy-start(bf16[1,768,128]{2,1,0:T(8,128)(2,1)} %coupling.7) | copy-start | bytes 589828
  16.4 10.2 %copy-start.7 = (s32[1,128]{1,0:T(1,128)S(1)}, s32[1,128]{1,0:T(1,128)}, u32[]{:S(2)}) copy-start(s32[1,128]{1,0:T(1,128)} %corner_map.7) | copy-start | bytes 1540
  17.8 5.1 %collective-permute-start.6 = (f32[32,128]{1,0:T(8,128)S(1)}, f32[32,128]{1,0:T(8,128)S(1)}, u32[]{:S(2)}, u32[]{:S(2)}) collective-permute-start(f32[32,128]{1,0:T(8,128)S(1)} %get-tuple-element.60), channel_id=1, source_target_pairs={{0,32},{32,0},{64,96},{96,64},{128,160},{160,128},{192,224},{224,1... | collective-permute-start | bytes 49160 | tf_op jit(solution)/shard_map/ppermute | solution.py:308
  17.8 6.6 %collective-permute-start.7 = (f32[32,128]{1,0:T(8,128)S(1)}, f32[32,128]{1,0:T(8,128)S(1)}, u32[]{:S(2)}, u32[]{:S(2)}) collective-permute-start(f32[32,128]{1,0:T(8,128)S(1)} %get-tuple-element.61), channel_id=1, source_target_pairs={{32,64},{64,32},{96,128},{128,96},{160,192},{192,160},{224,0},{0,2... | collective-permute-start | bytes 49160 | tf_op jit(solution)/shard_map/ppermute | solution.py:308
  18.6 5.7 %collective-permute-start.8 = (f32[32,128]{1,0:T(8,128)S(1)}, f32[32,128]{1,0:T(8,128)S(1)}, u32[]{:S(2)}, u32[]{:S(2)}) collective-permute-start(f32[32,128]{1,0:T(8,128)S(1)} %get-tuple-element.62), channel_id=1, source_target_pairs={{0,4},{4,0},{8,12},{12,8},{16,20},{20,16},{24,28},{28,24},{1,5},{5... | collective-permute-start | bytes 49160 | tf_op jit(solution)/shard_map/ppermute | solution.py:308
  18.6 5.7 %collective-permute-start.9 = (f32[32,128]{1,0:T(8,128)S(1)}, f32[32,128]{1,0:T(8,128)S(1)}, u32[]{:S(2)}, u32[]{:S(2)}) collective-permute-start(f32[32,128]{1,0:T(8,128)S(1)} %get-tuple-element.63), channel_id=1, source_target_pairs={{4,8},{8,4},{12,16},{16,12},{20,24},{24,20},{28,0},{0,28},{5,9},{9... | collective-permute-start | bytes 49160 | tf_op jit(solution)/shard_map/ppermute | solution.py:308
  20.7 3.9 %collective-permute-start.10 = (f32[32,128]{1,0:T(8,128)S(1)}, f32[32,128]{1,0:T(8,128)S(1)}, u32[]{:S(2)}, u32[]{:S(2)}) collective-permute-start(f32[32,128]{1,0:T(8,128)S(1)} %get-tuple-element.64), channel_id=1, source_target_pairs={{0,1},{1,0},{2,3},{3,2},{4,5},{5,4},{6,7},{7,6},{8,9},{9,8},{10,11... | collective-permute-start | bytes 49160 | tf_op jit(solution)/shard_map/ppermute | solution.py:308
  22.8 3.7 %collective-permute-start.11 = (f32[32,128]{1,0:T(8,128)S(1)}, f32[32,128]{1,0:T(8,128)S(1)}, u32[]{:S(2)}, u32[]{:S(2)}) collective-permute-start(f32[32,128]{1,0:T(8,128)S(1)} %get-tuple-element.65), channel_id=1, source_target_pairs={{1,2},{2,1},{3,0},{0,3},{5,6},{6,5},{7,4},{4,7},{9,10},{10,9},{11,... | collective-permute-start | bytes 49160 | tf_op jit(solution)/shard_map/ppermute | solution.py:308
  26.6 26.0 %copy-start.1 = (f32[512,512]{1,0:T(8,128)S(1)}, f32[512,512]{1,0:T(8,128)}, u32[]{:S(2)}) copy-start(f32[512,512]{1,0:T(8,128)} %inverse.3) | copy-start | bytes 3145732
  53.7 4.6 %collective-permute-start.12 = (f32[32,128]{1,0:T(8,128)S(1)}, f32[32,128]{1,0:T(8,128)S(1)}, u32[]{:S(2)}, u32[]{:S(2)}) collective-permute-start(f32[32,128]{1,0:T(8,128)S(1)} %get-tuple-element.70), channel_id=1, source_target_pairs={{0,32},{32,0},{64,96},{96,64},{128,160},{160,128},{192,224},{224,1... | collective-permute-start | bytes 49160 | tf_op jit(solution)/shard_map/ppermute | solution.py:308
  53.8 5.3 %collective-permute-start.13 = (f32[32,128]{1,0:T(8,128)S(1)}, f32[32,128]{1,0:T(8,128)S(1)}, u32[]{:S(2)}, u32[]{:S(2)}) collective-permute-start(f32[32,128]{1,0:T(8,128)S(1)} %get-tuple-element.71), channel_id=1, source_target_pairs={{32,64},{64,32},{96,128},{128,96},{160,192},{192,160},{224,0},{0,2... | collective-permute-start | bytes 49160 | tf_op jit(solution)/shard_map/ppermute | solution.py:308
  55.1 4.1 %collective-permute-start.14 = (f32[32,128]{1,0:T(8,128)S(1)}, f32[32,128]{1,0:T(8,128)S(1)}, u32[]{:S(2)}, u32[]{:S(2)}) collective-permute-start(f32[32,128]{1,0:T(8,128)S(1)} %get-tuple-element.72), channel_id=1, source_target_pairs={{0,4},{4,0},{8,12},{12,8},{16,20},{20,16},{24,28},{28,24},{1,5},{5... | collective-permute-start | bytes 49160 | tf_op jit(solution)/shard_map/ppermute | solution.py:308
  56.4 4.9 %collective-permute-start.15 = (f32[32,128]{1,0:T(8,128)S(1)}, f32[32,128]{1,0:T(8,128)S(1)}, u32[]{:S(2)}, u32[]{:S(2)}) collective-permute-start(f32[32,128]{1,0:T(8,128)S(1)} %get-tuple-element.73), channel_id=1, source_target_pairs={{4,8},{8,4},{12,16},{16,12},{20,24},{24,20},{28,0},{0,28},{5,9},{9... | collective-permute-start | bytes 49160 | tf_op jit(solution)/shard_map/ppermute | solution.py:308
  57.0 4.4 %collective-permute-start.16 = (f32[32,128]{1,0:T(8,128)S(1)}, f32[32,128]{1,0:T(8,128)S(1)}, u32[]{:S(2)}, u32[]{:S(2)}) collective-permute-start(f32[32,128]{1,0:T(8,128)S(1)} %get-tuple-element.74), channel_id=1, source_target_pairs={{0,1},{1,0},{2,3},{3,2},{4,5},{5,4},{6,7},{7,6},{8,9},{9,8},{10,11... | collective-permute-start | bytes 49160 | tf_op jit(solution)/shard_map/ppermute | solution.py:308
  58.3 3.7 %collective-permute-start.17 = (f32[32,128]{1,0:T(8,128)S(1)}, f32[32,128]{1,0:T(8,128)S(1)}, u32[]{:S(2)}, u32[]{:S(2)}) collective-permute-start(f32[32,128]{1,0:T(8,128)S(1)} %get-tuple-element.75), channel_id=1, source_target_pairs={{1,2},{2,1},{3,0},{0,3},{5,6},{6,5},{7,4},{4,7},{9,10},{10,9},{11,... | collective-permute-start | bytes 49160 | tf_op jit(solution)/shard_map/ppermute | solution.py:308
  62.6 4.9 %collective-permute-start.18 = (f32[32,128]{1,0:T(8,128)S(1)}, f32[32,128]{1,0:T(8,128)S(1)}, u32[]{:S(2)}, u32[]{:S(2)}) collective-permute-start(f32[32,128]{1,0:T(8,128)S(1)} %get-tuple-element.78), channel_id=1, source_target_pairs={{0,32},{32,0},{64,96},{96,64},{128,160},{160,128},{192,224},{224,1... | collective-permute-start | bytes 49160 | tf_op jit(solution)/shard_map/ppermute | solution.py:308
  62.7 5.2 %collective-permute-start.19 = (f32[32,128]{1,0:T(8,128)S(1)}, f32[32,128]{1,0:T(8,128)S(1)}, u32[]{:S(2)}, u32[]{:S(2)}) collective-permute-start(f32[32,128]{1,0:T(8,128)S(1)} %get-tuple-element.79), channel_id=1, source_target_pairs={{32,64},{64,32},{96,128},{128,96},{160,192},{192,160},{224,0},{0,2... | collective-permute-start | bytes 49160 | tf_op jit(solution)/shard_map/ppermute | solution.py:308
  62.9 4.9 %collective-permute-start.20 = (f32[32,128]{1,0:T(8,128)S(1)}, f32[32,128]{1,0:T(8,128)S(1)}, u32[]{:S(2)}, u32[]{:S(2)}) collective-permute-start(f32[32,128]{1,0:T(8,128)S(1)} %get-tuple-element.80), channel_id=1, source_target_pairs={{0,4},{4,0},{8,12},{12,8},{16,20},{20,16},{24,28},{28,24},{1,5},{5... | collective-permute-start | bytes 49160 | tf_op jit(solution)/shard_map/ppermute | solution.py:308
  63.7 4.9 %collective-permute-start.21 = (f32[32,128]{1,0:T(8,128)S(1)}, f32[32,128]{1,0:T(8,128)S(1)}, u32[]{:S(2)}, u32[]{:S(2)}) collective-permute-start(f32[32,128]{1,0:T(8,128)S(1)} %get-tuple-element.81), channel_id=1, source_target_pairs={{4,8},{8,4},{12,16},{16,12},{20,24},{24,20},{28,0},{0,28},{5,9},{9... | collective-permute-start | bytes 49160 | tf_op jit(solution)/shard_map/ppermute | solution.py:308
  65.7 3.7 %collective-permute-start.22 = (f32[32,128]{1,0:T(8,128)S(1)}, f32[32,128]{1,0:T(8,128)S(1)}, u32[]{:S(2)}, u32[]{:S(2)}) collective-permute-start(f32[32,128]{1,0:T(8,128)S(1)} %get-tuple-element.82), channel_id=1, source_target_pairs={{0,1},{1,0},{2,3},{3,2},{4,5},{5,4},{6,7},{7,6},{8,9},{9,8},{10,11... | collective-permute-start | bytes 49160 | tf_op jit(solution)/shard_map/ppermute | solution.py:308
  67.5 3.7 %collective-permute-start.23 = (f32[32,128]{1,0:T(8,128)S(1)}, f32[32,128]{1,0:T(8,128)S(1)}, u32[]{:S(2)}, u32[]{:S(2)}) collective-permute-start(f32[32,128]{1,0:T(8,128)S(1)} %get-tuple-element.83), channel_id=1, source_target_pairs={{1,2},{2,1},{3,0},{0,3},{5,6},{6,5},{7,4},{4,7},{9,10},{10,9},{11,... | collective-permute-start | bytes 49160 | tf_op jit(solution)/shard_map/ppermute | solution.py:308
  101.0 4.5 %collective-permute-start.24 = (f32[32,128]{1,0:T(8,128)S(1)}, f32[32,128]{1,0:T(8,128)S(1)}, u32[]{:S(2)}, u32[]{:S(2)}) collective-permute-start(f32[32,128]{1,0:T(8,128)S(1)} %get-tuple-element.92), channel_id=1, source_target_pairs={{0,32},{32,0},{64,96},{96,64},{128,160},{160,128},{192,224},{224,1... | collective-permute-start | bytes 49160 | tf_op jit(solution)/shard_map/ppermute | solution.py:308
  101.0 5.3 %collective-permute-start.25 = (f32[32,128]{1,0:T(8,128)S(1)}, f32[32,128]{1,0:T(8,128)S(1)}, u32[]{:S(2)}, u32[]{:S(2)}) collective-permute-start(f32[32,128]{1,0:T(8,128)S(1)} %get-tuple-element.93), channel_id=1, source_target_pairs={{32,64},{64,32},{96,128},{128,96},{160,192},{192,160},{224,0},{0,2... | collective-permute-start | bytes 49160 | tf_op jit(solution)/shard_map/ppermute | solution.py:308
  102.3 4.0 %collective-permute-start.26 = (f32[32,128]{1,0:T(8,128)S(1)}, f32[32,128]{1,0:T(8,128)S(1)}, u32[]{:S(2)}, u32[]{:S(2)}) collective-permute-start(f32[32,128]{1,0:T(8,128)S(1)} %get-tuple-element.94), channel_id=1, source_target_pairs={{0,4},{4,0},{8,12},{12,8},{16,20},{20,16},{24,28},{28,24},{1,5},{5... | collective-permute-start | bytes 49160 | tf_op jit(solution)/shard_map/ppermute | solution.py:308
  103.7 4.9 %collective-permute-start.27 = (f32[32,128]{1,0:T(8,128)S(1)}, f32[32,128]{1,0:T(8,128)S(1)}, u32[]{:S(2)}, u32[]{:S(2)}) collective-permute-start(f32[32,128]{1,0:T(8,128)S(1)} %get-tuple-element.95), channel_id=1, source_target_pairs={{4,8},{8,4},{12,16},{16,12},{20,24},{24,20},{28,0},{0,28},{5,9},{9... | collective-permute-start | bytes 49160 | tf_op jit(solution)/shard_map/ppermute | solution.py:308
  104.1 4.6 %collective-permute-start.28 = (f32[32,128]{1,0:T(8,128)S(1)}, f32[32,128]{1,0:T(8,128)S(1)}, u32[]{:S(2)}, u32[]{:S(2)}) collective-permute-start(f32[32,128]{1,0:T(8,128)S(1)} %get-tuple-element.96), channel_id=1, source_target_pairs={{0,1},{1,0},{2,3},{3,2},{4,5},{5,4},{6,7},{7,6},{8,9},{9,8},{10,11... | collective-permute-start | bytes 49160 | tf_op jit(solution)/shard_map/ppermute | solution.py:308
  105.5 3.7 %collective-permute-start.29 = (f32[32,128]{1,0:T(8,128)S(1)}, f32[32,128]{1,0:T(8,128)S(1)}, u32[]{:S(2)}, u32[]{:S(2)}) collective-permute-start(f32[32,128]{1,0:T(8,128)S(1)} %get-tuple-element.97), channel_id=1, source_target_pairs={{1,2},{2,1},{3,0},{0,3},{5,6},{6,5},{7,4},{4,7},{9,10},{10,9},{11,... | collective-permute-start | bytes 49160 | tf_op jit(solution)/shard_map/ppermute | solution.py:308

commit v3 on v2

--- a/solution.py
+++ b/solution.py
@@ -14,6 +14,8 @@
 MULT = 768
 COARSE = 512
 SIDE = 32
+HALF = 16
+DEVICES = 256
 HIGHEST = lax.Precision.HIGHEST
 VM = pl.BlockSpec(memory_space=pltpu.VMEM)
 SMEM = pl.BlockSpec(memory_space=pltpu.SMEM)
@@ -111,31 +113,32 @@
 
 def corner_message(corner_map, corner_terms, scalars):
     place = coords()
-    devices = []
-    for step in ((0, 0, 0), (1, 0, 0), (-1, 0, 0), None, (0, 1, 0), (0, -1, 0), (0, 0, 1), (0, 0, -1)):
-        if step is None:
-            devices.append(None)
-            continue
-        a, b, c = [(p + s + n) % n for p, s, n in zip(place, step, SIZES)]
-        devices.append((a * SIZES[1] + b) * SIZES[2] + c)
+    steps = ((0, 0, 0), (0, 1, 0), (1, 0, 0), (0, -1, 0), (-1, 0, 0), (0, 0, 1), None, (0, 0, -1))
     row = lax.broadcasted_iota(jnp.int32, (16, FACE), 0)
     target = jnp.full((16, FACE), -1, jnp.int32)
-    for index, device in enumerate(devices):
-        for which in range(2):
-            at = which * 8 + (index % 2) * 4 + index // 2
-            if device is not None:
-                target = jnp.where(row == at, device * 2 + which, target)
+    for index, step in enumerate(steps):
+        if step is not None:
+            a, b, c = [(p + s + n) % n for p, s, n in zip(place, step, SIZES)]
+            owned = 2 * ((a * SIZES[1] + b) * SIZES[2] + c)
+            target = jnp.where(row == index, owned, target)
+            target = jnp.where(row == index + 8, owned + 1, target)
     chosen = (target == corner_map[0:1, :]).astype(F32)
     sums = matmul_nt(chosen, corner_terms, HIGHEST)
-    body = jnp.concatenate([sums[0:4], sums[8:12], sums[4:8], sums[12:16]], axis=1)
-    zero = jnp.zeros((1, LOADS), F32)
-    tail = jnp.concatenate(list(scalars) + [zero] * (4 - len(scalars)), axis=1)
-    return jnp.concatenate([body, jnp.broadcast_to(tail, (4, FACE))], axis=0)
-
-
-def send_message(out, message):
-    for peer in range(out.shape[0]):
-        out[peer] = message
+    line = lax.broadcasted_iota(jnp.int32, (8, LOADS), 0)
+    pair = [
+        jnp.where(line == 6, scalar, sums[8 * i : 8 * i + 8]) for i, scalar in enumerate(scalars)
+    ]
+    messages = []
+    for k in range(2):
+        part = jnp.concatenate([value[:, k * HALF : (k + 1) * HALF] for value in pair], axis=1)
+        messages.append(jnp.concatenate([part[2 * i : 2 * i + 2] for i in range(4)], axis=1))
+    return messages
+
+
+def send_message(out, messages):
+    for a in range(SIZES[0]):
+        block = jnp.broadcast_to(messages[a % 2][None], (SIDE, 2, FACE))
+        out[a * SIDE : (a + 1) * SIDE] = block
 
 
 def second_kernel(live_ref, pairing, corner_map, schur, coupling, terms, dots, *refs):
@@ -151,41 +154,50 @@
     send_message(out, corner_message(corner_map, corner_terms, (dots[0:1], curve[0:1])))
 
 
-def plane_kernel(got, out):
-    rows = lax.broadcasted_iota(jnp.int32, (SIDE, FACE), 0) % SIZES[2]
-    lane = lax.broadcasted_iota(jnp.int32, (SIDE, FACE), 1)
-    along_b = got[:, 2, :]
-    along_c = got[:, 3, :]
-    b_up = pltpu.roll(along_b, SIZES[2], 0)
-    b_down = pltpu.roll(pltpu.roll(along_b, SIDE - SIZES[2], 0), 64, 1)
-    c_up = jnp.where(rows == 0, pltpu.roll(along_c, SIDE - 3, 0), pltpu.roll(along_c, 1, 0))
-    c_down = jnp.where(rows == 3, pltpu.roll(along_c, 3, 0), pltpu.roll(along_c, SIDE - 1, 0))
-    c_down = pltpu.roll(c_down, 64, 1)
-    own = got[:, 0, :] + jnp.where(lane < 64, (b_up + b_down) + (c_up + c_down), 0.0)
-    down = got[:, 1, :]
-    scalars = jnp.broadcast_to(jnp.sum(got[:, 4, :], axis=0, keepdims=True), (8, FACE))
-    half = SIDE // 2
-    down = jnp.where(lane[:half] < 64, down[:half], pltpu.roll(down[half:], 64, 1))
-    for peer in range(SIZES[0]):
-        out[peer, 0:32, :] = own
-        out[peer, 32:48, :] = down
-        out[peer, 48:56, :] = scalars
-
-
-def coarse_sums(got, scratch):
-    pieces = []
+def combine_kernel(got, out):
+    third = lax.broadcasted_iota(jnp.int32, (SIDE, FACE), 0) % SIZES[2]
+    total = jnp.zeros((8, FACE), F32)
     for a in range(SIZES[0]):
-        below, above = (a + 7) % 8, (a + 1) % 8
-        down = got[above, 32:48, :]
-        down = jnp.concatenate([down, pltpu.roll(down, 64, 1)], axis=0)
-        pieces.append(got[a, 0:32, :] + pltpu.roll(got[below, 0:32, :], 64, 1) + down)
-    whole = jnp.concatenate(pieces, axis=0)
-    scratch[pl.Slice(0, COARSE // 2, 2), :] = whole[:, 0:32]
-    scratch[pl.Slice(1, COARSE // 2, 2), :] = whole[:, 32:64]
-    scalars = got[0, 48:56, :]
-    for a in range(1, SIZES[0]):
-        scalars = scalars + got[a, 48:56, :]
-    return scratch[...], [scalars[0:1, i * 32 : i * 32 + 32] for i in range(4)]
+        def plane(index, line):
+            first = (index % SIZES[0]) * SIDE
+            return got[first : first + SIDE, line, :]
+
+        here, side = plane(a, 0), plane(a, 1)
+        b_up = pltpu.roll(side, SIZES[2], 0)
+        b_down = pltpu.roll(side, SIDE - SIZES[2], 0)
+        c_up = jnp.where(third == 0, pltpu.roll(side, SIDE - 3, 0), pltpu.roll(side, 1, 0))
+        c_down = jnp.where(third == 3, pltpu.roll(side, 3, 0), pltpu.roll(side, SIDE - 1, 0))
+        near = here + b_up
+        near = near + pltpu.roll(plane(a - 1, 0) + b_down, 96, 1)
+        near = near + pltpu.roll(plane(a + 1, 0) + c_up, 64, 1)
+        near = near + pltpu.roll(c_down, 32, 1)
+        out[a * SIDE : (a + 1) * SIDE, :] = near
+        total = total + (here[0:8] + here[8:16]) + (here[16:24] + here[24:32])
+    out[DEVICES : DEVICES + 8, :] = jnp.broadcast_to(
+        jnp.sum(total, axis=0, keepdims=True), (8, FACE)
+    )
+
+
+def coarse_sums(mine, other, scratch):
+    odd = coords()[0] % 2 == 1
+
+    def pieces(rows):
+        low = jnp.where(odd, other[rows, :], mine[rows, :])
+        high = jnp.where(odd, mine[rows, :], other[rows, :])
+        return low, high
+
+    def joined(low, high, start):
+        at = pltpu.roll(low, (FACE - start) % FACE, 1) if start else low
+        to = pltpu.roll(high, (FACE - start + HALF) % FACE, 1)
+        lane = lax.broadcasted_iota(jnp.int32, low.shape, 1)
+        return jnp.where(lane < HALF, at, to)[:, 0:LOADS]
+
+    low, high = pieces(slice(0, DEVICES))
+    scratch[pl.Slice(0, DEVICES, 2), :] = joined(low, high, 0)
+    scratch[pl.Slice(1, DEVICES, 2), :] = joined(low, high, HALF)
+    low, high = pieces(slice(DEVICES, DEVICES + 8))
+    scalars = [joined(low, high, 96 + i * HALF)[0:1] for i in range(2)]
+    return scratch[...], scalars
 
 
 def halves(value):
@@ -204,22 +216,27 @@
     picked = lax.dot_general(
         solved, chosen, (((0,), (0,)), ((), ())), preferred_element_type=F32
     ).astype(BF16)
-    energy = jnp.sum(solved.astype(F32) * gathered, axis=0, keepdims=True)
-    return matmul_nt(picked, coupling[0]), energy
-
-
-def third_kernel(live_ref, corner_map, coupling, inverse, got, local_ref, *refs):
-    image_ref, gathered_ref, scalar_ref = refs[:3]
-    sends, scratch = refs[3:9], refs[9]
-    live = live_ref[0:1, 0:1]
-    gathered, (resid_dot, local_curve, _, _) = coarse_sums(got, scratch)
-    coarse_terms, energy = coarse_solve(inverse, gathered, corner_map, coupling)
+    return matmul_nt(picked, coupling[0]), solved.astype(F32)
+
+
+def coarse_dot(solved, gathered):
+    return jnp.sum(solved * gathered, axis=0, keepdims=True)
+
+
+def third_kernel(live_ref, corner_map, coupling, inverse, mine, other, local_ref, *refs):
+    image_ref, gathered_ref, solved_ref, scalar_ref = refs[:4]
+    sends, scratch = refs[4:10], refs[10]
+    live = live_ref[0:1, 0:1]
+    gathered, (resid_dot, local_curve) = coarse_sums(mine, other, scratch)
+    coarse_terms, solved = coarse_solve(inverse, gathered, corner_map, coupling)
     image = live * (local_ref[...] + coarse_terms)
-    step_size = resid_dot / (local_curve + energy)
+    curvature = local_curve + coarse_dot(solved, gathered)
+    step_size = resid_dot / curvature
     image_ref[...] = image
     gathered_ref[...] = gathered
+    solved_ref[...] = solved
     scalar_ref[...] = jnp.concatenate(
-        [resid_dot, local_curve, step_size, jnp.zeros((5, LOADS), F32)], axis=0
+        [resid_dot, local_curve, step_size, curvature, jnp.zeros((4, LOADS), F32)], axis=0
     )
     store_sends(sends, split_faces(image))
 
@@ -236,7 +253,7 @@
     store_sends(sends, split_faces(applied))
 
 
-def fifth_kernel(live_ref, pairing, corner_map, schur, coupling, terms, dots, local_ref, *refs):
+def fifth_kernel(live_ref, pairing, corner_map, schur, coupling, terms, dots, *refs):
     recvs, (precond_ref, out) = refs[:6], refs[6:]
     live = live_ref[0:1, 0:1]
     precond = live * (terms[...] + partner(recvs, pairing))
@@ -246,23 +263,23 @@
     both = matmul(jnp.concatenate([high, low], axis=0), coupling[0])
     corner_terms = live * (both[:LOADS] + both[LOADS:])
     square = load_sums(precond, local_terms)
-    cross = load_sums(precond, local_ref[...])
-    scalars = (dots[0:1], square[0:1], cross[0:1])
-    send_message(out, corner_message(corner_map, corner_terms, scalars))
+    send_message(out, corner_message(corner_map, corner_terms, (dots[0:1], square[0:1])))
 
 
 def sixth_kernel(
-    live_ref, corner_map, schur, coupling, inverse, got, gathered_ref, scalar_ref, z_ref, precond_ref, *refs
+    live_ref, corner_map, schur, coupling, inverse, mine, other, gathered_ref, solved_ref,
+    scalar_ref, z_ref, precond_ref, *refs
 ):
     solution_ref, image_ref, step_ref = refs[:3]
     sends, scratch = refs[3:9], refs[9]
     live = live_ref[0:1, 0:1]
-    gathered, (new_dot, square, cross, _) = coarse_sums(got, scratch)
+    gathered, (new_dot, square) = coarse_sums(mine, other, scratch)
     beta = new_dot / scalar_ref[0:1, :]
+    cross = -beta * scalar_ref[3:4, :] - coarse_dot(solved_ref[...], gathered)
     gathered = gathered + beta * gathered_ref[...]
-    coarse_terms, energy = coarse_solve(inverse, gathered, corner_map, coupling)
-    local_curve = square + 2.0 * beta * cross + beta * beta * scalar_ref[1:2, :]
-    step_size = new_dot / (local_curve + energy)
+    coarse_terms, solved = coarse_solve(inverse, gathered, corner_map, coupling)
+    local_curve = square + beta * (2.0 * cross + beta * scalar_ref[1:2, :])
+    step_size = new_dot / (local_curve + coarse_dot(solved, gathered))
     first = z_ref[...]
     direction = precond_ref[...] + column(beta) * first
     local_terms = matmul(direction.astype(BF16), schur[0])
@@ -310,8 +327,9 @@
     ]
 
 
-def spread(message, axes):
-    return lax.all_to_all(message, axes, 0, 0)
+def total_sums(message):
+    (mine,) = call(combine_kernel, [(DEVICES + 8, FACE)], lax.all_to_all(message, AXES, 0, 0))
+    return mine, lax.ppermute(mine, AXES[0], matched(SIZES[0], 0))
 
 
 def local(loads, schur, dirichlet, coupling, coarse_inverse, pairing, corner_map, counts):
@@ -331,13 +349,12 @@
         live, loads, pairing, dirichlet, *exchange(sends),
     )
     first, local_terms, message = call(
-        second_kernel, [vector, vector, (SIDE, 8, FACE)],
+        second_kernel, [vector, vector, (DEVICES, 2, FACE)],
         live, pairing, corner_map, schur, coupling, terms, dots, *exchange(sends),
     )
-    (message,) = call(plane_kernel, [(SIZES[0], 56, FACE)], spread(message, ("gy", "gz")))
-    image, gathered, scalars, *sends = call(
-        third_kernel, [vector, (COARSE, LOADS), small] + faces,
-        live, corner_map, coupling, inverse, spread(message, "region"), local_terms,
+    image, gathered, solved, scalars, *sends = call(
+        third_kernel, [vector, (COARSE, LOADS), (COARSE, LOADS), small] + faces,
+        live, corner_map, coupling, inverse, *total_sums(message), local_terms,
         scratch=solver_scratch,
     )
     resid, terms, dots, *sends = call(
@@ -345,14 +362,13 @@
         live, pairing, dirichlet, resid, weight, image, scalars, *exchange(sends),
     )
     precond, message = call(
-        fifth_kernel, [vector, (SIDE, 8, FACE)],
-        live, pairing, corner_map, schur, coupling, terms, dots, local_terms, *exchange(sends),
-    )
-    (message,) = call(plane_kernel, [(SIZES[0], 56, FACE)], spread(message, ("gy", "gz")))
+        fifth_kernel, [vector, (DEVICES, 2, FACE)],
+        live, pairing, corner_map, schur, coupling, terms, dots, *exchange(sends),
+    )
     solution_out, image, step, *sends = call(
         sixth_kernel, [(1,) + vector, vector, small] + faces,
-        live, corner_map, schur, coupling, inverse, spread(message, "region"),
-        gathered, scalars, first, precond, scratch=solver_scratch,
+        live, corner_map, schur, coupling, inverse, *total_sums(message),
+        gathered, solved, scalars, first, precond, scratch=solver_scratch,
     )
     (residual_out,) = call(
         seventh_kernel, [(1,) + vector],

time: 111 us -> 108 us (0.973)
  blocking collectives: 52.1 us -> 44.2 us
  waiting for transfers between devices: 11.9 us -> 16.3 us
    all_to_all x4 -> x2, blocking collectives: 52.1 us -> 44.2 us  [total_sums(): lax.all_to_all(message, AXES, 0, 0)]
    ppermute x0 -> x2, waiting for transfers between devices: none -> 2.48 us  [total_sums(): return (mine, lax.ppermute(mine, AXES[0], matched(SIZES[0], 0)))]
    ppermute x30, waiting for transfers between devices: 11.9 us -> 13.8 us  [exchange(): lax.ppermute(value, AXES[k // 2], matched(SIZES[k // 2], k % 2))]
  transfers between devices with their start and end apart: 30 -> 32, of which waited for: 10 -> 14; matrix products, arithmetic and copies ran while one was open for 0% -> 0% of each run, Pallas kernels for 0% -> 0%
where the time goes in v3:
time: 108 us; the launch traced here: 107 us
  blocking collectives  44.2 us (41%)
  starting transfers between devices  35.2 us (33%)
  waiting for transfers between devices  16.3 us (15%)
  Pallas kernels  7.21 us (7%)
  local copies, waits for them, and re-layouts  2.59 us (2%)
  between operations  1.45 us (1%)
    all_to_all x2, blocking collectives, total_sums(): lax.all_to_all(message, AXES, 0, 0)  44.2 us
    ppermute x30, starting transfers between devices, exchange(): lax.ppermute(value, AXES[k // 2], matched(SIZES[k // 2], k % 2))  34.8 us
    ppermute x30, waiting for transfers between devices, exchange(): lax.ppermute(value, AXES[k // 2], matched(SIZES[k // 2], k % 2))  13.8 us
    pallas_call x12, Pallas kernels, call(): pl.pallas_call(kernel, out_shape=[shape if hasattr(shape, 'dtype') else j...  7.21 us
    unnamed x16, local copies, waits for them, and re-layouts  2.59 us
    ppermute x2, waiting for transfers between devices, total_sums(): return (mine, lax.ppermute(mine, AXES[0], matched(SIZES[0], 0)))  2.48 us
  transfers between devices with their start and end apart: 32, of which 14 were waited for; matrix products, arithmetic and copies ran while one was open for 0% of the time, Pallas kernels for 0%

profile of v3, /device:TPU:2, one launch (start us, length us, event | category | flops | bytes accessed | tf_op | source)
XLA Modules:
  0.0 106.9 jit_solution(865347689165246016)
XLA Ops:
  1.3 0.0 copy-start.4
  1.3 0.9 copy-done.4
  2.2 0.1 collective-permute-start
  2.3 3.1 %collective-permute-start.1 = (f32[40,128]{1,0:T(8,128)S(1)}, f32[40,128]{1,0:T(8,128)S(1)}, u32[]{:S(2)}, u32[]{:S(2)}) collective-permute-start(f32[40,128]{1,0:T(8,128)S(1)} %get-tuple-element.52), channel_id=1, source_target_pairs={{32,64},{64,32},{96,128},{128,96},{160,192},{192,160},{224,0},{0,2... | collective-permute-start | bytes 61448 | tf_op jit(solution)/shard_map/ppermute | solution.py:325
  5.5 1.9 %collective-permute-start.2 = (f32[40,128]{1,0:T(8,128)S(1)}, f32[40,128]{1,0:T(8,128)S(1)}, u32[]{:S(2)}, u32[]{:S(2)}) collective-permute-start(f32[40,128]{1,0:T(8,128)S(1)} %get-tuple-element.53), channel_id=1, source_target_pairs={{0,4},{4,0},{8,12},{12,8},{16,20},{20,16},{24,28},{28,24},{1,5},{5... | collective-permute-start | bytes 61448 | tf_op jit(solution)/shard_map/ppermute | solution.py:325
  7.4 4.9 %collective-permute-start.3 = (f32[40,128]{1,0:T(8,128)S(1)}, f32[40,128]{1,0:T(8,128)S(1)}, u32[]{:S(2)}, u32[]{:S(2)}) collective-permute-start(f32[40,128]{1,0:T(8,128)S(1)} %get-tuple-element.54), channel_id=1, source_target_pairs={{4,8},{8,4},{12,16},{16,12},{20,24},{24,20},{28,0},{0,28},{5,9},{9... | collective-permute-start | bytes 61448 | tf_op jit(solution)/shard_map/ppermute | solution.py:325
  12.3 0.5 collective-permute-start.4
  12.9 0.0 collective-permute-done.refs_0_
  12.9 2.2 %collective-permute-start.5 = (f32[40,128]{1,0:T(8,128)S(1)}, f32[40,128]{1,0:T(8,128)S(1)}, u32[]{:S(2)}, u32[]{:S(2)}) collective-permute-start(f32[40,128]{1,0:T(8,128)S(1)} %get-tuple-element.56), channel_id=1, source_target_pairs={{1,2},{2,1},{3,0},{0,3},{5,6},{6,5},{7,4},{4,7},{9,10},{10,9},{11,... | collective-permute-start | bytes 61448 | tf_op jit(solution)/shard_map/ppermute | solution.py:325
  15.0 1.3 %copy-done.3 = bf16[1,768,768]{2,1,0:T(8,128)(2,1)S(1)} copy-done((bf16[1,768,768]{2,1,0:T(8,128)(2,1)S(1)}, bf16[1,768,768]{2,1,0:T(8,128)(2,1)}, u32[]{:S(2)}) %copy-start.3) | copy-done | bytes 1179672
  16.3 0.1 shard_map.96.dirichlet
  16.4 0.0 copy-start
  16.4 0.0 copy-start.2
  16.4 0.0 copy-start.7
  16.4 0.0 collective-permute-done.1.refs_1_
  16.4 0.0 collective-permute-done.2.refs_2_
  16.4 0.0 collective-permute-done.4.refs_4_
  16.4 0.3 collective-permute-done.5.refs_5_
  16.8 0.4 copy-done.5
  17.2 0.6 shard_map.98
  17.8 0.9 collective-permute-start.7
  18.6 2.0 %collective-permute-start.9 = (f32[32,128]{1,0:T(8,128)S(1)}, f32[32,128]{1,0:T(8,128)S(1)}, u32[]{:S(2)}, u32[]{:S(2)}) collective-permute-start(f32[32,128]{1,0:T(8,128)S(1)} %get-tuple-element.64), channel_id=1, source_target_pairs={{4,8},{8,4},{12,16},{16,12},{20,24},{24,20},{28,0},{0,28},{5,9},{9... | collective-permute-start | bytes 49160 | tf_op jit(solution)/shard_map/ppermute | solution.py:325
  20.7 2.2 %collective-permute-start.10 = (f32[32,128]{1,0:T(8,128)S(1)}, f32[32,128]{1,0:T(8,128)S(1)}, u32[]{:S(2)}, u32[]{:S(2)}) collective-permute-start(f32[32,128]{1,0:T(8,128)S(1)} %get-tuple-element.65), channel_id=1, source_target_pairs={{0,1},{1,0},{2,3},{3,2},{4,5},{5,4},{6,7},{7,6},{8,9},{9,8},{10,11... | collective-permute-start | bytes 49160 | tf_op jit(solution)/shard_map/ppermute | solution.py:325
  22.8 1.5 %collective-permute-start.11 = (f32[32,128]{1,0:T(8,128)S(1)}, f32[32,128]{1,0:T(8,128)S(1)}, u32[]{:S(2)}, u32[]{:S(2)}) collective-permute-start(f32[32,128]{1,0:T(8,128)S(1)} %get-tuple-element.66), channel_id=1, source_target_pairs={{1,2},{2,1},{3,0},{0,3},{5,6},{6,5},{7,4},{4,7},{9,10},{10,9},{11,... | collective-permute-start | bytes 49160 | tf_op jit(solution)/shard_map/ppermute | solution.py:325
  24.3 0.2 collective-permute-done.10.refs_4_
  24.5 2.0 %collective-permute-done.11.refs_5_ = f32[32,128]{1,0:T(8,128)S(1)} collective-permute-done((f32[32,128]{1,0:T(8,128)S(1)}, f32[32,128]{1,0:T(8,128)S(1)}, u32[]{:S(2)}, u32[]{:S(2)}) %collective-permute-start.11) | collective-permute-done | bytes 16416 | tf_op jit(solution)/shard_map/ppermute | solution.py:325
  26.6 0.0 copy-start.1
  26.6 0.8 shard_map.99
  27.4 21.9 %all_to_all.10.got = f32[256,2,128]{2,1,0:T(2,128)S(1)} all-to-all(f32[256,2,128]{2,1,0:T(2,128)S(1)} %get-tuple-element.67), channel_id=1, replica_groups=mesh['region'=8,'gy'=8,'gz'=4] {'region','gy','gz'}, dimensions={0} | all-to-all | bytes 524288 | tf_op jit(solution)/shard_map/all_to_all | solution.py:331
  49.3 0.3 shard_map.100.mine
  49.7 0.2 collective-permute-start.12
  49.9 1.2 %collective-permute-done.12.other = f32[264,128]{1,0:T(8,128)S(1)} collective-permute-done((f32[264,128]{1,0:T(8,128)S(1)}, f32[264,128]{1,0:T(8,128)S(1)}, u32[]{:S(2)}, u32[]{:S(2)}) %collective-permute-start.12) | collective-permute-done | bytes 135200 | tf_op jit(solution)/shard_map/ppermute | solution.py:332
  51.1 1.0 shard_map.101
  52.1 0.2 collective-permute-start.13
  52.4 1.1 %collective-permute-start.14 = (f32[32,128]{1,0:T(8,128)S(1)}, f32[32,128]{1,0:T(8,128)S(1)}, u32[]{:S(2)}, u32[]{:S(2)}) collective-permute-start(f32[32,128]{1,0:T(8,128)S(1)} %get-tuple-element.72), channel_id=1, source_target_pairs={{32,64},{64,32},{96,128},{128,96},{160,192},{192,160},{224,0},{0,2... | collective-permute-start | bytes 49160 | tf_op jit(solution)/shard_map/ppermute | solution.py:325
  53.5 1.1 %collective-permute-start.15 = (f32[32,128]{1,0:T(8,128)S(1)}, f32[32,128]{1,0:T(8,128)S(1)}, u32[]{:S(2)}, u32[]{:S(2)}) collective-permute-start(f32[32,128]{1,0:T(8,128)S(1)} %get-tuple-element.73), channel_id=1, source_target_pairs={{0,4},{4,0},{8,12},{12,8},{16,20},{20,16},{24,28},{28,24},{1,5},{5... | collective-permute-start | bytes 49160 | tf_op jit(solution)/shard_map/ppermute | solution.py:325
  54.6 0.9 collective-permute-start.16
  55.5 1.5 %collective-permute-start.17 = (f32[32,128]{1,0:T(8,128)S(1)}, f32[32,128]{1,0:T(8,128)S(1)}, u32[]{:S(2)}, u32[]{:S(2)}) collective-permute-start(f32[32,128]{1,0:T(8,128)S(1)} %get-tuple-element.75), channel_id=1, source_target_pairs={{0,1},{1,0},{2,3},{3,2},{4,5},{5,4},{6,7},{7,6},{8,9},{9,8},{10,11... | collective-permute-start | bytes 49160 | tf_op jit(solution)/shard_map/ppermute | solution.py:325
  57.0 0.2 collective-permute-done.15.refs_2_
  57.2 2.3 %collective-permute-done.16.refs_3_ = f32[32,128]{1,0:T(8,128)S(1)} collective-permute-done((f32[32,128]{1,0:T(8,128)S(1)}, f32[32,128]{1,0:T(8,128)S(1)}, u32[]{:S(2)}, u32[]{:S(2)}) %collective-permute-start.16) | collective-permute-done | bytes 16416 | tf_op jit(solution)/shard_map/ppermute | solution.py:325
  59.5 1.2 %collective-permute-done.18.refs_5_ = f32[32,128]{1,0:T(8,128)S(1)} collective-permute-done((f32[32,128]{1,0:T(8,128)S(1)}, f32[32,128]{1,0:T(8,128)S(1)}, u32[]{:S(2)}, u32[]{:S(2)}) %collective-permute-start.18) | collective-permute-done | bytes 16416 | tf_op jit(solution)/shard_map/ppermute | solution.py:325
  60.7 0.6 shard_map.102
  61.3 0.8 collective-permute-start.20
  62.1 1.0 collective-permute-start.21
  63.1 2.3 %collective-permute-start.22 = (f32[32,128]{1,0:T(8,128)S(1)}, f32[32,128]{1,0:T(8,128)S(1)}, u32[]{:S(2)}, u32[]{:S(2)}) collective-permute-start(f32[32,128]{1,0:T(8,128)S(1)} %get-tuple-element.82), channel_id=1, source_target_pairs={{4,8},{8,4},{12,16},{16,12},{20,24},{24,20},{28,0},{0,28},{5,9},{9... | collective-permute-start | bytes 49160 | tf_op jit(solution)/shard_map/ppermute | solution.py:325
  65.3 1.8 %collective-permute-start.23 = (f32[32,128]{1,0:T(8,128)S(1)}, f32[32,128]{1,0:T(8,128)S(1)}, u32[]{:S(2)}, u32[]{:S(2)}) collective-permute-start(f32[32,128]{1,0:T(8,128)S(1)} %get-tuple-element.83), channel_id=1, source_target_pairs={{0,1},{1,0},{2,3},{3,2},{4,5},{5,4},{6,7},{7,6},{8,9},{9,8},{10,11... | collective-permute-start | bytes 49160 | tf_op jit(solution)/shard_map/ppermute | solution.py:325
  67.2 0.8 collective-permute-done.22.refs_3_
  68.0 1.0 collective-permute-done.23.refs_4_
  69.1 1.8 %collective-permute-done.24.refs_5_ = f32[32,128]{1,0:T(8,128)S(1)} collective-permute-done((f32[32,128]{1,0:T(8,128)S(1)}, f32[32,128]{1,0:T(8,128)S(1)}, u32[]{:S(2)}, u32[]{:S(2)}) %collective-permute-start.24) | collective-permute-done | bytes 16416 | tf_op jit(solution)/shard_map/ppermute | solution.py:325
  70.9 0.8 shard_map.103
  71.7 22.2 %all_to_all.11.got = f32[256,2,128]{2,1,0:T(2,128)S(1)} all-to-all(f32[256,2,128]{2,1,0:T(2,128)S(1)} %get-tuple-element.85), channel_id=1, replica_groups=mesh['region'=8,'gy'=8,'gz'=4] {'region','gy','gz'}, dimensions={0} | all-to-all | bytes 524288 | tf_op jit(solution)/shard_map/all_to_all | solution.py:331
  93.9 0.3 shard_map.104.mine
  94.3 0.2 collective-permute-start.25
  94.5 1.2 %collective-permute-done.25.other = f32[264,128]{1,0:T(8,128)S(1)} collective-permute-done((f32[264,128]{1,0:T(8,128)S(1)}, f32[264,128]{1,0:T(8,128)S(1)}, u32[]{:S(2)}, u32[]{:S(2)}) %collective-permute-start.25) | collective-permute-done | bytes 135200 | tf_op jit(solution)/shard_map/ppermute | solution.py:332
  95.7 1.9 %shard_map.105 = (f32[1,32,768]{2,1,0:T(8,128)}, f32[32,768]{1,0:T(8,128)S(1)}, f32[8,32]{1,0:T(8,128)S(1)}, f32[32,128]{1,0:T(8,128)S(1)}, f32[32,128]{1,0:T(8,...) custom-call(f32[8,128]{1,0:T(8,128)S(1)} %shard_map.95.live_ref, ...), custom_call_target="tpu_custom_call" | custom-call | tf_op jit(solution)/shard_map/pallas_call | solution.py:301
  97.6 0.1 collective-permute-start.26
  97.7 1.1 %collective-permute-start.27 = (f32[32,128]{1,0:T(8,128)S(1)}, f32[32,128]{1,0:T(8,128)S(1)}, u32[]{:S(2)}, u32[]{:S(2)}) collective-permute-start(f32[32,128]{1,0:T(8,128)S(1)} %get-tuple-element.95), channel_id=1, source_target_pairs={{32,64},{64,32},{96,128},{128,96},{160,192},{192,160},{224,0},{0,2... | collective-permute-start | bytes 49160 | tf_op jit(solution)/shard_map/ppermute | solution.py:325
  98.8 1.1 %collective-permute-start.28 = (f32[32,128]{1,0:T(8,128)S(1)}, f32[32,128]{1,0:T(8,128)S(1)}, u32[]{:S(2)}, u32[]{:S(2)}) collective-permute-start(f32[32,128]{1,0:T(8,128)S(1)} %get-tuple-element.96), channel_id=1, source_target_pairs={{0,4},{4,0},{8,12},{12,8},{16,20},{20,16},{24,28},{28,24},{1,5},{5... | collective-permute-start | bytes 49160 | tf_op jit(solution)/shard_map/ppermute | solution.py:325
  99.9 0.9 collective-permute-start.29
  100.9 1.4 %collective-permute-start.30 = (f32[32,128]{1,0:T(8,128)S(1)}, f32[32,128]{1,0:T(8,128)S(1)}, u32[]{:S(2)}, u32[]{:S(2)}) collective-permute-start(f32[32,128]{1,0:T(8,128)S(1)} %get-tuple-element.98), channel_id=1, source_target_pairs={{0,1},{1,0},{2,3},{3,2},{4,5},{5,4},{6,7},{7,6},{8,9},{9,8},{10,11... | collective-permute-start | bytes 49160 | tf_op jit(solution)/shard_map/ppermute | solution.py:325
  102.3 0.2 collective-permute-done.28.refs_2_
  102.6 2.3 %collective-permute-done.29.refs_3_ = f32[32,128]{1,0:T(8,128)S(1)} collective-permute-done((f32[32,128]{1,0:T(8,128)S(1)}, f32[32,128]{1,0:T(8,128)S(1)}, u32[]{:S(2)}, u32[]{:S(2)}) %collective-permute-start.29) | collective-permute-done | bytes 16416 | tf_op jit(solution)/shard_map/ppermute | solution.py:325
  104.9 1.2 %collective-permute-done.31.refs_5_ = f32[32,128]{1,0:T(8,128)S(1)} collective-permute-done((f32[32,128]{1,0:T(8,128)S(1)}, f32[32,128]{1,0:T(8,128)S(1)}, u32[]{:S(2)}, u32[]{:S(2)}) %collective-permute-start.31) | collective-permute-done | bytes 16416 | tf_op jit(solution)/shard_map/ppermute | solution.py:325
  106.1 0.8 shard_map.106
  (30 shorter events, 0.1 us)
Async XLA Ops:
  1.3 0.9 copy-start.4
  2.2 10.6 %collective-permute-start = (f32[40,128]{1,0:T(8,128)S(1)}, f32[40,128]{1,0:T(8,128)S(1)}, u32[]{:S(2)}, u32[]{:S(2)}) collective-permute-start(f32[40,128]{1,0:T(8,128)S(1)} %get-tuple-element.51), channel_id=1, source_target_pairs={{0,32},{32,0},{64,96},{96,64},{128,160},{160,128},{192,224},{224,1... | collective-permute-start | bytes 61448 | tf_op jit(solution)/shard_map/ppermute | solution.py:325
  2.3 14.1 %collective-permute-start.1 = (f32[40,128]{1,0:T(8,128)S(1)}, f32[40,128]{1,0:T(8,128)S(1)}, u32[]{:S(2)}, u32[]{:S(2)}) collective-permute-start(f32[40,128]{1,0:T(8,128)S(1)} %get-tuple-element.52), channel_id=1, source_target_pairs={{32,64},{64,32},{96,128},{128,96},{160,192},{192,160},{224,0},{0,2... | collective-permute-start | bytes 61448 | tf_op jit(solution)/shard_map/ppermute | solution.py:325
  5.5 11.0 %collective-permute-start.2 = (f32[40,128]{1,0:T(8,128)S(1)}, f32[40,128]{1,0:T(8,128)S(1)}, u32[]{:S(2)}, u32[]{:S(2)}) collective-permute-start(f32[40,128]{1,0:T(8,128)S(1)} %get-tuple-element.53), channel_id=1, source_target_pairs={{0,4},{4,0},{8,12},{12,8},{16,20},{20,16},{24,28},{28,24},{1,5},{5... | collective-permute-start | bytes 61448 | tf_op jit(solution)/shard_map/ppermute | solution.py:325
  7.4 9.1 %collective-permute-start.3 = (f32[40,128]{1,0:T(8,128)S(1)}, f32[40,128]{1,0:T(8,128)S(1)}, u32[]{:S(2)}, u32[]{:S(2)}) collective-permute-start(f32[40,128]{1,0:T(8,128)S(1)} %get-tuple-element.54), channel_id=1, source_target_pairs={{4,8},{8,4},{12,16},{16,12},{20,24},{24,20},{28,0},{0,28},{5,9},{9... | collective-permute-start | bytes 61448 | tf_op jit(solution)/shard_map/ppermute | solution.py:325
  12.3 4.1 %collective-permute-start.4 = (f32[40,128]{1,0:T(8,128)S(1)}, f32[40,128]{1,0:T(8,128)S(1)}, u32[]{:S(2)}, u32[]{:S(2)}) collective-permute-start(f32[40,128]{1,0:T(8,128)S(1)} %get-tuple-element.55), channel_id=1, source_target_pairs={{0,1},{1,0},{2,3},{3,2},{4,5},{5,4},{6,7},{7,6},{8,9},{9,8},{10,11... | collective-permute-start | bytes 61448 | tf_op jit(solution)/shard_map/ppermute | solution.py:325
  12.9 3.9 %collective-permute-start.5 = (f32[40,128]{1,0:T(8,128)S(1)}, f32[40,128]{1,0:T(8,128)S(1)}, u32[]{:S(2)}, u32[]{:S(2)}) collective-permute-start(f32[40,128]{1,0:T(8,128)S(1)} %get-tuple-element.56), channel_id=1, source_target_pairs={{1,2},{2,1},{3,0},{0,3},{5,6},{6,5},{7,4},{4,7},{9,10},{10,9},{11,... | collective-permute-start | bytes 61448 | tf_op jit(solution)/shard_map/ppermute | solution.py:325
  15.0 1.3 %copy-start.3 = (bf16[1,768,768]{2,1,0:T(8,128)(2,1)S(1)}, bf16[1,768,768]{2,1,0:T(8,128)(2,1)}, u32[]{:S(2)}) copy-start(bf16[1,768,768]{2,1,0:T(8,128)(2,1)} %source.1) | copy-start | bytes 3538948
  16.3 0.9 copy-start.5
  16.3 0.9 copy-start.6
  16.4 10.2 %copy-start = (bf16[1,768,768]{2,1,0:T(8,128)(2,1)S(1)}, bf16[1,768,768]{2,1,0:T(8,128)(2,1)}, u32[]{:S(2)}) copy-start(bf16[1,768,768]{2,1,0:T(8,128)(2,1)} %schur.5) | copy-start | bytes 3538948
  16.4 10.2 %copy-start.2 = (bf16[1,768,128]{2,1,0:T(8,128)(2,1)S(1)}, bf16[1,768,128]{2,1,0:T(8,128)(2,1)}, u32[]{:S(2)}) copy-start(bf16[1,768,128]{2,1,0:T(8,128)(2,1)} %coupling.7) | copy-start | bytes 589828
  16.4 10.2 %copy-start.7 = (s32[1,128]{1,0:T(1,128)S(1)}, s32[1,128]{1,0:T(1,128)}, u32[]{:S(2)}) copy-start(s32[1,128]{1,0:T(1,128)} %corner_map.7) | copy-start | bytes 1540
  17.7 5.1 %collective-permute-start.6 = (f32[32,128]{1,0:T(8,128)S(1)}, f32[32,128]{1,0:T(8,128)S(1)}, u32[]{:S(2)}, u32[]{:S(2)}) collective-permute-start(f32[32,128]{1,0:T(8,128)S(1)} %get-tuple-element.61), channel_id=1, source_target_pairs={{0,32},{32,0},{64,96},{96,64},{128,160},{160,128},{192,224},{224,1... | collective-permute-start | bytes 49160 | tf_op jit(solution)/shard_map/ppermute | solution.py:325
  17.8 6.6 %collective-permute-start.7 = (f32[32,128]{1,0:T(8,128)S(1)}, f32[32,128]{1,0:T(8,128)S(1)}, u32[]{:S(2)}, u32[]{:S(2)}) collective-permute-start(f32[32,128]{1,0:T(8,128)S(1)} %get-tuple-element.62), channel_id=1, source_target_pairs={{32,64},{64,32},{96,128},{128,96},{160,192},{192,160},{224,0},{0,2... | collective-permute-start | bytes 49160 | tf_op jit(solution)/shard_map/ppermute | solution.py:325
  18.6 5.7 %collective-permute-start.8 = (f32[32,128]{1,0:T(8,128)S(1)}, f32[32,128]{1,0:T(8,128)S(1)}, u32[]{:S(2)}, u32[]{:S(2)}) collective-permute-start(f32[32,128]{1,0:T(8,128)S(1)} %get-tuple-element.63), channel_id=1, source_target_pairs={{0,4},{4,0},{8,12},{12,8},{16,20},{20,16},{24,28},{28,24},{1,5},{5... | collective-permute-start | bytes 49160 | tf_op jit(solution)/shard_map/ppermute | solution.py:325
  18.6 5.7 %collective-permute-start.9 = (f32[32,128]{1,0:T(8,128)S(1)}, f32[32,128]{1,0:T(8,128)S(1)}, u32[]{:S(2)}, u32[]{:S(2)}) collective-permute-start(f32[32,128]{1,0:T(8,128)S(1)} %get-tuple-element.64), channel_id=1, source_target_pairs={{4,8},{8,4},{12,16},{16,12},{20,24},{24,20},{28,0},{0,28},{5,9},{9... | collective-permute-start | bytes 49160 | tf_op jit(solution)/shard_map/ppermute | solution.py:325
  20.7 3.9 %collective-permute-start.10 = (f32[32,128]{1,0:T(8,128)S(1)}, f32[32,128]{1,0:T(8,128)S(1)}, u32[]{:S(2)}, u32[]{:S(2)}) collective-permute-start(f32[32,128]{1,0:T(8,128)S(1)} %get-tuple-element.65), channel_id=1, source_target_pairs={{0,1},{1,0},{2,3},{3,2},{4,5},{5,4},{6,7},{7,6},{8,9},{9,8},{10,11... | collective-permute-start | bytes 49160 | tf_op jit(solution)/shard_map/ppermute | solution.py:325
  22.8 3.7 %collective-permute-start.11 = (f32[32,128]{1,0:T(8,128)S(1)}, f32[32,128]{1,0:T(8,128)S(1)}, u32[]{:S(2)}, u32[]{:S(2)}) collective-permute-start(f32[32,128]{1,0:T(8,128)S(1)} %get-tuple-element.66), channel_id=1, source_target_pairs={{1,2},{2,1},{3,0},{0,3},{5,6},{6,5},{7,4},{4,7},{9,10},{10,9},{11,... | collective-permute-start | bytes 49160 | tf_op jit(solution)/shard_map/ppermute | solution.py:325
  26.6 24.6 %copy-start.1 = (f32[512,512]{1,0:T(8,128)S(1)}, f32[512,512]{1,0:T(8,128)}, u32[]{:S(2)}) copy-start(f32[512,512]{1,0:T(8,128)} %inverse.3) | copy-start | bytes 3145732
  49.7 1.4 %collective-permute-start.12 = (f32[264,128]{1,0:T(8,128)S(1)}, f32[264,128]{1,0:T(8,128)S(1)}, u32[]{:S(2)}, u32[]{:S(2)}) collective-permute-start(f32[264,128]{1,0:T(8,128)S(1)} %shard_map.100.mine), channel_id=1, source_target_pairs={{0,32},{32,0},{64,96},{96,64},{128,160},{160,128},{192,224},{224,1... | collective-permute-start | bytes 405512 | tf_op jit(solution)/shard_map/ppermute | solution.py:332
  52.1 4.8 %collective-permute-start.13 = (f32[32,128]{1,0:T(8,128)S(1)}, f32[32,128]{1,0:T(8,128)S(1)}, u32[]{:S(2)}, u32[]{:S(2)}) collective-permute-start(f32[32,128]{1,0:T(8,128)S(1)} %get-tuple-element.71), channel_id=1, source_target_pairs={{0,32},{32,0},{64,96},{96,64},{128,160},{160,128},{192,224},{224,1... | collective-permute-start | bytes 49160 | tf_op jit(solution)/shard_map/ppermute | solution.py:325
  52.4 4.6 %collective-permute-start.14 = (f32[32,128]{1,0:T(8,128)S(1)}, f32[32,128]{1,0:T(8,128)S(1)}, u32[]{:S(2)}, u32[]{:S(2)}) collective-permute-start(f32[32,128]{1,0:T(8,128)S(1)} %get-tuple-element.72), channel_id=1, source_target_pairs={{32,64},{64,32},{96,128},{128,96},{160,192},{192,160},{224,0},{0,2... | collective-permute-start | bytes 49160 | tf_op jit(solution)/shard_map/ppermute | solution.py:325
  53.5 3.7 %collective-permute-start.15 = (f32[32,128]{1,0:T(8,128)S(1)}, f32[32,128]{1,0:T(8,128)S(1)}, u32[]{:S(2)}, u32[]{:S(2)}) collective-permute-start(f32[32,128]{1,0:T(8,128)S(1)} %get-tuple-element.73), channel_id=1, source_target_pairs={{0,4},{4,0},{8,12},{12,8},{16,20},{20,16},{24,28},{28,24},{1,5},{5... | collective-permute-start | bytes 49160 | tf_op jit(solution)/shard_map/ppermute | solution.py:325
  54.6 4.9 %collective-permute-start.16 = (f32[32,128]{1,0:T(8,128)S(1)}, f32[32,128]{1,0:T(8,128)S(1)}, u32[]{:S(2)}, u32[]{:S(2)}) collective-permute-start(f32[32,128]{1,0:T(8,128)S(1)} %get-tuple-element.74), channel_id=1, source_target_pairs={{4,8},{8,4},{12,16},{16,12},{20,24},{24,20},{28,0},{0,28},{5,9},{9... | collective-permute-start | bytes 49160 | tf_op jit(solution)/shard_map/ppermute | solution.py:325
  55.5 4.0 %collective-permute-start.17 = (f32[32,128]{1,0:T(8,128)S(1)}, f32[32,128]{1,0:T(8,128)S(1)}, u32[]{:S(2)}, u32[]{:S(2)}) collective-permute-start(f32[32,128]{1,0:T(8,128)S(1)} %get-tuple-element.75), channel_id=1, source_target_pairs={{0,1},{1,0},{2,3},{3,2},{4,5},{5,4},{6,7},{7,6},{8,9},{9,8},{10,11... | collective-permute-start | bytes 49160 | tf_op jit(solution)/shard_map/ppermute | solution.py:325
  57.0 3.7 %collective-permute-start.18 = (f32[32,128]{1,0:T(8,128)S(1)}, f32[32,128]{1,0:T(8,128)S(1)}, u32[]{:S(2)}, u32[]{:S(2)}) collective-permute-start(f32[32,128]{1,0:T(8,128)S(1)} %get-tuple-element.76), channel_id=1, source_target_pairs={{1,2},{2,1},{3,0},{0,3},{5,6},{6,5},{7,4},{4,7},{9,10},{10,9},{11,... | collective-permute-start | bytes 49160 | tf_op jit(solution)/shard_map/ppermute | solution.py:325
  61.3 5.9 %collective-permute-start.19 = (f32[32,128]{1,0:T(8,128)S(1)}, f32[32,128]{1,0:T(8,128)S(1)}, u32[]{:S(2)}, u32[]{:S(2)}) collective-permute-start(f32[32,128]{1,0:T(8,128)S(1)} %get-tuple-element.79), channel_id=1, source_target_pairs={{0,32},{32,0},{64,96},{96,64},{128,160},{160,128},{192,224},{224,1... | collective-permute-start | bytes 49160 | tf_op jit(solution)/shard_map/ppermute | solution.py:325
  61.3 5.9 %collective-permute-start.20 = (f32[32,128]{1,0:T(8,128)S(1)}, f32[32,128]{1,0:T(8,128)S(1)}, u32[]{:S(2)}, u32[]{:S(2)}) collective-permute-start(f32[32,128]{1,0:T(8,128)S(1)} %get-tuple-element.80), channel_id=1, source_target_pairs={{32,64},{64,32},{96,128},{128,96},{160,192},{192,160},{224,0},{0,2... | collective-permute-start | bytes 49160 | tf_op jit(solution)/shard_map/ppermute | solution.py:325
  62.1 5.1 %collective-permute-start.21 = (f32[32,128]{1,0:T(8,128)S(1)}, f32[32,128]{1,0:T(8,128)S(1)}, u32[]{:S(2)}, u32[]{:S(2)}) collective-permute-start(f32[32,128]{1,0:T(8,128)S(1)} %get-tuple-element.81), channel_id=1, source_target_pairs={{0,4},{4,0},{8,12},{12,8},{16,20},{20,16},{24,28},{28,24},{1,5},{5... | collective-permute-start | bytes 49160 | tf_op jit(solution)/shard_map/ppermute | solution.py:325
  63.1 4.9 %collective-permute-start.22 = (f32[32,128]{1,0:T(8,128)S(1)}, f32[32,128]{1,0:T(8,128)S(1)}, u32[]{:S(2)}, u32[]{:S(2)}) collective-permute-start(f32[32,128]{1,0:T(8,128)S(1)} %get-tuple-element.82), channel_id=1, source_target_pairs={{4,8},{8,4},{12,16},{16,12},{20,24},{24,20},{28,0},{0,28},{5,9},{9... | collective-permute-start | bytes 49160 | tf_op jit(solution)/shard_map/ppermute | solution.py:325
  65.3 3.7 %collective-permute-start.23 = (f32[32,128]{1,0:T(8,128)S(1)}, f32[32,128]{1,0:T(8,128)S(1)}, u32[]{:S(2)}, u32[]{:S(2)}) collective-permute-start(f32[32,128]{1,0:T(8,128)S(1)} %get-tuple-element.83), channel_id=1, source_target_pairs={{0,1},{1,0},{2,3},{3,2},{4,5},{5,4},{6,7},{7,6},{8,9},{9,8},{10,11... | collective-permute-start | bytes 49160 | tf_op jit(solution)/shard_map/ppermute | solution.py:325
  67.2 3.7 %collective-permute-start.24 = (f32[32,128]{1,0:T(8,128)S(1)}, f32[32,128]{1,0:T(8,128)S(1)}, u32[]{:S(2)}, u32[]{:S(2)}) collective-permute-start(f32[32,128]{1,0:T(8,128)S(1)} %get-tuple-element.84), channel_id=1, source_target_pairs={{1,2},{2,1},{3,0},{0,3},{5,6},{6,5},{7,4},{4,7},{9,10},{10,9},{11,... | collective-permute-start | bytes 49160 | tf_op jit(solution)/shard_map/ppermute | solution.py:325
  94.3 1.4 %collective-permute-start.25 = (f32[264,128]{1,0:T(8,128)S(1)}, f32[264,128]{1,0:T(8,128)S(1)}, u32[]{:S(2)}, u32[]{:S(2)}) collective-permute-start(f32[264,128]{1,0:T(8,128)S(1)} %shard_map.104.mine), channel_id=1, source_target_pairs={{0,32},{32,0},{64,96},{96,64},{128,160},{160,128},{192,224},{224,1... | collective-permute-start | bytes 405512 | tf_op jit(solution)/shard_map/ppermute | solution.py:332
  97.6 4.7 %collective-permute-start.26 = (f32[32,128]{1,0:T(8,128)S(1)}, f32[32,128]{1,0:T(8,128)S(1)}, u32[]{:S(2)}, u32[]{:S(2)}) collective-permute-start(f32[32,128]{1,0:T(8,128)S(1)} %get-tuple-element.94), channel_id=1, source_target_pairs={{0,32},{32,0},{64,96},{96,64},{128,160},{160,128},{192,224},{224,1... | collective-permute-start | bytes 49160 | tf_op jit(solution)/shard_map/ppermute | solution.py:325
  97.7 4.6 %collective-permute-start.27 = (f32[32,128]{1,0:T(8,128)S(1)}, f32[32,128]{1,0:T(8,128)S(1)}, u32[]{:S(2)}, u32[]{:S(2)}) collective-permute-start(f32[32,128]{1,0:T(8,128)S(1)} %get-tuple-element.95), channel_id=1, source_target_pairs={{32,64},{64,32},{96,128},{128,96},{160,192},{192,160},{224,0},{0,2... | collective-permute-start | bytes 49160 | tf_op jit(solution)/shard_map/ppermute | solution.py:325
  98.8 3.7 %collective-permute-start.28 = (f32[32,128]{1,0:T(8,128)S(1)}, f32[32,128]{1,0:T(8,128)S(1)}, u32[]{:S(2)}, u32[]{:S(2)}) collective-permute-start(f32[32,128]{1,0:T(8,128)S(1)} %get-tuple-element.96), channel_id=1, source_target_pairs={{0,4},{4,0},{8,12},{12,8},{16,20},{20,16},{24,28},{28,24},{1,5},{5... | collective-permute-start | bytes 49160 | tf_op jit(solution)/shard_map/ppermute | solution.py:325
  99.9 4.9 %collective-permute-start.29 = (f32[32,128]{1,0:T(8,128)S(1)}, f32[32,128]{1,0:T(8,128)S(1)}, u32[]{:S(2)}, u32[]{:S(2)}) collective-permute-start(f32[32,128]{1,0:T(8,128)S(1)} %get-tuple-element.97), channel_id=1, source_target_pairs={{4,8},{8,4},{12,16},{16,12},{20,24},{24,20},{28,0},{0,28},{5,9},{9... | collective-permute-start | bytes 49160 | tf_op jit(solution)/shard_map/ppermute | solution.py:325
  100.9 4.0 %collective-permute-start.30 = (f32[32,128]{1,0:T(8,128)S(1)}, f32[32,128]{1,0:T(8,128)S(1)}, u32[]{:S(2)}, u32[]{:S(2)}) collective-permute-start(f32[32,128]{1,0:T(8,128)S(1)} %get-tuple-element.98), channel_id=1, source_target_pairs={{0,1},{1,0},{2,3},{3,2},{4,5},{5,4},{6,7},{7,6},{8,9},{9,8},{10,11... | collective-permute-start | bytes 49160 | tf_op jit(solution)/shard_map/ppermute | solution.py:325
  102.3 3.7 %collective-permute-start.31 = (f32[32,128]{1,0:T(8,128)S(1)}, f32[32,128]{1,0:T(8,128)S(1)}, u32[]{:S(2)}, u32[]{:S(2)}) collective-permute-start(f32[32,128]{1,0:T(8,128)S(1)} %get-tuple-element.99), channel_id=1, source_target_pairs={{1,2},{2,1},{3,0},{0,3},{5,6},{6,5},{7,4},{4,7},{9,10},{10,9},{11,... | collective-permute-start | bytes 49160 | tf_op jit(solution)/shard_map/ppermute | solution.py:325

commit v4 on v3

--- a/solution.py
+++ b/solution.py
@@ -16,7 +16,6 @@
 SIDE = 32
 HALF = 16
 DEVICES = 256
-HIGHEST = lax.Precision.HIGHEST
 VM = pl.BlockSpec(memory_space=pltpu.VMEM)
 SMEM = pl.BlockSpec(memory_space=pltpu.SMEM)
 
@@ -25,28 +24,36 @@
     return jnp.dot(left, right, preferred_element_type=F32)
 
 
-def matmul_nt(left, right, precision=None):
-    return lax.dot_general(
-        left, right, (((1,), (1,)), ((), ())), precision=precision, preferred_element_type=F32
-    )
+def halves(value):
+    high = value.astype(BF16)
+    return high, (value - high.astype(F32)).astype(BF16)
+
+
+def matmul_nt(left, right):
+    return lax.dot_general(left, right, (((1,), (1,)), ((), ())), preferred_element_type=F32)
 
 
 def coords():
     return [lax.axis_index(axis) for axis in AXES]
+
+
+ORDER = (1, 2, 3, 4, 5, 0)
 
 
 def store_sends(sends, faces):
     for e, place in enumerate(coords()):
         odd = place % 2 == 1
-        sends[2 * e][...] = jnp.where(odd, faces[2 * e], faces[2 * e + 1])
-        sends[2 * e + 1][...] = jnp.where(odd, faces[2 * e + 1], faces[2 * e])
+        first, second = ORDER.index(2 * e), ORDER.index(2 * e + 1)
+        sends[first][...] = jnp.where(odd, faces[2 * e], faces[2 * e + 1])
+        sends[second][...] = jnp.where(odd, faces[2 * e + 1], faces[2 * e])
 
 
 def received_faces(recvs, rows):
     out = []
     for e, place in enumerate(coords()):
         odd = place % 2 == 1
-        first, second = recvs[2 * e][rows, :], recvs[2 * e + 1][rows, :]
+        first = recvs[ORDER.index(2 * e)][rows, :]
+        second = recvs[ORDER.index(2 * e + 1)][rows, :]
         lower = jnp.where(odd, first, second)
         upper = jnp.where(odd, second, first)
         out.append(jnp.where(place > 0, lower, 0.0))
@@ -67,8 +74,16 @@
     return [value[:, f * FACE : (f + 1) * FACE] for f in range(6)]
 
 
+def select_nt(table, value):
+    rows = value.shape[0]
+    high, _ = halves(value)
+    middle, low = halves(value - high.astype(F32))
+    out = matmul_nt(table, jnp.concatenate([high, middle, low], axis=0))
+    return out[:, :rows] + (out[:, rows : 2 * rows] + out[:, 2 * rows :])
+
+
 def load_sums(left, right):
-    return matmul_nt(jnp.ones((8, MULT), F32), left * right, HIGHEST)
+    return select_nt(jnp.ones((8, MULT), BF16), left * right)
 
 
 def column(row):
@@ -90,6 +105,10 @@
 
 def copy_kernel(source, out):
     out[...] = source[...]
+
+
+def halves_kernel(source, after, out):
+    out[0], out[1] = halves(source[...])
 
 
 def precondition(weight, residual, dirichlet):
@@ -122,8 +141,8 @@
             owned = 2 * ((a * SIZES[1] + b) * SIZES[2] + c)
             target = jnp.where(row == index, owned, target)
             target = jnp.where(row == index + 8, owned + 1, target)
-    chosen = (target == corner_map[0:1, :]).astype(F32)
-    sums = matmul_nt(chosen, corner_terms, HIGHEST)
+    chosen = (target == corner_map[0:1, :]).astype(F32).astype(BF16)
+    sums = select_nt(chosen, corner_terms)
     line = lax.broadcasted_iota(jnp.int32, (8, LOADS), 0)
     pair = [
         jnp.where(line == 6, scalar, sums[8 * i : 8 * i + 8]) for i, scalar in enumerate(scalars)
@@ -136,9 +155,9 @@
 
 
 def send_message(out, messages):
-    for a in range(SIZES[0]):
-        block = jnp.broadcast_to(messages[a % 2][None], (SIDE, 2, FACE))
-        out[a * SIDE : (a + 1) * SIDE] = block
+    block = jnp.stack(messages * (SIZES[0] // 2))
+    for i in range(SIDE):
+        out[i * SIZES[0] : (i + 1) * SIZES[0]] = block
 
 
 def second_kernel(live_ref, pairing, corner_map, schur, coupling, terms, dots, *refs):
@@ -154,25 +173,25 @@
     send_message(out, corner_message(corner_map, corner_terms, (dots[0:1], curve[0:1])))
 
 
+BY_COLUMN = ("gy", "gz", "region")
+
+
 def combine_kernel(got, out):
-    third = lax.broadcasted_iota(jnp.int32, (SIDE, FACE), 0) % SIZES[2]
     total = jnp.zeros((8, FACE), F32)
-    for a in range(SIZES[0]):
-        def plane(index, line):
-            first = (index % SIZES[0]) * SIDE
-            return got[first : first + SIDE, line, :]
-
-        here, side = plane(a, 0), plane(a, 1)
-        b_up = pltpu.roll(side, SIZES[2], 0)
-        b_down = pltpu.roll(side, SIDE - SIZES[2], 0)
-        c_up = jnp.where(third == 0, pltpu.roll(side, SIDE - 3, 0), pltpu.roll(side, 1, 0))
-        c_down = jnp.where(third == 3, pltpu.roll(side, 3, 0), pltpu.roll(side, SIDE - 1, 0))
-        near = here + b_up
-        near = near + pltpu.roll(plane(a - 1, 0) + b_down, 96, 1)
-        near = near + pltpu.roll(plane(a + 1, 0) + c_up, 64, 1)
-        near = near + pltpu.roll(c_down, 32, 1)
-        out[a * SIDE : (a + 1) * SIDE, :] = near
-        total = total + (here[0:8] + here[8:16]) + (here[16:24] + here[24:32])
+
+    def column(b, c, line):
+        first = (b % SIZES[1] * SIZES[2] + c % SIZES[2]) * SIZES[0]
+        return got[first : first + SIZES[0], line, :]
+
+    for b in range(SIZES[1]):
+        for c in range(SIZES[2]):
+            here = column(b, c, 0)
+            near = here + column(b - 1, c, 1)
+            near = near + pltpu.roll(pltpu.roll(here, 1, 0) + column(b + 1, c, 1), 96, 1)
+            near = near + pltpu.roll(pltpu.roll(here, 7, 0) + column(b, c - 1, 1), 64, 1)
+            near = near + pltpu.roll(column(b, c + 1, 1), 32, 1)
+            out[pl.Slice(b * SIZES[2] + c, SIZES[0], SIDE), :] = near
+            total = total + here
     out[DEVICES : DEVICES + 8, :] = jnp.broadcast_to(
         jnp.sum(total, axis=0, keepdims=True), (8, FACE)
     )
@@ -200,16 +219,10 @@
     return scratch[...], scalars
 
 
-def halves(value):
-    high = value.astype(BF16)
-    return high, (value - high.astype(F32)).astype(BF16)
-
-
 def coarse_solve(inverse, gathered, corner_map, coupling):
-    mat_high, mat_low = halves(inverse[...])
     vec_high, vec_low = halves(gathered)
-    both = matmul(mat_high, jnp.concatenate([vec_high, vec_low], axis=1))
-    solved = both[:, :LOADS] + (both[:, LOADS:] + matmul(mat_low, vec_high))
+    both = matmul(inverse[0], jnp.concatenate([vec_high, vec_low], axis=1))
+    solved = both[:, :LOADS] + (both[:, LOADS:] + matmul(inverse[1], vec_high))
     solved = solved.astype(BF16)
     row = lax.broadcasted_iota(jnp.int32, (COARSE, FACE), 0)
     chosen = (row == corner_map[0:1, :]).astype(F32).astype(BF16)
@@ -270,7 +283,7 @@
     live_ref, corner_map, schur, coupling, inverse, mine, other, gathered_ref, solved_ref,
     scalar_ref, z_ref, precond_ref, *refs
 ):
-    solution_ref, image_ref, step_ref = refs[:3]
+    direction_ref, image_ref, step_ref = refs[:3]
     sends, scratch = refs[3:9], refs[9]
     live = live_ref[0:1, 0:1]
     gathered, (new_dot, square) = coarse_sums(mine, other, scratch)
@@ -287,7 +300,11 @@
     image_ref[...] = image
     store_sends(sends, split_faces(image))
     step_ref[...] = jnp.broadcast_to(step_size, (8, LOADS))
-    solution_ref[0] = column(scalar_ref[2:3, :]) * first + column(step_size) * direction
+    direction_ref[...] = direction
+
+
+def solution_kernel(scalar_ref, first, step_ref, direction, out):
+    out[0] = column(scalar_ref[2:3, :]) * first[...] + column(step_ref[0:1, :]) * direction[...]
 
 
 def seventh_kernel(live_ref, pairing, resid, image_ref, step_ref, *refs):
@@ -323,12 +340,12 @@
 def exchange(sends):
     return [
         lax.ppermute(value, AXES[k // 2], matched(SIZES[k // 2], k % 2))
-        for k, value in enumerate(sends)
+        for k, value in zip(ORDER, sends)
     ]
 
 
 def total_sums(message):
-    (mine,) = call(combine_kernel, [(DEVICES + 8, FACE)], lax.all_to_all(message, AXES, 0, 0))
+    (mine,) = call(combine_kernel, [(DEVICES + 8, FACE)], lax.all_to_all(message, BY_COLUMN, 0, 0))
     return mine, lax.ppermute(mine, AXES[0], matched(SIZES[0], 0))
 
 
@@ -343,10 +360,12 @@
     (live,) = call(living_kernel, [(8, FACE)], counts, spec=SMEM, cost=cost)
     sends = call(prepare_kernel, [(LOADS + 8, FACE)] * 6, live, loads)
     (dirichlet,) = call(copy_kernel, [jax.ShapeDtypeStruct(dirichlet.shape, BF16)], dirichlet)
-    inverse = coarse_inverse
     resid, weight, terms, dots, *sends = call(
         first_kernel, [vector, (8, MULT), vector, small] + faces,
         live, loads, pairing, dirichlet, *exchange(sends),
+    )
+    (inverse,) = call(
+        halves_kernel, [jax.ShapeDtypeStruct((2, COARSE, COARSE), BF16)], coarse_inverse, dots
     )
     first, local_terms, message = call(
         second_kernel, [vector, vector, (DEVICES, 2, FACE)],
@@ -365,11 +384,12 @@
         fifth_kernel, [vector, (DEVICES, 2, FACE)],
         live, pairing, corner_map, schur, coupling, terms, dots, *exchange(sends),
     )
-    solution_out, image, step, *sends = call(
-        sixth_kernel, [(1,) + vector, vector, small] + faces,
+    direction, image, step, *sends = call(
+        sixth_kernel, [vector, vector, small] + faces,
         live, corner_map, schur, coupling, inverse, *total_sums(message),
         gathered, solved, scalars, first, precond, scratch=solver_scratch,
     )
+    (solution_out,) = call(solution_kernel, [(1,) + vector], scalars, first, step, direction)
     (residual_out,) = call(
         seventh_kernel, [(1,) + vector],
         live, pairing, resid, image, step, *exchange(sends),

time: 108 us -> 105 us (0.972)
  starting transfers between devices: 35.2 us -> 32.2 us
  waiting for transfers between devices: 16.3 us -> 14.7 us
    ppermute x30, starting transfers between devices: 34.8 us -> 32 us  [exchange(): lax.ppermute(value, AXES[k // 2], matched(SIZES[k // 2], k % 2))]
    ppermute x30, waiting for transfers between devices: 13.8 us -> 12.2 us  [exchange(): lax.ppermute(value, AXES[k // 2], matched(SIZES[k // 2], k % 2))]
    pallas_call x12 -> x14, Pallas kernels: 7.21 us -> 8.16 us  [call(): pl.pallas_call(kernel, out_shape=[shape if hasattr(shape, 'dtype') else j...]
  transfers between devices with their start and end apart: 32 -> 32, of which waited for: 14 -> 17; matrix products, arithmetic and copies ran while one was open for 0% -> 0% of each run, Pallas kernels for 0% -> 1%
where the time goes in v4:
time: 105 us; the launch traced here: 104 us
  blocking collectives  45 us (43%)
  starting transfers between devices  32.2 us (31%)
  waiting for transfers between devices  14.7 us (14%)
  Pallas kernels  8.16 us (8%)
  local copies, waits for them, and re-layouts  2.6 us (2%)
  between operations  1.47 us (1%)
    all_to_all x2, blocking collectives, total_sums(): lax.all_to_all(message, BY_COLUMN, 0, 0)  45 us
    ppermute x30, starting transfers between devices, exchange(): lax.ppermute(value, AXES[k // 2], matched(SIZES[k // 2], k % 2))  32 us
    ppermute x30, waiting for transfers between devices, exchange(): lax.ppermute(value, AXES[k // 2], matched(SIZES[k // 2], k % 2))  12.2 us
    pallas_call x14, Pallas kernels, call(): pl.pallas_call(kernel, out_shape=[shape if hasattr(shape, 'dtype') else j...  8.16 us
    unnamed x16, local copies, waits for them, and re-layouts  2.6 us
    ppermute x2, waiting for transfers between devices, total_sums(): return (mine, lax.ppermute(mine, AXES[0], matched(SIZES[0], 0)))  2.52 us
  transfers between devices with their start and end apart: 32, of which 17 were waited for; matrix products, arithmetic and copies ran while one was open for 0% of the time, Pallas kernels for 1%

profile of v4, /device:TPU:2, one launch (start us, length us, event | category | flops | bytes accessed | tf_op | source)
XLA Modules:
  0.0 104.1 jit_solution(335370437724091093)
XLA Ops:
  1.3 0.0 copy-start.4
  1.3 0.9 copy-done.4
  2.2 2.5 %collective-permute-start = (f32[40,128]{1,0:T(8,128)S(1)}, f32[40,128]{1,0:T(8,128)S(1)}, u32[]{:S(2)}, u32[]{:S(2)}) collective-permute-start(f32[40,128]{1,0:T(8,128)S(1)} %get-tuple-element.51), channel_id=1, source_target_pairs={{32,64},{64,32},{96,128},{128,96},{160,192},{192,160},{224,0},{0,2... | collective-permute-start | bytes 61448 | tf_op jit(solution)/shard_map/ppermute | solution.py:342
  4.8 1.9 %collective-permute-start.1 = (f32[40,128]{1,0:T(8,128)S(1)}, f32[40,128]{1,0:T(8,128)S(1)}, u32[]{:S(2)}, u32[]{:S(2)}) collective-permute-start(f32[40,128]{1,0:T(8,128)S(1)} %get-tuple-element.52), channel_id=1, source_target_pairs={{0,4},{4,0},{8,12},{12,8},{16,20},{20,16},{24,28},{28,24},{1,5},{5... | collective-permute-start | bytes 61448 | tf_op jit(solution)/shard_map/ppermute | solution.py:342
  6.7 4.9 %collective-permute-start.2 = (f32[40,128]{1,0:T(8,128)S(1)}, f32[40,128]{1,0:T(8,128)S(1)}, u32[]{:S(2)}, u32[]{:S(2)}) collective-permute-start(f32[40,128]{1,0:T(8,128)S(1)} %get-tuple-element.53), channel_id=1, source_target_pairs={{4,8},{8,4},{12,16},{16,12},{20,24},{24,20},{28,0},{0,28},{5,9},{9... | collective-permute-start | bytes 61448 | tf_op jit(solution)/shard_map/ppermute | solution.py:342
  11.6 0.5 collective-permute-start.3
  12.2 2.2 %collective-permute-start.4 = (f32[40,128]{1,0:T(8,128)S(1)}, f32[40,128]{1,0:T(8,128)S(1)}, u32[]{:S(2)}, u32[]{:S(2)}) collective-permute-start(f32[40,128]{1,0:T(8,128)S(1)} %get-tuple-element.55), channel_id=1, source_target_pairs={{1,2},{2,1},{3,0},{0,3},{5,6},{6,5},{7,4},{4,7},{9,10},{10,9},{11,... | collective-permute-start | bytes 61448 | tf_op jit(solution)/shard_map/ppermute | solution.py:342
  14.3 1.3 %copy-done.2 = bf16[1,768,768]{2,1,0:T(8,128)(2,1)S(1)} copy-done((bf16[1,768,768]{2,1,0:T(8,128)(2,1)S(1)}, bf16[1,768,768]{2,1,0:T(8,128)(2,1)}, u32[]{:S(2)}) %copy-start.2) | copy-done | bytes 1179672
  15.6 0.1 shard_map.96.dirichlet
  15.7 0.0 copy-start
  15.7 0.0 copy-start.1
  15.7 0.0 copy-start.7
  15.8 0.3 collective-permute-done.4.refs_4_
  16.1 0.4 copy-done.5
  16.5 0.7 shard_map.98
  17.2 0.9 collective-permute-start.6
  18.1 2.0 %collective-permute-start.8 = (f32[32,128]{1,0:T(8,128)S(1)}, f32[32,128]{1,0:T(8,128)S(1)}, u32[]{:S(2)}, u32[]{:S(2)}) collective-permute-start(f32[32,128]{1,0:T(8,128)S(1)} %get-tuple-element.61), channel_id=1, source_target_pairs={{4,8},{8,4},{12,16},{16,12},{20,24},{24,20},{28,0},{0,28},{5,9},{9... | collective-permute-start | bytes 49160 | tf_op jit(solution)/shard_map/ppermute | solution.py:342
  20.1 1.4 %collective-permute-start.9 = (f32[32,128]{1,0:T(8,128)S(1)}, f32[32,128]{1,0:T(8,128)S(1)}, u32[]{:S(2)}, u32[]{:S(2)}) collective-permute-start(f32[32,128]{1,0:T(8,128)S(1)} %get-tuple-element.62), channel_id=1, source_target_pairs={{0,1},{1,0},{2,3},{3,2},{4,5},{5,4},{6,7},{7,6},{8,9},{9,8},{10,11... | collective-permute-start | bytes 49160 | tf_op jit(solution)/shard_map/ppermute | solution.py:342
  21.5 1.4 %collective-permute-start.10 = (f32[32,128]{1,0:T(8,128)S(1)}, f32[32,128]{1,0:T(8,128)S(1)}, u32[]{:S(2)}, u32[]{:S(2)}) collective-permute-start(f32[32,128]{1,0:T(8,128)S(1)} %get-tuple-element.63), channel_id=1, source_target_pairs={{1,2},{2,1},{3,0},{0,3},{5,6},{6,5},{7,4},{4,7},{9,10},{10,9},{11,... | collective-permute-start | bytes 49160 | tf_op jit(solution)/shard_map/ppermute | solution.py:342
  22.9 0.1 collective-permute-done.8.refs_2_
  23.0 0.8 collective-permute-done.9.refs_3_
  23.8 1.4 %collective-permute-done.10.refs_4_ = f32[32,128]{1,0:T(8,128)S(1)} collective-permute-done((f32[32,128]{1,0:T(8,128)S(1)}, f32[32,128]{1,0:T(8,128)S(1)}, u32[]{:S(2)}, u32[]{:S(2)}) %collective-permute-start.10) | collective-permute-done | bytes 16416 | tf_op jit(solution)/shard_map/ppermute | solution.py:342
  25.3 0.0 copy-start.3
  25.3 0.9 shard_map.100
  26.2 22.4 %all_to_all.10.got = f32[256,2,128]{2,1,0:T(2,128)S(1)} all-to-all(f32[256,2,128]{2,1,0:T(2,128)S(1)} %get-tuple-element.65), channel_id=1, replica_groups=mesh['region'=8,'gy'=8,'gz'=4] {'gy','gz','region'}, dimensions={0} | all-to-all | bytes 524288 | tf_op jit(solution)/shard_map/all_to_all | solution.py:348
  48.5 0.4 shard_map.101.mine
  49.0 0.1 collective-permute-start.12
  49.1 0.2 shard_map.99.inverse
  49.2 1.2 %collective-permute-done.12.other = f32[264,128]{1,0:T(8,128)S(1)} collective-permute-done((f32[264,128]{1,0:T(8,128)S(1)}, f32[264,128]{1,0:T(8,128)S(1)}, u32[]{:S(2)}, u32[]{:S(2)}) %collective-permute-start.12) | collective-permute-done | bytes 135200 | tf_op jit(solution)/shard_map/ppermute | solution.py:349
  50.4 1.0 shard_map.102
  51.4 1.6 %collective-permute-start.13 = (f32[32,128]{1,0:T(8,128)S(1)}, f32[32,128]{1,0:T(8,128)S(1)}, u32[]{:S(2)}, u32[]{:S(2)}) collective-permute-start(f32[32,128]{1,0:T(8,128)S(1)} %get-tuple-element.72), channel_id=1, source_target_pairs={{32,64},{64,32},{96,128},{128,96},{160,192},{192,160},{224,0},{0,2... | collective-permute-start | bytes 49160 | tf_op jit(solution)/shard_map/ppermute | solution.py:342
  53.0 1.0 collective-permute-start.14
  54.0 1.5 %collective-permute-start.16 = (f32[32,128]{1,0:T(8,128)S(1)}, f32[32,128]{1,0:T(8,128)S(1)}, u32[]{:S(2)}, u32[]{:S(2)}) collective-permute-start(f32[32,128]{1,0:T(8,128)S(1)} %get-tuple-element.75), channel_id=1, source_target_pairs={{0,1},{1,0},{2,3},{3,2},{4,5},{5,4},{6,7},{7,6},{8,9},{9,8},{10,11... | collective-permute-start | bytes 49160 | tf_op jit(solution)/shard_map/ppermute | solution.py:342
  55.5 0.1 collective-permute-start.17
  55.6 0.2 collective-permute-done.13.refs_0_
  55.9 0.8 collective-permute-done.14.refs_1_
  56.7 2.3 %collective-permute-done.15.refs_2_ = f32[32,128]{1,0:T(8,128)S(1)} collective-permute-done((f32[32,128]{1,0:T(8,128)S(1)}, f32[32,128]{1,0:T(8,128)S(1)}, u32[]{:S(2)}, u32[]{:S(2)}) %collective-permute-start.15) | collective-permute-done | bytes 16416 | tf_op jit(solution)/shard_map/ppermute | solution.py:342
  59.0 0.3 collective-permute-done.17.refs_4_
  59.2 0.7 shard_map.103
  59.9 0.2 collective-permute-start.19
  60.1 0.8 collective-permute-start.20
  60.9 2.3 %collective-permute-start.21 = (f32[32,128]{1,0:T(8,128)S(1)}, f32[32,128]{1,0:T(8,128)S(1)}, u32[]{:S(2)}, u32[]{:S(2)}) collective-permute-start(f32[32,128]{1,0:T(8,128)S(1)} %get-tuple-element.82), channel_id=1, source_target_pairs={{4,8},{8,4},{12,16},{16,12},{20,24},{24,20},{28,0},{0,28},{5,9},{9... | collective-permute-start | bytes 49160 | tf_op jit(solution)/shard_map/ppermute | solution.py:342
  63.2 1.8 %collective-permute-start.22 = (f32[32,128]{1,0:T(8,128)S(1)}, f32[32,128]{1,0:T(8,128)S(1)}, u32[]{:S(2)}, u32[]{:S(2)}) collective-permute-start(f32[32,128]{1,0:T(8,128)S(1)} %get-tuple-element.83), channel_id=1, source_target_pairs={{0,1},{1,0},{2,3},{3,2},{4,5},{5,4},{6,7},{7,6},{8,9},{9,8},{10,11... | collective-permute-start | bytes 49160 | tf_op jit(solution)/shard_map/ppermute | solution.py:342
  65.0 0.6 collective-permute-start.23
  65.7 0.1 collective-permute-start.24
  65.7 0.1 collective-permute-done.21.refs_2_
  65.9 1.1 %collective-permute-done.22.refs_3_ = f32[32,128]{1,0:T(8,128)S(1)} collective-permute-done((f32[32,128]{1,0:T(8,128)S(1)}, f32[32,128]{1,0:T(8,128)S(1)}, u32[]{:S(2)}, u32[]{:S(2)}) %collective-permute-start.22) | collective-permute-done | bytes 16416 | tf_op jit(solution)/shard_map/ppermute | solution.py:342
  67.0 1.8 %collective-permute-done.23.refs_4_ = f32[32,128]{1,0:T(8,128)S(1)} collective-permute-done((f32[32,128]{1,0:T(8,128)S(1)}, f32[32,128]{1,0:T(8,128)S(1)}, u32[]{:S(2)}, u32[]{:S(2)}) %collective-permute-start.23) | collective-permute-done | bytes 16416 | tf_op jit(solution)/shard_map/ppermute | solution.py:342
  68.7 0.9 shard_map.104
  69.6 22.6 %all_to_all.11.got = f32[256,2,128]{2,1,0:T(2,128)S(1)} all-to-all(f32[256,2,128]{2,1,0:T(2,128)S(1)} %get-tuple-element.86), channel_id=1, replica_groups=mesh['region'=8,'gy'=8,'gz'=4] {'gy','gz','region'}, dimensions={0} | all-to-all | bytes 524288 | tf_op jit(solution)/shard_map/all_to_all | solution.py:348
  92.3 0.4 shard_map.105.mine
  92.7 0.1 collective-permute-start.25
  92.8 1.3 %collective-permute-done.25.other = f32[264,128]{1,0:T(8,128)S(1)} collective-permute-done((f32[264,128]{1,0:T(8,128)S(1)}, f32[264,128]{1,0:T(8,128)S(1)}, u32[]{:S(2)}, u32[]{:S(2)}) %collective-permute-start.25) | collective-permute-done | bytes 135200 | tf_op jit(solution)/shard_map/ppermute | solution.py:349
  94.1 1.4 %shard_map.106 = (f32[32,768]{1,0:T(8,128)S(1)}, f32[32,768]{1,0:T(8,128)S(1)}, f32[8,32]{1,0:T(8,128)S(1)}, f32[32,128]{1,0:T(8,128)S(1)}, f32[32,128]{1,0:T(8,...) custom-call(f32[8,128]{1,0:T(8,128)S(1)} %shard_map.95.live_ref, ...), custom_call_target="tpu_custom_call" | custom-call | tf_op jit(solution)/shard_map/pallas_call | solution.py:318
  95.5 1.5 %collective-permute-start.26 = (f32[32,128]{1,0:T(8,128)S(1)}, f32[32,128]{1,0:T(8,128)S(1)}, u32[]{:S(2)}, u32[]{:S(2)}) collective-permute-start(f32[32,128]{1,0:T(8,128)S(1)} %get-tuple-element.94), channel_id=1, source_target_pairs={{32,64},{64,32},{96,128},{128,96},{160,192},{192,160},{224,0},{0,2... | collective-permute-start | bytes 49160 | tf_op jit(solution)/shard_map/ppermute | solution.py:342
  97.0 1.0 collective-permute-start.27
  98.1 1.5 %collective-permute-start.29 = (f32[32,128]{1,0:T(8,128)S(1)}, f32[32,128]{1,0:T(8,128)S(1)}, u32[]{:S(2)}, u32[]{:S(2)}) collective-permute-start(f32[32,128]{1,0:T(8,128)S(1)} %get-tuple-element.97), channel_id=1, source_target_pairs={{0,1},{1,0},{2,3},{3,2},{4,5},{5,4},{6,7},{7,6},{8,9},{9,8},{10,11... | collective-permute-start | bytes 49160 | tf_op jit(solution)/shard_map/ppermute | solution.py:342
  99.5 0.1 collective-permute-start.30
  99.7 0.2 collective-permute-done.26.refs_0_
  99.9 0.7 shard_map.107
  100.7 0.1 collective-permute-done.27.refs_1_
  100.8 2.3 %collective-permute-done.28.refs_2_ = f32[32,128]{1,0:T(8,128)S(1)} collective-permute-done((f32[32,128]{1,0:T(8,128)S(1)}, f32[32,128]{1,0:T(8,128)S(1)}, u32[]{:S(2)}, u32[]{:S(2)}) %collective-permute-start.28) | collective-permute-done | bytes 16416 | tf_op jit(solution)/shard_map/ppermute | solution.py:342
  103.0 0.3 collective-permute-done.30.refs_4_
  103.3 0.8 shard_map.108
  (32 shorter events, 0.1 us)
Async XLA Ops:
  1.3 0.9 copy-start.4
  2.2 12.1 %collective-permute-start = (f32[40,128]{1,0:T(8,128)S(1)}, f32[40,128]{1,0:T(8,128)S(1)}, u32[]{:S(2)}, u32[]{:S(2)}) collective-permute-start(f32[40,128]{1,0:T(8,128)S(1)} %get-tuple-element.51), channel_id=1, source_target_pairs={{32,64},{64,32},{96,128},{128,96},{160,192},{192,160},{224,0},{0,2... | collective-permute-start | bytes 61448 | tf_op jit(solution)/shard_map/ppermute | solution.py:342
  4.8 11.0 %collective-permute-start.1 = (f32[40,128]{1,0:T(8,128)S(1)}, f32[40,128]{1,0:T(8,128)S(1)}, u32[]{:S(2)}, u32[]{:S(2)}) collective-permute-start(f32[40,128]{1,0:T(8,128)S(1)} %get-tuple-element.52), channel_id=1, source_target_pairs={{0,4},{4,0},{8,12},{12,8},{16,20},{20,16},{24,28},{28,24},{1,5},{5... | collective-permute-start | bytes 61448 | tf_op jit(solution)/shard_map/ppermute | solution.py:342
  6.7 9.0 %collective-permute-start.2 = (f32[40,128]{1,0:T(8,128)S(1)}, f32[40,128]{1,0:T(8,128)S(1)}, u32[]{:S(2)}, u32[]{:S(2)}) collective-permute-start(f32[40,128]{1,0:T(8,128)S(1)} %get-tuple-element.53), channel_id=1, source_target_pairs={{4,8},{8,4},{12,16},{16,12},{20,24},{24,20},{28,0},{0,28},{5,9},{9... | collective-permute-start | bytes 61448 | tf_op jit(solution)/shard_map/ppermute | solution.py:342
  11.6 4.1 %collective-permute-start.3 = (f32[40,128]{1,0:T(8,128)S(1)}, f32[40,128]{1,0:T(8,128)S(1)}, u32[]{:S(2)}, u32[]{:S(2)}) collective-permute-start(f32[40,128]{1,0:T(8,128)S(1)} %get-tuple-element.54), channel_id=1, source_target_pairs={{0,1},{1,0},{2,3},{3,2},{4,5},{5,4},{6,7},{7,6},{8,9},{9,8},{10,11... | collective-permute-start | bytes 61448 | tf_op jit(solution)/shard_map/ppermute | solution.py:342
  12.2 3.9 %collective-permute-start.4 = (f32[40,128]{1,0:T(8,128)S(1)}, f32[40,128]{1,0:T(8,128)S(1)}, u32[]{:S(2)}, u32[]{:S(2)}) collective-permute-start(f32[40,128]{1,0:T(8,128)S(1)} %get-tuple-element.55), channel_id=1, source_target_pairs={{1,2},{2,1},{3,0},{0,3},{5,6},{6,5},{7,4},{4,7},{9,10},{10,9},{11,... | collective-permute-start | bytes 61448 | tf_op jit(solution)/shard_map/ppermute | solution.py:342
  14.3 1.8 %collective-permute-start.5 = (f32[40,128]{1,0:T(8,128)S(1)}, f32[40,128]{1,0:T(8,128)S(1)}, u32[]{:S(2)}, u32[]{:S(2)}) collective-permute-start(f32[40,128]{1,0:T(8,128)S(1)} %get-tuple-element.56), channel_id=1, source_target_pairs={{0,32},{32,0},{64,96},{96,64},{128,160},{160,128},{192,224},{224,1... | collective-permute-start | bytes 61448 | tf_op jit(solution)/shard_map/ppermute | solution.py:342
  14.3 1.3 %copy-start.2 = (bf16[1,768,768]{2,1,0:T(8,128)(2,1)S(1)}, bf16[1,768,768]{2,1,0:T(8,128)(2,1)}, u32[]{:S(2)}) copy-start(bf16[1,768,768]{2,1,0:T(8,128)(2,1)} %source.2) | copy-start | bytes 3538948
  15.6 0.9 copy-start.5
  15.6 0.9 copy-start.6
  15.7 9.6 %copy-start = (bf16[1,768,768]{2,1,0:T(8,128)(2,1)S(1)}, bf16[1,768,768]{2,1,0:T(8,128)(2,1)}, u32[]{:S(2)}) copy-start(bf16[1,768,768]{2,1,0:T(8,128)(2,1)} %schur.5) | copy-start | bytes 3538948
  15.7 9.6 %copy-start.1 = (bf16[1,768,128]{2,1,0:T(8,128)(2,1)S(1)}, bf16[1,768,128]{2,1,0:T(8,128)(2,1)}, u32[]{:S(2)}) copy-start(bf16[1,768,128]{2,1,0:T(8,128)(2,1)} %coupling.7) | copy-start | bytes 589828
  15.7 9.5 %copy-start.7 = (s32[1,128]{1,0:T(1,128)S(1)}, s32[1,128]{1,0:T(1,128)}, u32[]{:S(2)}) copy-start(s32[1,128]{1,0:T(1,128)} %corner_map.7) | copy-start | bytes 1540
  17.2 5.7 %collective-permute-start.6 = (f32[32,128]{1,0:T(8,128)S(1)}, f32[32,128]{1,0:T(8,128)S(1)}, u32[]{:S(2)}, u32[]{:S(2)}) collective-permute-start(f32[32,128]{1,0:T(8,128)S(1)} %get-tuple-element.59), channel_id=1, source_target_pairs={{32,64},{64,32},{96,128},{128,96},{160,192},{192,160},{224,0},{0,2... | collective-permute-start | bytes 49160 | tf_op jit(solution)/shard_map/ppermute | solution.py:342
  18.1 4.8 %collective-permute-start.7 = (f32[32,128]{1,0:T(8,128)S(1)}, f32[32,128]{1,0:T(8,128)S(1)}, u32[]{:S(2)}, u32[]{:S(2)}) collective-permute-start(f32[32,128]{1,0:T(8,128)S(1)} %get-tuple-element.60), channel_id=1, source_target_pairs={{0,4},{4,0},{8,12},{12,8},{16,20},{20,16},{24,28},{28,24},{1,5},{5... | collective-permute-start | bytes 49160 | tf_op jit(solution)/shard_map/ppermute | solution.py:342
  18.1 4.9 %collective-permute-start.8 = (f32[32,128]{1,0:T(8,128)S(1)}, f32[32,128]{1,0:T(8,128)S(1)}, u32[]{:S(2)}, u32[]{:S(2)}) collective-permute-start(f32[32,128]{1,0:T(8,128)S(1)} %get-tuple-element.61), channel_id=1, source_target_pairs={{4,8},{8,4},{12,16},{16,12},{20,24},{24,20},{28,0},{0,28},{5,9},{9... | collective-permute-start | bytes 49160 | tf_op jit(solution)/shard_map/ppermute | solution.py:342
  20.1 3.7 %collective-permute-start.9 = (f32[32,128]{1,0:T(8,128)S(1)}, f32[32,128]{1,0:T(8,128)S(1)}, u32[]{:S(2)}, u32[]{:S(2)}) collective-permute-start(f32[32,128]{1,0:T(8,128)S(1)} %get-tuple-element.62), channel_id=1, source_target_pairs={{0,1},{1,0},{2,3},{3,2},{4,5},{5,4},{6,7},{7,6},{8,9},{9,8},{10,11... | collective-permute-start | bytes 49160 | tf_op jit(solution)/shard_map/ppermute | solution.py:342
  21.5 3.7 %collective-permute-start.10 = (f32[32,128]{1,0:T(8,128)S(1)}, f32[32,128]{1,0:T(8,128)S(1)}, u32[]{:S(2)}, u32[]{:S(2)}) collective-permute-start(f32[32,128]{1,0:T(8,128)S(1)} %get-tuple-element.63), channel_id=1, source_target_pairs={{1,2},{2,1},{3,0},{0,3},{5,6},{6,5},{7,4},{4,7},{9,10},{10,9},{11,... | collective-permute-start | bytes 49160 | tf_op jit(solution)/shard_map/ppermute | solution.py:342
  22.9 2.4 %collective-permute-start.11 = (f32[32,128]{1,0:T(8,128)S(1)}, f32[32,128]{1,0:T(8,128)S(1)}, u32[]{:S(2)}, u32[]{:S(2)}) collective-permute-start(f32[32,128]{1,0:T(8,128)S(1)} %get-tuple-element.64), channel_id=1, source_target_pairs={{0,32},{32,0},{64,96},{96,64},{128,160},{160,128},{192,224},{224,1... | collective-permute-start | bytes 49160 | tf_op jit(solution)/shard_map/ppermute | solution.py:342
  25.3 23.8 %copy-start.3 = (f32[512,512]{1,0:T(8,128)S(1)}, f32[512,512]{1,0:T(8,128)}, u32[]{:S(2)}) copy-start(f32[512,512]{1,0:T(8,128)} %source.3) | copy-start | bytes 3145732
  49.0 1.4 %collective-permute-start.12 = (f32[264,128]{1,0:T(8,128)S(1)}, f32[264,128]{1,0:T(8,128)S(1)}, u32[]{:S(2)}, u32[]{:S(2)}) collective-permute-start(f32[264,128]{1,0:T(8,128)S(1)} %shard_map.101.mine), channel_id=1, source_target_pairs={{0,32},{32,0},{64,96},{96,64},{128,160},{160,128},{192,224},{224,1... | collective-permute-start | bytes 405512 | tf_op jit(solution)/shard_map/ppermute | solution.py:349
  51.4 4.5 %collective-permute-start.13 = (f32[32,128]{1,0:T(8,128)S(1)}, f32[32,128]{1,0:T(8,128)S(1)}, u32[]{:S(2)}, u32[]{:S(2)}) collective-permute-start(f32[32,128]{1,0:T(8,128)S(1)} %get-tuple-element.72), channel_id=1, source_target_pairs={{32,64},{64,32},{96,128},{128,96},{160,192},{192,160},{224,0},{0,2... | collective-permute-start | bytes 49160 | tf_op jit(solution)/shard_map/ppermute | solution.py:342
  53.0 3.7 %collective-permute-start.14 = (f32[32,128]{1,0:T(8,128)S(1)}, f32[32,128]{1,0:T(8,128)S(1)}, u32[]{:S(2)}, u32[]{:S(2)}) collective-permute-start(f32[32,128]{1,0:T(8,128)S(1)} %get-tuple-element.73), channel_id=1, source_target_pairs={{0,4},{4,0},{8,12},{12,8},{16,20},{20,16},{24,28},{28,24},{1,5},{5... | collective-permute-start | bytes 49160 | tf_op jit(solution)/shard_map/ppermute | solution.py:342
  54.0 5.0 %collective-permute-start.15 = (f32[32,128]{1,0:T(8,128)S(1)}, f32[32,128]{1,0:T(8,128)S(1)}, u32[]{:S(2)}, u32[]{:S(2)}) collective-permute-start(f32[32,128]{1,0:T(8,128)S(1)} %get-tuple-element.74), channel_id=1, source_target_pairs={{4,8},{8,4},{12,16},{16,12},{20,24},{24,20},{28,0},{0,28},{5,9},{9... | collective-permute-start | bytes 49160 | tf_op jit(solution)/shard_map/ppermute | solution.py:342
  54.0 4.9 %collective-permute-start.16 = (f32[32,128]{1,0:T(8,128)S(1)}, f32[32,128]{1,0:T(8,128)S(1)}, u32[]{:S(2)}, u32[]{:S(2)}) collective-permute-start(f32[32,128]{1,0:T(8,128)S(1)} %get-tuple-element.75), channel_id=1, source_target_pairs={{0,1},{1,0},{2,3},{3,2},{4,5},{5,4},{6,7},{7,6},{8,9},{9,8},{10,11... | collective-permute-start | bytes 49160 | tf_op jit(solution)/shard_map/ppermute | solution.py:342
  55.5 3.7 %collective-permute-start.17 = (f32[32,128]{1,0:T(8,128)S(1)}, f32[32,128]{1,0:T(8,128)S(1)}, u32[]{:S(2)}, u32[]{:S(2)}) collective-permute-start(f32[32,128]{1,0:T(8,128)S(1)} %get-tuple-element.76), channel_id=1, source_target_pairs={{1,2},{2,1},{3,0},{0,3},{5,6},{6,5},{7,4},{4,7},{9,10},{10,9},{11,... | collective-permute-start | bytes 49160 | tf_op jit(solution)/shard_map/ppermute | solution.py:342
  55.9 3.3 %collective-permute-start.18 = (f32[32,128]{1,0:T(8,128)S(1)}, f32[32,128]{1,0:T(8,128)S(1)}, u32[]{:S(2)}, u32[]{:S(2)}) collective-permute-start(f32[32,128]{1,0:T(8,128)S(1)} %get-tuple-element.77), channel_id=1, source_target_pairs={{0,32},{32,0},{64,96},{96,64},{128,160},{160,128},{192,224},{224,1... | collective-permute-start | bytes 49160 | tf_op jit(solution)/shard_map/ppermute | solution.py:342
  59.9 5.7 %collective-permute-start.19 = (f32[32,128]{1,0:T(8,128)S(1)}, f32[32,128]{1,0:T(8,128)S(1)}, u32[]{:S(2)}, u32[]{:S(2)}) collective-permute-start(f32[32,128]{1,0:T(8,128)S(1)} %get-tuple-element.80), channel_id=1, source_target_pairs={{32,64},{64,32},{96,128},{128,96},{160,192},{192,160},{224,0},{0,2... | collective-permute-start | bytes 49160 | tf_op jit(solution)/shard_map/ppermute | solution.py:342
  60.1 5.7 %collective-permute-start.20 = (f32[32,128]{1,0:T(8,128)S(1)}, f32[32,128]{1,0:T(8,128)S(1)}, u32[]{:S(2)}, u32[]{:S(2)}) collective-permute-start(f32[32,128]{1,0:T(8,128)S(1)} %get-tuple-element.81), channel_id=1, source_target_pairs={{0,4},{4,0},{8,12},{12,8},{16,20},{20,16},{24,28},{28,24},{1,5},{5... | collective-permute-start | bytes 49160 | tf_op jit(solution)/shard_map/ppermute | solution.py:342
  60.9 4.9 %collective-permute-start.21 = (f32[32,128]{1,0:T(8,128)S(1)}, f32[32,128]{1,0:T(8,128)S(1)}, u32[]{:S(2)}, u32[]{:S(2)}) collective-permute-start(f32[32,128]{1,0:T(8,128)S(1)} %get-tuple-element.82), channel_id=1, source_target_pairs={{4,8},{8,4},{12,16},{16,12},{20,24},{24,20},{28,0},{0,28},{5,9},{9... | collective-permute-start | bytes 49160 | tf_op jit(solution)/shard_map/ppermute | solution.py:342
  63.2 3.7 %collective-permute-start.22 = (f32[32,128]{1,0:T(8,128)S(1)}, f32[32,128]{1,0:T(8,128)S(1)}, u32[]{:S(2)}, u32[]{:S(2)}) collective-permute-start(f32[32,128]{1,0:T(8,128)S(1)} %get-tuple-element.83), channel_id=1, source_target_pairs={{0,1},{1,0},{2,3},{3,2},{4,5},{5,4},{6,7},{7,6},{8,9},{9,8},{10,11... | collective-permute-start | bytes 49160 | tf_op jit(solution)/shard_map/ppermute | solution.py:342
  65.0 3.7 %collective-permute-start.23 = (f32[32,128]{1,0:T(8,128)S(1)}, f32[32,128]{1,0:T(8,128)S(1)}, u32[]{:S(2)}, u32[]{:S(2)}) collective-permute-start(f32[32,128]{1,0:T(8,128)S(1)} %get-tuple-element.84), channel_id=1, source_target_pairs={{1,2},{2,1},{3,0},{0,3},{5,6},{6,5},{7,4},{4,7},{9,10},{10,9},{11,... | collective-permute-start | bytes 49160 | tf_op jit(solution)/shard_map/ppermute | solution.py:342
  65.7 3.1 %collective-permute-start.24 = (f32[32,128]{1,0:T(8,128)S(1)}, f32[32,128]{1,0:T(8,128)S(1)}, u32[]{:S(2)}, u32[]{:S(2)}) collective-permute-start(f32[32,128]{1,0:T(8,128)S(1)} %get-tuple-element.85), channel_id=1, source_target_pairs={{0,32},{32,0},{64,96},{96,64},{128,160},{160,128},{192,224},{224,1... | collective-permute-start | bytes 49160 | tf_op jit(solution)/shard_map/ppermute | solution.py:342
  92.7 1.4 %collective-permute-start.25 = (f32[264,128]{1,0:T(8,128)S(1)}, f32[264,128]{1,0:T(8,128)S(1)}, u32[]{:S(2)}, u32[]{:S(2)}) collective-permute-start(f32[264,128]{1,0:T(8,128)S(1)} %shard_map.105.mine), channel_id=1, source_target_pairs={{0,32},{32,0},{64,96},{96,64},{128,160},{160,128},{192,224},{224,1... | collective-permute-start | bytes 405512 | tf_op jit(solution)/shard_map/ppermute | solution.py:349
  95.5 4.4 %collective-permute-start.26 = (f32[32,128]{1,0:T(8,128)S(1)}, f32[32,128]{1,0:T(8,128)S(1)}, u32[]{:S(2)}, u32[]{:S(2)}) collective-permute-start(f32[32,128]{1,0:T(8,128)S(1)} %get-tuple-element.94), channel_id=1, source_target_pairs={{32,64},{64,32},{96,128},{128,96},{160,192},{192,160},{224,0},{0,2... | collective-permute-start | bytes 49160 | tf_op jit(solution)/shard_map/ppermute | solution.py:342
  97.0 3.7 %collective-permute-start.27 = (f32[32,128]{1,0:T(8,128)S(1)}, f32[32,128]{1,0:T(8,128)S(1)}, u32[]{:S(2)}, u32[]{:S(2)}) collective-permute-start(f32[32,128]{1,0:T(8,128)S(1)} %get-tuple-element.95), channel_id=1, source_target_pairs={{0,4},{4,0},{8,12},{12,8},{16,20},{20,16},{24,28},{28,24},{1,5},{5... | collective-permute-start | bytes 49160 | tf_op jit(solution)/shard_map/ppermute | solution.py:342
  98.1 4.9 %collective-permute-start.28 = (f32[32,128]{1,0:T(8,128)S(1)}, f32[32,128]{1,0:T(8,128)S(1)}, u32[]{:S(2)}, u32[]{:S(2)}) collective-permute-start(f32[32,128]{1,0:T(8,128)S(1)} %get-tuple-element.96), channel_id=1, source_target_pairs={{4,8},{8,4},{12,16},{16,12},{20,24},{24,20},{28,0},{0,28},{5,9},{9... | collective-permute-start | bytes 49160 | tf_op jit(solution)/shard_map/ppermute | solution.py:342
  98.1 4.9 %collective-permute-start.29 = (f32[32,128]{1,0:T(8,128)S(1)}, f32[32,128]{1,0:T(8,128)S(1)}, u32[]{:S(2)}, u32[]{:S(2)}) collective-permute-start(f32[32,128]{1,0:T(8,128)S(1)} %get-tuple-element.97), channel_id=1, source_target_pairs={{0,1},{1,0},{2,3},{3,2},{4,5},{5,4},{6,7},{7,6},{8,9},{9,8},{10,11... | collective-permute-start | bytes 49160 | tf_op jit(solution)/shard_map/ppermute | solution.py:342
  99.5 3.7 %collective-permute-start.30 = (f32[32,128]{1,0:T(8,128)S(1)}, f32[32,128]{1,0:T(8,128)S(1)}, u32[]{:S(2)}, u32[]{:S(2)}) collective-permute-start(f32[32,128]{1,0:T(8,128)S(1)} %get-tuple-element.98), channel_id=1, source_target_pairs={{1,2},{2,1},{3,0},{0,3},{5,6},{6,5},{7,4},{4,7},{9,10},{10,9},{11,... | collective-permute-start | bytes 49160 | tf_op jit(solution)/shard_map/ppermute | solution.py:342
  99.9 3.3 %collective-permute-start.31 = (f32[32,128]{1,0:T(8,128)S(1)}, f32[32,128]{1,0:T(8,128)S(1)}, u32[]{:S(2)}, u32[]{:S(2)}) collective-permute-start(f32[32,128]{1,0:T(8,128)S(1)} %get-tuple-element.99), channel_id=1, source_target_pairs={{0,32},{32,0},{64,96},{96,64},{128,160},{160,128},{192,224},{224,1... | collective-permute-start | bytes 49160 | tf_op jit(solution)/shard_map/ppermute | solution.py:342

commit v5 on v4

--- a/solution.py
+++ b/solution.py
@@ -16,6 +16,7 @@
 SIDE = 32
 HALF = 16
 DEVICES = 256
+HIGHEST = lax.Precision.HIGHEST
 VM = pl.BlockSpec(memory_space=pltpu.VMEM)
 SMEM = pl.BlockSpec(memory_space=pltpu.SMEM)
 
@@ -74,22 +75,16 @@
     return [value[:, f * FACE : (f + 1) * FACE] for f in range(6)]
 
 
-def select_nt(table, value):
-    rows = value.shape[0]
-    high, _ = halves(value)
-    middle, low = halves(value - high.astype(F32))
-    out = matmul_nt(table, jnp.concatenate([high, middle, low], axis=0))
-    return out[:, :rows] + (out[:, rows : 2 * rows] + out[:, 2 * rows :])
+def matmul_nt_exact(left, right):
+    return lax.dot_general(
+        left, right, (((1,), (1,)), ((), ())), precision=HIGHEST, preferred_element_type=F32
+    )
 
 
 def load_sums(left, right):
-    return select_nt(jnp.ones((8, MULT), BF16), left * right)
-
-
-def column(row):
-    r = lax.broadcasted_iota(jnp.int32, (LOADS, LOADS), 0)
-    c = lax.broadcasted_iota(jnp.int32, (LOADS, LOADS), 1)
-    return jnp.sum(jnp.where(r == c, row, 0.0), axis=1, keepdims=True)
+    parts = split_faces(left * right)
+    total = (parts[0] + parts[1]) + (parts[2] + parts[3]) + (parts[4] + parts[5])
+    return matmul_nt_exact(jnp.ones((8, FACE), F32), total)
 
 
 def living_kernel(counts, live_ref):
@@ -107,8 +102,20 @@
     out[...] = source[...]
 
 
-def halves_kernel(source, after, out):
-    out[0], out[1] = halves(source[...])
+def halves_kernel(source, after, out, whole, turned):
+    for c in range(COARSE // FACE):
+        whole[c] = source[:, c * FACE : (c + 1) * FACE]
+    for i in range(2):
+        for c in range(COARSE // FACE):
+            part = whole[c, pl.Slice(i, DEVICES, 2), :].T
+            for h in range(2):
+                turned[h, c * FACE : (c + 1) * FACE, :] = part[:, h * FACE : (h + 1) * FACE]
+        for j in range(2):
+            for h in range(2):
+                high, low = halves(turned[h, pl.Slice(j, DEVICES, 2), :])
+                first, start = j * DEVICES, i * DEVICES + h * FACE
+                out[0, first : first + DEVICES, start : start + FACE] = high
+                out[1, first : first + DEVICES, start : start + FACE] = low
 
 
 def precondition(weight, residual, dirichlet):
@@ -141,8 +148,8 @@
             owned = 2 * ((a * SIZES[1] + b) * SIZES[2] + c)
             target = jnp.where(row == index, owned, target)
             target = jnp.where(row == index + 8, owned + 1, target)
-    chosen = (target == corner_map[0:1, :]).astype(F32).astype(BF16)
-    sums = select_nt(chosen, corner_terms)
+    chosen = (target == corner_map[0:1, :]).astype(F32)
+    sums = matmul_nt_exact(chosen, corner_terms)
     line = lax.broadcasted_iota(jnp.int32, (8, LOADS), 0)
     pair = [
         jnp.where(line == 6, scalar, sums[8 * i : 8 * i + 8]) for i, scalar in enumerate(scalars)
@@ -176,71 +183,69 @@
 BY_COLUMN = ("gy", "gz", "region")
 
 
-def combine_kernel(got, out):
+def combine_kernel(got, out, scratch):
     total = jnp.zeros((8, FACE), F32)
 
-    def column(b, c, line):
+    def line(b, c, index):
         first = (b % SIZES[1] * SIZES[2] + c % SIZES[2]) * SIZES[0]
-        return got[first : first + SIZES[0], line, :]
+        return got[first : first + SIZES[0], index, :]
 
     for b in range(SIZES[1]):
         for c in range(SIZES[2]):
-            here = column(b, c, 0)
-            near = here + column(b - 1, c, 1)
-            near = near + pltpu.roll(pltpu.roll(here, 1, 0) + column(b + 1, c, 1), 96, 1)
-            near = near + pltpu.roll(pltpu.roll(here, 7, 0) + column(b, c - 1, 1), 64, 1)
-            near = near + pltpu.roll(column(b, c + 1, 1), 32, 1)
-            out[pl.Slice(b * SIZES[2] + c, SIZES[0], SIDE), :] = near
+            here = line(b, c, 0)
+            near = here + line(b - 1, c, 1)
+            near = near + pltpu.roll(pltpu.roll(here, 1, 0) + line(b + 1, c, 1), 96, 1)
+            near = near + pltpu.roll(pltpu.roll(here, 7, 0) + line(b, c - 1, 1), 64, 1)
+            near = near + pltpu.roll(line(b, c + 1, 1), 32, 1)
+            scratch[pl.Slice(b * SIZES[2] + c, SIZES[0], SIDE), :] = near
             total = total + here
-    out[DEVICES : DEVICES + 8, :] = jnp.broadcast_to(
-        jnp.sum(total, axis=0, keepdims=True), (8, FACE)
-    )
-
-
-def coarse_sums(mine, other, scratch):
+    out[:, 0:DEVICES] = scratch[...].T[0:LOADS]
+    scalars = jnp.broadcast_to(jnp.sum(total, axis=0, keepdims=True), (FACE, FACE)).T
+    out[:, DEVICES : DEVICES + FACE] = scalars[96:128]
+
+
+def coarse_sums(mine, other):
     odd = coords()[0] % 2 == 1
-
-    def pieces(rows):
-        low = jnp.where(odd, other[rows, :], mine[rows, :])
-        high = jnp.where(odd, mine[rows, :], other[rows, :])
-        return low, high
-
-    def joined(low, high, start):
-        at = pltpu.roll(low, (FACE - start) % FACE, 1) if start else low
-        to = pltpu.roll(high, (FACE - start + HALF) % FACE, 1)
-        lane = lax.broadcasted_iota(jnp.int32, low.shape, 1)
-        return jnp.where(lane < HALF, at, to)[:, 0:LOADS]
-
-    low, high = pieces(slice(0, DEVICES))
-    scratch[pl.Slice(0, DEVICES, 2), :] = joined(low, high, 0)
-    scratch[pl.Slice(1, DEVICES, 2), :] = joined(low, high, HALF)
-    low, high = pieces(slice(DEVICES, DEVICES + 8))
-    scalars = [joined(low, high, 96 + i * HALF)[0:1] for i in range(2)]
-    return scratch[...], scalars
+    low = jnp.where(odd, other[...], mine[...])
+    high = jnp.where(odd, mine[...], other[...])
+    both = [
+        jnp.concatenate([low[i * HALF : (i + 1) * HALF], high[i * HALF : (i + 1) * HALF]], axis=0)
+        for i in range(2)
+    ]
+    gathered = jnp.concatenate([value[:, 0:DEVICES] for value in both], axis=1)
+    return gathered, [value[:, DEVICES : DEVICES + 1] for value in both]
 
 
 def coarse_solve(inverse, gathered, corner_map, coupling):
-    vec_high, vec_low = halves(gathered)
-    both = matmul(inverse[0], jnp.concatenate([vec_high, vec_low], axis=1))
-    solved = both[:, :LOADS] + (both[:, LOADS:] + matmul(inverse[1], vec_high))
+    high, low = halves(gathered)
+    both = matmul(jnp.concatenate([high, low], axis=0), inverse[0])
+    solved = both[:LOADS] + (both[LOADS:] + matmul(high, inverse[1]))
     solved = solved.astype(BF16)
     row = lax.broadcasted_iota(jnp.int32, (COARSE, FACE), 0)
-    chosen = (row == corner_map[0:1, :]).astype(F32).astype(BF16)
-    picked = lax.dot_general(
-        solved, chosen, (((0,), (0,)), ((), ())), preferred_element_type=F32
-    ).astype(BF16)
+    index = corner_map[0:1, :]
+    index = (index & 1) * DEVICES + (index >> 1)
+    chosen = (row == index).astype(F32).astype(BF16)
+    picked = matmul(solved, chosen).astype(BF16)
     return matmul_nt(picked, coupling[0]), solved.astype(F32)
 
 
 def coarse_dot(solved, gathered):
-    return jnp.sum(solved * gathered, axis=0, keepdims=True)
+    return jnp.sum(solved * gathered, axis=1, keepdims=True)
+
+
+def lanes(*columns):
+    lane = lax.broadcasted_iota(jnp.int32, (LOADS, FACE), 1)
+    out = jnp.zeros((LOADS, FACE), F32)
+    for index, value in enumerate(columns):
+        out = jnp.where(lane == index, value, out)
+    return out
 
 
 def third_kernel(live_ref, corner_map, coupling, inverse, mine, other, local_ref, *refs):
     image_ref, gathered_ref, solved_ref, scalar_ref = refs[:4]
-    sends, scratch = refs[4:10], refs[10]
-    live = live_ref[0:1, 0:1]
-    gathered, (resid_dot, local_curve) = coarse_sums(mine, other, scratch)
+    sends = refs[4:]
+    live = live_ref[0:1, 0:1]
+    gathered, (resid_dot, local_curve) = coarse_sums(mine, other)
     coarse_terms, solved = coarse_solve(inverse, gathered, corner_map, coupling)
     image = live * (local_ref[...] + coarse_terms)
     curvature = local_curve + coarse_dot(solved, gathered)
@@ -248,16 +253,14 @@
     image_ref[...] = image
     gathered_ref[...] = gathered
     solved_ref[...] = solved
-    scalar_ref[...] = jnp.concatenate(
-        [resid_dot, local_curve, step_size, curvature, jnp.zeros((4, LOADS), F32)], axis=0
-    )
+    scalar_ref[...] = lanes(resid_dot, local_curve, step_size, curvature)
     store_sends(sends, split_faces(image))
 
 
 def fourth_kernel(live_ref, pairing, dirichlet, resid, weight_ref, image_ref, scalar_ref, *refs):
     recvs, (resid_out, terms, dots), sends = refs[:6], refs[6:9], refs[9:]
     live = live_ref[0:1, 0:1]
-    step_size = column(scalar_ref[2:3, :])
+    step_size = scalar_ref[:, 2:3]
     residual = resid[...] - step_size * (live * (image_ref[...] + partner(recvs, pairing)))
     resid_out[...] = residual
     applied = precondition(weight_ref[0:1, :], residual, dirichlet)
@@ -284,34 +287,34 @@
     scalar_ref, z_ref, precond_ref, *refs
 ):
     direction_ref, image_ref, step_ref = refs[:3]
-    sends, scratch = refs[3:9], refs[9]
-    live = live_ref[0:1, 0:1]
-    gathered, (new_dot, square) = coarse_sums(mine, other, scratch)
-    beta = new_dot / scalar_ref[0:1, :]
-    cross = -beta * scalar_ref[3:4, :] - coarse_dot(solved_ref[...], gathered)
+    sends = refs[3:]
+    live = live_ref[0:1, 0:1]
+    gathered, (new_dot, square) = coarse_sums(mine, other)
+    beta = new_dot / scalar_ref[:, 0:1]
+    cross = -beta * scalar_ref[:, 3:4] - coarse_dot(solved_ref[...], gathered)
     gathered = gathered + beta * gathered_ref[...]
     coarse_terms, solved = coarse_solve(inverse, gathered, corner_map, coupling)
-    local_curve = square + beta * (2.0 * cross + beta * scalar_ref[1:2, :])
+    local_curve = square + beta * (2.0 * cross + beta * scalar_ref[:, 1:2])
     step_size = new_dot / (local_curve + coarse_dot(solved, gathered))
     first = z_ref[...]
-    direction = precond_ref[...] + column(beta) * first
+    direction = precond_ref[...] + beta * first
     local_terms = matmul(direction.astype(BF16), schur[0])
     image = live * (local_terms + coarse_terms)
     image_ref[...] = image
     store_sends(sends, split_faces(image))
-    step_ref[...] = jnp.broadcast_to(step_size, (8, LOADS))
+    step_ref[...] = lanes(step_size)
     direction_ref[...] = direction
 
 
 def solution_kernel(scalar_ref, first, step_ref, direction, out):
-    out[0] = column(scalar_ref[2:3, :]) * first[...] + column(step_ref[0:1, :]) * direction[...]
+    out[0] = scalar_ref[:, 2:3] * first[...] + step_ref[:, 0:1] * direction[...]
 
 
 def seventh_kernel(live_ref, pairing, resid, image_ref, step_ref, *refs):
     recvs, (out,) = refs[:6], refs[6:]
     live = live_ref[0:1, 0:1]
     image = live * (image_ref[...] + partner(recvs, pairing))
-    out[0] = resid[...] - column(step_ref[0:1, :]) * image
+    out[0] = resid[...] - step_ref[:, 0:1] * image
 
 
 def call(kernel, shapes, *operands, scratch=(), cost=None, spec=VM):
@@ -345,7 +348,10 @@
 
 
 def total_sums(message):
-    (mine,) = call(combine_kernel, [(DEVICES + 8, FACE)], lax.all_to_all(message, BY_COLUMN, 0, 0))
+    (mine,) = call(
+        combine_kernel, [(LOADS, DEVICES + FACE)], lax.all_to_all(message, BY_COLUMN, 0, 0),
+        scratch=[pltpu.VMEM((DEVICES, FACE), F32)],
+    )
     return mine, lax.ppermute(mine, AXES[0], matched(SIZES[0], 0))
 
 
@@ -353,7 +359,7 @@
     vector = (LOADS, MULT)
     faces = [(LOADS, FACE)] * 6
     small = (8, LOADS)
-    solver_scratch = [pltpu.VMEM((COARSE, LOADS), F32)]
+    wide = (LOADS, FACE)
 
     pairing = pairing.reshape(6, 1, FACE)
     cost = pl.CostEstimate(flops=0, bytes_accessed=4 << 20, transcendentals=0)
@@ -365,16 +371,19 @@
         live, loads, pairing, dirichlet, *exchange(sends),
     )
     (inverse,) = call(
-        halves_kernel, [jax.ShapeDtypeStruct((2, COARSE, COARSE), BF16)], coarse_inverse, dots
+        halves_kernel, [jax.ShapeDtypeStruct((2, COARSE, COARSE), BF16)], coarse_inverse, dots,
+        scratch=[
+            pltpu.VMEM((COARSE // FACE, COARSE, FACE), F32),
+            pltpu.VMEM((2, COARSE, FACE), F32),
+        ],
     )
     first, local_terms, message = call(
         second_kernel, [vector, vector, (DEVICES, 2, FACE)],
         live, pairing, corner_map, schur, coupling, terms, dots, *exchange(sends),
     )
     image, gathered, solved, scalars, *sends = call(
-        third_kernel, [vector, (COARSE, LOADS), (COARSE, LOADS), small] + faces,
+        third_kernel, [vector, (LOADS, COARSE), (LOADS, COARSE), wide] + faces,
         live, corner_map, coupling, inverse, *total_sums(message), local_terms,
-        scratch=solver_scratch,
     )
     resid, terms, dots, *sends = call(
         fourth_kernel, [vector, vector, small] + faces,
@@ -385,9 +394,9 @@
         live, pairing, corner_map, schur, coupling, terms, dots, *exchange(sends),
     )
     direction, image, step, *sends = call(
-        sixth_kernel, [vector, vector, small] + faces,
+        sixth_kernel, [vector, vector, wide] + faces,
         live, corner_map, schur, coupling, inverse, *total_sums(message),
-        gathered, solved, scalars, first, precond, scratch=solver_scratch,
+        gathered, solved, scalars, first, precond,
     )
     (solution_out,) = call(solution_kernel, [(1,) + vector], scalars, first, step, direction)
     (residual_out,) = call(

time: 105 us -> 103 us (0.981)
  Pallas kernels: 8.16 us -> 7.05 us
    pallas_call x14, Pallas kernels: 8.16 us -> 7.05 us  [call(): pl.pallas_call(kernel, out_shape=[shape if hasattr(shape, 'dtype') else j...]
  transfers between devices with their start and end apart: 32 -> 32, of which waited for: 17 -> 16; matrix products, arithmetic and copies ran while one was open for 0% -> 0% of each run, Pallas kernels for 1% -> 1%
where the time goes in v5:
time: 103 us
  blocking collectives  45 us (44%)
  starting transfers between devices  32.3 us (31%)
  waiting for transfers between devices  14.1 us (14%)
  Pallas kernels  7.05 us (7%)
  local copies, waits for them, and re-layouts  2.6 us (3%)
  between operations  1.46 us (1%)
    all_to_all x2, blocking collectives, total_sums(): lax.all_to_all(message, BY_COLUMN, 0, 0)  45 us
    ppermute x30, starting transfers between devices, exchange(): lax.ppermute(value, AXES[k // 2], matched(SIZES[k // 2], k % 2))  32.2 us
    ppermute x30, waiting for transfers between devices, exchange(): lax.ppermute(value, AXES[k // 2], matched(SIZES[k // 2], k % 2))  12.2 us
    pallas_call x14, Pallas kernels, call(): pl.pallas_call(kernel, out_shape=[shape if hasattr(shape, 'dtype') else j...  7.05 us
    unnamed x16, local copies, waits for them, and re-layouts  2.6 us
  transfers between devices with their start and end apart: 32, of which 16 were waited for; matrix products, arithmetic and copies ran while one was open for 0% of the time, Pallas kernels for 1%

profile of v5, /device:TPU:2, one launch (start us, length us, event | category | flops | bytes accessed | tf_op | source)
XLA Modules:
  0.0 102.6 jit_solution(8257461935658933250)
XLA Ops:
  1.3 0.0 copy-start.4
  1.3 0.9 copy-done.4
  2.2 2.5 %collective-permute-start = (f32[40,128]{1,0:T(8,128)S(1)}, f32[40,128]{1,0:T(8,128)S(1)}, u32[]{:S(2)}, u32[]{:S(2)}) collective-permute-start(f32[40,128]{1,0:T(8,128)S(1)} %get-tuple-element.51), channel_id=1, source_target_pairs={{32,64},{64,32},{96,128},{128,96},{160,192},{192,160},{224,0},{0,2... | collective-permute-start | bytes 61448 | tf_op jit(solution)/shard_map/ppermute | solution.py:345
  4.8 1.9 %collective-permute-start.1 = (f32[40,128]{1,0:T(8,128)S(1)}, f32[40,128]{1,0:T(8,128)S(1)}, u32[]{:S(2)}, u32[]{:S(2)}) collective-permute-start(f32[40,128]{1,0:T(8,128)S(1)} %get-tuple-element.52), channel_id=1, source_target_pairs={{0,4},{4,0},{8,12},{12,8},{16,20},{20,16},{24,28},{28,24},{1,5},{5... | collective-permute-start | bytes 61448 | tf_op jit(solution)/shard_map/ppermute | solution.py:345
  6.7 4.9 %collective-permute-start.2 = (f32[40,128]{1,0:T(8,128)S(1)}, f32[40,128]{1,0:T(8,128)S(1)}, u32[]{:S(2)}, u32[]{:S(2)}) collective-permute-start(f32[40,128]{1,0:T(8,128)S(1)} %get-tuple-element.53), channel_id=1, source_target_pairs={{4,8},{8,4},{12,16},{16,12},{20,24},{24,20},{28,0},{0,28},{5,9},{9... | collective-permute-start | bytes 61448 | tf_op jit(solution)/shard_map/ppermute | solution.py:345
  11.6 0.5 collective-permute-start.3
  12.2 2.2 %collective-permute-start.4 = (f32[40,128]{1,0:T(8,128)S(1)}, f32[40,128]{1,0:T(8,128)S(1)}, u32[]{:S(2)}, u32[]{:S(2)}) collective-permute-start(f32[40,128]{1,0:T(8,128)S(1)} %get-tuple-element.55), channel_id=1, source_target_pairs={{1,2},{2,1},{3,0},{0,3},{5,6},{6,5},{7,4},{4,7},{9,10},{10,9},{11,... | collective-permute-start | bytes 61448 | tf_op jit(solution)/shard_map/ppermute | solution.py:345
  14.3 1.3 %copy-done.2 = bf16[1,768,768]{2,1,0:T(8,128)(2,1)S(1)} copy-done((bf16[1,768,768]{2,1,0:T(8,128)(2,1)S(1)}, bf16[1,768,768]{2,1,0:T(8,128)(2,1)}, u32[]{:S(2)}) %copy-start.2) | copy-done | bytes 1179672
  15.6 0.1 shard_map.96.dirichlet
  15.7 0.0 copy-start
  15.7 0.0 copy-start.1
  15.7 0.0 copy-start.7
  15.8 0.3 collective-permute-done.4.refs_4_
  16.1 0.4 copy-done.5
  16.5 0.5 shard_map.98
  17.0 0.9 collective-permute-start.6
  17.9 2.0 %collective-permute-start.8 = (f32[32,128]{1,0:T(8,128)S(1)}, f32[32,128]{1,0:T(8,128)S(1)}, u32[]{:S(2)}, u32[]{:S(2)}) collective-permute-start(f32[32,128]{1,0:T(8,128)S(1)} %get-tuple-element.61), channel_id=1, source_target_pairs={{4,8},{8,4},{12,16},{16,12},{20,24},{24,20},{28,0},{0,28},{5,9},{9... | collective-permute-start | bytes 49160 | tf_op jit(solution)/shard_map/ppermute | solution.py:345
  19.9 1.4 %collective-permute-start.9 = (f32[32,128]{1,0:T(8,128)S(1)}, f32[32,128]{1,0:T(8,128)S(1)}, u32[]{:S(2)}, u32[]{:S(2)}) collective-permute-start(f32[32,128]{1,0:T(8,128)S(1)} %get-tuple-element.62), channel_id=1, source_target_pairs={{0,1},{1,0},{2,3},{3,2},{4,5},{5,4},{6,7},{7,6},{8,9},{9,8},{10,11... | collective-permute-start | bytes 49160 | tf_op jit(solution)/shard_map/ppermute | solution.py:345
  21.3 1.4 %collective-permute-start.10 = (f32[32,128]{1,0:T(8,128)S(1)}, f32[32,128]{1,0:T(8,128)S(1)}, u32[]{:S(2)}, u32[]{:S(2)}) collective-permute-start(f32[32,128]{1,0:T(8,128)S(1)} %get-tuple-element.63), channel_id=1, source_target_pairs={{1,2},{2,1},{3,0},{0,3},{5,6},{6,5},{7,4},{4,7},{9,10},{10,9},{11,... | collective-permute-start | bytes 49160 | tf_op jit(solution)/shard_map/ppermute | solution.py:345
  22.8 0.0 collective-permute-done.8.refs_2_
  22.8 0.8 collective-permute-done.9.refs_3_
  23.6 1.4 %collective-permute-done.10.refs_4_ = f32[32,128]{1,0:T(8,128)S(1)} collective-permute-done((f32[32,128]{1,0:T(8,128)S(1)}, f32[32,128]{1,0:T(8,128)S(1)}, u32[]{:S(2)}, u32[]{:S(2)}) %collective-permute-start.10) | collective-permute-done | bytes 16416 | tf_op jit(solution)/shard_map/ppermute | solution.py:345
  25.1 0.0 copy-start.3
  25.1 0.7 shard_map.100
  25.9 22.4 %all_to_all.10.got = f32[256,2,128]{2,1,0:T(2,128)S(1)} all-to-all(f32[256,2,128]{2,1,0:T(2,128)S(1)} %get-tuple-element.65), channel_id=1, replica_groups=mesh['region'=8,'gy'=8,'gz'=4] {'gy','gz','region'}, dimensions={0} | all-to-all | bytes 524288 | tf_op jit(solution)/shard_map/all_to_all | solution.py:352
  48.3 0.5 shard_map.101.mine
  48.8 0.1 collective-permute-start.12
  48.9 0.5 shard_map.99.inverse
  49.4 0.7 collective-permute-done.12.other
  50.1 0.6 shard_map.102
  50.7 1.6 %collective-permute-start.13 = (f32[32,128]{1,0:T(8,128)S(1)}, f32[32,128]{1,0:T(8,128)S(1)}, u32[]{:S(2)}, u32[]{:S(2)}) collective-permute-start(f32[32,128]{1,0:T(8,128)S(1)} %get-tuple-element.72), channel_id=1, source_target_pairs={{32,64},{64,32},{96,128},{128,96},{160,192},{192,160},{224,0},{0,2... | collective-permute-start | bytes 49160 | tf_op jit(solution)/shard_map/ppermute | solution.py:345
  52.2 1.0 %collective-permute-start.14 = (f32[32,128]{1,0:T(8,128)S(1)}, f32[32,128]{1,0:T(8,128)S(1)}, u32[]{:S(2)}, u32[]{:S(2)}) collective-permute-start(f32[32,128]{1,0:T(8,128)S(1)} %get-tuple-element.73), channel_id=1, source_target_pairs={{0,4},{4,0},{8,12},{12,8},{16,20},{20,16},{24,28},{28,24},{1,5},{5... | collective-permute-start | bytes 49160 | tf_op jit(solution)/shard_map/ppermute | solution.py:345
  53.3 1.5 %collective-permute-start.16 = (f32[32,128]{1,0:T(8,128)S(1)}, f32[32,128]{1,0:T(8,128)S(1)}, u32[]{:S(2)}, u32[]{:S(2)}) collective-permute-start(f32[32,128]{1,0:T(8,128)S(1)} %get-tuple-element.75), channel_id=1, source_target_pairs={{0,1},{1,0},{2,3},{3,2},{4,5},{5,4},{6,7},{7,6},{8,9},{9,8},{10,11... | collective-permute-start | bytes 49160 | tf_op jit(solution)/shard_map/ppermute | solution.py:345
  54.7 0.1 collective-permute-start.17
  54.9 0.2 collective-permute-done.13.refs_0_
  55.1 0.8 collective-permute-done.14.refs_1_
  56.0 2.3 %collective-permute-done.15.refs_2_ = f32[32,128]{1,0:T(8,128)S(1)} collective-permute-done((f32[32,128]{1,0:T(8,128)S(1)}, f32[32,128]{1,0:T(8,128)S(1)}, u32[]{:S(2)}, u32[]{:S(2)}) %collective-permute-start.15) | collective-permute-done | bytes 16416 | tf_op jit(solution)/shard_map/ppermute | solution.py:345
  58.2 0.3 collective-permute-done.17.refs_4_
  58.5 0.5 shard_map.103
  58.9 0.2 collective-permute-start.19
  59.1 0.9 collective-permute-start.20
  60.0 2.4 %collective-permute-start.21 = (f32[32,128]{1,0:T(8,128)S(1)}, f32[32,128]{1,0:T(8,128)S(1)}, u32[]{:S(2)}, u32[]{:S(2)}) collective-permute-start(f32[32,128]{1,0:T(8,128)S(1)} %get-tuple-element.82), channel_id=1, source_target_pairs={{4,8},{8,4},{12,16},{16,12},{20,24},{24,20},{28,0},{0,28},{5,9},{9... | collective-permute-start | bytes 49160 | tf_op jit(solution)/shard_map/ppermute | solution.py:345
  62.4 1.8 %collective-permute-start.22 = (f32[32,128]{1,0:T(8,128)S(1)}, f32[32,128]{1,0:T(8,128)S(1)}, u32[]{:S(2)}, u32[]{:S(2)}) collective-permute-start(f32[32,128]{1,0:T(8,128)S(1)} %get-tuple-element.83), channel_id=1, source_target_pairs={{0,1},{1,0},{2,3},{3,2},{4,5},{5,4},{6,7},{7,6},{8,9},{9,8},{10,11... | collective-permute-start | bytes 49160 | tf_op jit(solution)/shard_map/ppermute | solution.py:345
  64.2 0.5 collective-permute-start.23
  64.7 0.1 collective-permute-start.24
  64.8 0.2 collective-permute-done.21.refs_2_
  65.0 1.2 %collective-permute-done.22.refs_3_ = f32[32,128]{1,0:T(8,128)S(1)} collective-permute-done((f32[32,128]{1,0:T(8,128)S(1)}, f32[32,128]{1,0:T(8,128)S(1)}, u32[]{:S(2)}, u32[]{:S(2)}) %collective-permute-start.22) | collective-permute-done | bytes 16416 | tf_op jit(solution)/shard_map/ppermute | solution.py:345
  66.1 1.8 %collective-permute-done.23.refs_4_ = f32[32,128]{1,0:T(8,128)S(1)} collective-permute-done((f32[32,128]{1,0:T(8,128)S(1)}, f32[32,128]{1,0:T(8,128)S(1)}, u32[]{:S(2)}, u32[]{:S(2)}) %collective-permute-start.23) | collective-permute-done | bytes 16416 | tf_op jit(solution)/shard_map/ppermute | solution.py:345
  67.9 0.8 shard_map.104
  68.7 22.6 %all_to_all.11.got = f32[256,2,128]{2,1,0:T(2,128)S(1)} all-to-all(f32[256,2,128]{2,1,0:T(2,128)S(1)} %get-tuple-element.86), channel_id=1, replica_groups=mesh['region'=8,'gy'=8,'gz'=4] {'gy','gz','region'}, dimensions={0} | all-to-all | bytes 524288 | tf_op jit(solution)/shard_map/all_to_all | solution.py:352
  91.3 0.5 shard_map.105.mine
  91.8 0.1 collective-permute-start.25
  91.9 1.2 %collective-permute-done.25.other = f32[32,384]{1,0:T(8,128)S(1)} collective-permute-done((f32[32,384]{1,0:T(8,128)S(1)}, f32[32,384]{1,0:T(8,128)S(1)}, u32[]{:S(2)}, u32[]{:S(2)}) %collective-permute-start.25) | collective-permute-done | bytes 49184 | tf_op jit(solution)/shard_map/ppermute | solution.py:355
  93.1 0.9 shard_map.106
  94.0 1.5 %collective-permute-start.26 = (f32[32,128]{1,0:T(8,128)S(1)}, f32[32,128]{1,0:T(8,128)S(1)}, u32[]{:S(2)}, u32[]{:S(2)}) collective-permute-start(f32[32,128]{1,0:T(8,128)S(1)} %get-tuple-element.94), channel_id=1, source_target_pairs={{32,64},{64,32},{96,128},{128,96},{160,192},{192,160},{224,0},{0,2... | collective-permute-start | bytes 49160 | tf_op jit(solution)/shard_map/ppermute | solution.py:345
  95.5 1.0 %collective-permute-start.27 = (f32[32,128]{1,0:T(8,128)S(1)}, f32[32,128]{1,0:T(8,128)S(1)}, u32[]{:S(2)}, u32[]{:S(2)}) collective-permute-start(f32[32,128]{1,0:T(8,128)S(1)} %get-tuple-element.95), channel_id=1, source_target_pairs={{0,4},{4,0},{8,12},{12,8},{16,20},{20,16},{24,28},{28,24},{1,5},{5... | collective-permute-start | bytes 49160 | tf_op jit(solution)/shard_map/ppermute | solution.py:345
  96.6 1.5 %collective-permute-start.29 = (f32[32,128]{1,0:T(8,128)S(1)}, f32[32,128]{1,0:T(8,128)S(1)}, u32[]{:S(2)}, u32[]{:S(2)}) collective-permute-start(f32[32,128]{1,0:T(8,128)S(1)} %get-tuple-element.97), channel_id=1, source_target_pairs={{0,1},{1,0},{2,3},{3,2},{4,5},{5,4},{6,7},{7,6},{8,9},{9,8},{10,11... | collective-permute-start | bytes 49160 | tf_op jit(solution)/shard_map/ppermute | solution.py:345
  98.0 0.1 collective-permute-start.30
  98.2 0.2 collective-permute-done.26.refs_0_
  98.4 0.7 shard_map.107
  99.2 0.1 collective-permute-done.27.refs_1_
  99.3 2.2 %collective-permute-done.28.refs_2_ = f32[32,128]{1,0:T(8,128)S(1)} collective-permute-done((f32[32,128]{1,0:T(8,128)S(1)}, f32[32,128]{1,0:T(8,128)S(1)}, u32[]{:S(2)}, u32[]{:S(2)}) %collective-permute-start.28) | collective-permute-done | bytes 16416 | tf_op jit(solution)/shard_map/ppermute | solution.py:345
  101.5 0.3 collective-permute-done.30.refs_4_
  101.8 0.8 shard_map.108
  (32 shorter events, 0.1 us)
Async XLA Ops:
  1.3 0.9 copy-start.4
  2.2 12.1 %collective-permute-start = (f32[40,128]{1,0:T(8,128)S(1)}, f32[40,128]{1,0:T(8,128)S(1)}, u32[]{:S(2)}, u32[]{:S(2)}) collective-permute-start(f32[40,128]{1,0:T(8,128)S(1)} %get-tuple-element.51), channel_id=1, source_target_pairs={{32,64},{64,32},{96,128},{128,96},{160,192},{192,160},{224,0},{0,2... | collective-permute-start | bytes 61448 | tf_op jit(solution)/shard_map/ppermute | solution.py:345
  4.8 11.0 %collective-permute-start.1 = (f32[40,128]{1,0:T(8,128)S(1)}, f32[40,128]{1,0:T(8,128)S(1)}, u32[]{:S(2)}, u32[]{:S(2)}) collective-permute-start(f32[40,128]{1,0:T(8,128)S(1)} %get-tuple-element.52), channel_id=1, source_target_pairs={{0,4},{4,0},{8,12},{12,8},{16,20},{20,16},{24,28},{28,24},{1,5},{5... | collective-permute-start | bytes 61448 | tf_op jit(solution)/shard_map/ppermute | solution.py:345
  6.7 9.0 %collective-permute-start.2 = (f32[40,128]{1,0:T(8,128)S(1)}, f32[40,128]{1,0:T(8,128)S(1)}, u32[]{:S(2)}, u32[]{:S(2)}) collective-permute-start(f32[40,128]{1,0:T(8,128)S(1)} %get-tuple-element.53), channel_id=1, source_target_pairs={{4,8},{8,4},{12,16},{16,12},{20,24},{24,20},{28,0},{0,28},{5,9},{9... | collective-permute-start | bytes 61448 | tf_op jit(solution)/shard_map/ppermute | solution.py:345
  11.6 4.1 %collective-permute-start.3 = (f32[40,128]{1,0:T(8,128)S(1)}, f32[40,128]{1,0:T(8,128)S(1)}, u32[]{:S(2)}, u32[]{:S(2)}) collective-permute-start(f32[40,128]{1,0:T(8,128)S(1)} %get-tuple-element.54), channel_id=1, source_target_pairs={{0,1},{1,0},{2,3},{3,2},{4,5},{5,4},{6,7},{7,6},{8,9},{9,8},{10,11... | collective-permute-start | bytes 61448 | tf_op jit(solution)/shard_map/ppermute | solution.py:345
  12.2 3.9 %collective-permute-start.4 = (f32[40,128]{1,0:T(8,128)S(1)}, f32[40,128]{1,0:T(8,128)S(1)}, u32[]{:S(2)}, u32[]{:S(2)}) collective-permute-start(f32[40,128]{1,0:T(8,128)S(1)} %get-tuple-element.55), channel_id=1, source_target_pairs={{1,2},{2,1},{3,0},{0,3},{5,6},{6,5},{7,4},{4,7},{9,10},{10,9},{11,... | collective-permute-start | bytes 61448 | tf_op jit(solution)/shard_map/ppermute | solution.py:345
  14.3 1.8 %collective-permute-start.5 = (f32[40,128]{1,0:T(8,128)S(1)}, f32[40,128]{1,0:T(8,128)S(1)}, u32[]{:S(2)}, u32[]{:S(2)}) collective-permute-start(f32[40,128]{1,0:T(8,128)S(1)} %get-tuple-element.56), channel_id=1, source_target_pairs={{0,32},{32,0},{64,96},{96,64},{128,160},{160,128},{192,224},{224,1... | collective-permute-start | bytes 61448 | tf_op jit(solution)/shard_map/ppermute | solution.py:345
  14.3 1.3 %copy-start.2 = (bf16[1,768,768]{2,1,0:T(8,128)(2,1)S(1)}, bf16[1,768,768]{2,1,0:T(8,128)(2,1)}, u32[]{:S(2)}) copy-start(bf16[1,768,768]{2,1,0:T(8,128)(2,1)} %source.2) | copy-start | bytes 3538948
  15.6 0.9 copy-start.5
  15.6 0.9 copy-start.6
  15.7 9.4 %copy-start = (bf16[1,768,768]{2,1,0:T(8,128)(2,1)S(1)}, bf16[1,768,768]{2,1,0:T(8,128)(2,1)}, u32[]{:S(2)}) copy-start(bf16[1,768,768]{2,1,0:T(8,128)(2,1)} %schur.5) | copy-start | bytes 3538948
  15.7 9.4 %copy-start.1 = (bf16[1,768,128]{2,1,0:T(8,128)(2,1)S(1)}, bf16[1,768,128]{2,1,0:T(8,128)(2,1)}, u32[]{:S(2)}) copy-start(bf16[1,768,128]{2,1,0:T(8,128)(2,1)} %coupling.7) | copy-start | bytes 589828
  15.7 9.4 %copy-start.7 = (s32[1,128]{1,0:T(1,128)S(1)}, s32[1,128]{1,0:T(1,128)}, u32[]{:S(2)}) copy-start(s32[1,128]{1,0:T(1,128)} %corner_map.7) | copy-start | bytes 1540
  17.0 5.8 %collective-permute-start.6 = (f32[32,128]{1,0:T(8,128)S(1)}, f32[32,128]{1,0:T(8,128)S(1)}, u32[]{:S(2)}, u32[]{:S(2)}) collective-permute-start(f32[32,128]{1,0:T(8,128)S(1)} %get-tuple-element.59), channel_id=1, source_target_pairs={{32,64},{64,32},{96,128},{128,96},{160,192},{192,160},{224,0},{0,2... | collective-permute-start | bytes 49160 | tf_op jit(solution)/shard_map/ppermute | solution.py:345
  17.9 4.9 %collective-permute-start.7 = (f32[32,128]{1,0:T(8,128)S(1)}, f32[32,128]{1,0:T(8,128)S(1)}, u32[]{:S(2)}, u32[]{:S(2)}) collective-permute-start(f32[32,128]{1,0:T(8,128)S(1)} %get-tuple-element.60), channel_id=1, source_target_pairs={{0,4},{4,0},{8,12},{12,8},{16,20},{20,16},{24,28},{28,24},{1,5},{5... | collective-permute-start | bytes 49160 | tf_op jit(solution)/shard_map/ppermute | solution.py:345
  17.9 4.9 %collective-permute-start.8 = (f32[32,128]{1,0:T(8,128)S(1)}, f32[32,128]{1,0:T(8,128)S(1)}, u32[]{:S(2)}, u32[]{:S(2)}) collective-permute-start(f32[32,128]{1,0:T(8,128)S(1)} %get-tuple-element.61), channel_id=1, source_target_pairs={{4,8},{8,4},{12,16},{16,12},{20,24},{24,20},{28,0},{0,28},{5,9},{9... | collective-permute-start | bytes 49160 | tf_op jit(solution)/shard_map/ppermute | solution.py:345
  19.9 3.7 %collective-permute-start.9 = (f32[32,128]{1,0:T(8,128)S(1)}, f32[32,128]{1,0:T(8,128)S(1)}, u32[]{:S(2)}, u32[]{:S(2)}) collective-permute-start(f32[32,128]{1,0:T(8,128)S(1)} %get-tuple-element.62), channel_id=1, source_target_pairs={{0,1},{1,0},{2,3},{3,2},{4,5},{5,4},{6,7},{7,6},{8,9},{9,8},{10,11... | collective-permute-start | bytes 49160 | tf_op jit(solution)/shard_map/ppermute | solution.py:345
  21.3 3.7 %collective-permute-start.10 = (f32[32,128]{1,0:T(8,128)S(1)}, f32[32,128]{1,0:T(8,128)S(1)}, u32[]{:S(2)}, u32[]{:S(2)}) collective-permute-start(f32[32,128]{1,0:T(8,128)S(1)} %get-tuple-element.63), channel_id=1, source_target_pairs={{1,2},{2,1},{3,0},{0,3},{5,6},{6,5},{7,4},{4,7},{9,10},{10,9},{11,... | collective-permute-start | bytes 49160 | tf_op jit(solution)/shard_map/ppermute | solution.py:345
  22.8 2.3 %collective-permute-start.11 = (f32[32,128]{1,0:T(8,128)S(1)}, f32[32,128]{1,0:T(8,128)S(1)}, u32[]{:S(2)}, u32[]{:S(2)}) collective-permute-start(f32[32,128]{1,0:T(8,128)S(1)} %get-tuple-element.64), channel_id=1, source_target_pairs={{0,32},{32,0},{64,96},{96,64},{128,160},{160,128},{192,224},{224,1... | collective-permute-start | bytes 49160 | tf_op jit(solution)/shard_map/ppermute | solution.py:345
  25.1 23.8 %copy-start.3 = (f32[512,512]{1,0:T(8,128)S(1)}, f32[512,512]{1,0:T(8,128)}, u32[]{:S(2)}) copy-start(f32[512,512]{1,0:T(8,128)} %source.3) | copy-start | bytes 3145732
  48.8 1.3 %collective-permute-start.12 = (f32[32,384]{1,0:T(8,128)S(1)}, f32[32,384]{1,0:T(8,128)S(1)}, u32[]{:S(2)}, u32[]{:S(2)}) collective-permute-start(f32[32,384]{1,0:T(8,128)S(1)} %shard_map.101.mine), channel_id=1, source_target_pairs={{0,32},{32,0},{64,96},{96,64},{128,160},{160,128},{192,224},{224,1... | collective-permute-start | bytes 147464 | tf_op jit(solution)/shard_map/ppermute | solution.py:355
  50.7 4.5 %collective-permute-start.13 = (f32[32,128]{1,0:T(8,128)S(1)}, f32[32,128]{1,0:T(8,128)S(1)}, u32[]{:S(2)}, u32[]{:S(2)}) collective-permute-start(f32[32,128]{1,0:T(8,128)S(1)} %get-tuple-element.72), channel_id=1, source_target_pairs={{32,64},{64,32},{96,128},{128,96},{160,192},{192,160},{224,0},{0,2... | collective-permute-start | bytes 49160 | tf_op jit(solution)/shard_map/ppermute | solution.py:345
  52.2 3.7 %collective-permute-start.14 = (f32[32,128]{1,0:T(8,128)S(1)}, f32[32,128]{1,0:T(8,128)S(1)}, u32[]{:S(2)}, u32[]{:S(2)}) collective-permute-start(f32[32,128]{1,0:T(8,128)S(1)} %get-tuple-element.73), channel_id=1, source_target_pairs={{0,4},{4,0},{8,12},{12,8},{16,20},{20,16},{24,28},{28,24},{1,5},{5... | collective-permute-start | bytes 49160 | tf_op jit(solution)/shard_map/ppermute | solution.py:345
  53.3 5.0 %collective-permute-start.15 = (f32[32,128]{1,0:T(8,128)S(1)}, f32[32,128]{1,0:T(8,128)S(1)}, u32[]{:S(2)}, u32[]{:S(2)}) collective-permute-start(f32[32,128]{1,0:T(8,128)S(1)} %get-tuple-element.74), channel_id=1, source_target_pairs={{4,8},{8,4},{12,16},{16,12},{20,24},{24,20},{28,0},{0,28},{5,9},{9... | collective-permute-start | bytes 49160 | tf_op jit(solution)/shard_map/ppermute | solution.py:345
  53.3 4.9 %collective-permute-start.16 = (f32[32,128]{1,0:T(8,128)S(1)}, f32[32,128]{1,0:T(8,128)S(1)}, u32[]{:S(2)}, u32[]{:S(2)}) collective-permute-start(f32[32,128]{1,0:T(8,128)S(1)} %get-tuple-element.75), channel_id=1, source_target_pairs={{0,1},{1,0},{2,3},{3,2},{4,5},{5,4},{6,7},{7,6},{8,9},{9,8},{10,11... | collective-permute-start | bytes 49160 | tf_op jit(solution)/shard_map/ppermute | solution.py:345
  54.7 3.7 %collective-permute-start.17 = (f32[32,128]{1,0:T(8,128)S(1)}, f32[32,128]{1,0:T(8,128)S(1)}, u32[]{:S(2)}, u32[]{:S(2)}) collective-permute-start(f32[32,128]{1,0:T(8,128)S(1)} %get-tuple-element.76), channel_id=1, source_target_pairs={{1,2},{2,1},{3,0},{0,3},{5,6},{6,5},{7,4},{4,7},{9,10},{10,9},{11,... | collective-permute-start | bytes 49160 | tf_op jit(solution)/shard_map/ppermute | solution.py:345
  55.1 3.4 %collective-permute-start.18 = (f32[32,128]{1,0:T(8,128)S(1)}, f32[32,128]{1,0:T(8,128)S(1)}, u32[]{:S(2)}, u32[]{:S(2)}) collective-permute-start(f32[32,128]{1,0:T(8,128)S(1)} %get-tuple-element.77), channel_id=1, source_target_pairs={{0,32},{32,0},{64,96},{96,64},{128,160},{160,128},{192,224},{224,1... | collective-permute-start | bytes 49160 | tf_op jit(solution)/shard_map/ppermute | solution.py:345
  58.9 5.8 %collective-permute-start.19 = (f32[32,128]{1,0:T(8,128)S(1)}, f32[32,128]{1,0:T(8,128)S(1)}, u32[]{:S(2)}, u32[]{:S(2)}) collective-permute-start(f32[32,128]{1,0:T(8,128)S(1)} %get-tuple-element.80), channel_id=1, source_target_pairs={{32,64},{64,32},{96,128},{128,96},{160,192},{192,160},{224,0},{0,2... | collective-permute-start | bytes 49160 | tf_op jit(solution)/shard_map/ppermute | solution.py:345
  59.1 5.7 %collective-permute-start.20 = (f32[32,128]{1,0:T(8,128)S(1)}, f32[32,128]{1,0:T(8,128)S(1)}, u32[]{:S(2)}, u32[]{:S(2)}) collective-permute-start(f32[32,128]{1,0:T(8,128)S(1)} %get-tuple-element.81), channel_id=1, source_target_pairs={{0,4},{4,0},{8,12},{12,8},{16,20},{20,16},{24,28},{28,24},{1,5},{5... | collective-permute-start | bytes 49160 | tf_op jit(solution)/shard_map/ppermute | solution.py:345
  60.0 4.9 %collective-permute-start.21 = (f32[32,128]{1,0:T(8,128)S(1)}, f32[32,128]{1,0:T(8,128)S(1)}, u32[]{:S(2)}, u32[]{:S(2)}) collective-permute-start(f32[32,128]{1,0:T(8,128)S(1)} %get-tuple-element.82), channel_id=1, source_target_pairs={{4,8},{8,4},{12,16},{16,12},{20,24},{24,20},{28,0},{0,28},{5,9},{9... | collective-permute-start | bytes 49160 | tf_op jit(solution)/shard_map/ppermute | solution.py:345
  62.4 3.7 %collective-permute-start.22 = (f32[32,128]{1,0:T(8,128)S(1)}, f32[32,128]{1,0:T(8,128)S(1)}, u32[]{:S(2)}, u32[]{:S(2)}) collective-permute-start(f32[32,128]{1,0:T(8,128)S(1)} %get-tuple-element.83), channel_id=1, source_target_pairs={{0,1},{1,0},{2,3},{3,2},{4,5},{5,4},{6,7},{7,6},{8,9},{9,8},{10,11... | collective-permute-start | bytes 49160 | tf_op jit(solution)/shard_map/ppermute | solution.py:345
  64.2 3.7 %collective-permute-start.23 = (f32[32,128]{1,0:T(8,128)S(1)}, f32[32,128]{1,0:T(8,128)S(1)}, u32[]{:S(2)}, u32[]{:S(2)}) collective-permute-start(f32[32,128]{1,0:T(8,128)S(1)} %get-tuple-element.84), channel_id=1, source_target_pairs={{1,2},{2,1},{3,0},{0,3},{5,6},{6,5},{7,4},{4,7},{9,10},{10,9},{11,... | collective-permute-start | bytes 49160 | tf_op jit(solution)/shard_map/ppermute | solution.py:345
  64.7 3.2 %collective-permute-start.24 = (f32[32,128]{1,0:T(8,128)S(1)}, f32[32,128]{1,0:T(8,128)S(1)}, u32[]{:S(2)}, u32[]{:S(2)}) collective-permute-start(f32[32,128]{1,0:T(8,128)S(1)} %get-tuple-element.85), channel_id=1, source_target_pairs={{0,32},{32,0},{64,96},{96,64},{128,160},{160,128},{192,224},{224,1... | collective-permute-start | bytes 49160 | tf_op jit(solution)/shard_map/ppermute | solution.py:345
  91.8 1.3 %collective-permute-start.25 = (f32[32,384]{1,0:T(8,128)S(1)}, f32[32,384]{1,0:T(8,128)S(1)}, u32[]{:S(2)}, u32[]{:S(2)}) collective-permute-start(f32[32,384]{1,0:T(8,128)S(1)} %shard_map.105.mine), channel_id=1, source_target_pairs={{0,32},{32,0},{64,96},{96,64},{128,160},{160,128},{192,224},{224,1... | collective-permute-start | bytes 147464 | tf_op jit(solution)/shard_map/ppermute | solution.py:355
  94.0 4.4 %collective-permute-start.26 = (f32[32,128]{1,0:T(8,128)S(1)}, f32[32,128]{1,0:T(8,128)S(1)}, u32[]{:S(2)}, u32[]{:S(2)}) collective-permute-start(f32[32,128]{1,0:T(8,128)S(1)} %get-tuple-element.94), channel_id=1, source_target_pairs={{32,64},{64,32},{96,128},{128,96},{160,192},{192,160},{224,0},{0,2... | collective-permute-start | bytes 49160 | tf_op jit(solution)/shard_map/ppermute | solution.py:345
  95.5 3.7 %collective-permute-start.27 = (f32[32,128]{1,0:T(8,128)S(1)}, f32[32,128]{1,0:T(8,128)S(1)}, u32[]{:S(2)}, u32[]{:S(2)}) collective-permute-start(f32[32,128]{1,0:T(8,128)S(1)} %get-tuple-element.95), channel_id=1, source_target_pairs={{0,4},{4,0},{8,12},{12,8},{16,20},{20,16},{24,28},{28,24},{1,5},{5... | collective-permute-start | bytes 49160 | tf_op jit(solution)/shard_map/ppermute | solution.py:345
  96.6 4.9 %collective-permute-start.28 = (f32[32,128]{1,0:T(8,128)S(1)}, f32[32,128]{1,0:T(8,128)S(1)}, u32[]{:S(2)}, u32[]{:S(2)}) collective-permute-start(f32[32,128]{1,0:T(8,128)S(1)} %get-tuple-element.96), channel_id=1, source_target_pairs={{4,8},{8,4},{12,16},{16,12},{20,24},{24,20},{28,0},{0,28},{5,9},{9... | collective-permute-start | bytes 49160 | tf_op jit(solution)/shard_map/ppermute | solution.py:345
  96.6 4.9 %collective-permute-start.29 = (f32[32,128]{1,0:T(8,128)S(1)}, f32[32,128]{1,0:T(8,128)S(1)}, u32[]{:S(2)}, u32[]{:S(2)}) collective-permute-start(f32[32,128]{1,0:T(8,128)S(1)} %get-tuple-element.97), channel_id=1, source_target_pairs={{0,1},{1,0},{2,3},{3,2},{4,5},{5,4},{6,7},{7,6},{8,9},{9,8},{10,11... | collective-permute-start | bytes 49160 | tf_op jit(solution)/shard_map/ppermute | solution.py:345
  98.0 3.7 %collective-permute-start.30 = (f32[32,128]{1,0:T(8,128)S(1)}, f32[32,128]{1,0:T(8,128)S(1)}, u32[]{:S(2)}, u32[]{:S(2)}) collective-permute-start(f32[32,128]{1,0:T(8,128)S(1)} %get-tuple-element.98), channel_id=1, source_target_pairs={{1,2},{2,1},{3,0},{0,3},{5,6},{6,5},{7,4},{4,7},{9,10},{10,9},{11,... | collective-permute-start | bytes 49160 | tf_op jit(solution)/shard_map/ppermute | solution.py:345
  98.4 3.4 %collective-permute-start.31 = (f32[32,128]{1,0:T(8,128)S(1)}, f32[32,128]{1,0:T(8,128)S(1)}, u32[]{:S(2)}, u32[]{:S(2)}) collective-permute-start(f32[32,128]{1,0:T(8,128)S(1)} %get-tuple-element.99), channel_id=1, source_target_pairs={{0,32},{32,0},{64,96},{96,64},{128,160},{160,128},{192,224},{224,1... | collective-permute-start | bytes 49160 | tf_op jit(solution)/shard_map/ppermute | solution.py:345

commit v6 on v5

--- a/solution.py
+++ b/solution.py
@@ -38,7 +38,7 @@
     return [lax.axis_index(axis) for axis in AXES]
 
 
-ORDER = (1, 2, 3, 4, 5, 0)
+ORDER = (2, 3, 1, 4, 5, 0)
 
 
 def store_sends(sends, faces):
@@ -332,18 +332,25 @@
     )(*operands)
 
 
-def matched(count, start):
-    pairs = []
-    for low in range(start, count, 2):
-        high = (low + 1) % count
-        pairs += [(low, high), (high, low)]
-    return pairs
+def pairs(axis, start):
+    out = []
+    for a in range(SIZES[0]):
+        for b in range(SIZES[1]):
+            for c in range(SIZES[2]):
+                here, there = (a, b, c), [a, b, c]
+                if start and here[axis] in (0, SIZES[axis] - 1):
+                    other = 1 if axis == 0 else 0
+                    there[other] = here[other] ^ 1
+                else:
+                    there[axis] += 1 if (here[axis] - start) % 2 == 0 else -1
+                place = [(p * SIZES[1] + q) * SIZES[2] + r for p, q, r in (here, there)]
+                out.append(tuple(place))
+    return out
 
 
 def exchange(sends):
     return [
-        lax.ppermute(value, AXES[k // 2], matched(SIZES[k // 2], k % 2))
-        for k, value in zip(ORDER, sends)
+        lax.ppermute(value, AXES, pairs(k // 2, k % 2)) for k, value in zip(ORDER, sends)
     ]
 
 
@@ -352,7 +359,7 @@
         combine_kernel, [(LOADS, DEVICES + FACE)], lax.all_to_all(message, BY_COLUMN, 0, 0),
         scratch=[pltpu.VMEM((DEVICES, FACE), F32)],
     )
-    return mine, lax.ppermute(mine, AXES[0], matched(SIZES[0], 0))
+    return mine, lax.ppermute(mine, AXES, pairs(0, 0))
 
 
 def local(loads, schur, dirichlet, coupling, coarse_inverse, pairing, corner_map, counts):

time: 103 us -> 98.3 us (0.954)
  starting transfers between devices: 32.3 us -> 29 us
    ppermute x32, starting transfers between devices: 32.3 us -> 29 us  [the longest x30 28.8 us: exchange(): lax.ppermute(value, AXES, pairs(k // 2, k % 2))]
  transfers between devices with their start and end apart: 32 -> 32, of which waited for: 16 -> 12; matrix products, arithmetic and copies ran while one was open for 0% -> 0% of each run, Pallas kernels for 1% -> 1%
where the time goes in v6:
time: 98.3 us; the launch traced here: 98.1 us
  blocking collectives  44.8 us (46%)
  starting transfers between devices  29 us (30%)
  waiting for transfers between devices  13.2 us (13%)
  Pallas kernels  7.05 us (7%)
  local copies, waits for them, and re-layouts  2.6 us (3%)
  between operations  1.47 us (1%)
    all_to_all x2, blocking collectives, total_sums(): lax.all_to_all(message, BY_COLUMN, 0, 0)  44.8 us
    ppermute x30, starting transfers between devices, exchange(): lax.ppermute(value, AXES, pairs(k // 2, k % 2))  28.8 us
    ppermute x30, waiting for transfers between devices, exchange(): lax.ppermute(value, AXES, pairs(k // 2, k % 2))  11.2 us
    pallas_call x14, Pallas kernels, call(): pl.pallas_call(kernel, out_shape=[shape if hasattr(shape, 'dtype') else j...  7.05 us
    unnamed x16, local copies, waits for them, and re-layouts  2.6 us
  transfers between devices with their start and end apart: 32, of which 12 were waited for; matrix products, arithmetic and copies ran while one was open for 0% of the time, Pallas kernels for 1%

profile of v6, /device:TPU:2, one launch (start us, length us, event | category | flops | bytes accessed | tf_op | source)
XLA Modules:
  0.0 98.1 jit_solution(4222524854586757655)
XLA Ops:
  1.3 0.0 copy-start.4
  1.3 0.9 copy-done.4
  2.2 2.0 %collective-permute-start = (f32[40,128]{1,0:T(8,128)S(1)}, f32[40,128]{1,0:T(8,128)S(1)}, u32[]{:S(2)}, u32[]{:S(2)}) collective-permute-start(f32[40,128]{1,0:T(8,128)S(1)} %get-tuple-element.51), channel_id=1, source_target_pairs={{0,4},{1,5},{2,6},{3,7},{4,0},{5,1},{6,2},{7,3},{8,12},{9,13},{10,... | collective-permute-start | bytes 61448 | tf_op jit(solution)/shard_map/ppermute | solution.py:353
  4.2 3.8 %collective-permute-start.2 = (f32[40,128]{1,0:T(8,128)S(1)}, f32[40,128]{1,0:T(8,128)S(1)}, u32[]{:S(2)}, u32[]{:S(2)}) collective-permute-start(f32[40,128]{1,0:T(8,128)S(1)} %get-tuple-element.53), channel_id=1, source_target_pairs={{0,4},{1,5},{2,6},{3,7},{4,0},{5,1},{6,2},{7,3},{8,12},{9,13},{10,... | collective-permute-start | bytes 61448 | tf_op jit(solution)/shard_map/ppermute | solution.py:353
  8.1 0.5 collective-permute-start.3
  8.6 2.2 %collective-permute-start.4 = (f32[40,128]{1,0:T(8,128)S(1)}, f32[40,128]{1,0:T(8,128)S(1)}, u32[]{:S(2)}, u32[]{:S(2)}) collective-permute-start(f32[40,128]{1,0:T(8,128)S(1)} %get-tuple-element.55), channel_id=1, source_target_pairs={{0,32},{1,2},{2,1},{3,35},{4,36},{5,6},{6,5},{7,39},{8,40},{9,10},... | collective-permute-start | bytes 61448 | tf_op jit(solution)/shard_map/ppermute | solution.py:353
  10.8 1.3 %copy-done.2 = bf16[1,768,768]{2,1,0:T(8,128)(2,1)S(1)} copy-done((bf16[1,768,768]{2,1,0:T(8,128)(2,1)S(1)}, bf16[1,768,768]{2,1,0:T(8,128)(2,1)}, u32[]{:S(2)}) %copy-start.2) | copy-done | bytes 1179672
  12.0 0.1 shard_map.96.dirichlet
  12.1 0.0 copy-start
  12.1 0.0 copy-start.1
  12.2 0.0 copy-start.7
  12.2 0.0 collective-permute-done.1.refs_1_
  12.2 0.0 collective-permute-done.3.refs_3_
  12.2 0.3 collective-permute-done.4.refs_4_
  12.5 0.0 collective-permute-done.5.refs_5_
  12.5 0.4 copy-done.5
  12.9 0.5 shard_map.98
  13.4 1.2 %collective-permute-start.6 = (f32[32,128]{1,0:T(8,128)S(1)}, f32[32,128]{1,0:T(8,128)S(1)}, u32[]{:S(2)}, u32[]{:S(2)}) collective-permute-start(f32[32,128]{1,0:T(8,128)S(1)} %get-tuple-element.59), channel_id=1, source_target_pairs={{0,4},{1,5},{2,6},{3,7},{4,0},{5,1},{6,2},{7,3},{8,12},{9,13},{10,... | collective-permute-start | bytes 49160 | tf_op jit(solution)/shard_map/ppermute | solution.py:353
  14.6 0.0 collective-permute-start.7
  14.6 4.1 %collective-permute-start.8 = (f32[32,128]{1,0:T(8,128)S(1)}, f32[32,128]{1,0:T(8,128)S(1)}, u32[]{:S(2)}, u32[]{:S(2)}) collective-permute-start(f32[32,128]{1,0:T(8,128)S(1)} %get-tuple-element.61), channel_id=1, source_target_pairs={{0,4},{1,5},{2,6},{3,7},{4,0},{5,1},{6,2},{7,3},{8,12},{9,13},{10,... | collective-permute-start | bytes 49160 | tf_op jit(solution)/shard_map/ppermute | solution.py:353
  18.7 1.1 %collective-permute-start.10 = (f32[32,128]{1,0:T(8,128)S(1)}, f32[32,128]{1,0:T(8,128)S(1)}, u32[]{:S(2)}, u32[]{:S(2)}) collective-permute-start(f32[32,128]{1,0:T(8,128)S(1)} %get-tuple-element.63), channel_id=1, source_target_pairs={{0,32},{1,2},{2,1},{3,35},{4,36},{5,6},{6,5},{7,39},{8,40},{9,10},... | collective-permute-start | bytes 49160 | tf_op jit(solution)/shard_map/ppermute | solution.py:353
  19.9 0.0 collective-permute-start.11
  19.9 0.0 collective-permute-done.7.refs_1_
  19.9 0.6 collective-permute-done.8.refs_2_
  20.5 2.0 %collective-permute-done.9.refs_3_ = f32[32,128]{1,0:T(8,128)S(1)} collective-permute-done((f32[32,128]{1,0:T(8,128)S(1)}, f32[32,128]{1,0:T(8,128)S(1)}, u32[]{:S(2)}, u32[]{:S(2)}) %collective-permute-start.9) | collective-permute-done | bytes 16416 | tf_op jit(solution)/shard_map/ppermute | solution.py:353
  22.5 0.0 collective-permute-done.10.refs_4_
  22.5 0.0 collective-permute-done.11.refs_5_
  22.5 0.0 copy-start.3
  22.5 0.7 shard_map.100
  23.3 23.3 %all_to_all.10.got = f32[256,2,128]{2,1,0:T(2,128)S(1)} all-to-all(f32[256,2,128]{2,1,0:T(2,128)S(1)} %get-tuple-element.65), channel_id=1, replica_groups=mesh['region'=8,'gy'=8,'gz'=4] {'gy','gz','region'}, dimensions={0} | all-to-all | bytes 524288 | tf_op jit(solution)/shard_map/all_to_all | solution.py:359
  46.6 0.5 shard_map.101.mine
  47.1 0.1 collective-permute-start.12
  47.2 0.5 shard_map.99.inverse
  47.7 0.7 collective-permute-done.12.other
  48.4 0.6 shard_map.102
  49.0 1.1 %collective-permute-start.13 = (f32[32,128]{1,0:T(8,128)S(1)}, f32[32,128]{1,0:T(8,128)S(1)}, u32[]{:S(2)}, u32[]{:S(2)}) collective-permute-start(f32[32,128]{1,0:T(8,128)S(1)} %get-tuple-element.72), channel_id=1, source_target_pairs={{0,4},{1,5},{2,6},{3,7},{4,0},{5,1},{6,2},{7,3},{8,12},{9,13},{10,... | collective-permute-start | bytes 49160 | tf_op jit(solution)/shard_map/ppermute | solution.py:353
  50.1 0.0 collective-permute-start.14
  50.1 1.3 %collective-permute-start.15 = (f32[32,128]{1,0:T(8,128)S(1)}, f32[32,128]{1,0:T(8,128)S(1)}, u32[]{:S(2)}, u32[]{:S(2)}) collective-permute-start(f32[32,128]{1,0:T(8,128)S(1)} %get-tuple-element.74), channel_id=1, source_target_pairs={{0,4},{1,5},{2,6},{3,7},{4,0},{5,1},{6,2},{7,3},{8,12},{9,13},{10,... | collective-permute-start | bytes 49160 | tf_op jit(solution)/shard_map/ppermute | solution.py:353
  51.5 1.5 %collective-permute-start.16 = (f32[32,128]{1,0:T(8,128)S(1)}, f32[32,128]{1,0:T(8,128)S(1)}, u32[]{:S(2)}, u32[]{:S(2)}) collective-permute-start(f32[32,128]{1,0:T(8,128)S(1)} %get-tuple-element.75), channel_id=1, source_target_pairs={{0,1},{1,0},{2,3},{3,2},{4,5},{5,4},{6,7},{7,6},{8,9},{9,8},{10,11... | collective-permute-start | bytes 49160 | tf_op jit(solution)/shard_map/ppermute | solution.py:353
  53.0 0.7 collective-permute-start.17
  53.7 0.2 collective-permute-done.15.refs_2_
  53.9 1.3 %collective-permute-done.16.refs_3_ = f32[32,128]{1,0:T(8,128)S(1)} collective-permute-done((f32[32,128]{1,0:T(8,128)S(1)}, f32[32,128]{1,0:T(8,128)S(1)}, u32[]{:S(2)}, u32[]{:S(2)}) %collective-permute-start.16) | collective-permute-done | bytes 16416 | tf_op jit(solution)/shard_map/ppermute | solution.py:353
  55.2 1.5 %collective-permute-done.17.refs_4_ = f32[32,128]{1,0:T(8,128)S(1)} collective-permute-done((f32[32,128]{1,0:T(8,128)S(1)}, f32[32,128]{1,0:T(8,128)S(1)}, u32[]{:S(2)}, u32[]{:S(2)}) %collective-permute-start.17) | collective-permute-done | bytes 16416 | tf_op jit(solution)/shard_map/ppermute | solution.py:353
  56.7 0.0 collective-permute-done.18.refs_5_
  56.7 0.5 shard_map.103
  57.2 0.7 collective-permute-start.19
  57.9 3.1 %collective-permute-start.21 = (f32[32,128]{1,0:T(8,128)S(1)}, f32[32,128]{1,0:T(8,128)S(1)}, u32[]{:S(2)}, u32[]{:S(2)}) collective-permute-start(f32[32,128]{1,0:T(8,128)S(1)} %get-tuple-element.82), channel_id=1, source_target_pairs={{0,4},{1,5},{2,6},{3,7},{4,0},{5,1},{6,2},{7,3},{8,12},{9,13},{10,... | collective-permute-start | bytes 49160 | tf_op jit(solution)/shard_map/ppermute | solution.py:353
  60.9 0.8 collective-permute-start.23
  61.8 0.9 collective-permute-done.21.refs_2_
  62.6 2.0 %collective-permute-done.22.refs_3_ = f32[32,128]{1,0:T(8,128)S(1)} collective-permute-done((f32[32,128]{1,0:T(8,128)S(1)}, f32[32,128]{1,0:T(8,128)S(1)}, u32[]{:S(2)}, u32[]{:S(2)}) %collective-permute-start.22) | collective-permute-done | bytes 16416 | tf_op jit(solution)/shard_map/ppermute | solution.py:353
  64.7 0.8 shard_map.104
  65.4 21.5 %all_to_all.11.got = f32[256,2,128]{2,1,0:T(2,128)S(1)} all-to-all(f32[256,2,128]{2,1,0:T(2,128)S(1)} %get-tuple-element.86), channel_id=1, replica_groups=mesh['region'=8,'gy'=8,'gz'=4] {'gy','gz','region'}, dimensions={0} | all-to-all | bytes 524288 | tf_op jit(solution)/shard_map/all_to_all | solution.py:359
  86.9 0.5 shard_map.105.mine
  87.4 0.1 collective-permute-start.25
  87.5 1.2 %collective-permute-done.25.other = f32[32,384]{1,0:T(8,128)S(1)} collective-permute-done((f32[32,384]{1,0:T(8,128)S(1)}, f32[32,384]{1,0:T(8,128)S(1)}, u32[]{:S(2)}, u32[]{:S(2)}) %collective-permute-start.25) | collective-permute-done | bytes 49184 | tf_op jit(solution)/shard_map/ppermute | solution.py:362
  88.7 0.9 shard_map.106
  89.6 1.1 %collective-permute-start.26 = (f32[32,128]{1,0:T(8,128)S(1)}, f32[32,128]{1,0:T(8,128)S(1)}, u32[]{:S(2)}, u32[]{:S(2)}) collective-permute-start(f32[32,128]{1,0:T(8,128)S(1)} %get-tuple-element.94), channel_id=1, source_target_pairs={{0,4},{1,5},{2,6},{3,7},{4,0},{5,1},{6,2},{7,3},{8,12},{9,13},{10,... | collective-permute-start | bytes 49160 | tf_op jit(solution)/shard_map/ppermute | solution.py:353
  90.7 1.3 %collective-permute-start.28 = (f32[32,128]{1,0:T(8,128)S(1)}, f32[32,128]{1,0:T(8,128)S(1)}, u32[]{:S(2)}, u32[]{:S(2)}) collective-permute-start(f32[32,128]{1,0:T(8,128)S(1)} %get-tuple-element.96), channel_id=1, source_target_pairs={{0,4},{1,5},{2,6},{3,7},{4,0},{5,1},{6,2},{7,3},{8,12},{9,13},{10,... | collective-permute-start | bytes 49160 | tf_op jit(solution)/shard_map/ppermute | solution.py:353
  92.1 1.5 %collective-permute-start.29 = (f32[32,128]{1,0:T(8,128)S(1)}, f32[32,128]{1,0:T(8,128)S(1)}, u32[]{:S(2)}, u32[]{:S(2)}) collective-permute-start(f32[32,128]{1,0:T(8,128)S(1)} %get-tuple-element.97), channel_id=1, source_target_pairs={{0,1},{1,0},{2,3},{3,2},{4,5},{5,4},{6,7},{7,6},{8,9},{9,8},{10,11... | collective-permute-start | bytes 49160 | tf_op jit(solution)/shard_map/ppermute | solution.py:353
  93.6 0.7 collective-permute-start.30
  94.2 0.7 shard_map.107
  95.0 0.8 collective-permute-done.29.refs_3_
  95.8 1.5 %collective-permute-done.30.refs_4_ = f32[32,128]{1,0:T(8,128)S(1)} collective-permute-done((f32[32,128]{1,0:T(8,128)S(1)}, f32[32,128]{1,0:T(8,128)S(1)}, u32[]{:S(2)}, u32[]{:S(2)}) %collective-permute-start.30) | collective-permute-done | bytes 16416 | tf_op jit(solution)/shard_map/ppermute | solution.py:353
  97.3 0.8 shard_map.108
  (32 shorter events, 0.1 us)
Async XLA Ops:
  1.3 0.9 copy-start.4
  2.2 8.5 %collective-permute-start = (f32[40,128]{1,0:T(8,128)S(1)}, f32[40,128]{1,0:T(8,128)S(1)}, u32[]{:S(2)}, u32[]{:S(2)}) collective-permute-start(f32[40,128]{1,0:T(8,128)S(1)} %get-tuple-element.51), channel_id=1, source_target_pairs={{0,4},{1,5},{2,6},{3,7},{4,0},{5,1},{6,2},{7,3},{8,12},{9,13},{10,... | collective-permute-start | bytes 61448 | tf_op jit(solution)/shard_map/ppermute | solution.py:353
  4.2 7.9 %collective-permute-start.1 = (f32[40,128]{1,0:T(8,128)S(1)}, f32[40,128]{1,0:T(8,128)S(1)}, u32[]{:S(2)}, u32[]{:S(2)}) collective-permute-start(f32[40,128]{1,0:T(8,128)S(1)} %get-tuple-element.52), channel_id=1, source_target_pairs={{0,32},{1,33},{2,34},{3,35},{4,8},{5,9},{6,10},{7,11},{8,4},{9,5},... | collective-permute-start | bytes 61448 | tf_op jit(solution)/shard_map/ppermute | solution.py:353
  4.2 7.9 %collective-permute-start.2 = (f32[40,128]{1,0:T(8,128)S(1)}, f32[40,128]{1,0:T(8,128)S(1)}, u32[]{:S(2)}, u32[]{:S(2)}) collective-permute-start(f32[40,128]{1,0:T(8,128)S(1)} %get-tuple-element.53), channel_id=1, source_target_pairs={{0,4},{1,5},{2,6},{3,7},{4,0},{5,1},{6,2},{7,3},{8,12},{9,13},{10,... | collective-permute-start | bytes 61448 | tf_op jit(solution)/shard_map/ppermute | solution.py:353
  8.1 4.1 %collective-permute-start.3 = (f32[40,128]{1,0:T(8,128)S(1)}, f32[40,128]{1,0:T(8,128)S(1)}, u32[]{:S(2)}, u32[]{:S(2)}) collective-permute-start(f32[40,128]{1,0:T(8,128)S(1)} %get-tuple-element.54), channel_id=1, source_target_pairs={{0,1},{1,0},{2,3},{3,2},{4,5},{5,4},{6,7},{7,6},{8,9},{9,8},{10,11... | collective-permute-start | bytes 61448 | tf_op jit(solution)/shard_map/ppermute | solution.py:353
  8.6 3.9 %collective-permute-start.4 = (f32[40,128]{1,0:T(8,128)S(1)}, f32[40,128]{1,0:T(8,128)S(1)}, u32[]{:S(2)}, u32[]{:S(2)}) collective-permute-start(f32[40,128]{1,0:T(8,128)S(1)} %get-tuple-element.55), channel_id=1, source_target_pairs={{0,32},{1,2},{2,1},{3,35},{4,36},{5,6},{6,5},{7,39},{8,40},{9,10},... | collective-permute-start | bytes 61448 | tf_op jit(solution)/shard_map/ppermute | solution.py:353
  10.8 1.8 %collective-permute-start.5 = (f32[40,128]{1,0:T(8,128)S(1)}, f32[40,128]{1,0:T(8,128)S(1)}, u32[]{:S(2)}, u32[]{:S(2)}) collective-permute-start(f32[40,128]{1,0:T(8,128)S(1)} %get-tuple-element.56), channel_id=1, source_target_pairs={{0,32},{1,33},{2,34},{3,35},{4,36},{5,37},{6,38},{7,39},{8,40},{9,... | collective-permute-start | bytes 61448 | tf_op jit(solution)/shard_map/ppermute | solution.py:353
  10.8 1.3 %copy-start.2 = (bf16[1,768,768]{2,1,0:T(8,128)(2,1)S(1)}, bf16[1,768,768]{2,1,0:T(8,128)(2,1)}, u32[]{:S(2)}) copy-start(bf16[1,768,768]{2,1,0:T(8,128)(2,1)} %source.2) | copy-start | bytes 3538948
  12.0 0.9 copy-start.5
  12.0 0.9 copy-start.6
  12.1 10.4 %copy-start = (bf16[1,768,768]{2,1,0:T(8,128)(2,1)S(1)}, bf16[1,768,768]{2,1,0:T(8,128)(2,1)}, u32[]{:S(2)}) copy-start(bf16[1,768,768]{2,1,0:T(8,128)(2,1)} %schur.5) | copy-start | bytes 3538948
  12.1 10.4 %copy-start.1 = (bf16[1,768,128]{2,1,0:T(8,128)(2,1)S(1)}, bf16[1,768,128]{2,1,0:T(8,128)(2,1)}, u32[]{:S(2)}) copy-start(bf16[1,768,128]{2,1,0:T(8,128)(2,1)} %coupling.7) | copy-start | bytes 589828
  12.2 10.4 %copy-start.7 = (s32[1,128]{1,0:T(1,128)S(1)}, s32[1,128]{1,0:T(1,128)}, u32[]{:S(2)}) copy-start(s32[1,128]{1,0:T(1,128)} %corner_map.7) | copy-start | bytes 1540
  13.4 6.5 %collective-permute-start.6 = (f32[32,128]{1,0:T(8,128)S(1)}, f32[32,128]{1,0:T(8,128)S(1)}, u32[]{:S(2)}, u32[]{:S(2)}) collective-permute-start(f32[32,128]{1,0:T(8,128)S(1)} %get-tuple-element.59), channel_id=1, source_target_pairs={{0,4},{1,5},{2,6},{3,7},{4,0},{5,1},{6,2},{7,3},{8,12},{9,13},{10,... | collective-permute-start | bytes 49160 | tf_op jit(solution)/shard_map/ppermute | solution.py:353
  14.6 5.3 %collective-permute-start.7 = (f32[32,128]{1,0:T(8,128)S(1)}, f32[32,128]{1,0:T(8,128)S(1)}, u32[]{:S(2)}, u32[]{:S(2)}) collective-permute-start(f32[32,128]{1,0:T(8,128)S(1)} %get-tuple-element.60), channel_id=1, source_target_pairs={{0,32},{1,33},{2,34},{3,35},{4,8},{5,9},{6,10},{7,11},{8,4},{9,5},... | collective-permute-start | bytes 49160 | tf_op jit(solution)/shard_map/ppermute | solution.py:353
  14.6 5.9 %collective-permute-start.8 = (f32[32,128]{1,0:T(8,128)S(1)}, f32[32,128]{1,0:T(8,128)S(1)}, u32[]{:S(2)}, u32[]{:S(2)}) collective-permute-start(f32[32,128]{1,0:T(8,128)S(1)} %get-tuple-element.61), channel_id=1, source_target_pairs={{0,4},{1,5},{2,6},{3,7},{4,0},{5,1},{6,2},{7,3},{8,12},{9,13},{10,... | collective-permute-start | bytes 49160 | tf_op jit(solution)/shard_map/ppermute | solution.py:353
  18.7 3.7 %collective-permute-start.9 = (f32[32,128]{1,0:T(8,128)S(1)}, f32[32,128]{1,0:T(8,128)S(1)}, u32[]{:S(2)}, u32[]{:S(2)}) collective-permute-start(f32[32,128]{1,0:T(8,128)S(1)} %get-tuple-element.62), channel_id=1, source_target_pairs={{0,1},{1,0},{2,3},{3,2},{4,5},{5,4},{6,7},{7,6},{8,9},{9,8},{10,11... | collective-permute-start | bytes 49160 | tf_op jit(solution)/shard_map/ppermute | solution.py:353
  18.7 3.7 %collective-permute-start.10 = (f32[32,128]{1,0:T(8,128)S(1)}, f32[32,128]{1,0:T(8,128)S(1)}, u32[]{:S(2)}, u32[]{:S(2)}) collective-permute-start(f32[32,128]{1,0:T(8,128)S(1)} %get-tuple-element.63), channel_id=1, source_target_pairs={{0,32},{1,2},{2,1},{3,35},{4,36},{5,6},{6,5},{7,39},{8,40},{9,10},... | collective-permute-start | bytes 49160 | tf_op jit(solution)/shard_map/ppermute | solution.py:353
  19.9 2.6 %collective-permute-start.11 = (f32[32,128]{1,0:T(8,128)S(1)}, f32[32,128]{1,0:T(8,128)S(1)}, u32[]{:S(2)}, u32[]{:S(2)}) collective-permute-start(f32[32,128]{1,0:T(8,128)S(1)} %get-tuple-element.64), channel_id=1, source_target_pairs={{0,32},{1,33},{2,34},{3,35},{4,36},{5,37},{6,38},{7,39},{8,40},{9,... | collective-permute-start | bytes 49160 | tf_op jit(solution)/shard_map/ppermute | solution.py:353
  22.5 24.7 %copy-start.3 = (f32[512,512]{1,0:T(8,128)S(1)}, f32[512,512]{1,0:T(8,128)}, u32[]{:S(2)}) copy-start(f32[512,512]{1,0:T(8,128)} %source.3) | copy-start | bytes 3145732
  47.1 1.3 %collective-permute-start.12 = (f32[32,384]{1,0:T(8,128)S(1)}, f32[32,384]{1,0:T(8,128)S(1)}, u32[]{:S(2)}, u32[]{:S(2)}) collective-permute-start(f32[32,384]{1,0:T(8,128)S(1)} %shard_map.101.mine), channel_id=1, source_target_pairs={{0,32},{1,33},{2,34},{3,35},{4,36},{5,37},{6,38},{7,39},{8,40},{9,... | collective-permute-start | bytes 147464 | tf_op jit(solution)/shard_map/ppermute | solution.py:362
  49.0 4.6 %collective-permute-start.13 = (f32[32,128]{1,0:T(8,128)S(1)}, f32[32,128]{1,0:T(8,128)S(1)}, u32[]{:S(2)}, u32[]{:S(2)}) collective-permute-start(f32[32,128]{1,0:T(8,128)S(1)} %get-tuple-element.72), channel_id=1, source_target_pairs={{0,4},{1,5},{2,6},{3,7},{4,0},{5,1},{6,2},{7,3},{8,12},{9,13},{10,... | collective-permute-start | bytes 49160 | tf_op jit(solution)/shard_map/ppermute | solution.py:353
  50.1 3.5 %collective-permute-start.14 = (f32[32,128]{1,0:T(8,128)S(1)}, f32[32,128]{1,0:T(8,128)S(1)}, u32[]{:S(2)}, u32[]{:S(2)}) collective-permute-start(f32[32,128]{1,0:T(8,128)S(1)} %get-tuple-element.73), channel_id=1, source_target_pairs={{0,32},{1,33},{2,34},{3,35},{4,8},{5,9},{6,10},{7,11},{8,4},{9,5},... | collective-permute-start | bytes 49160 | tf_op jit(solution)/shard_map/ppermute | solution.py:353
  50.1 3.7 %collective-permute-start.15 = (f32[32,128]{1,0:T(8,128)S(1)}, f32[32,128]{1,0:T(8,128)S(1)}, u32[]{:S(2)}, u32[]{:S(2)}) collective-permute-start(f32[32,128]{1,0:T(8,128)S(1)} %get-tuple-element.74), channel_id=1, source_target_pairs={{0,4},{1,5},{2,6},{3,7},{4,0},{5,1},{6,2},{7,3},{8,12},{9,13},{10,... | collective-permute-start | bytes 49160 | tf_op jit(solution)/shard_map/ppermute | solution.py:353
  51.5 3.7 %collective-permute-start.16 = (f32[32,128]{1,0:T(8,128)S(1)}, f32[32,128]{1,0:T(8,128)S(1)}, u32[]{:S(2)}, u32[]{:S(2)}) collective-permute-start(f32[32,128]{1,0:T(8,128)S(1)} %get-tuple-element.75), channel_id=1, source_target_pairs={{0,1},{1,0},{2,3},{3,2},{4,5},{5,4},{6,7},{7,6},{8,9},{9,8},{10,11... | collective-permute-start | bytes 49160 | tf_op jit(solution)/shard_map/ppermute | solution.py:353
  53.0 3.7 %collective-permute-start.17 = (f32[32,128]{1,0:T(8,128)S(1)}, f32[32,128]{1,0:T(8,128)S(1)}, u32[]{:S(2)}, u32[]{:S(2)}) collective-permute-start(f32[32,128]{1,0:T(8,128)S(1)} %get-tuple-element.76), channel_id=1, source_target_pairs={{0,32},{1,2},{2,1},{3,35},{4,36},{5,6},{6,5},{7,39},{8,40},{9,10},... | collective-permute-start | bytes 49160 | tf_op jit(solution)/shard_map/ppermute | solution.py:353
  53.7 3.0 %collective-permute-start.18 = (f32[32,128]{1,0:T(8,128)S(1)}, f32[32,128]{1,0:T(8,128)S(1)}, u32[]{:S(2)}, u32[]{:S(2)}) collective-permute-start(f32[32,128]{1,0:T(8,128)S(1)} %get-tuple-element.77), channel_id=1, source_target_pairs={{0,32},{1,33},{2,34},{3,35},{4,36},{5,37},{6,38},{7,39},{8,40},{9,... | collective-permute-start | bytes 49160 | tf_op jit(solution)/shard_map/ppermute | solution.py:353
  57.2 4.6 %collective-permute-start.19 = (f32[32,128]{1,0:T(8,128)S(1)}, f32[32,128]{1,0:T(8,128)S(1)}, u32[]{:S(2)}, u32[]{:S(2)}) collective-permute-start(f32[32,128]{1,0:T(8,128)S(1)} %get-tuple-element.80), channel_id=1, source_target_pairs={{0,4},{1,5},{2,6},{3,7},{4,0},{5,1},{6,2},{7,3},{8,12},{9,13},{10,... | collective-permute-start | bytes 49160 | tf_op jit(solution)/shard_map/ppermute | solution.py:353
  57.9 3.9 %collective-permute-start.20 = (f32[32,128]{1,0:T(8,128)S(1)}, f32[32,128]{1,0:T(8,128)S(1)}, u32[]{:S(2)}, u32[]{:S(2)}) collective-permute-start(f32[32,128]{1,0:T(8,128)S(1)} %get-tuple-element.81), channel_id=1, source_target_pairs={{0,32},{1,33},{2,34},{3,35},{4,8},{5,9},{6,10},{7,11},{8,4},{9,5},... | collective-permute-start | bytes 49160 | tf_op jit(solution)/shard_map/ppermute | solution.py:353
  57.9 4.8 %collective-permute-start.21 = (f32[32,128]{1,0:T(8,128)S(1)}, f32[32,128]{1,0:T(8,128)S(1)}, u32[]{:S(2)}, u32[]{:S(2)}) collective-permute-start(f32[32,128]{1,0:T(8,128)S(1)} %get-tuple-element.82), channel_id=1, source_target_pairs={{0,4},{1,5},{2,6},{3,7},{4,0},{5,1},{6,2},{7,3},{8,12},{9,13},{10,... | collective-permute-start | bytes 49160 | tf_op jit(solution)/shard_map/ppermute | solution.py:353
  60.9 3.7 %collective-permute-start.22 = (f32[32,128]{1,0:T(8,128)S(1)}, f32[32,128]{1,0:T(8,128)S(1)}, u32[]{:S(2)}, u32[]{:S(2)}) collective-permute-start(f32[32,128]{1,0:T(8,128)S(1)} %get-tuple-element.83), channel_id=1, source_target_pairs={{0,1},{1,0},{2,3},{3,2},{4,5},{5,4},{6,7},{7,6},{8,9},{9,8},{10,11... | collective-permute-start | bytes 49160 | tf_op jit(solution)/shard_map/ppermute | solution.py:353
  60.9 3.7 %collective-permute-start.23 = (f32[32,128]{1,0:T(8,128)S(1)}, f32[32,128]{1,0:T(8,128)S(1)}, u32[]{:S(2)}, u32[]{:S(2)}) collective-permute-start(f32[32,128]{1,0:T(8,128)S(1)} %get-tuple-element.84), channel_id=1, source_target_pairs={{0,32},{1,2},{2,1},{3,35},{4,36},{5,6},{6,5},{7,39},{8,40},{9,10},... | collective-permute-start | bytes 49160 | tf_op jit(solution)/shard_map/ppermute | solution.py:353
  61.8 2.9 %collective-permute-start.24 = (f32[32,128]{1,0:T(8,128)S(1)}, f32[32,128]{1,0:T(8,128)S(1)}, u32[]{:S(2)}, u32[]{:S(2)}) collective-permute-start(f32[32,128]{1,0:T(8,128)S(1)} %get-tuple-element.85), channel_id=1, source_target_pairs={{0,32},{1,33},{2,34},{3,35},{4,36},{5,37},{6,38},{7,39},{8,40},{9,... | collective-permute-start | bytes 49160 | tf_op jit(solution)/shard_map/ppermute | solution.py:353
  87.4 1.3 %collective-permute-start.25 = (f32[32,384]{1,0:T(8,128)S(1)}, f32[32,384]{1,0:T(8,128)S(1)}, u32[]{:S(2)}, u32[]{:S(2)}) collective-permute-start(f32[32,384]{1,0:T(8,128)S(1)} %shard_map.105.mine), channel_id=1, source_target_pairs={{0,32},{1,33},{2,34},{3,35},{4,36},{5,37},{6,38},{7,39},{8,40},{9,... | collective-permute-start | bytes 147464 | tf_op jit(solution)/shard_map/ppermute | solution.py:362
  89.6 4.6 %collective-permute-start.26 = (f32[32,128]{1,0:T(8,128)S(1)}, f32[32,128]{1,0:T(8,128)S(1)}, u32[]{:S(2)}, u32[]{:S(2)}) collective-permute-start(f32[32,128]{1,0:T(8,128)S(1)} %get-tuple-element.94), channel_id=1, source_target_pairs={{0,4},{1,5},{2,6},{3,7},{4,0},{5,1},{6,2},{7,3},{8,12},{9,13},{10,... | collective-permute-start | bytes 49160 | tf_op jit(solution)/shard_map/ppermute | solution.py:353
  90.7 4.2 %collective-permute-start.27 = (f32[32,128]{1,0:T(8,128)S(1)}, f32[32,128]{1,0:T(8,128)S(1)}, u32[]{:S(2)}, u32[]{:S(2)}) collective-permute-start(f32[32,128]{1,0:T(8,128)S(1)} %get-tuple-element.95), channel_id=1, source_target_pairs={{0,32},{1,33},{2,34},{3,35},{4,8},{5,9},{6,10},{7,11},{8,4},{9,5},... | collective-permute-start | bytes 49160 | tf_op jit(solution)/shard_map/ppermute | solution.py:353
  90.7 4.2 %collective-permute-start.28 = (f32[32,128]{1,0:T(8,128)S(1)}, f32[32,128]{1,0:T(8,128)S(1)}, u32[]{:S(2)}, u32[]{:S(2)}) collective-permute-start(f32[32,128]{1,0:T(8,128)S(1)} %get-tuple-element.96), channel_id=1, source_target_pairs={{0,4},{1,5},{2,6},{3,7},{4,0},{5,1},{6,2},{7,3},{8,12},{9,13},{10,... | collective-permute-start | bytes 49160 | tf_op jit(solution)/shard_map/ppermute | solution.py:353
  92.1 3.7 %collective-permute-start.29 = (f32[32,128]{1,0:T(8,128)S(1)}, f32[32,128]{1,0:T(8,128)S(1)}, u32[]{:S(2)}, u32[]{:S(2)}) collective-permute-start(f32[32,128]{1,0:T(8,128)S(1)} %get-tuple-element.97), channel_id=1, source_target_pairs={{0,1},{1,0},{2,3},{3,2},{4,5},{5,4},{6,7},{7,6},{8,9},{9,8},{10,11... | collective-permute-start | bytes 49160 | tf_op jit(solution)/shard_map/ppermute | solution.py:353
  93.6 3.7 %collective-permute-start.30 = (f32[32,128]{1,0:T(8,128)S(1)}, f32[32,128]{1,0:T(8,128)S(1)}, u32[]{:S(2)}, u32[]{:S(2)}) collective-permute-start(f32[32,128]{1,0:T(8,128)S(1)} %get-tuple-element.98), channel_id=1, source_target_pairs={{0,32},{1,2},{2,1},{3,35},{4,36},{5,6},{6,5},{7,39},{8,40},{9,10},... | collective-permute-start | bytes 49160 | tf_op jit(solution)/shard_map/ppermute | solution.py:353
  94.2 3.0 %collective-permute-start.31 = (f32[32,128]{1,0:T(8,128)S(1)}, f32[32,128]{1,0:T(8,128)S(1)}, u32[]{:S(2)}, u32[]{:S(2)}) collective-permute-start(f32[32,128]{1,0:T(8,128)S(1)} %get-tuple-element.99), channel_id=1, source_target_pairs={{0,32},{1,33},{2,34},{3,35},{4,36},{5,37},{6,38},{7,39},{8,40},{9,... | collective-permute-start | bytes 49160 | tf_op jit(solution)/shard_map/ppermute | solution.py:353

commit v7 on v6

--- a/solution.py
+++ b/solution.py
@@ -91,9 +91,10 @@
     live_ref[...] = jnp.full((8, FACE), (counts[0] > 0).astype(F32), F32)
 
 
-def prepare_kernel(live_ref, loads, *sends):
+def prepare_kernel(live_ref, loads, value_ref, *sends):
     mark = live_ref[...]
     value = loads[0] * mark[0:1, 0:1]
+    value_ref[...] = value
     faces = [jnp.concatenate([face, mark], axis=0) for face in split_faces(value)]
     store_sends(sends, faces)
 
@@ -123,10 +124,10 @@
     return weight * matmul(scaled, dirichlet[0])
 
 
-def first_kernel(live_ref, loads, pairing, dirichlet, *refs):
+def first_kernel(live_ref, value_ref, pairing, dirichlet, *refs):
     recvs, (resid, weight_ref, terms, dots), sends = refs[:6], refs[6:10], refs[10:]
     live = live_ref[0:1, 0:1]
-    residual = live * (loads[0] * live + partner(recvs, pairing))
+    residual = live * (value_ref[...] + partner(recvs, pairing))
     multiplicity = live * (live + partner(recvs, pairing, slice(LOADS, LOADS + 8)))
     weight = live / jnp.maximum(multiplicity, 1.0)
     weight_ref[...] = weight
@@ -162,9 +163,9 @@
 
 
 def send_message(out, messages):
-    block = jnp.stack(messages * (SIZES[0] // 2))
-    for i in range(SIDE):
-        out[i * SIZES[0] : (i + 1) * SIZES[0]] = block
+    block = jnp.concatenate(messages * 4, axis=0)
+    for i in range(2 * DEVICES // 16):
+        out[i * 16 : (i + 1) * 16] = block
 
 
 def second_kernel(live_ref, pairing, corner_map, schur, coupling, terms, dots, *refs):
@@ -188,7 +189,7 @@
 
     def line(b, c, index):
         first = (b % SIZES[1] * SIZES[2] + c % SIZES[2]) * SIZES[0]
-        return got[first : first + SIZES[0], index, :]
+        return got[pl.Slice(2 * first + index, SIZES[0], 2), :]
 
     for b in range(SIZES[1]):
         for c in range(SIZES[2]):
@@ -355,8 +356,9 @@
 
 
 def total_sums(message):
+    message = lax.all_to_all(message.reshape(DEVICES, 2, FACE), BY_COLUMN, 0, 0)
     (mine,) = call(
-        combine_kernel, [(LOADS, DEVICES + FACE)], lax.all_to_all(message, BY_COLUMN, 0, 0),
+        combine_kernel, [(LOADS, DEVICES + FACE)], message.reshape(2 * DEVICES, FACE),
         scratch=[pltpu.VMEM((DEVICES, FACE), F32)],
     )
     return mine, lax.ppermute(mine, AXES, pairs(0, 0))
@@ -371,11 +373,11 @@
     pairing = pairing.reshape(6, 1, FACE)
     cost = pl.CostEstimate(flops=0, bytes_accessed=4 << 20, transcendentals=0)
     (live,) = call(living_kernel, [(8, FACE)], counts, spec=SMEM, cost=cost)
-    sends = call(prepare_kernel, [(LOADS + 8, FACE)] * 6, live, loads)
+    value, *sends = call(prepare_kernel, [vector] + [(LOADS + 8, FACE)] * 6, live, loads)
     (dirichlet,) = call(copy_kernel, [jax.ShapeDtypeStruct(dirichlet.shape, BF16)], dirichlet)
     resid, weight, terms, dots, *sends = call(
         first_kernel, [vector, (8, MULT), vector, small] + faces,
-        live, loads, pairing, dirichlet, *exchange(sends),
+        live, value, pairing, dirichlet, *exchange(sends),
     )
     (inverse,) = call(
         halves_kernel, [jax.ShapeDtypeStruct((2, COARSE, COARSE), BF16)], coarse_inverse, dots,
@@ -385,7 +387,7 @@
         ],
     )
     first, local_terms, message = call(
-        second_kernel, [vector, vector, (DEVICES, 2, FACE)],
+        second_kernel, [vector, vector, (2 * DEVICES, FACE)],
         live, pairing, corner_map, schur, coupling, terms, dots, *exchange(sends),
     )
     image, gathered, solved, scalars, *sends = call(
@@ -397,7 +399,7 @@
         live, pairing, dirichlet, resid, weight, image, scalars, *exchange(sends),
     )
     precond, message = call(
-        fifth_kernel, [vector, (DEVICES, 2, FACE)],
+        fifth_kernel, [vector, (2 * DEVICES, FACE)],
         live, pairing, corner_map, schur, coupling, terms, dots, *exchange(sends),
     )
     direction, image, step, *sends = call(

time: 98.3 us -> 97.5 us (level)
    unnamed x16 -> x14, local copies, waits for them, and re-layouts: 2.6 us -> 2.38 us
where the time goes in v7:
time: 97.5 us; the launch traced here: 97.3 us
  blocking collectives  44.8 us (46%)
  starting transfers between devices  29 us (30%)
  waiting for transfers between devices  13.1 us (13%)
  Pallas kernels  6.49 us (7%)
  local copies, waits for them, and re-layouts  2.38 us (2%)
  between operations  1.47 us (2%)
    all_to_all x2, blocking collectives, total_sums(): message = lax.all_to_all(message.reshape(DEVICES, 2, FACE), BY_COLUMN, 0, 0)  44.8 us
    ppermute x30, starting transfers between devices, exchange(): lax.ppermute(value, AXES, pairs(k // 2, k % 2))  28.8 us
    ppermute x30, waiting for transfers between devices, exchange(): lax.ppermute(value, AXES, pairs(k // 2, k % 2))  11.2 us
    pallas_call x14, Pallas kernels, call(): pl.pallas_call(kernel, out_shape=[shape if hasattr(shape, 'dtype') else j...  6.49 us
    unnamed x14, local copies, waits for them, and re-layouts  2.38 us
  transfers between devices with their start and end apart: 32, of which 12 were waited for; matrix products, arithmetic and copies ran while one was open for 0% of the time, Pallas kernels for 1%

profile of v7, /device:TPU:2, one launch (start us, length us, event | category | flops | bytes accessed | tf_op | source)
XLA Modules:
  0.0 97.3 jit_solution(11419995892664370580)
XLA Ops:
  1.3 0.0 copy-start.4
  1.3 0.9 copy-done.4
  2.2 2.0 %collective-permute-start = (f32[40,128]{1,0:T(8,128)S(1)}, f32[40,128]{1,0:T(8,128)S(1)}, u32[]{:S(2)}, u32[]{:S(2)}) collective-permute-start(f32[40,128]{1,0:T(8,128)S(1)} %get-tuple-element.53), channel_id=1, source_target_pairs={{0,4},{1,5},{2,6},{3,7},{4,0},{5,1},{6,2},{7,3},{8,12},{9,13},{10,... | collective-permute-start | bytes 61448 | tf_op jit(solution)/shard_map/ppermute | solution.py:354
  4.2 0.0 collective-permute-start.1
  4.2 3.8 %collective-permute-start.2 = (f32[40,128]{1,0:T(8,128)S(1)}, f32[40,128]{1,0:T(8,128)S(1)}, u32[]{:S(2)}, u32[]{:S(2)}) collective-permute-start(f32[40,128]{1,0:T(8,128)S(1)} %get-tuple-element.55), channel_id=1, source_target_pairs={{0,4},{1,5},{2,6},{3,7},{4,0},{5,1},{6,2},{7,3},{8,12},{9,13},{10,... | collective-permute-start | bytes 61448 | tf_op jit(solution)/shard_map/ppermute | solution.py:354
  8.1 0.5 collective-permute-start.3
  8.6 2.2 %collective-permute-start.4 = (f32[40,128]{1,0:T(8,128)S(1)}, f32[40,128]{1,0:T(8,128)S(1)}, u32[]{:S(2)}, u32[]{:S(2)}) collective-permute-start(f32[40,128]{1,0:T(8,128)S(1)} %get-tuple-element.57), channel_id=1, source_target_pairs={{0,32},{1,2},{2,1},{3,35},{4,36},{5,6},{6,5},{7,39},{8,40},{9,10},... | collective-permute-start | bytes 61448 | tf_op jit(solution)/shard_map/ppermute | solution.py:354
  10.8 1.3 %copy-done.2 = bf16[1,768,768]{2,1,0:T(8,128)(2,1)S(1)} copy-done((bf16[1,768,768]{2,1,0:T(8,128)(2,1)S(1)}, bf16[1,768,768]{2,1,0:T(8,128)(2,1)}, u32[]{:S(2)}) %copy-start.2) | copy-done | bytes 1179672
  12.1 0.1 shard_map.97.dirichlet
  12.1 0.0 copy-start
  12.1 0.0 copy-start.1
  12.2 0.0 copy-start.6
  12.2 0.0 collective-permute-done.1.refs_1_
  12.2 0.0 collective-permute-done.3.refs_3_
  12.2 0.3 collective-permute-done.4.refs_4_
  12.5 0.2 copy-done.5
  12.7 0.5 shard_map.98
  13.2 1.2 %collective-permute-start.6 = (f32[32,128]{1,0:T(8,128)S(1)}, f32[32,128]{1,0:T(8,128)S(1)}, u32[]{:S(2)}, u32[]{:S(2)}) collective-permute-start(f32[32,128]{1,0:T(8,128)S(1)} %get-tuple-element.61), channel_id=1, source_target_pairs={{0,4},{1,5},{2,6},{3,7},{4,0},{5,1},{6,2},{7,3},{8,12},{9,13},{10,... | collective-permute-start | bytes 49160 | tf_op jit(solution)/shard_map/ppermute | solution.py:354
  14.4 0.0 collective-permute-start.7
  14.4 4.1 %collective-permute-start.8 = (f32[32,128]{1,0:T(8,128)S(1)}, f32[32,128]{1,0:T(8,128)S(1)}, u32[]{:S(2)}, u32[]{:S(2)}) collective-permute-start(f32[32,128]{1,0:T(8,128)S(1)} %get-tuple-element.63), channel_id=1, source_target_pairs={{0,4},{1,5},{2,6},{3,7},{4,0},{5,1},{6,2},{7,3},{8,12},{9,13},{10,... | collective-permute-start | bytes 49160 | tf_op jit(solution)/shard_map/ppermute | solution.py:354
  18.5 0.0 collective-permute-start.9
  18.5 1.1 %collective-permute-start.10 = (f32[32,128]{1,0:T(8,128)S(1)}, f32[32,128]{1,0:T(8,128)S(1)}, u32[]{:S(2)}, u32[]{:S(2)}) collective-permute-start(f32[32,128]{1,0:T(8,128)S(1)} %get-tuple-element.65), channel_id=1, source_target_pairs={{0,32},{1,2},{2,1},{3,35},{4,36},{5,6},{6,5},{7,39},{8,40},{9,10},... | collective-permute-start | bytes 49160 | tf_op jit(solution)/shard_map/ppermute | solution.py:354
  19.7 0.6 collective-permute-done.8.refs_2_
  20.3 2.0 %collective-permute-done.9.refs_3_ = f32[32,128]{1,0:T(8,128)S(1)} collective-permute-done((f32[32,128]{1,0:T(8,128)S(1)}, f32[32,128]{1,0:T(8,128)S(1)}, u32[]{:S(2)}, u32[]{:S(2)}) %collective-permute-start.9) | collective-permute-done | bytes 16416 | tf_op jit(solution)/shard_map/ppermute | solution.py:354
  22.3 0.0 copy-start.3
  22.3 0.7 shard_map.100
  23.0 23.3 %all_to_all.10 = f32[256,2,128]{2,1,0:T(2,128)S(1)} all-to-all(f32[256,2,128]{2,1,0:T(2,128)S(1)} %bitcast.7), channel_id=1, replica_groups=mesh['region'=8,'gy'=8,'gz'=4] {'gy','gz','region'}, dimensions={0} | all-to-all | bytes 524288 | tf_op jit(solution)/shard_map/all_to_all | solution.py:359
  46.4 0.3 shard_map.101.mine
  46.6 0.1 collective-permute-start.12
  46.7 0.5 shard_map.99.inverse
  47.2 0.7 collective-permute-done.12.other
  47.9 0.6 shard_map.102
  48.5 1.1 %collective-permute-start.13 = (f32[32,128]{1,0:T(8,128)S(1)}, f32[32,128]{1,0:T(8,128)S(1)}, u32[]{:S(2)}, u32[]{:S(2)}) collective-permute-start(f32[32,128]{1,0:T(8,128)S(1)} %get-tuple-element.74), channel_id=1, source_target_pairs={{0,4},{1,5},{2,6},{3,7},{4,0},{5,1},{6,2},{7,3},{8,12},{9,13},{10,... | collective-permute-start | bytes 49160 | tf_op jit(solution)/shard_map/ppermute | solution.py:354
  49.7 0.0 collective-permute-start.14
  49.7 1.3 %collective-permute-start.15 = (f32[32,128]{1,0:T(8,128)S(1)}, f32[32,128]{1,0:T(8,128)S(1)}, u32[]{:S(2)}, u32[]{:S(2)}) collective-permute-start(f32[32,128]{1,0:T(8,128)S(1)} %get-tuple-element.76), channel_id=1, source_target_pairs={{0,4},{1,5},{2,6},{3,7},{4,0},{5,1},{6,2},{7,3},{8,12},{9,13},{10,... | collective-permute-start | bytes 49160 | tf_op jit(solution)/shard_map/ppermute | solution.py:354
  51.0 1.5 %collective-permute-start.16 = (f32[32,128]{1,0:T(8,128)S(1)}, f32[32,128]{1,0:T(8,128)S(1)}, u32[]{:S(2)}, u32[]{:S(2)}) collective-permute-start(f32[32,128]{1,0:T(8,128)S(1)} %get-tuple-element.77), channel_id=1, source_target_pairs={{0,1},{1,0},{2,3},{3,2},{4,5},{5,4},{6,7},{7,6},{8,9},{9,8},{10,11... | collective-permute-start | bytes 49160 | tf_op jit(solution)/shard_map/ppermute | solution.py:354
  52.5 0.7 collective-permute-start.17
  53.2 0.2 collective-permute-done.15.refs_2_
  53.4 1.3 %collective-permute-done.16.refs_3_ = f32[32,128]{1,0:T(8,128)S(1)} collective-permute-done((f32[32,128]{1,0:T(8,128)S(1)}, f32[32,128]{1,0:T(8,128)S(1)}, u32[]{:S(2)}, u32[]{:S(2)}) %collective-permute-start.16) | collective-permute-done | bytes 16416 | tf_op jit(solution)/shard_map/ppermute | solution.py:354
  54.7 1.5 %collective-permute-done.17.refs_4_ = f32[32,128]{1,0:T(8,128)S(1)} collective-permute-done((f32[32,128]{1,0:T(8,128)S(1)}, f32[32,128]{1,0:T(8,128)S(1)}, u32[]{:S(2)}, u32[]{:S(2)}) %collective-permute-start.17) | collective-permute-done | bytes 16416 | tf_op jit(solution)/shard_map/ppermute | solution.py:354
  56.2 0.0 collective-permute-done.18.refs_5_
  56.2 0.5 shard_map.103
  56.7 0.7 collective-permute-start.19
  57.4 3.0 %collective-permute-start.21 = (f32[32,128]{1,0:T(8,128)S(1)}, f32[32,128]{1,0:T(8,128)S(1)}, u32[]{:S(2)}, u32[]{:S(2)}) collective-permute-start(f32[32,128]{1,0:T(8,128)S(1)} %get-tuple-element.84), channel_id=1, source_target_pairs={{0,4},{1,5},{2,6},{3,7},{4,0},{5,1},{6,2},{7,3},{8,12},{9,13},{10,... | collective-permute-start | bytes 49160 | tf_op jit(solution)/shard_map/ppermute | solution.py:354
  60.4 0.8 collective-permute-start.23
  61.3 0.0 collective-permute-done.19.refs_0_
  61.3 0.9 collective-permute-done.21.refs_2_
  62.1 2.0 %collective-permute-done.22.refs_3_ = f32[32,128]{1,0:T(8,128)S(1)} collective-permute-done((f32[32,128]{1,0:T(8,128)S(1)}, f32[32,128]{1,0:T(8,128)S(1)}, u32[]{:S(2)}, u32[]{:S(2)}) %collective-permute-start.22) | collective-permute-done | bytes 16416 | tf_op jit(solution)/shard_map/ppermute | solution.py:354
  64.2 0.0 collective-permute-done.23.refs_4_
  64.2 0.0 collective-permute-done.24.refs_5_
  64.2 0.7 shard_map.104
  64.9 21.5 %all_to_all.11 = f32[256,2,128]{2,1,0:T(2,128)S(1)} all-to-all(f32[256,2,128]{2,1,0:T(2,128)S(1)} %bitcast.8), channel_id=1, replica_groups=mesh['region'=8,'gy'=8,'gz'=4] {'gy','gz','region'}, dimensions={0} | all-to-all | bytes 524288 | tf_op jit(solution)/shard_map/all_to_all | solution.py:359
  86.4 0.3 shard_map.105.mine
  86.7 0.1 collective-permute-start.25
  86.7 1.2 %collective-permute-done.25.other = f32[32,384]{1,0:T(8,128)S(1)} collective-permute-done((f32[32,384]{1,0:T(8,128)S(1)}, f32[32,384]{1,0:T(8,128)S(1)}, u32[]{:S(2)}, u32[]{:S(2)}) %collective-permute-start.25) | collective-permute-done | bytes 49184 | tf_op jit(solution)/shard_map/ppermute | solution.py:364
  88.0 0.9 shard_map.106
  88.9 1.1 %collective-permute-start.26 = (f32[32,128]{1,0:T(8,128)S(1)}, f32[32,128]{1,0:T(8,128)S(1)}, u32[]{:S(2)}, u32[]{:S(2)}) collective-permute-start(f32[32,128]{1,0:T(8,128)S(1)} %get-tuple-element.96), channel_id=1, source_target_pairs={{0,4},{1,5},{2,6},{3,7},{4,0},{5,1},{6,2},{7,3},{8,12},{9,13},{10,... | collective-permute-start | bytes 49160 | tf_op jit(solution)/shard_map/ppermute | solution.py:354
  90.0 1.3 %collective-permute-start.28 = (f32[32,128]{1,0:T(8,128)S(1)}, f32[32,128]{1,0:T(8,128)S(1)}, u32[]{:S(2)}, u32[]{:S(2)}) collective-permute-start(f32[32,128]{1,0:T(8,128)S(1)} %get-tuple-element.98), channel_id=1, source_target_pairs={{0,4},{1,5},{2,6},{3,7},{4,0},{5,1},{6,2},{7,3},{8,12},{9,13},{10,... | collective-permute-start | bytes 49160 | tf_op jit(solution)/shard_map/ppermute | solution.py:354
  91.3 1.5 %collective-permute-start.29 = (f32[32,128]{1,0:T(8,128)S(1)}, f32[32,128]{1,0:T(8,128)S(1)}, u32[]{:S(2)}, u32[]{:S(2)}) collective-permute-start(f32[32,128]{1,0:T(8,128)S(1)} %get-tuple-element.99), channel_id=1, source_target_pairs={{0,1},{1,0},{2,3},{3,2},{4,5},{5,4},{6,7},{7,6},{8,9},{9,8},{10,11... | collective-permute-start | bytes 49160 | tf_op jit(solution)/shard_map/ppermute | solution.py:354
  92.8 0.7 collective-permute-start.30
  93.5 0.7 shard_map.107
  94.2 0.8 collective-permute-done.29.refs_3_
  95.0 1.5 %collective-permute-done.30.refs_4_ = f32[32,128]{1,0:T(8,128)S(1)} collective-permute-done((f32[32,128]{1,0:T(8,128)S(1)}, f32[32,128]{1,0:T(8,128)S(1)}, u32[]{:S(2)}, u32[]{:S(2)}) %collective-permute-start.30) | collective-permute-done | bytes 16416 | tf_op jit(solution)/shard_map/ppermute | solution.py:354
  96.5 0.8 shard_map.108
  (30 shorter events, 0.1 us)
Async XLA Ops:
  1.3 0.9 copy-start.4
  2.2 8.5 %collective-permute-start = (f32[40,128]{1,0:T(8,128)S(1)}, f32[40,128]{1,0:T(8,128)S(1)}, u32[]{:S(2)}, u32[]{:S(2)}) collective-permute-start(f32[40,128]{1,0:T(8,128)S(1)} %get-tuple-element.53), channel_id=1, source_target_pairs={{0,4},{1,5},{2,6},{3,7},{4,0},{5,1},{6,2},{7,3},{8,12},{9,13},{10,... | collective-permute-start | bytes 61448 | tf_op jit(solution)/shard_map/ppermute | solution.py:354
  4.2 7.9 %collective-permute-start.1 = (f32[40,128]{1,0:T(8,128)S(1)}, f32[40,128]{1,0:T(8,128)S(1)}, u32[]{:S(2)}, u32[]{:S(2)}) collective-permute-start(f32[40,128]{1,0:T(8,128)S(1)} %get-tuple-element.54), channel_id=1, source_target_pairs={{0,32},{1,33},{2,34},{3,35},{4,8},{5,9},{6,10},{7,11},{8,4},{9,5},... | collective-permute-start | bytes 61448 | tf_op jit(solution)/shard_map/ppermute | solution.py:354
  4.2 7.9 %collective-permute-start.2 = (f32[40,128]{1,0:T(8,128)S(1)}, f32[40,128]{1,0:T(8,128)S(1)}, u32[]{:S(2)}, u32[]{:S(2)}) collective-permute-start(f32[40,128]{1,0:T(8,128)S(1)} %get-tuple-element.55), channel_id=1, source_target_pairs={{0,4},{1,5},{2,6},{3,7},{4,0},{5,1},{6,2},{7,3},{8,12},{9,13},{10,... | collective-permute-start | bytes 61448 | tf_op jit(solution)/shard_map/ppermute | solution.py:354
  8.1 4.1 %collective-permute-start.3 = (f32[40,128]{1,0:T(8,128)S(1)}, f32[40,128]{1,0:T(8,128)S(1)}, u32[]{:S(2)}, u32[]{:S(2)}) collective-permute-start(f32[40,128]{1,0:T(8,128)S(1)} %get-tuple-element.56), channel_id=1, source_target_pairs={{0,1},{1,0},{2,3},{3,2},{4,5},{5,4},{6,7},{7,6},{8,9},{9,8},{10,11... | collective-permute-start | bytes 61448 | tf_op jit(solution)/shard_map/ppermute | solution.py:354
  8.6 3.9 %collective-permute-start.4 = (f32[40,128]{1,0:T(8,128)S(1)}, f32[40,128]{1,0:T(8,128)S(1)}, u32[]{:S(2)}, u32[]{:S(2)}) collective-permute-start(f32[40,128]{1,0:T(8,128)S(1)} %get-tuple-element.57), channel_id=1, source_target_pairs={{0,32},{1,2},{2,1},{3,35},{4,36},{5,6},{6,5},{7,39},{8,40},{9,10},... | collective-permute-start | bytes 61448 | tf_op jit(solution)/shard_map/ppermute | solution.py:354
  10.8 1.8 %collective-permute-start.5 = (f32[40,128]{1,0:T(8,128)S(1)}, f32[40,128]{1,0:T(8,128)S(1)}, u32[]{:S(2)}, u32[]{:S(2)}) collective-permute-start(f32[40,128]{1,0:T(8,128)S(1)} %get-tuple-element.58), channel_id=1, source_target_pairs={{0,32},{1,33},{2,34},{3,35},{4,36},{5,37},{6,38},{7,39},{8,40},{9,... | collective-permute-start | bytes 61448 | tf_op jit(solution)/shard_map/ppermute | solution.py:354
  10.8 1.3 %copy-start.2 = (bf16[1,768,768]{2,1,0:T(8,128)(2,1)S(1)}, bf16[1,768,768]{2,1,0:T(8,128)(2,1)}, u32[]{:S(2)}) copy-start(bf16[1,768,768]{2,1,0:T(8,128)(2,1)} %source.2) | copy-start | bytes 3538948
  12.0 0.7 copy-start.5
  12.1 10.2 %copy-start = (bf16[1,768,768]{2,1,0:T(8,128)(2,1)S(1)}, bf16[1,768,768]{2,1,0:T(8,128)(2,1)}, u32[]{:S(2)}) copy-start(bf16[1,768,768]{2,1,0:T(8,128)(2,1)} %schur.5) | copy-start | bytes 3538948
  12.1 10.1 %copy-start.1 = (bf16[1,768,128]{2,1,0:T(8,128)(2,1)S(1)}, bf16[1,768,128]{2,1,0:T(8,128)(2,1)}, u32[]{:S(2)}) copy-start(bf16[1,768,128]{2,1,0:T(8,128)(2,1)} %coupling.7) | copy-start | bytes 589828
  12.2 10.1 %copy-start.6 = (s32[1,128]{1,0:T(1,128)S(1)}, s32[1,128]{1,0:T(1,128)}, u32[]{:S(2)}) copy-start(s32[1,128]{1,0:T(1,128)} %corner_map.7) | copy-start | bytes 1540
  13.2 6.5 %collective-permute-start.6 = (f32[32,128]{1,0:T(8,128)S(1)}, f32[32,128]{1,0:T(8,128)S(1)}, u32[]{:S(2)}, u32[]{:S(2)}) collective-permute-start(f32[32,128]{1,0:T(8,128)S(1)} %get-tuple-element.61), channel_id=1, source_target_pairs={{0,4},{1,5},{2,6},{3,7},{4,0},{5,1},{6,2},{7,3},{8,12},{9,13},{10,... | collective-permute-start | bytes 49160 | tf_op jit(solution)/shard_map/ppermute | solution.py:354
  14.4 5.3 %collective-permute-start.7 = (f32[32,128]{1,0:T(8,128)S(1)}, f32[32,128]{1,0:T(8,128)S(1)}, u32[]{:S(2)}, u32[]{:S(2)}) collective-permute-start(f32[32,128]{1,0:T(8,128)S(1)} %get-tuple-element.62), channel_id=1, source_target_pairs={{0,32},{1,33},{2,34},{3,35},{4,8},{5,9},{6,10},{7,11},{8,4},{9,5},... | collective-permute-start | bytes 49160 | tf_op jit(solution)/shard_map/ppermute | solution.py:354
  14.4 5.9 %collective-permute-start.8 = (f32[32,128]{1,0:T(8,128)S(1)}, f32[32,128]{1,0:T(8,128)S(1)}, u32[]{:S(2)}, u32[]{:S(2)}) collective-permute-start(f32[32,128]{1,0:T(8,128)S(1)} %get-tuple-element.63), channel_id=1, source_target_pairs={{0,4},{1,5},{2,6},{3,7},{4,0},{5,1},{6,2},{7,3},{8,12},{9,13},{10,... | collective-permute-start | bytes 49160 | tf_op jit(solution)/shard_map/ppermute | solution.py:354
  18.5 3.7 %collective-permute-start.9 = (f32[32,128]{1,0:T(8,128)S(1)}, f32[32,128]{1,0:T(8,128)S(1)}, u32[]{:S(2)}, u32[]{:S(2)}) collective-permute-start(f32[32,128]{1,0:T(8,128)S(1)} %get-tuple-element.64), channel_id=1, source_target_pairs={{0,1},{1,0},{2,3},{3,2},{4,5},{5,4},{6,7},{7,6},{8,9},{9,8},{10,11... | collective-permute-start | bytes 49160 | tf_op jit(solution)/shard_map/ppermute | solution.py:354
  18.5 3.7 %collective-permute-start.10 = (f32[32,128]{1,0:T(8,128)S(1)}, f32[32,128]{1,0:T(8,128)S(1)}, u32[]{:S(2)}, u32[]{:S(2)}) collective-permute-start(f32[32,128]{1,0:T(8,128)S(1)} %get-tuple-element.65), channel_id=1, source_target_pairs={{0,32},{1,2},{2,1},{3,35},{4,36},{5,6},{6,5},{7,39},{8,40},{9,10},... | collective-permute-start | bytes 49160 | tf_op jit(solution)/shard_map/ppermute | solution.py:354
  19.7 2.6 %collective-permute-start.11 = (f32[32,128]{1,0:T(8,128)S(1)}, f32[32,128]{1,0:T(8,128)S(1)}, u32[]{:S(2)}, u32[]{:S(2)}) collective-permute-start(f32[32,128]{1,0:T(8,128)S(1)} %get-tuple-element.66), channel_id=1, source_target_pairs={{0,32},{1,33},{2,34},{3,35},{4,36},{5,37},{6,38},{7,39},{8,40},{9,... | collective-permute-start | bytes 49160 | tf_op jit(solution)/shard_map/ppermute | solution.py:354
  22.3 24.4 %copy-start.3 = (f32[512,512]{1,0:T(8,128)S(1)}, f32[512,512]{1,0:T(8,128)}, u32[]{:S(2)}) copy-start(f32[512,512]{1,0:T(8,128)} %source.3) | copy-start | bytes 3145732
  46.6 1.3 %collective-permute-start.12 = (f32[32,384]{1,0:T(8,128)S(1)}, f32[32,384]{1,0:T(8,128)S(1)}, u32[]{:S(2)}, u32[]{:S(2)}) collective-permute-start(f32[32,384]{1,0:T(8,128)S(1)} %shard_map.101.mine), channel_id=1, source_target_pairs={{0,32},{1,33},{2,34},{3,35},{4,36},{5,37},{6,38},{7,39},{8,40},{9,... | collective-permute-start | bytes 147464 | tf_op jit(solution)/shard_map/ppermute | solution.py:364
  48.5 4.6 %collective-permute-start.13 = (f32[32,128]{1,0:T(8,128)S(1)}, f32[32,128]{1,0:T(8,128)S(1)}, u32[]{:S(2)}, u32[]{:S(2)}) collective-permute-start(f32[32,128]{1,0:T(8,128)S(1)} %get-tuple-element.74), channel_id=1, source_target_pairs={{0,4},{1,5},{2,6},{3,7},{4,0},{5,1},{6,2},{7,3},{8,12},{9,13},{10,... | collective-permute-start | bytes 49160 | tf_op jit(solution)/shard_map/ppermute | solution.py:354
  49.7 3.5 %collective-permute-start.14 = (f32[32,128]{1,0:T(8,128)S(1)}, f32[32,128]{1,0:T(8,128)S(1)}, u32[]{:S(2)}, u32[]{:S(2)}) collective-permute-start(f32[32,128]{1,0:T(8,128)S(1)} %get-tuple-element.75), channel_id=1, source_target_pairs={{0,32},{1,33},{2,34},{3,35},{4,8},{5,9},{6,10},{7,11},{8,4},{9,5},... | collective-permute-start | bytes 49160 | tf_op jit(solution)/shard_map/ppermute | solution.py:354
  49.7 3.7 %collective-permute-start.15 = (f32[32,128]{1,0:T(8,128)S(1)}, f32[32,128]{1,0:T(8,128)S(1)}, u32[]{:S(2)}, u32[]{:S(2)}) collective-permute-start(f32[32,128]{1,0:T(8,128)S(1)} %get-tuple-element.76), channel_id=1, source_target_pairs={{0,4},{1,5},{2,6},{3,7},{4,0},{5,1},{6,2},{7,3},{8,12},{9,13},{10,... | collective-permute-start | bytes 49160 | tf_op jit(solution)/shard_map/ppermute | solution.py:354
  51.0 3.7 %collective-permute-start.16 = (f32[32,128]{1,0:T(8,128)S(1)}, f32[32,128]{1,0:T(8,128)S(1)}, u32[]{:S(2)}, u32[]{:S(2)}) collective-permute-start(f32[32,128]{1,0:T(8,128)S(1)} %get-tuple-element.77), channel_id=1, source_target_pairs={{0,1},{1,0},{2,3},{3,2},{4,5},{5,4},{6,7},{7,6},{8,9},{9,8},{10,11... | collective-permute-start | bytes 49160 | tf_op jit(solution)/shard_map/ppermute | solution.py:354
  52.5 3.7 %collective-permute-start.17 = (f32[32,128]{1,0:T(8,128)S(1)}, f32[32,128]{1,0:T(8,128)S(1)}, u32[]{:S(2)}, u32[]{:S(2)}) collective-permute-start(f32[32,128]{1,0:T(8,128)S(1)} %get-tuple-element.78), channel_id=1, source_target_pairs={{0,32},{1,2},{2,1},{3,35},{4,36},{5,6},{6,5},{7,39},{8,40},{9,10},... | collective-permute-start | bytes 49160 | tf_op jit(solution)/shard_map/ppermute | solution.py:354
  53.2 3.0 %collective-permute-start.18 = (f32[32,128]{1,0:T(8,128)S(1)}, f32[32,128]{1,0:T(8,128)S(1)}, u32[]{:S(2)}, u32[]{:S(2)}) collective-permute-start(f32[32,128]{1,0:T(8,128)S(1)} %get-tuple-element.79), channel_id=1, source_target_pairs={{0,32},{1,33},{2,34},{3,35},{4,36},{5,37},{6,38},{7,39},{8,40},{9,... | collective-permute-start | bytes 49160 | tf_op jit(solution)/shard_map/ppermute | solution.py:354
  56.7 4.6 %collective-permute-start.19 = (f32[32,128]{1,0:T(8,128)S(1)}, f32[32,128]{1,0:T(8,128)S(1)}, u32[]{:S(2)}, u32[]{:S(2)}) collective-permute-start(f32[32,128]{1,0:T(8,128)S(1)} %get-tuple-element.82), channel_id=1, source_target_pairs={{0,4},{1,5},{2,6},{3,7},{4,0},{5,1},{6,2},{7,3},{8,12},{9,13},{10,... | collective-permute-start | bytes 49160 | tf_op jit(solution)/shard_map/ppermute | solution.py:354
  57.4 3.9 %collective-permute-start.20 = (f32[32,128]{1,0:T(8,128)S(1)}, f32[32,128]{1,0:T(8,128)S(1)}, u32[]{:S(2)}, u32[]{:S(2)}) collective-permute-start(f32[32,128]{1,0:T(8,128)S(1)} %get-tuple-element.83), channel_id=1, source_target_pairs={{0,32},{1,33},{2,34},{3,35},{4,8},{5,9},{6,10},{7,11},{8,4},{9,5},... | collective-permute-start | bytes 49160 | tf_op jit(solution)/shard_map/ppermute | solution.py:354
  57.4 4.8 %collective-permute-start.21 = (f32[32,128]{1,0:T(8,128)S(1)}, f32[32,128]{1,0:T(8,128)S(1)}, u32[]{:S(2)}, u32[]{:S(2)}) collective-permute-start(f32[32,128]{1,0:T(8,128)S(1)} %get-tuple-element.84), channel_id=1, source_target_pairs={{0,4},{1,5},{2,6},{3,7},{4,0},{5,1},{6,2},{7,3},{8,12},{9,13},{10,... | collective-permute-start | bytes 49160 | tf_op jit(solution)/shard_map/ppermute | solution.py:354
  60.4 3.7 %collective-permute-start.22 = (f32[32,128]{1,0:T(8,128)S(1)}, f32[32,128]{1,0:T(8,128)S(1)}, u32[]{:S(2)}, u32[]{:S(2)}) collective-permute-start(f32[32,128]{1,0:T(8,128)S(1)} %get-tuple-element.85), channel_id=1, source_target_pairs={{0,1},{1,0},{2,3},{3,2},{4,5},{5,4},{6,7},{7,6},{8,9},{9,8},{10,11... | collective-permute-start | bytes 49160 | tf_op jit(solution)/shard_map/ppermute | solution.py:354
  60.4 3.7 %collective-permute-start.23 = (f32[32,128]{1,0:T(8,128)S(1)}, f32[32,128]{1,0:T(8,128)S(1)}, u32[]{:S(2)}, u32[]{:S(2)}) collective-permute-start(f32[32,128]{1,0:T(8,128)S(1)} %get-tuple-element.86), channel_id=1, source_target_pairs={{0,32},{1,2},{2,1},{3,35},{4,36},{5,6},{6,5},{7,39},{8,40},{9,10},... | collective-permute-start | bytes 49160 | tf_op jit(solution)/shard_map/ppermute | solution.py:354
  61.3 2.9 %collective-permute-start.24 = (f32[32,128]{1,0:T(8,128)S(1)}, f32[32,128]{1,0:T(8,128)S(1)}, u32[]{:S(2)}, u32[]{:S(2)}) collective-permute-start(f32[32,128]{1,0:T(8,128)S(1)} %get-tuple-element.87), channel_id=1, source_target_pairs={{0,32},{1,33},{2,34},{3,35},{4,36},{5,37},{6,38},{7,39},{8,40},{9,... | collective-permute-start | bytes 49160 | tf_op jit(solution)/shard_map/ppermute | solution.py:354
  86.7 1.3 %collective-permute-start.25 = (f32[32,384]{1,0:T(8,128)S(1)}, f32[32,384]{1,0:T(8,128)S(1)}, u32[]{:S(2)}, u32[]{:S(2)}) collective-permute-start(f32[32,384]{1,0:T(8,128)S(1)} %shard_map.105.mine), channel_id=1, source_target_pairs={{0,32},{1,33},{2,34},{3,35},{4,36},{5,37},{6,38},{7,39},{8,40},{9,... | collective-permute-start | bytes 147464 | tf_op jit(solution)/shard_map/ppermute | solution.py:364
  88.9 4.6 %collective-permute-start.26 = (f32[32,128]{1,0:T(8,128)S(1)}, f32[32,128]{1,0:T(8,128)S(1)}, u32[]{:S(2)}, u32[]{:S(2)}) collective-permute-start(f32[32,128]{1,0:T(8,128)S(1)} %get-tuple-element.96), channel_id=1, source_target_pairs={{0,4},{1,5},{2,6},{3,7},{4,0},{5,1},{6,2},{7,3},{8,12},{9,13},{10,... | collective-permute-start | bytes 49160 | tf_op jit(solution)/shard_map/ppermute | solution.py:354
  90.0 4.2 %collective-permute-start.27 = (f32[32,128]{1,0:T(8,128)S(1)}, f32[32,128]{1,0:T(8,128)S(1)}, u32[]{:S(2)}, u32[]{:S(2)}) collective-permute-start(f32[32,128]{1,0:T(8,128)S(1)} %get-tuple-element.97), channel_id=1, source_target_pairs={{0,32},{1,33},{2,34},{3,35},{4,8},{5,9},{6,10},{7,11},{8,4},{9,5},... | collective-permute-start | bytes 49160 | tf_op jit(solution)/shard_map/ppermute | solution.py:354
  90.0 4.2 %collective-permute-start.28 = (f32[32,128]{1,0:T(8,128)S(1)}, f32[32,128]{1,0:T(8,128)S(1)}, u32[]{:S(2)}, u32[]{:S(2)}) collective-permute-start(f32[32,128]{1,0:T(8,128)S(1)} %get-tuple-element.98), channel_id=1, source_target_pairs={{0,4},{1,5},{2,6},{3,7},{4,0},{5,1},{6,2},{7,3},{8,12},{9,13},{10,... | collective-permute-start | bytes 49160 | tf_op jit(solution)/shard_map/ppermute | solution.py:354
  91.3 3.7 %collective-permute-start.29 = (f32[32,128]{1,0:T(8,128)S(1)}, f32[32,128]{1,0:T(8,128)S(1)}, u32[]{:S(2)}, u32[]{:S(2)}) collective-permute-start(f32[32,128]{1,0:T(8,128)S(1)} %get-tuple-element.99), channel_id=1, source_target_pairs={{0,1},{1,0},{2,3},{3,2},{4,5},{5,4},{6,7},{7,6},{8,9},{9,8},{10,11... | collective-permute-start | bytes 49160 | tf_op jit(solution)/shard_map/ppermute | solution.py:354
  92.8 3.7 %collective-permute-start.30 = (f32[32,128]{1,0:T(8,128)S(1)}, f32[32,128]{1,0:T(8,128)S(1)}, u32[]{:S(2)}, u32[]{:S(2)}) collective-permute-start(f32[32,128]{1,0:T(8,128)S(1)} %get-tuple-element.100), channel_id=1, source_target_pairs={{0,32},{1,2},{2,1},{3,35},{4,36},{5,6},{6,5},{7,39},{8,40},{9,10},... | collective-permute-start | bytes 49160 | tf_op jit(solution)/shard_map/ppermute | solution.py:354
  93.5 3.0 %collective-permute-start.31 = (f32[32,128]{1,0:T(8,128)S(1)}, f32[32,128]{1,0:T(8,128)S(1)}, u32[]{:S(2)}, u32[]{:S(2)}) collective-permute-start(f32[32,128]{1,0:T(8,128)S(1)} %get-tuple-element.101), channel_id=1, source_target_pairs={{0,32},{1,33},{2,34},{3,35},{4,36},{5,37},{6,38},{7,39},{8,40},{9,... | collective-permute-start | bytes 49160 | tf_op jit(solution)/shard_map/ppermute | solution.py:354

commit v8 on v7

--- a/solution.py
+++ b/solution.py
@@ -38,7 +38,7 @@
     return [lax.axis_index(axis) for axis in AXES]
 
 
-ORDER = (2, 3, 1, 4, 5, 0)
+ORDER = (3, 2, 1, 4, 5, 0)
 
 
 def store_sends(sends, faces):
@@ -99,8 +99,9 @@
     store_sends(sends, faces)
 
 
-def copy_kernel(source, out):
-    out[...] = source[...]
+def stage_kernel(matrix, table, matrix_out, table_out):
+    matrix_out[...] = matrix[...]
+    table_out[...] = table[...]
 
 
 def halves_kernel(source, after, out, whole, turned):
@@ -374,7 +375,11 @@
     cost = pl.CostEstimate(flops=0, bytes_accessed=4 << 20, transcendentals=0)
     (live,) = call(living_kernel, [(8, FACE)], counts, spec=SMEM, cost=cost)
     value, *sends = call(prepare_kernel, [vector] + [(LOADS + 8, FACE)] * 6, live, loads)
-    (dirichlet,) = call(copy_kernel, [jax.ShapeDtypeStruct(dirichlet.shape, BF16)], dirichlet)
+    dirichlet, pairing = call(
+        stage_kernel,
+        [jax.ShapeDtypeStruct(x.shape, x.dtype) for x in (dirichlet, pairing)],
+        dirichlet, pairing,
+    )
     resid, weight, terms, dots, *sends = call(
         first_kernel, [vector, (8, MULT), vector, small] + faces,
         live, value, pairing, dirichlet, *exchange(sends),

time: 97.5 us -> 96.6 us (level)
  waiting for transfers between devices: 13.1 us -> 11.5 us
  blocking collectives: 44.8 us -> 45.9 us
    ppermute x30, waiting for transfers between devices: 11.2 us -> 9.57 us  [exchange(): lax.ppermute(value, AXES, pairs(k // 2, k % 2))]
    all_to_all x2, blocking collectives: 44.8 us -> 45.9 us  [total_sums(): message = lax.all_to_all(message.reshape(DEVICES, 2, FACE), BY_COLUMN, 0, 0)]
  transfers between devices with their start and end apart: 32 -> 32, of which waited for: 12 -> 11; matrix products, arithmetic and copies ran while one was open for 0% -> 0% of each run, Pallas kernels for 1% -> 1%
where the time goes in v8:
time: 96.6 us; the launch traced here: 96.4 us
  blocking collectives  45.9 us (48%)
  starting transfers between devices  28.1 us (29%)
  waiting for transfers between devices  11.5 us (12%)
  Pallas kernels  6.5 us (7%)
  local copies, waits for them, and re-layouts  2.86 us (3%)
  between operations  1.47 us (2%)
    all_to_all x2, blocking collectives, total_sums(): message = lax.all_to_all(message.reshape(DEVICES, 2, FACE), BY_COLUMN, 0, 0)  45.9 us
    ppermute x30, starting transfers between devices, exchange(): lax.ppermute(value, AXES, pairs(k // 2, k % 2))  27.9 us
    ppermute x30, waiting for transfers between devices, exchange(): lax.ppermute(value, AXES, pairs(k // 2, k % 2))  9.57 us
    pallas_call x14, Pallas kernels, call(): pl.pallas_call(kernel, out_shape=[shape if hasattr(shape, 'dtype') else j...  6.5 us
    unnamed x14, local copies, waits for them, and re-layouts  2.86 us
    ppermute x2, waiting for transfers between devices, total_sums(): return (mine, lax.ppermute(mine, AXES, pairs(0, 0)))  1.93 us
  transfers between devices with their start and end apart: 32, of which 11 were waited for; matrix products, arithmetic and copies ran while one was open for 0% of the time, Pallas kernels for 1%

profile of v8, /device:TPU:2, one launch (start us, length us, event | category | flops | bytes accessed | tf_op | source)
XLA Modules:
  0.0 96.4 jit_solution(12441133059098960305)
XLA Ops:
  1.3 0.0 copy-start.4
  1.3 0.9 copy-done.4
  2.2 0.1 collective-permute-start
  2.3 3.8 %collective-permute-start.1 = (f32[40,128]{1,0:T(8,128)S(1)}, f32[40,128]{1,0:T(8,128)S(1)}, u32[]{:S(2)}, u32[]{:S(2)}) collective-permute-start(f32[40,128]{1,0:T(8,128)S(1)} %get-tuple-element.58), channel_id=1, source_target_pairs={{0,4},{1,5},{2,6},{3,7},{4,0},{5,1},{6,2},{7,3},{8,12},{9,13},{10,... | collective-permute-start | bytes 61448 | tf_op jit(solution)/shard_map/ppermute | solution.py:355
  6.2 0.0 collective-permute-start.2
  6.2 0.5 collective-permute-start.3
  6.7 2.1 %collective-permute-start.4 = (f32[40,128]{1,0:T(8,128)S(1)}, f32[40,128]{1,0:T(8,128)S(1)}, u32[]{:S(2)}, u32[]{:S(2)}) collective-permute-start(f32[40,128]{1,0:T(8,128)S(1)} %get-tuple-element.61), channel_id=1, source_target_pairs={{0,32},{1,2},{2,1},{3,35},{4,36},{5,6},{6,5},{7,39},{8,40},{9,10},... | collective-permute-start | bytes 61448 | tf_op jit(solution)/shard_map/ppermute | solution.py:355
  8.9 0.0 collective-permute-done.refs_0_
  8.9 1.1 %collective-permute-start.5 = (f32[40,128]{1,0:T(8,128)S(1)}, f32[40,128]{1,0:T(8,128)S(1)}, u32[]{:S(2)}, u32[]{:S(2)}) collective-permute-start(f32[40,128]{1,0:T(8,128)S(1)} %get-tuple-element.62), channel_id=1, source_target_pairs={{0,32},{1,33},{2,34},{3,35},{4,36},{5,37},{6,38},{7,39},{8,40},{9,... | collective-permute-start | bytes 61448 | tf_op jit(solution)/shard_map/ppermute | solution.py:355
  10.0 1.3 %copy-done.2 = bf16[1,768,768]{2,1,0:T(8,128)(2,1)S(1)} copy-done((bf16[1,768,768]{2,1,0:T(8,128)(2,1)S(1)}, bf16[1,768,768]{2,1,0:T(8,128)(2,1)}, u32[]{:S(2)}) %copy-start.2) | copy-done | bytes 1179672
  11.3 0.7 copy-done.6
  12.0 0.1 shard_map.97
  12.0 0.0 collective-permute-done.1.refs_1_
  12.1 0.0 collective-permute-done.3.refs_3_
  12.1 0.5 shard_map.98
  12.6 0.1 collective-permute-start.6
  12.6 5.0 %collective-permute-start.7 = (f32[32,128]{1,0:T(8,128)S(1)}, f32[32,128]{1,0:T(8,128)S(1)}, u32[]{:S(2)}, u32[]{:S(2)}) collective-permute-start(f32[32,128]{1,0:T(8,128)S(1)} %get-tuple-element.66), channel_id=1, source_target_pairs={{0,4},{1,5},{2,6},{3,7},{4,0},{5,1},{6,2},{7,3},{8,12},{9,13},{10,... | collective-permute-start | bytes 49160 | tf_op jit(solution)/shard_map/ppermute | solution.py:355
  17.7 0.0 collective-permute-start.8
  17.7 1.1 %collective-permute-start.10 = (f32[32,128]{1,0:T(8,128)S(1)}, f32[32,128]{1,0:T(8,128)S(1)}, u32[]{:S(2)}, u32[]{:S(2)}) collective-permute-start(f32[32,128]{1,0:T(8,128)S(1)} %get-tuple-element.69), channel_id=1, source_target_pairs={{0,32},{1,2},{2,1},{3,35},{4,36},{5,6},{6,5},{7,39},{8,40},{9,10},... | collective-permute-start | bytes 49160 | tf_op jit(solution)/shard_map/ppermute | solution.py:355
  18.8 1.1 %collective-permute-start.11 = (f32[32,128]{1,0:T(8,128)S(1)}, f32[32,128]{1,0:T(8,128)S(1)}, u32[]{:S(2)}, u32[]{:S(2)}) collective-permute-start(f32[32,128]{1,0:T(8,128)S(1)} %get-tuple-element.70), channel_id=1, source_target_pairs={{0,32},{1,33},{2,34},{3,35},{4,36},{5,37},{6,38},{7,39},{8,40},{9,... | collective-permute-start | bytes 49160 | tf_op jit(solution)/shard_map/ppermute | solution.py:355
  19.9 1.5 %collective-permute-done.8.refs_2_ = f32[32,128]{1,0:T(8,128)S(1)} collective-permute-done((f32[32,128]{1,0:T(8,128)S(1)}, f32[32,128]{1,0:T(8,128)S(1)}, u32[]{:S(2)}, u32[]{:S(2)}) %collective-permute-start.8) | collective-permute-done | bytes 16416 | tf_op jit(solution)/shard_map/ppermute | solution.py:355
  21.4 0.0 collective-permute-done.9.refs_3_
  21.5 0.0 copy-start.3
  21.5 0.7 shard_map.100
  22.2 23.8 %all_to_all.10 = f32[256,2,128]{2,1,0:T(2,128)S(1)} all-to-all(f32[256,2,128]{2,1,0:T(2,128)S(1)} %bitcast.7), channel_id=1, replica_groups=mesh['region'=8,'gy'=8,'gz'=4] {'gy','gz','region'}, dimensions={0} | all-to-all | bytes 524288 | tf_op jit(solution)/shard_map/all_to_all | solution.py:360
  46.0 0.3 shard_map.101.mine
  46.3 0.1 collective-permute-start.12
  46.4 0.5 shard_map.99.inverse
  46.9 0.7 collective-permute-done.12.other
  47.6 0.6 shard_map.102
  48.2 0.2 collective-permute-start.13
  48.4 1.8 %collective-permute-start.14 = (f32[32,128]{1,0:T(8,128)S(1)}, f32[32,128]{1,0:T(8,128)S(1)}, u32[]{:S(2)}, u32[]{:S(2)}) collective-permute-start(f32[32,128]{1,0:T(8,128)S(1)} %get-tuple-element.79), channel_id=1, source_target_pairs={{0,4},{1,5},{2,6},{3,7},{4,0},{5,1},{6,2},{7,3},{8,12},{9,13},{10,... | collective-permute-start | bytes 49160 | tf_op jit(solution)/shard_map/ppermute | solution.py:355
  50.2 0.3 collective-permute-start.15
  50.5 1.5 %collective-permute-start.16 = (f32[32,128]{1,0:T(8,128)S(1)}, f32[32,128]{1,0:T(8,128)S(1)}, u32[]{:S(2)}, u32[]{:S(2)}) collective-permute-start(f32[32,128]{1,0:T(8,128)S(1)} %get-tuple-element.81), channel_id=1, source_target_pairs={{0,1},{1,0},{2,3},{3,2},{4,5},{5,4},{6,7},{7,6},{8,9},{9,8},{10,11... | collective-permute-start | bytes 49160 | tf_op jit(solution)/shard_map/ppermute | solution.py:355
  51.9 0.8 collective-permute-start.17
  52.8 1.1 %collective-permute-done.15.refs_2_ = f32[32,128]{1,0:T(8,128)S(1)} collective-permute-done((f32[32,128]{1,0:T(8,128)S(1)}, f32[32,128]{1,0:T(8,128)S(1)}, u32[]{:S(2)}, u32[]{:S(2)}) %collective-permute-start.15) | collective-permute-done | bytes 16416 | tf_op jit(solution)/shard_map/ppermute | solution.py:355
  53.9 0.3 collective-permute-done.16.refs_3_
  54.2 1.5 %collective-permute-done.17.refs_4_ = f32[32,128]{1,0:T(8,128)S(1)} collective-permute-done((f32[32,128]{1,0:T(8,128)S(1)}, f32[32,128]{1,0:T(8,128)S(1)}, u32[]{:S(2)}, u32[]{:S(2)}) %collective-permute-start.17) | collective-permute-done | bytes 16416 | tf_op jit(solution)/shard_map/ppermute | solution.py:355
  55.7 0.5 shard_map.103
  56.1 0.0 collective-permute-start.19
  56.2 2.9 %collective-permute-start.20 = (f32[32,128]{1,0:T(8,128)S(1)}, f32[32,128]{1,0:T(8,128)S(1)}, u32[]{:S(2)}, u32[]{:S(2)}) collective-permute-start(f32[32,128]{1,0:T(8,128)S(1)} %get-tuple-element.87), channel_id=1, source_target_pairs={{0,4},{1,5},{2,6},{3,7},{4,0},{5,1},{6,2},{7,3},{8,12},{9,13},{10,... | collective-permute-start | bytes 49160 | tf_op jit(solution)/shard_map/ppermute | solution.py:355
  59.1 0.0 collective-permute-start.21
  59.1 0.0 collective-permute-start.22
  59.1 0.8 collective-permute-start.23
  59.9 0.9 collective-permute-done.20.refs_1_
  60.8 2.0 %collective-permute-done.21.refs_2_ = f32[32,128]{1,0:T(8,128)S(1)} collective-permute-done((f32[32,128]{1,0:T(8,128)S(1)}, f32[32,128]{1,0:T(8,128)S(1)}, u32[]{:S(2)}, u32[]{:S(2)}) %collective-permute-start.21) | collective-permute-done | bytes 16416 | tf_op jit(solution)/shard_map/ppermute | solution.py:355
  62.8 0.0 collective-permute-done.22.refs_3_
  62.8 0.0 collective-permute-done.23.refs_4_
  62.8 0.7 shard_map.104
  63.6 22.1 %all_to_all.11 = f32[256,2,128]{2,1,0:T(2,128)S(1)} all-to-all(f32[256,2,128]{2,1,0:T(2,128)S(1)} %bitcast.8), channel_id=1, replica_groups=mesh['region'=8,'gy'=8,'gz'=4] {'gy','gz','region'}, dimensions={0} | all-to-all | bytes 524288 | tf_op jit(solution)/shard_map/all_to_all | solution.py:360
  85.6 0.3 shard_map.105.mine
  85.9 0.1 collective-permute-start.25
  86.0 1.2 %collective-permute-done.25.other = f32[32,384]{1,0:T(8,128)S(1)} collective-permute-done((f32[32,384]{1,0:T(8,128)S(1)}, f32[32,384]{1,0:T(8,128)S(1)}, u32[]{:S(2)}, u32[]{:S(2)}) %collective-permute-start.25) | collective-permute-done | bytes 49184 | tf_op jit(solution)/shard_map/ppermute | solution.py:365
  87.2 0.9 shard_map.106
  88.1 0.2 collective-permute-start.26
  88.3 1.8 %collective-permute-start.27 = (f32[32,128]{1,0:T(8,128)S(1)}, f32[32,128]{1,0:T(8,128)S(1)}, u32[]{:S(2)}, u32[]{:S(2)}) collective-permute-start(f32[32,128]{1,0:T(8,128)S(1)} %get-tuple-element.101), channel_id=1, source_target_pairs={{0,4},{1,5},{2,6},{3,7},{4,0},{5,1},{6,2},{7,3},{8,12},{9,13},{10,... | collective-permute-start | bytes 49160 | tf_op jit(solution)/shard_map/ppermute | solution.py:355
  90.1 0.3 collective-permute-start.28
  90.4 1.5 %collective-permute-start.29 = (f32[32,128]{1,0:T(8,128)S(1)}, f32[32,128]{1,0:T(8,128)S(1)}, u32[]{:S(2)}, u32[]{:S(2)}) collective-permute-start(f32[32,128]{1,0:T(8,128)S(1)} %get-tuple-element.103), channel_id=1, source_target_pairs={{0,1},{1,0},{2,3},{3,2},{4,5},{5,4},{6,7},{7,6},{8,9},{9,8},{10,11... | collective-permute-start | bytes 49160 | tf_op jit(solution)/shard_map/ppermute | solution.py:355
  91.8 0.8 collective-permute-start.30
  92.7 0.7 shard_map.107
  93.4 0.4 collective-permute-done.28.refs_2_
  93.8 0.3 collective-permute-done.29.refs_3_
  94.1 1.5 %collective-permute-done.30.refs_4_ = f32[32,128]{1,0:T(8,128)S(1)} collective-permute-done((f32[32,128]{1,0:T(8,128)S(1)}, f32[32,128]{1,0:T(8,128)S(1)}, u32[]{:S(2)}, u32[]{:S(2)}) %collective-permute-start.30) | collective-permute-done | bytes 16416 | tf_op jit(solution)/shard_map/ppermute | solution.py:355
  95.6 0.8 shard_map.108
  (30 shorter events, 0.1 us)
Async XLA Ops:
  1.3 0.9 copy-start.4
  2.2 6.6 %collective-permute-start = (f32[40,128]{1,0:T(8,128)S(1)}, f32[40,128]{1,0:T(8,128)S(1)}, u32[]{:S(2)}, u32[]{:S(2)}) collective-permute-start(f32[40,128]{1,0:T(8,128)S(1)} %get-tuple-element.57), channel_id=1, source_target_pairs={{0,32},{1,33},{2,34},{3,35},{4,8},{5,9},{6,10},{7,11},{8,4},{9,5},... | collective-permute-start | bytes 61448 | tf_op jit(solution)/shard_map/ppermute | solution.py:355
  2.3 9.7 %collective-permute-start.1 = (f32[40,128]{1,0:T(8,128)S(1)}, f32[40,128]{1,0:T(8,128)S(1)}, u32[]{:S(2)}, u32[]{:S(2)}) collective-permute-start(f32[40,128]{1,0:T(8,128)S(1)} %get-tuple-element.58), channel_id=1, source_target_pairs={{0,4},{1,5},{2,6},{3,7},{4,0},{5,1},{6,2},{7,3},{8,12},{9,13},{10,... | collective-permute-start | bytes 61448 | tf_op jit(solution)/shard_map/ppermute | solution.py:355
  6.2 5.9 %collective-permute-start.2 = (f32[40,128]{1,0:T(8,128)S(1)}, f32[40,128]{1,0:T(8,128)S(1)}, u32[]{:S(2)}, u32[]{:S(2)}) collective-permute-start(f32[40,128]{1,0:T(8,128)S(1)} %get-tuple-element.59), channel_id=1, source_target_pairs={{0,4},{1,5},{2,6},{3,7},{4,0},{5,1},{6,2},{7,3},{8,12},{9,13},{10,... | collective-permute-start | bytes 61448 | tf_op jit(solution)/shard_map/ppermute | solution.py:355
  6.2 5.9 %collective-permute-start.3 = (f32[40,128]{1,0:T(8,128)S(1)}, f32[40,128]{1,0:T(8,128)S(1)}, u32[]{:S(2)}, u32[]{:S(2)}) collective-permute-start(f32[40,128]{1,0:T(8,128)S(1)} %get-tuple-element.60), channel_id=1, source_target_pairs={{0,1},{1,0},{2,3},{3,2},{4,5},{5,4},{6,7},{7,6},{8,9},{9,8},{10,11... | collective-permute-start | bytes 61448 | tf_op jit(solution)/shard_map/ppermute | solution.py:355
  6.7 5.3 %collective-permute-start.4 = (f32[40,128]{1,0:T(8,128)S(1)}, f32[40,128]{1,0:T(8,128)S(1)}, u32[]{:S(2)}, u32[]{:S(2)}) collective-permute-start(f32[40,128]{1,0:T(8,128)S(1)} %get-tuple-element.61), channel_id=1, source_target_pairs={{0,32},{1,2},{2,1},{3,35},{4,36},{5,6},{6,5},{7,39},{8,40},{9,10},... | collective-permute-start | bytes 61448 | tf_op jit(solution)/shard_map/ppermute | solution.py:355
  8.9 3.2 %collective-permute-start.5 = (f32[40,128]{1,0:T(8,128)S(1)}, f32[40,128]{1,0:T(8,128)S(1)}, u32[]{:S(2)}, u32[]{:S(2)}) collective-permute-start(f32[40,128]{1,0:T(8,128)S(1)} %get-tuple-element.62), channel_id=1, source_target_pairs={{0,32},{1,33},{2,34},{3,35},{4,36},{5,37},{6,38},{7,39},{8,40},{9,... | collective-permute-start | bytes 61448 | tf_op jit(solution)/shard_map/ppermute | solution.py:355
  10.0 1.3 %copy-start.2 = (bf16[1,768,768]{2,1,0:T(8,128)(2,1)S(1)}, bf16[1,768,768]{2,1,0:T(8,128)(2,1)}, u32[]{:S(2)}) copy-start(bf16[1,768,768]{2,1,0:T(8,128)(2,1)} %matrix.1) | copy-start | bytes 3538948
  11.3 0.7 copy-start.6
  11.9 9.5 %copy-start = (bf16[1,768,768]{2,1,0:T(8,128)(2,1)S(1)}, bf16[1,768,768]{2,1,0:T(8,128)(2,1)}, u32[]{:S(2)}) copy-start(bf16[1,768,768]{2,1,0:T(8,128)(2,1)} %schur.5) | copy-start | bytes 3538948
  11.9 9.5 %copy-start.1 = (bf16[1,768,128]{2,1,0:T(8,128)(2,1)S(1)}, bf16[1,768,128]{2,1,0:T(8,128)(2,1)}, u32[]{:S(2)}) copy-start(bf16[1,768,128]{2,1,0:T(8,128)(2,1)} %coupling.7) | copy-start | bytes 589828
  11.9 9.5 %copy-start.5 = (s32[1,128]{1,0:T(1,128)S(1)}, s32[1,128]{1,0:T(1,128)}, u32[]{:S(2)}) copy-start(s32[1,128]{1,0:T(1,128)} %corner_map.7) | copy-start | bytes 1540
  12.6 6.3 %collective-permute-start.6 = (f32[32,128]{1,0:T(8,128)S(1)}, f32[32,128]{1,0:T(8,128)S(1)}, u32[]{:S(2)}, u32[]{:S(2)}) collective-permute-start(f32[32,128]{1,0:T(8,128)S(1)} %get-tuple-element.65), channel_id=1, source_target_pairs={{0,32},{1,33},{2,34},{3,35},{4,8},{5,9},{6,10},{7,11},{8,4},{9,5},... | collective-permute-start | bytes 49160 | tf_op jit(solution)/shard_map/ppermute | solution.py:355
  12.6 7.3 %collective-permute-start.7 = (f32[32,128]{1,0:T(8,128)S(1)}, f32[32,128]{1,0:T(8,128)S(1)}, u32[]{:S(2)}, u32[]{:S(2)}) collective-permute-start(f32[32,128]{1,0:T(8,128)S(1)} %get-tuple-element.66), channel_id=1, source_target_pairs={{0,4},{1,5},{2,6},{3,7},{4,0},{5,1},{6,2},{7,3},{8,12},{9,13},{10,... | collective-permute-start | bytes 49160 | tf_op jit(solution)/shard_map/ppermute | solution.py:355
  17.7 3.7 %collective-permute-start.8 = (f32[32,128]{1,0:T(8,128)S(1)}, f32[32,128]{1,0:T(8,128)S(1)}, u32[]{:S(2)}, u32[]{:S(2)}) collective-permute-start(f32[32,128]{1,0:T(8,128)S(1)} %get-tuple-element.67), channel_id=1, source_target_pairs={{0,4},{1,5},{2,6},{3,7},{4,0},{5,1},{6,2},{7,3},{8,12},{9,13},{10,... | collective-permute-start | bytes 49160 | tf_op jit(solution)/shard_map/ppermute | solution.py:355
  17.7 3.7 %collective-permute-start.9 = (f32[32,128]{1,0:T(8,128)S(1)}, f32[32,128]{1,0:T(8,128)S(1)}, u32[]{:S(2)}, u32[]{:S(2)}) collective-permute-start(f32[32,128]{1,0:T(8,128)S(1)} %get-tuple-element.68), channel_id=1, source_target_pairs={{0,1},{1,0},{2,3},{3,2},{4,5},{5,4},{6,7},{7,6},{8,9},{9,8},{10,11... | collective-permute-start | bytes 49160 | tf_op jit(solution)/shard_map/ppermute | solution.py:355
  17.7 3.7 %collective-permute-start.10 = (f32[32,128]{1,0:T(8,128)S(1)}, f32[32,128]{1,0:T(8,128)S(1)}, u32[]{:S(2)}, u32[]{:S(2)}) collective-permute-start(f32[32,128]{1,0:T(8,128)S(1)} %get-tuple-element.69), channel_id=1, source_target_pairs={{0,32},{1,2},{2,1},{3,35},{4,36},{5,6},{6,5},{7,39},{8,40},{9,10},... | collective-permute-start | bytes 49160 | tf_op jit(solution)/shard_map/ppermute | solution.py:355
  18.8 2.6 %collective-permute-start.11 = (f32[32,128]{1,0:T(8,128)S(1)}, f32[32,128]{1,0:T(8,128)S(1)}, u32[]{:S(2)}, u32[]{:S(2)}) collective-permute-start(f32[32,128]{1,0:T(8,128)S(1)} %get-tuple-element.70), channel_id=1, source_target_pairs={{0,32},{1,33},{2,34},{3,35},{4,36},{5,37},{6,38},{7,39},{8,40},{9,... | collective-permute-start | bytes 49160 | tf_op jit(solution)/shard_map/ppermute | solution.py:355
  21.5 24.9 %copy-start.3 = (f32[512,512]{1,0:T(8,128)S(1)}, f32[512,512]{1,0:T(8,128)}, u32[]{:S(2)}) copy-start(f32[512,512]{1,0:T(8,128)} %source.1) | copy-start | bytes 3145732
  46.3 1.3 %collective-permute-start.12 = (f32[32,384]{1,0:T(8,128)S(1)}, f32[32,384]{1,0:T(8,128)S(1)}, u32[]{:S(2)}, u32[]{:S(2)}) collective-permute-start(f32[32,384]{1,0:T(8,128)S(1)} %shard_map.101.mine), channel_id=1, source_target_pairs={{0,32},{1,33},{2,34},{3,35},{4,36},{5,37},{6,38},{7,39},{8,40},{9,... | collective-permute-start | bytes 147464 | tf_op jit(solution)/shard_map/ppermute | solution.py:365
  48.2 4.6 %collective-permute-start.13 = (f32[32,128]{1,0:T(8,128)S(1)}, f32[32,128]{1,0:T(8,128)S(1)}, u32[]{:S(2)}, u32[]{:S(2)}) collective-permute-start(f32[32,128]{1,0:T(8,128)S(1)} %get-tuple-element.78), channel_id=1, source_target_pairs={{0,32},{1,33},{2,34},{3,35},{4,8},{5,9},{6,10},{7,11},{8,4},{9,5},... | collective-permute-start | bytes 49160 | tf_op jit(solution)/shard_map/ppermute | solution.py:355
  48.4 4.3 %collective-permute-start.14 = (f32[32,128]{1,0:T(8,128)S(1)}, f32[32,128]{1,0:T(8,128)S(1)}, u32[]{:S(2)}, u32[]{:S(2)}) collective-permute-start(f32[32,128]{1,0:T(8,128)S(1)} %get-tuple-element.79), channel_id=1, source_target_pairs={{0,4},{1,5},{2,6},{3,7},{4,0},{5,1},{6,2},{7,3},{8,12},{9,13},{10,... | collective-permute-start | bytes 49160 | tf_op jit(solution)/shard_map/ppermute | solution.py:355
  50.2 3.7 %collective-permute-start.15 = (f32[32,128]{1,0:T(8,128)S(1)}, f32[32,128]{1,0:T(8,128)S(1)}, u32[]{:S(2)}, u32[]{:S(2)}) collective-permute-start(f32[32,128]{1,0:T(8,128)S(1)} %get-tuple-element.80), channel_id=1, source_target_pairs={{0,4},{1,5},{2,6},{3,7},{4,0},{5,1},{6,2},{7,3},{8,12},{9,13},{10,... | collective-permute-start | bytes 49160 | tf_op jit(solution)/shard_map/ppermute | solution.py:355
  50.5 3.7 %collective-permute-start.16 = (f32[32,128]{1,0:T(8,128)S(1)}, f32[32,128]{1,0:T(8,128)S(1)}, u32[]{:S(2)}, u32[]{:S(2)}) collective-permute-start(f32[32,128]{1,0:T(8,128)S(1)} %get-tuple-element.81), channel_id=1, source_target_pairs={{0,1},{1,0},{2,3},{3,2},{4,5},{5,4},{6,7},{7,6},{8,9},{9,8},{10,11... | collective-permute-start | bytes 49160 | tf_op jit(solution)/shard_map/ppermute | solution.py:355
  51.9 3.7 %collective-permute-start.17 = (f32[32,128]{1,0:T(8,128)S(1)}, f32[32,128]{1,0:T(8,128)S(1)}, u32[]{:S(2)}, u32[]{:S(2)}) collective-permute-start(f32[32,128]{1,0:T(8,128)S(1)} %get-tuple-element.82), channel_id=1, source_target_pairs={{0,32},{1,2},{2,1},{3,35},{4,36},{5,6},{6,5},{7,39},{8,40},{9,10},... | collective-permute-start | bytes 49160 | tf_op jit(solution)/shard_map/ppermute | solution.py:355
  52.8 2.9 %collective-permute-start.18 = (f32[32,128]{1,0:T(8,128)S(1)}, f32[32,128]{1,0:T(8,128)S(1)}, u32[]{:S(2)}, u32[]{:S(2)}) collective-permute-start(f32[32,128]{1,0:T(8,128)S(1)} %get-tuple-element.83), channel_id=1, source_target_pairs={{0,32},{1,33},{2,34},{3,35},{4,36},{5,37},{6,38},{7,39},{8,40},{9,... | collective-permute-start | bytes 49160 | tf_op jit(solution)/shard_map/ppermute | solution.py:355
  56.1 3.7 %collective-permute-start.19 = (f32[32,128]{1,0:T(8,128)S(1)}, f32[32,128]{1,0:T(8,128)S(1)}, u32[]{:S(2)}, u32[]{:S(2)}) collective-permute-start(f32[32,128]{1,0:T(8,128)S(1)} %get-tuple-element.86), channel_id=1, source_target_pairs={{0,32},{1,33},{2,34},{3,35},{4,8},{5,9},{6,10},{7,11},{8,4},{9,5},... | collective-permute-start | bytes 49160 | tf_op jit(solution)/shard_map/ppermute | solution.py:355
  56.2 4.6 %collective-permute-start.20 = (f32[32,128]{1,0:T(8,128)S(1)}, f32[32,128]{1,0:T(8,128)S(1)}, u32[]{:S(2)}, u32[]{:S(2)}) collective-permute-start(f32[32,128]{1,0:T(8,128)S(1)} %get-tuple-element.87), channel_id=1, source_target_pairs={{0,4},{1,5},{2,6},{3,7},{4,0},{5,1},{6,2},{7,3},{8,12},{9,13},{10,... | collective-permute-start | bytes 49160 | tf_op jit(solution)/shard_map/ppermute | solution.py:355
  59.1 3.7 %collective-permute-start.21 = (f32[32,128]{1,0:T(8,128)S(1)}, f32[32,128]{1,0:T(8,128)S(1)}, u32[]{:S(2)}, u32[]{:S(2)}) collective-permute-start(f32[32,128]{1,0:T(8,128)S(1)} %get-tuple-element.88), channel_id=1, source_target_pairs={{0,4},{1,5},{2,6},{3,7},{4,0},{5,1},{6,2},{7,3},{8,12},{9,13},{10,... | collective-permute-start | bytes 49160 | tf_op jit(solution)/shard_map/ppermute | solution.py:355
  59.1 3.7 %collective-permute-start.22 = (f32[32,128]{1,0:T(8,128)S(1)}, f32[32,128]{1,0:T(8,128)S(1)}, u32[]{:S(2)}, u32[]{:S(2)}) collective-permute-start(f32[32,128]{1,0:T(8,128)S(1)} %get-tuple-element.89), channel_id=1, source_target_pairs={{0,1},{1,0},{2,3},{3,2},{4,5},{5,4},{6,7},{7,6},{8,9},{9,8},{10,11... | collective-permute-start | bytes 49160 | tf_op jit(solution)/shard_map/ppermute | solution.py:355
  59.1 3.7 %collective-permute-start.23 = (f32[32,128]{1,0:T(8,128)S(1)}, f32[32,128]{1,0:T(8,128)S(1)}, u32[]{:S(2)}, u32[]{:S(2)}) collective-permute-start(f32[32,128]{1,0:T(8,128)S(1)} %get-tuple-element.90), channel_id=1, source_target_pairs={{0,32},{1,2},{2,1},{3,35},{4,36},{5,6},{6,5},{7,39},{8,40},{9,10},... | collective-permute-start | bytes 49160 | tf_op jit(solution)/shard_map/ppermute | solution.py:355
  59.9 3.0 %collective-permute-start.24 = (f32[32,128]{1,0:T(8,128)S(1)}, f32[32,128]{1,0:T(8,128)S(1)}, u32[]{:S(2)}, u32[]{:S(2)}) collective-permute-start(f32[32,128]{1,0:T(8,128)S(1)} %get-tuple-element.91), channel_id=1, source_target_pairs={{0,32},{1,33},{2,34},{3,35},{4,36},{5,37},{6,38},{7,39},{8,40},{9,... | collective-permute-start | bytes 49160 | tf_op jit(solution)/shard_map/ppermute | solution.py:355
  85.9 1.3 %collective-permute-start.25 = (f32[32,384]{1,0:T(8,128)S(1)}, f32[32,384]{1,0:T(8,128)S(1)}, u32[]{:S(2)}, u32[]{:S(2)}) collective-permute-start(f32[32,384]{1,0:T(8,128)S(1)} %shard_map.105.mine), channel_id=1, source_target_pairs={{0,32},{1,33},{2,34},{3,35},{4,36},{5,37},{6,38},{7,39},{8,40},{9,... | collective-permute-start | bytes 147464 | tf_op jit(solution)/shard_map/ppermute | solution.py:365
  88.1 4.5 %collective-permute-start.26 = (f32[32,128]{1,0:T(8,128)S(1)}, f32[32,128]{1,0:T(8,128)S(1)}, u32[]{:S(2)}, u32[]{:S(2)}) collective-permute-start(f32[32,128]{1,0:T(8,128)S(1)} %get-tuple-element.100), channel_id=1, source_target_pairs={{0,32},{1,33},{2,34},{3,35},{4,8},{5,9},{6,10},{7,11},{8,4},{9,5},... | collective-permute-start | bytes 49160 | tf_op jit(solution)/shard_map/ppermute | solution.py:355
  88.3 5.1 %collective-permute-start.27 = (f32[32,128]{1,0:T(8,128)S(1)}, f32[32,128]{1,0:T(8,128)S(1)}, u32[]{:S(2)}, u32[]{:S(2)}) collective-permute-start(f32[32,128]{1,0:T(8,128)S(1)} %get-tuple-element.101), channel_id=1, source_target_pairs={{0,4},{1,5},{2,6},{3,7},{4,0},{5,1},{6,2},{7,3},{8,12},{9,13},{10,... | collective-permute-start | bytes 49160 | tf_op jit(solution)/shard_map/ppermute | solution.py:355
  90.1 3.7 %collective-permute-start.28 = (f32[32,128]{1,0:T(8,128)S(1)}, f32[32,128]{1,0:T(8,128)S(1)}, u32[]{:S(2)}, u32[]{:S(2)}) collective-permute-start(f32[32,128]{1,0:T(8,128)S(1)} %get-tuple-element.102), channel_id=1, source_target_pairs={{0,4},{1,5},{2,6},{3,7},{4,0},{5,1},{6,2},{7,3},{8,12},{9,13},{10,... | collective-permute-start | bytes 49160 | tf_op jit(solution)/shard_map/ppermute | solution.py:355
  90.4 3.7 %collective-permute-start.29 = (f32[32,128]{1,0:T(8,128)S(1)}, f32[32,128]{1,0:T(8,128)S(1)}, u32[]{:S(2)}, u32[]{:S(2)}) collective-permute-start(f32[32,128]{1,0:T(8,128)S(1)} %get-tuple-element.103), channel_id=1, source_target_pairs={{0,1},{1,0},{2,3},{3,2},{4,5},{5,4},{6,7},{7,6},{8,9},{9,8},{10,11... | collective-permute-start | bytes 49160 | tf_op jit(solution)/shard_map/ppermute | solution.py:355
  91.8 3.7 %collective-permute-start.30 = (f32[32,128]{1,0:T(8,128)S(1)}, f32[32,128]{1,0:T(8,128)S(1)}, u32[]{:S(2)}, u32[]{:S(2)}) collective-permute-start(f32[32,128]{1,0:T(8,128)S(1)} %get-tuple-element.104), channel_id=1, source_target_pairs={{0,32},{1,2},{2,1},{3,35},{4,36},{5,6},{6,5},{7,39},{8,40},{9,10},... | collective-permute-start | bytes 49160 | tf_op jit(solution)/shard_map/ppermute | solution.py:355
  92.7 2.9 %collective-permute-start.31 = (f32[32,128]{1,0:T(8,128)S(1)}, f32[32,128]{1,0:T(8,128)S(1)}, u32[]{:S(2)}, u32[]{:S(2)}) collective-permute-start(f32[32,128]{1,0:T(8,128)S(1)} %get-tuple-element.105), channel_id=1, source_target_pairs={{0,32},{1,33},{2,34},{3,35},{4,36},{5,37},{6,38},{7,39},{8,40},{9,... | collective-permute-start | bytes 49160 | tf_op jit(solution)/shard_map/ppermute | solution.py:355

commit v9 on v7

--- a/solution.py
+++ b/solution.py
@@ -38,7 +38,7 @@
     return [lax.axis_index(axis) for axis in AXES]
 
 
-ORDER = (2, 3, 1, 4, 5, 0)
+ORDER = (3, 2, 1, 4, 5, 0)
 
 
 def store_sends(sends, faces):
@@ -307,12 +307,11 @@
     direction_ref[...] = direction
 
 
-def solution_kernel(scalar_ref, first, step_ref, direction, out):
-    out[0] = scalar_ref[:, 2:3] * first[...] + step_ref[:, 0:1] * direction[...]
-
-
-def seventh_kernel(live_ref, pairing, resid, image_ref, step_ref, *refs):
-    recvs, (out,) = refs[:6], refs[6:]
+def seventh_kernel(
+    live_ref, pairing, resid, image_ref, scalar_ref, step_ref, first, direction, *refs
+):
+    recvs, (solution_ref, out) = refs[:6], refs[6:]
+    solution_ref[0] = scalar_ref[:, 2:3] * first[...] + step_ref[:, 0:1] * direction[...]
     live = live_ref[0:1, 0:1]
     image = live * (image_ref[...] + partner(recvs, pairing))
     out[0] = resid[...] - step_ref[:, 0:1] * image
@@ -407,10 +406,9 @@
         live, corner_map, schur, coupling, inverse, *total_sums(message),
         gathered, solved, scalars, first, precond,
     )
-    (solution_out,) = call(solution_kernel, [(1,) + vector], scalars, first, step, direction)
-    (residual_out,) = call(
-        seventh_kernel, [(1,) + vector],
-        live, pairing, resid, image, step, *exchange(sends),
+    solution_out, residual_out = call(
+        seventh_kernel, [(1,) + vector] * 2,
+        live, pairing, resid, image, scalars, step, first, direction, *exchange(sends),
     )
     return solution_out, residual_out
 

time: 97.5 us -> 96.6 us (level)
  blocking collectives: 44.8 us -> 46.1 us
    all_to_all x2, blocking collectives: 44.8 us -> 46.1 us  [total_sums(): message = lax.all_to_all(message.reshape(DEVICES, 2, FACE), BY_COLUMN, 0, 0)]
    pallas_call x14 -> x13, Pallas kernels: 6.49 us -> 5.79 us  [call(): pl.pallas_call(kernel, out_shape=[shape if hasattr(shape, 'dtype') else j...]
  transfers between devices with their start and end apart: 32 -> 32, of which waited for: 12 -> 11; matrix products, arithmetic and copies ran while one was open for 0% -> 0% of each run, Pallas kernels for 1% -> 1%
where the time goes in v9:
time: 96.6 us; the launch traced here: 96.4 us
  blocking collectives  46.1 us (48%)
  starting transfers between devices  28.1 us (29%)
  waiting for transfers between devices  12.2 us (13%)
  Pallas kernels  5.79 us (6%)
  local copies, waits for them, and re-layouts  2.7 us (3%)
  between operations  1.5 us (2%)
    all_to_all x2, blocking collectives, total_sums(): message = lax.all_to_all(message.reshape(DEVICES, 2, FACE), BY_COLUMN, 0, 0)  46.1 us
    ppermute x30, starting transfers between devices, exchange(): lax.ppermute(value, AXES, pairs(k // 2, k % 2))  27.9 us
    ppermute x30, waiting for transfers between devices, exchange(): lax.ppermute(value, AXES, pairs(k // 2, k % 2))  10.3 us
    pallas_call x13, Pallas kernels, call(): pl.pallas_call(kernel, out_shape=[shape if hasattr(shape, 'dtype') else j...  5.79 us
    unnamed x14, local copies, waits for them, and re-layouts  2.7 us
    ppermute x2, waiting for transfers between devices, total_sums(): return (mine, lax.ppermute(mine, AXES, pairs(0, 0)))  1.93 us
  transfers between devices with their start and end apart: 32, of which 11 were waited for; matrix products, arithmetic and copies ran while one was open for 0% of the time, Pallas kernels for 1%

profile of v9, /device:TPU:2, one launch (start us, length us, event | category | flops | bytes accessed | tf_op | source)
XLA Modules:
  0.0 96.4 jit_solution(14695597407028095826)
XLA Ops:
  1.3 0.0 copy-start.4
  1.3 0.9 copy-done.4
  2.2 0.1 collective-permute-start
  2.3 3.8 %collective-permute-start.1 = (f32[40,128]{1,0:T(8,128)S(1)}, f32[40,128]{1,0:T(8,128)S(1)}, u32[]{:S(2)}, u32[]{:S(2)}) collective-permute-start(f32[40,128]{1,0:T(8,128)S(1)} %get-tuple-element.54), channel_id=1, source_target_pairs={{0,4},{1,5},{2,6},{3,7},{4,0},{5,1},{6,2},{7,3},{8,12},{9,13},{10,... | collective-permute-start | bytes 61448 | tf_op jit(solution)/shard_map/ppermute | solution.py:353
  6.2 0.0 collective-permute-start.2
  6.2 0.5 collective-permute-start.3
  6.7 2.1 %collective-permute-start.4 = (f32[40,128]{1,0:T(8,128)S(1)}, f32[40,128]{1,0:T(8,128)S(1)}, u32[]{:S(2)}, u32[]{:S(2)}) collective-permute-start(f32[40,128]{1,0:T(8,128)S(1)} %get-tuple-element.57), channel_id=1, source_target_pairs={{0,32},{1,2},{2,1},{3,35},{4,36},{5,6},{6,5},{7,39},{8,40},{9,10},... | collective-permute-start | bytes 61448 | tf_op jit(solution)/shard_map/ppermute | solution.py:353
  8.9 0.0 collective-permute-done.refs_0_
  8.9 1.1 %collective-permute-start.5 = (f32[40,128]{1,0:T(8,128)S(1)}, f32[40,128]{1,0:T(8,128)S(1)}, u32[]{:S(2)}, u32[]{:S(2)}) collective-permute-start(f32[40,128]{1,0:T(8,128)S(1)} %get-tuple-element.58), channel_id=1, source_target_pairs={{0,32},{1,33},{2,34},{3,35},{4,36},{5,37},{6,38},{7,39},{8,40},{9,... | collective-permute-start | bytes 61448 | tf_op jit(solution)/shard_map/ppermute | solution.py:353
  10.0 1.3 %copy-done.2 = bf16[1,768,768]{2,1,0:T(8,128)(2,1)S(1)} copy-done((bf16[1,768,768]{2,1,0:T(8,128)(2,1)S(1)}, bf16[1,768,768]{2,1,0:T(8,128)(2,1)}, u32[]{:S(2)}) %copy-start.2) | copy-done | bytes 1179672
  11.3 0.1 shard_map.96.dirichlet
  11.3 0.0 copy-start
  11.4 0.0 copy-start.1
  11.4 0.0 copy-start.6
  11.4 0.0 collective-permute-done.1.refs_1_
  11.4 0.0 collective-permute-done.4.refs_4_
  11.4 0.5 copy-done.5
  11.9 0.5 shard_map.98
  12.4 0.1 collective-permute-start.6
  12.5 5.0 %collective-permute-start.7 = (f32[32,128]{1,0:T(8,128)S(1)}, f32[32,128]{1,0:T(8,128)S(1)}, u32[]{:S(2)}, u32[]{:S(2)}) collective-permute-start(f32[32,128]{1,0:T(8,128)S(1)} %get-tuple-element.64), channel_id=1, source_target_pairs={{0,4},{1,5},{2,6},{3,7},{4,0},{5,1},{6,2},{7,3},{8,12},{9,13},{10,... | collective-permute-start | bytes 49160 | tf_op jit(solution)/shard_map/ppermute | solution.py:353
  17.5 0.0 collective-permute-start.8
  17.6 1.1 %collective-permute-start.10 = (f32[32,128]{1,0:T(8,128)S(1)}, f32[32,128]{1,0:T(8,128)S(1)}, u32[]{:S(2)}, u32[]{:S(2)}) collective-permute-start(f32[32,128]{1,0:T(8,128)S(1)} %get-tuple-element.67), channel_id=1, source_target_pairs={{0,32},{1,2},{2,1},{3,35},{4,36},{5,6},{6,5},{7,39},{8,40},{9,10},... | collective-permute-start | bytes 49160 | tf_op jit(solution)/shard_map/ppermute | solution.py:353
  18.7 1.1 %collective-permute-start.11 = (f32[32,128]{1,0:T(8,128)S(1)}, f32[32,128]{1,0:T(8,128)S(1)}, u32[]{:S(2)}, u32[]{:S(2)}) collective-permute-start(f32[32,128]{1,0:T(8,128)S(1)} %get-tuple-element.68), channel_id=1, source_target_pairs={{0,32},{1,33},{2,34},{3,35},{4,36},{5,37},{6,38},{7,39},{8,40},{9,... | collective-permute-start | bytes 49160 | tf_op jit(solution)/shard_map/ppermute | solution.py:353
  19.8 1.5 %collective-permute-done.8.refs_2_ = f32[32,128]{1,0:T(8,128)S(1)} collective-permute-done((f32[32,128]{1,0:T(8,128)S(1)}, f32[32,128]{1,0:T(8,128)S(1)}, u32[]{:S(2)}, u32[]{:S(2)}) %collective-permute-start.8) | collective-permute-done | bytes 16416 | tf_op jit(solution)/shard_map/ppermute | solution.py:353
  21.3 0.0 collective-permute-done.9.refs_3_
  21.3 0.0 copy-start.3
  21.3 0.7 shard_map.100
  22.0 24.0 %all_to_all.10 = f32[256,2,128]{2,1,0:T(2,128)S(1)} all-to-all(f32[256,2,128]{2,1,0:T(2,128)S(1)} %bitcast.7), channel_id=1, replica_groups=mesh['region'=8,'gy'=8,'gz'=4] {'gy','gz','region'}, dimensions={0} | all-to-all | bytes 524288 | tf_op jit(solution)/shard_map/all_to_all | solution.py:358
  46.0 0.3 shard_map.101.mine
  46.3 0.1 collective-permute-start.12
  46.4 0.5 shard_map.99.inverse
  46.9 0.7 collective-permute-done.12.other
  47.6 0.6 shard_map.102
  48.2 0.2 collective-permute-start.13
  48.4 1.8 %collective-permute-start.14 = (f32[32,128]{1,0:T(8,128)S(1)}, f32[32,128]{1,0:T(8,128)S(1)}, u32[]{:S(2)}, u32[]{:S(2)}) collective-permute-start(f32[32,128]{1,0:T(8,128)S(1)} %get-tuple-element.74), channel_id=1, source_target_pairs={{0,4},{1,5},{2,6},{3,7},{4,0},{5,1},{6,2},{7,3},{8,12},{9,13},{10,... | collective-permute-start | bytes 49160 | tf_op jit(solution)/shard_map/ppermute | solution.py:353
  50.2 0.3 collective-permute-start.15
  50.5 1.5 %collective-permute-start.16 = (f32[32,128]{1,0:T(8,128)S(1)}, f32[32,128]{1,0:T(8,128)S(1)}, u32[]{:S(2)}, u32[]{:S(2)}) collective-permute-start(f32[32,128]{1,0:T(8,128)S(1)} %get-tuple-element.76), channel_id=1, source_target_pairs={{0,1},{1,0},{2,3},{3,2},{4,5},{5,4},{6,7},{7,6},{8,9},{9,8},{10,11... | collective-permute-start | bytes 49160 | tf_op jit(solution)/shard_map/ppermute | solution.py:353
  51.9 0.8 collective-permute-start.17
  52.8 1.1 %collective-permute-done.15.refs_2_ = f32[32,128]{1,0:T(8,128)S(1)} collective-permute-done((f32[32,128]{1,0:T(8,128)S(1)}, f32[32,128]{1,0:T(8,128)S(1)}, u32[]{:S(2)}, u32[]{:S(2)}) %collective-permute-start.15) | collective-permute-done | bytes 16416 | tf_op jit(solution)/shard_map/ppermute | solution.py:353
  53.9 0.3 collective-permute-done.16.refs_3_
  54.2 1.5 %collective-permute-done.17.refs_4_ = f32[32,128]{1,0:T(8,128)S(1)} collective-permute-done((f32[32,128]{1,0:T(8,128)S(1)}, f32[32,128]{1,0:T(8,128)S(1)}, u32[]{:S(2)}, u32[]{:S(2)}) %collective-permute-start.17) | collective-permute-done | bytes 16416 | tf_op jit(solution)/shard_map/ppermute | solution.py:353
  55.7 0.5 shard_map.103
  56.1 0.0 collective-permute-start.19
  56.2 2.9 %collective-permute-start.20 = (f32[32,128]{1,0:T(8,128)S(1)}, f32[32,128]{1,0:T(8,128)S(1)}, u32[]{:S(2)}, u32[]{:S(2)}) collective-permute-start(f32[32,128]{1,0:T(8,128)S(1)} %get-tuple-element.83), channel_id=1, source_target_pairs={{0,4},{1,5},{2,6},{3,7},{4,0},{5,1},{6,2},{7,3},{8,12},{9,13},{10,... | collective-permute-start | bytes 49160 | tf_op jit(solution)/shard_map/ppermute | solution.py:353
  59.1 0.0 collective-permute-start.21
  59.1 0.8 collective-permute-start.23
  59.9 0.9 collective-permute-done.20.refs_1_
  60.8 2.0 %collective-permute-done.21.refs_2_ = f32[32,128]{1,0:T(8,128)S(1)} collective-permute-done((f32[32,128]{1,0:T(8,128)S(1)}, f32[32,128]{1,0:T(8,128)S(1)}, u32[]{:S(2)}, u32[]{:S(2)}) %collective-permute-start.21) | collective-permute-done | bytes 16416 | tf_op jit(solution)/shard_map/ppermute | solution.py:353
  62.8 0.0 collective-permute-done.22.refs_3_
  62.8 0.7 shard_map.104
  63.6 22.1 %all_to_all.11 = f32[256,2,128]{2,1,0:T(2,128)S(1)} all-to-all(f32[256,2,128]{2,1,0:T(2,128)S(1)} %bitcast.8), channel_id=1, replica_groups=mesh['region'=8,'gy'=8,'gz'=4] {'gy','gz','region'}, dimensions={0} | all-to-all | bytes 524288 | tf_op jit(solution)/shard_map/all_to_all | solution.py:358
  85.7 0.3 shard_map.105.mine
  85.9 0.1 collective-permute-start.25
  86.0 1.2 %collective-permute-done.25.other = f32[32,384]{1,0:T(8,128)S(1)} collective-permute-done((f32[32,384]{1,0:T(8,128)S(1)}, f32[32,384]{1,0:T(8,128)S(1)}, u32[]{:S(2)}, u32[]{:S(2)}) %collective-permute-start.25) | collective-permute-done | bytes 49184 | tf_op jit(solution)/shard_map/ppermute | solution.py:363
  87.2 0.9 shard_map.106
  88.1 0.2 collective-permute-start.26
  88.3 1.8 %collective-permute-start.27 = (f32[32,128]{1,0:T(8,128)S(1)}, f32[32,128]{1,0:T(8,128)S(1)}, u32[]{:S(2)}, u32[]{:S(2)}) collective-permute-start(f32[32,128]{1,0:T(8,128)S(1)} %get-tuple-element.97), channel_id=1, source_target_pairs={{0,4},{1,5},{2,6},{3,7},{4,0},{5,1},{6,2},{7,3},{8,12},{9,13},{10,... | collective-permute-start | bytes 49160 | tf_op jit(solution)/shard_map/ppermute | solution.py:353
  90.1 0.3 collective-permute-start.28
  90.4 1.5 %collective-permute-start.29 = (f32[32,128]{1,0:T(8,128)S(1)}, f32[32,128]{1,0:T(8,128)S(1)}, u32[]{:S(2)}, u32[]{:S(2)}) collective-permute-start(f32[32,128]{1,0:T(8,128)S(1)} %get-tuple-element.99), channel_id=1, source_target_pairs={{0,1},{1,0},{2,3},{3,2},{4,5},{5,4},{6,7},{7,6},{8,9},{9,8},{10,11... | collective-permute-start | bytes 49160 | tf_op jit(solution)/shard_map/ppermute | solution.py:353
  91.8 0.8 collective-permute-start.30
  92.7 1.2 %collective-permute-done.28.refs_2_ = f32[32,128]{1,0:T(8,128)S(1)} collective-permute-done((f32[32,128]{1,0:T(8,128)S(1)}, f32[32,128]{1,0:T(8,128)S(1)}, u32[]{:S(2)}, u32[]{:S(2)}) %collective-permute-start.28) | collective-permute-done | bytes 16416 | tf_op jit(solution)/shard_map/ppermute | solution.py:353
  93.8 0.3 collective-permute-done.29.refs_3_
  94.1 1.5 %collective-permute-done.30.refs_4_ = f32[32,128]{1,0:T(8,128)S(1)} collective-permute-done((f32[32,128]{1,0:T(8,128)S(1)}, f32[32,128]{1,0:T(8,128)S(1)}, u32[]{:S(2)}, u32[]{:S(2)}) %collective-permute-start.30) | collective-permute-done | bytes 16416 | tf_op jit(solution)/shard_map/ppermute | solution.py:353
  95.6 0.8 shard_map.107
  (29 shorter events, 0.1 us)
Async XLA Ops:
  1.3 0.9 copy-start.4
  2.2 6.6 %collective-permute-start = (f32[40,128]{1,0:T(8,128)S(1)}, f32[40,128]{1,0:T(8,128)S(1)}, u32[]{:S(2)}, u32[]{:S(2)}) collective-permute-start(f32[40,128]{1,0:T(8,128)S(1)} %get-tuple-element.53), channel_id=1, source_target_pairs={{0,32},{1,33},{2,34},{3,35},{4,8},{5,9},{6,10},{7,11},{8,4},{9,5},... | collective-permute-start | bytes 61448 | tf_op jit(solution)/shard_map/ppermute | solution.py:353
  2.3 9.0 %collective-permute-start.1 = (f32[40,128]{1,0:T(8,128)S(1)}, f32[40,128]{1,0:T(8,128)S(1)}, u32[]{:S(2)}, u32[]{:S(2)}) collective-permute-start(f32[40,128]{1,0:T(8,128)S(1)} %get-tuple-element.54), channel_id=1, source_target_pairs={{0,4},{1,5},{2,6},{3,7},{4,0},{5,1},{6,2},{7,3},{8,12},{9,13},{10,... | collective-permute-start | bytes 61448 | tf_op jit(solution)/shard_map/ppermute | solution.py:353
  6.2 5.2 %collective-permute-start.2 = (f32[40,128]{1,0:T(8,128)S(1)}, f32[40,128]{1,0:T(8,128)S(1)}, u32[]{:S(2)}, u32[]{:S(2)}) collective-permute-start(f32[40,128]{1,0:T(8,128)S(1)} %get-tuple-element.55), channel_id=1, source_target_pairs={{0,4},{1,5},{2,6},{3,7},{4,0},{5,1},{6,2},{7,3},{8,12},{9,13},{10,... | collective-permute-start | bytes 61448 | tf_op jit(solution)/shard_map/ppermute | solution.py:353
  6.2 5.2 %collective-permute-start.3 = (f32[40,128]{1,0:T(8,128)S(1)}, f32[40,128]{1,0:T(8,128)S(1)}, u32[]{:S(2)}, u32[]{:S(2)}) collective-permute-start(f32[40,128]{1,0:T(8,128)S(1)} %get-tuple-element.56), channel_id=1, source_target_pairs={{0,1},{1,0},{2,3},{3,2},{4,5},{5,4},{6,7},{7,6},{8,9},{9,8},{10,11... | collective-permute-start | bytes 61448 | tf_op jit(solution)/shard_map/ppermute | solution.py:353
  6.7 4.7 %collective-permute-start.4 = (f32[40,128]{1,0:T(8,128)S(1)}, f32[40,128]{1,0:T(8,128)S(1)}, u32[]{:S(2)}, u32[]{:S(2)}) collective-permute-start(f32[40,128]{1,0:T(8,128)S(1)} %get-tuple-element.57), channel_id=1, source_target_pairs={{0,32},{1,2},{2,1},{3,35},{4,36},{5,6},{6,5},{7,39},{8,40},{9,10},... | collective-permute-start | bytes 61448 | tf_op jit(solution)/shard_map/ppermute | solution.py:353
  8.9 2.5 %collective-permute-start.5 = (f32[40,128]{1,0:T(8,128)S(1)}, f32[40,128]{1,0:T(8,128)S(1)}, u32[]{:S(2)}, u32[]{:S(2)}) collective-permute-start(f32[40,128]{1,0:T(8,128)S(1)} %get-tuple-element.58), channel_id=1, source_target_pairs={{0,32},{1,33},{2,34},{3,35},{4,36},{5,37},{6,38},{7,39},{8,40},{9,... | collective-permute-start | bytes 61448 | tf_op jit(solution)/shard_map/ppermute | solution.py:353
  10.0 1.3 %copy-start.2 = (bf16[1,768,768]{2,1,0:T(8,128)(2,1)S(1)}, bf16[1,768,768]{2,1,0:T(8,128)(2,1)}, u32[]{:S(2)}) copy-start(bf16[1,768,768]{2,1,0:T(8,128)(2,1)} %source.2) | copy-start | bytes 3538948
  11.3 0.7 copy-start.5
  11.3 10.0 %copy-start = (bf16[1,768,768]{2,1,0:T(8,128)(2,1)S(1)}, bf16[1,768,768]{2,1,0:T(8,128)(2,1)}, u32[]{:S(2)}) copy-start(bf16[1,768,768]{2,1,0:T(8,128)(2,1)} %schur.5) | copy-start | bytes 3538948
  11.4 10.0 %copy-start.1 = (bf16[1,768,128]{2,1,0:T(8,128)(2,1)S(1)}, bf16[1,768,128]{2,1,0:T(8,128)(2,1)}, u32[]{:S(2)}) copy-start(bf16[1,768,128]{2,1,0:T(8,128)(2,1)} %coupling.7) | copy-start | bytes 589828
  11.4 10.0 %copy-start.6 = (s32[1,128]{1,0:T(1,128)S(1)}, s32[1,128]{1,0:T(1,128)}, u32[]{:S(2)}) copy-start(s32[1,128]{1,0:T(1,128)} %corner_map.7) | copy-start | bytes 1540
  12.4 6.3 %collective-permute-start.6 = (f32[32,128]{1,0:T(8,128)S(1)}, f32[32,128]{1,0:T(8,128)S(1)}, u32[]{:S(2)}, u32[]{:S(2)}) collective-permute-start(f32[32,128]{1,0:T(8,128)S(1)} %get-tuple-element.63), channel_id=1, source_target_pairs={{0,32},{1,33},{2,34},{3,35},{4,8},{5,9},{6,10},{7,11},{8,4},{9,5},... | collective-permute-start | bytes 49160 | tf_op jit(solution)/shard_map/ppermute | solution.py:353
  12.5 7.3 %collective-permute-start.7 = (f32[32,128]{1,0:T(8,128)S(1)}, f32[32,128]{1,0:T(8,128)S(1)}, u32[]{:S(2)}, u32[]{:S(2)}) collective-permute-start(f32[32,128]{1,0:T(8,128)S(1)} %get-tuple-element.64), channel_id=1, source_target_pairs={{0,4},{1,5},{2,6},{3,7},{4,0},{5,1},{6,2},{7,3},{8,12},{9,13},{10,... | collective-permute-start | bytes 49160 | tf_op jit(solution)/shard_map/ppermute | solution.py:353
  17.5 3.7 %collective-permute-start.8 = (f32[32,128]{1,0:T(8,128)S(1)}, f32[32,128]{1,0:T(8,128)S(1)}, u32[]{:S(2)}, u32[]{:S(2)}) collective-permute-start(f32[32,128]{1,0:T(8,128)S(1)} %get-tuple-element.65), channel_id=1, source_target_pairs={{0,4},{1,5},{2,6},{3,7},{4,0},{5,1},{6,2},{7,3},{8,12},{9,13},{10,... | collective-permute-start | bytes 49160 | tf_op jit(solution)/shard_map/ppermute | solution.py:353
  17.6 3.7 %collective-permute-start.9 = (f32[32,128]{1,0:T(8,128)S(1)}, f32[32,128]{1,0:T(8,128)S(1)}, u32[]{:S(2)}, u32[]{:S(2)}) collective-permute-start(f32[32,128]{1,0:T(8,128)S(1)} %get-tuple-element.66), channel_id=1, source_target_pairs={{0,1},{1,0},{2,3},{3,2},{4,5},{5,4},{6,7},{7,6},{8,9},{9,8},{10,11... | collective-permute-start | bytes 49160 | tf_op jit(solution)/shard_map/ppermute | solution.py:353
  17.6 3.7 %collective-permute-start.10 = (f32[32,128]{1,0:T(8,128)S(1)}, f32[32,128]{1,0:T(8,128)S(1)}, u32[]{:S(2)}, u32[]{:S(2)}) collective-permute-start(f32[32,128]{1,0:T(8,128)S(1)} %get-tuple-element.67), channel_id=1, source_target_pairs={{0,32},{1,2},{2,1},{3,35},{4,36},{5,6},{6,5},{7,39},{8,40},{9,10},... | collective-permute-start | bytes 49160 | tf_op jit(solution)/shard_map/ppermute | solution.py:353
  18.7 2.6 %collective-permute-start.11 = (f32[32,128]{1,0:T(8,128)S(1)}, f32[32,128]{1,0:T(8,128)S(1)}, u32[]{:S(2)}, u32[]{:S(2)}) collective-permute-start(f32[32,128]{1,0:T(8,128)S(1)} %get-tuple-element.68), channel_id=1, source_target_pairs={{0,32},{1,33},{2,34},{3,35},{4,36},{5,37},{6,38},{7,39},{8,40},{9,... | collective-permute-start | bytes 49160 | tf_op jit(solution)/shard_map/ppermute | solution.py:353
  21.3 25.1 %copy-start.3 = (f32[512,512]{1,0:T(8,128)S(1)}, f32[512,512]{1,0:T(8,128)}, u32[]{:S(2)}) copy-start(f32[512,512]{1,0:T(8,128)} %source.3) | copy-start | bytes 3145732
  46.3 1.3 %collective-permute-start.12 = (f32[32,384]{1,0:T(8,128)S(1)}, f32[32,384]{1,0:T(8,128)S(1)}, u32[]{:S(2)}, u32[]{:S(2)}) collective-permute-start(f32[32,384]{1,0:T(8,128)S(1)} %shard_map.101.mine), channel_id=1, source_target_pairs={{0,32},{1,33},{2,34},{3,35},{4,36},{5,37},{6,38},{7,39},{8,40},{9,... | collective-permute-start | bytes 147464 | tf_op jit(solution)/shard_map/ppermute | solution.py:363
  48.2 4.6 %collective-permute-start.13 = (f32[32,128]{1,0:T(8,128)S(1)}, f32[32,128]{1,0:T(8,128)S(1)}, u32[]{:S(2)}, u32[]{:S(2)}) collective-permute-start(f32[32,128]{1,0:T(8,128)S(1)} %get-tuple-element.73), channel_id=1, source_target_pairs={{0,32},{1,33},{2,34},{3,35},{4,8},{5,9},{6,10},{7,11},{8,4},{9,5},... | collective-permute-start | bytes 49160 | tf_op jit(solution)/shard_map/ppermute | solution.py:353
  48.4 4.3 %collective-permute-start.14 = (f32[32,128]{1,0:T(8,128)S(1)}, f32[32,128]{1,0:T(8,128)S(1)}, u32[]{:S(2)}, u32[]{:S(2)}) collective-permute-start(f32[32,128]{1,0:T(8,128)S(1)} %get-tuple-element.74), channel_id=1, source_target_pairs={{0,4},{1,5},{2,6},{3,7},{4,0},{5,1},{6,2},{7,3},{8,12},{9,13},{10,... | collective-permute-start | bytes 49160 | tf_op jit(solution)/shard_map/ppermute | solution.py:353
  50.2 3.7 %collective-permute-start.15 = (f32[32,128]{1,0:T(8,128)S(1)}, f32[32,128]{1,0:T(8,128)S(1)}, u32[]{:S(2)}, u32[]{:S(2)}) collective-permute-start(f32[32,128]{1,0:T(8,128)S(1)} %get-tuple-element.75), channel_id=1, source_target_pairs={{0,4},{1,5},{2,6},{3,7},{4,0},{5,1},{6,2},{7,3},{8,12},{9,13},{10,... | collective-permute-start | bytes 49160 | tf_op jit(solution)/shard_map/ppermute | solution.py:353
  50.5 3.7 %collective-permute-start.16 = (f32[32,128]{1,0:T(8,128)S(1)}, f32[32,128]{1,0:T(8,128)S(1)}, u32[]{:S(2)}, u32[]{:S(2)}) collective-permute-start(f32[32,128]{1,0:T(8,128)S(1)} %get-tuple-element.76), channel_id=1, source_target_pairs={{0,1},{1,0},{2,3},{3,2},{4,5},{5,4},{6,7},{7,6},{8,9},{9,8},{10,11... | collective-permute-start | bytes 49160 | tf_op jit(solution)/shard_map/ppermute | solution.py:353
  51.9 3.7 %collective-permute-start.17 = (f32[32,128]{1,0:T(8,128)S(1)}, f32[32,128]{1,0:T(8,128)S(1)}, u32[]{:S(2)}, u32[]{:S(2)}) collective-permute-start(f32[32,128]{1,0:T(8,128)S(1)} %get-tuple-element.77), channel_id=1, source_target_pairs={{0,32},{1,2},{2,1},{3,35},{4,36},{5,6},{6,5},{7,39},{8,40},{9,10},... | collective-permute-start | bytes 49160 | tf_op jit(solution)/shard_map/ppermute | solution.py:353
  52.8 2.9 %collective-permute-start.18 = (f32[32,128]{1,0:T(8,128)S(1)}, f32[32,128]{1,0:T(8,128)S(1)}, u32[]{:S(2)}, u32[]{:S(2)}) collective-permute-start(f32[32,128]{1,0:T(8,128)S(1)} %get-tuple-element.78), channel_id=1, source_target_pairs={{0,32},{1,33},{2,34},{3,35},{4,36},{5,37},{6,38},{7,39},{8,40},{9,... | collective-permute-start | bytes 49160 | tf_op jit(solution)/shard_map/ppermute | solution.py:353
  56.1 3.7 %collective-permute-start.19 = (f32[32,128]{1,0:T(8,128)S(1)}, f32[32,128]{1,0:T(8,128)S(1)}, u32[]{:S(2)}, u32[]{:S(2)}) collective-permute-start(f32[32,128]{1,0:T(8,128)S(1)} %get-tuple-element.82), channel_id=1, source_target_pairs={{0,32},{1,33},{2,34},{3,35},{4,8},{5,9},{6,10},{7,11},{8,4},{9,5},... | collective-permute-start | bytes 49160 | tf_op jit(solution)/shard_map/ppermute | solution.py:353
  56.2 4.6 %collective-permute-start.20 = (f32[32,128]{1,0:T(8,128)S(1)}, f32[32,128]{1,0:T(8,128)S(1)}, u32[]{:S(2)}, u32[]{:S(2)}) collective-permute-start(f32[32,128]{1,0:T(8,128)S(1)} %get-tuple-element.83), channel_id=1, source_target_pairs={{0,4},{1,5},{2,6},{3,7},{4,0},{5,1},{6,2},{7,3},{8,12},{9,13},{10,... | collective-permute-start | bytes 49160 | tf_op jit(solution)/shard_map/ppermute | solution.py:353
  59.1 3.7 %collective-permute-start.21 = (f32[32,128]{1,0:T(8,128)S(1)}, f32[32,128]{1,0:T(8,128)S(1)}, u32[]{:S(2)}, u32[]{:S(2)}) collective-permute-start(f32[32,128]{1,0:T(8,128)S(1)} %get-tuple-element.84), channel_id=1, source_target_pairs={{0,4},{1,5},{2,6},{3,7},{4,0},{5,1},{6,2},{7,3},{8,12},{9,13},{10,... | collective-permute-start | bytes 49160 | tf_op jit(solution)/shard_map/ppermute | solution.py:353
  59.1 3.7 %collective-permute-start.22 = (f32[32,128]{1,0:T(8,128)S(1)}, f32[32,128]{1,0:T(8,128)S(1)}, u32[]{:S(2)}, u32[]{:S(2)}) collective-permute-start(f32[32,128]{1,0:T(8,128)S(1)} %get-tuple-element.85), channel_id=1, source_target_pairs={{0,1},{1,0},{2,3},{3,2},{4,5},{5,4},{6,7},{7,6},{8,9},{9,8},{10,11... | collective-permute-start | bytes 49160 | tf_op jit(solution)/shard_map/ppermute | solution.py:353
  59.1 3.7 %collective-permute-start.23 = (f32[32,128]{1,0:T(8,128)S(1)}, f32[32,128]{1,0:T(8,128)S(1)}, u32[]{:S(2)}, u32[]{:S(2)}) collective-permute-start(f32[32,128]{1,0:T(8,128)S(1)} %get-tuple-element.86), channel_id=1, source_target_pairs={{0,32},{1,2},{2,1},{3,35},{4,36},{5,6},{6,5},{7,39},{8,40},{9,10},... | collective-permute-start | bytes 49160 | tf_op jit(solution)/shard_map/ppermute | solution.py:353
  59.9 3.0 %collective-permute-start.24 = (f32[32,128]{1,0:T(8,128)S(1)}, f32[32,128]{1,0:T(8,128)S(1)}, u32[]{:S(2)}, u32[]{:S(2)}) collective-permute-start(f32[32,128]{1,0:T(8,128)S(1)} %get-tuple-element.87), channel_id=1, source_target_pairs={{0,32},{1,33},{2,34},{3,35},{4,36},{5,37},{6,38},{7,39},{8,40},{9,... | collective-permute-start | bytes 49160 | tf_op jit(solution)/shard_map/ppermute | solution.py:353
  85.9 1.3 %collective-permute-start.25 = (f32[32,384]{1,0:T(8,128)S(1)}, f32[32,384]{1,0:T(8,128)S(1)}, u32[]{:S(2)}, u32[]{:S(2)}) collective-permute-start(f32[32,384]{1,0:T(8,128)S(1)} %shard_map.105.mine), channel_id=1, source_target_pairs={{0,32},{1,33},{2,34},{3,35},{4,36},{5,37},{6,38},{7,39},{8,40},{9,... | collective-permute-start | bytes 147464 | tf_op jit(solution)/shard_map/ppermute | solution.py:363
  88.1 4.5 %collective-permute-start.26 = (f32[32,128]{1,0:T(8,128)S(1)}, f32[32,128]{1,0:T(8,128)S(1)}, u32[]{:S(2)}, u32[]{:S(2)}) collective-permute-start(f32[32,128]{1,0:T(8,128)S(1)} %get-tuple-element.96), channel_id=1, source_target_pairs={{0,32},{1,33},{2,34},{3,35},{4,8},{5,9},{6,10},{7,11},{8,4},{9,5},... | collective-permute-start | bytes 49160 | tf_op jit(solution)/shard_map/ppermute | solution.py:353
  88.3 4.3 %collective-permute-start.27 = (f32[32,128]{1,0:T(8,128)S(1)}, f32[32,128]{1,0:T(8,128)S(1)}, u32[]{:S(2)}, u32[]{:S(2)}) collective-permute-start(f32[32,128]{1,0:T(8,128)S(1)} %get-tuple-element.97), channel_id=1, source_target_pairs={{0,4},{1,5},{2,6},{3,7},{4,0},{5,1},{6,2},{7,3},{8,12},{9,13},{10,... | collective-permute-start | bytes 49160 | tf_op jit(solution)/shard_map/ppermute | solution.py:353
  90.1 3.7 %collective-permute-start.28 = (f32[32,128]{1,0:T(8,128)S(1)}, f32[32,128]{1,0:T(8,128)S(1)}, u32[]{:S(2)}, u32[]{:S(2)}) collective-permute-start(f32[32,128]{1,0:T(8,128)S(1)} %get-tuple-element.98), channel_id=1, source_target_pairs={{0,4},{1,5},{2,6},{3,7},{4,0},{5,1},{6,2},{7,3},{8,12},{9,13},{10,... | collective-permute-start | bytes 49160 | tf_op jit(solution)/shard_map/ppermute | solution.py:353
  90.4 3.7 %collective-permute-start.29 = (f32[32,128]{1,0:T(8,128)S(1)}, f32[32,128]{1,0:T(8,128)S(1)}, u32[]{:S(2)}, u32[]{:S(2)}) collective-permute-start(f32[32,128]{1,0:T(8,128)S(1)} %get-tuple-element.99), channel_id=1, source_target_pairs={{0,1},{1,0},{2,3},{3,2},{4,5},{5,4},{6,7},{7,6},{8,9},{9,8},{10,11... | collective-permute-start | bytes 49160 | tf_op jit(solution)/shard_map/ppermute | solution.py:353
  91.8 3.7 %collective-permute-start.30 = (f32[32,128]{1,0:T(8,128)S(1)}, f32[32,128]{1,0:T(8,128)S(1)}, u32[]{:S(2)}, u32[]{:S(2)}) collective-permute-start(f32[32,128]{1,0:T(8,128)S(1)} %get-tuple-element.100), channel_id=1, source_target_pairs={{0,32},{1,2},{2,1},{3,35},{4,36},{5,6},{6,5},{7,39},{8,40},{9,10},... | collective-permute-start | bytes 49160 | tf_op jit(solution)/shard_map/ppermute | solution.py:353
  92.7 2.9 %collective-permute-start.31 = (f32[32,128]{1,0:T(8,128)S(1)}, f32[32,128]{1,0:T(8,128)S(1)}, u32[]{:S(2)}, u32[]{:S(2)}) collective-permute-start(f32[32,128]{1,0:T(8,128)S(1)} %get-tuple-element.101), channel_id=1, source_target_pairs={{0,32},{1,33},{2,34},{3,35},{4,36},{5,37},{6,38},{7,39},{8,40},{9,... | collective-permute-start | bytes 49160 | tf_op jit(solution)/shard_map/ppermute | solution.py:353

commit v10 on v9

--- a/solution.py
+++ b/solution.py
@@ -84,7 +84,7 @@
 def load_sums(left, right):
     parts = split_faces(left * right)
     total = (parts[0] + parts[1]) + (parts[2] + parts[3]) + (parts[4] + parts[5])
-    return matmul_nt_exact(jnp.ones((8, FACE), F32), total)
+    return jnp.broadcast_to(jnp.sum(total.T, axis=0, keepdims=True), (8, LOADS))
 
 
 def living_kernel(counts, live_ref):

time: 96.6 us -> 96.7 us (level)
  no operation moved by 1% of the time
where the time goes in v10:
time: 96.7 us; the launch traced here: 96.5 us
  blocking collectives  46.1 us (48%)
  starting transfers between devices  28.1 us (29%)
  waiting for transfers between devices  12.2 us (13%)
  Pallas kernels  5.84 us (6%)
  local copies, waits for them, and re-layouts  2.7 us (3%)
  between operations  1.52 us (2%)
    all_to_all x2, blocking collectives, total_sums(): message = lax.all_to_all(message.reshape(DEVICES, 2, FACE), BY_COLUMN, 0, 0)  46.1 us
    ppermute x30, starting transfers between devices, exchange(): lax.ppermute(value, AXES, pairs(k // 2, k % 2))  28 us
    ppermute x30, waiting for transfers between devices, exchange(): lax.ppermute(value, AXES, pairs(k // 2, k % 2))  10.3 us
    pallas_call x13, Pallas kernels, call(): pl.pallas_call(kernel, out_shape=[shape if hasattr(shape, 'dtype') else j...  5.84 us
    unnamed x14, local copies, waits for them, and re-layouts  2.7 us
  transfers between devices with their start and end apart: 32, of which 11 were waited for; matrix products, arithmetic and copies ran while one was open for 0% of the time, Pallas kernels for 1%

profile of v10, /device:TPU:2, one launch (start us, length us, event | category | flops | bytes accessed | tf_op | source)
XLA Modules:
  0.0 96.5 jit_solution(12464464738028121631)
XLA Ops:
  1.3 0.0 copy-start.4
  1.3 0.9 copy-done.4
  2.2 0.1 collective-permute-start
  2.3 3.8 %collective-permute-start.1 = (f32[40,128]{1,0:T(8,128)S(1)}, f32[40,128]{1,0:T(8,128)S(1)}, u32[]{:S(2)}, u32[]{:S(2)}) collective-permute-start(f32[40,128]{1,0:T(8,128)S(1)} %get-tuple-element.54), channel_id=1, source_target_pairs={{0,4},{1,5},{2,6},{3,7},{4,0},{5,1},{6,2},{7,3},{8,12},{9,13},{10,... | collective-permute-start | bytes 61448 | tf_op jit(solution)/shard_map/ppermute | solution.py:353
  6.2 0.0 collective-permute-start.2
  6.2 0.5 collective-permute-start.3
  6.7 2.1 %collective-permute-start.4 = (f32[40,128]{1,0:T(8,128)S(1)}, f32[40,128]{1,0:T(8,128)S(1)}, u32[]{:S(2)}, u32[]{:S(2)}) collective-permute-start(f32[40,128]{1,0:T(8,128)S(1)} %get-tuple-element.57), channel_id=1, source_target_pairs={{0,32},{1,2},{2,1},{3,35},{4,36},{5,6},{6,5},{7,39},{8,40},{9,10},... | collective-permute-start | bytes 61448 | tf_op jit(solution)/shard_map/ppermute | solution.py:353
  8.9 0.0 collective-permute-done.refs_0_
  8.9 1.1 %collective-permute-start.5 = (f32[40,128]{1,0:T(8,128)S(1)}, f32[40,128]{1,0:T(8,128)S(1)}, u32[]{:S(2)}, u32[]{:S(2)}) collective-permute-start(f32[40,128]{1,0:T(8,128)S(1)} %get-tuple-element.58), channel_id=1, source_target_pairs={{0,32},{1,33},{2,34},{3,35},{4,36},{5,37},{6,38},{7,39},{8,40},{9,... | collective-permute-start | bytes 61448 | tf_op jit(solution)/shard_map/ppermute | solution.py:353
  10.0 1.3 %copy-done.2 = bf16[1,768,768]{2,1,0:T(8,128)(2,1)S(1)} copy-done((bf16[1,768,768]{2,1,0:T(8,128)(2,1)S(1)}, bf16[1,768,768]{2,1,0:T(8,128)(2,1)}, u32[]{:S(2)}) %copy-start.2) | copy-done | bytes 1179672
  11.3 0.1 shard_map.96.dirichlet
  11.3 0.0 copy-start
  11.4 0.0 copy-start.1
  11.4 0.0 copy-start.6
  11.4 0.5 copy-done.5
  11.9 0.5 shard_map.98
  12.4 0.1 collective-permute-start.6
  12.5 5.0 %collective-permute-start.7 = (f32[32,128]{1,0:T(8,128)S(1)}, f32[32,128]{1,0:T(8,128)S(1)}, u32[]{:S(2)}, u32[]{:S(2)}) collective-permute-start(f32[32,128]{1,0:T(8,128)S(1)} %get-tuple-element.64), channel_id=1, source_target_pairs={{0,4},{1,5},{2,6},{3,7},{4,0},{5,1},{6,2},{7,3},{8,12},{9,13},{10,... | collective-permute-start | bytes 49160 | tf_op jit(solution)/shard_map/ppermute | solution.py:353
  17.6 0.0 collective-permute-start.8
  17.6 1.1 %collective-permute-start.10 = (f32[32,128]{1,0:T(8,128)S(1)}, f32[32,128]{1,0:T(8,128)S(1)}, u32[]{:S(2)}, u32[]{:S(2)}) collective-permute-start(f32[32,128]{1,0:T(8,128)S(1)} %get-tuple-element.67), channel_id=1, source_target_pairs={{0,32},{1,2},{2,1},{3,35},{4,36},{5,6},{6,5},{7,39},{8,40},{9,10},... | collective-permute-start | bytes 49160 | tf_op jit(solution)/shard_map/ppermute | solution.py:353
  18.7 1.1 %collective-permute-start.11 = (f32[32,128]{1,0:T(8,128)S(1)}, f32[32,128]{1,0:T(8,128)S(1)}, u32[]{:S(2)}, u32[]{:S(2)}) collective-permute-start(f32[32,128]{1,0:T(8,128)S(1)} %get-tuple-element.68), channel_id=1, source_target_pairs={{0,32},{1,33},{2,34},{3,35},{4,36},{5,37},{6,38},{7,39},{8,40},{9,... | collective-permute-start | bytes 49160 | tf_op jit(solution)/shard_map/ppermute | solution.py:353
  19.8 1.5 %collective-permute-done.8.refs_2_ = f32[32,128]{1,0:T(8,128)S(1)} collective-permute-done((f32[32,128]{1,0:T(8,128)S(1)}, f32[32,128]{1,0:T(8,128)S(1)}, u32[]{:S(2)}, u32[]{:S(2)}) %collective-permute-start.8) | collective-permute-done | bytes 16416 | tf_op jit(solution)/shard_map/ppermute | solution.py:353
  21.3 0.0 collective-permute-done.9.refs_3_
  21.4 0.0 copy-start.3
  21.4 0.7 shard_map.100
  22.1 24.0 %all_to_all.10 = f32[256,2,128]{2,1,0:T(2,128)S(1)} all-to-all(f32[256,2,128]{2,1,0:T(2,128)S(1)} %bitcast.7), channel_id=1, replica_groups=mesh['region'=8,'gy'=8,'gz'=4] {'gy','gz','region'}, dimensions={0} | all-to-all | bytes 524288 | tf_op jit(solution)/shard_map/all_to_all | solution.py:358
  46.1 0.3 shard_map.101.mine
  46.4 0.1 collective-permute-start.12
  46.5 0.5 shard_map.99.inverse
  46.9 0.7 collective-permute-done.12.other
  47.7 0.6 shard_map.102
  48.2 0.2 collective-permute-start.13
  48.5 1.8 %collective-permute-start.14 = (f32[32,128]{1,0:T(8,128)S(1)}, f32[32,128]{1,0:T(8,128)S(1)}, u32[]{:S(2)}, u32[]{:S(2)}) collective-permute-start(f32[32,128]{1,0:T(8,128)S(1)} %get-tuple-element.74), channel_id=1, source_target_pairs={{0,4},{1,5},{2,6},{3,7},{4,0},{5,1},{6,2},{7,3},{8,12},{9,13},{10,... | collective-permute-start | bytes 49160 | tf_op jit(solution)/shard_map/ppermute | solution.py:353
  50.2 0.3 collective-permute-start.15
  50.5 1.5 %collective-permute-start.16 = (f32[32,128]{1,0:T(8,128)S(1)}, f32[32,128]{1,0:T(8,128)S(1)}, u32[]{:S(2)}, u32[]{:S(2)}) collective-permute-start(f32[32,128]{1,0:T(8,128)S(1)} %get-tuple-element.76), channel_id=1, source_target_pairs={{0,1},{1,0},{2,3},{3,2},{4,5},{5,4},{6,7},{7,6},{8,9},{9,8},{10,11... | collective-permute-start | bytes 49160 | tf_op jit(solution)/shard_map/ppermute | solution.py:353
  52.0 0.8 collective-permute-start.17
  52.8 1.2 %collective-permute-done.15.refs_2_ = f32[32,128]{1,0:T(8,128)S(1)} collective-permute-done((f32[32,128]{1,0:T(8,128)S(1)}, f32[32,128]{1,0:T(8,128)S(1)}, u32[]{:S(2)}, u32[]{:S(2)}) %collective-permute-start.15) | collective-permute-done | bytes 16416 | tf_op jit(solution)/shard_map/ppermute | solution.py:353
  54.0 0.3 collective-permute-done.16.refs_3_
  54.3 1.5 %collective-permute-done.17.refs_4_ = f32[32,128]{1,0:T(8,128)S(1)} collective-permute-done((f32[32,128]{1,0:T(8,128)S(1)}, f32[32,128]{1,0:T(8,128)S(1)}, u32[]{:S(2)}, u32[]{:S(2)}) %collective-permute-start.17) | collective-permute-done | bytes 16416 | tf_op jit(solution)/shard_map/ppermute | solution.py:353
  55.7 0.5 shard_map.103
  56.2 0.1 collective-permute-start.19
  56.3 2.8 %collective-permute-start.20 = (f32[32,128]{1,0:T(8,128)S(1)}, f32[32,128]{1,0:T(8,128)S(1)}, u32[]{:S(2)}, u32[]{:S(2)}) collective-permute-start(f32[32,128]{1,0:T(8,128)S(1)} %get-tuple-element.83), channel_id=1, source_target_pairs={{0,4},{1,5},{2,6},{3,7},{4,0},{5,1},{6,2},{7,3},{8,12},{9,13},{10,... | collective-permute-start | bytes 49160 | tf_op jit(solution)/shard_map/ppermute | solution.py:353
  59.2 0.0 collective-permute-start.21
  59.2 0.0 collective-permute-start.22
  59.2 0.8 collective-permute-start.23
  60.0 0.9 collective-permute-done.20.refs_1_
  60.9 2.0 %collective-permute-done.21.refs_2_ = f32[32,128]{1,0:T(8,128)S(1)} collective-permute-done((f32[32,128]{1,0:T(8,128)S(1)}, f32[32,128]{1,0:T(8,128)S(1)}, u32[]{:S(2)}, u32[]{:S(2)}) %collective-permute-start.21) | collective-permute-done | bytes 16416 | tf_op jit(solution)/shard_map/ppermute | solution.py:353
  62.9 0.0 collective-permute-done.22.refs_3_
  62.9 0.0 collective-permute-done.23.refs_4_
  63.0 0.7 shard_map.104
  63.7 22.1 %all_to_all.11 = f32[256,2,128]{2,1,0:T(2,128)S(1)} all-to-all(f32[256,2,128]{2,1,0:T(2,128)S(1)} %bitcast.8), channel_id=1, replica_groups=mesh['region'=8,'gy'=8,'gz'=4] {'gy','gz','region'}, dimensions={0} | all-to-all | bytes 524288 | tf_op jit(solution)/shard_map/all_to_all | solution.py:358
  85.8 0.3 shard_map.105.mine
  86.0 0.1 collective-permute-start.25
  86.1 1.2 %collective-permute-done.25.other = f32[32,384]{1,0:T(8,128)S(1)} collective-permute-done((f32[32,384]{1,0:T(8,128)S(1)}, f32[32,384]{1,0:T(8,128)S(1)}, u32[]{:S(2)}, u32[]{:S(2)}) %collective-permute-start.25) | collective-permute-done | bytes 49184 | tf_op jit(solution)/shard_map/ppermute | solution.py:363
  87.3 0.9 shard_map.106
  88.2 0.2 collective-permute-start.26
  88.4 1.8 %collective-permute-start.27 = (f32[32,128]{1,0:T(8,128)S(1)}, f32[32,128]{1,0:T(8,128)S(1)}, u32[]{:S(2)}, u32[]{:S(2)}) collective-permute-start(f32[32,128]{1,0:T(8,128)S(1)} %get-tuple-element.97), channel_id=1, source_target_pairs={{0,4},{1,5},{2,6},{3,7},{4,0},{5,1},{6,2},{7,3},{8,12},{9,13},{10,... | collective-permute-start | bytes 49160 | tf_op jit(solution)/shard_map/ppermute | solution.py:353
  90.2 0.3 collective-permute-start.28
  90.5 1.5 %collective-permute-start.29 = (f32[32,128]{1,0:T(8,128)S(1)}, f32[32,128]{1,0:T(8,128)S(1)}, u32[]{:S(2)}, u32[]{:S(2)}) collective-permute-start(f32[32,128]{1,0:T(8,128)S(1)} %get-tuple-element.99), channel_id=1, source_target_pairs={{0,1},{1,0},{2,3},{3,2},{4,5},{5,4},{6,7},{7,6},{8,9},{9,8},{10,11... | collective-permute-start | bytes 49160 | tf_op jit(solution)/shard_map/ppermute | solution.py:353
  91.9 0.8 collective-permute-start.30
  92.8 1.2 %collective-permute-done.28.refs_2_ = f32[32,128]{1,0:T(8,128)S(1)} collective-permute-done((f32[32,128]{1,0:T(8,128)S(1)}, f32[32,128]{1,0:T(8,128)S(1)}, u32[]{:S(2)}, u32[]{:S(2)}) %collective-permute-start.28) | collective-permute-done | bytes 16416 | tf_op jit(solution)/shard_map/ppermute | solution.py:353
  93.9 0.3 collective-permute-done.29.refs_3_
  94.2 1.5 %collective-permute-done.30.refs_4_ = f32[32,128]{1,0:T(8,128)S(1)} collective-permute-done((f32[32,128]{1,0:T(8,128)S(1)}, f32[32,128]{1,0:T(8,128)S(1)}, u32[]{:S(2)}, u32[]{:S(2)}) %collective-permute-start.30) | collective-permute-done | bytes 16416 | tf_op jit(solution)/shard_map/ppermute | solution.py:353
  95.7 0.8 shard_map.107
  (29 shorter events, 0.1 us)
Async XLA Ops:
  1.3 0.9 copy-start.4
  2.2 6.6 %collective-permute-start = (f32[40,128]{1,0:T(8,128)S(1)}, f32[40,128]{1,0:T(8,128)S(1)}, u32[]{:S(2)}, u32[]{:S(2)}) collective-permute-start(f32[40,128]{1,0:T(8,128)S(1)} %get-tuple-element.53), channel_id=1, source_target_pairs={{0,32},{1,33},{2,34},{3,35},{4,8},{5,9},{6,10},{7,11},{8,4},{9,5},... | collective-permute-start | bytes 61448 | tf_op jit(solution)/shard_map/ppermute | solution.py:353
  2.3 9.0 %collective-permute-start.1 = (f32[40,128]{1,0:T(8,128)S(1)}, f32[40,128]{1,0:T(8,128)S(1)}, u32[]{:S(2)}, u32[]{:S(2)}) collective-permute-start(f32[40,128]{1,0:T(8,128)S(1)} %get-tuple-element.54), channel_id=1, source_target_pairs={{0,4},{1,5},{2,6},{3,7},{4,0},{5,1},{6,2},{7,3},{8,12},{9,13},{10,... | collective-permute-start | bytes 61448 | tf_op jit(solution)/shard_map/ppermute | solution.py:353
  6.2 5.2 %collective-permute-start.2 = (f32[40,128]{1,0:T(8,128)S(1)}, f32[40,128]{1,0:T(8,128)S(1)}, u32[]{:S(2)}, u32[]{:S(2)}) collective-permute-start(f32[40,128]{1,0:T(8,128)S(1)} %get-tuple-element.55), channel_id=1, source_target_pairs={{0,4},{1,5},{2,6},{3,7},{4,0},{5,1},{6,2},{7,3},{8,12},{9,13},{10,... | collective-permute-start | bytes 61448 | tf_op jit(solution)/shard_map/ppermute | solution.py:353
  6.2 5.2 %collective-permute-start.3 = (f32[40,128]{1,0:T(8,128)S(1)}, f32[40,128]{1,0:T(8,128)S(1)}, u32[]{:S(2)}, u32[]{:S(2)}) collective-permute-start(f32[40,128]{1,0:T(8,128)S(1)} %get-tuple-element.56), channel_id=1, source_target_pairs={{0,1},{1,0},{2,3},{3,2},{4,5},{5,4},{6,7},{7,6},{8,9},{9,8},{10,11... | collective-permute-start | bytes 61448 | tf_op jit(solution)/shard_map/ppermute | solution.py:353
  6.7 4.7 %collective-permute-start.4 = (f32[40,128]{1,0:T(8,128)S(1)}, f32[40,128]{1,0:T(8,128)S(1)}, u32[]{:S(2)}, u32[]{:S(2)}) collective-permute-start(f32[40,128]{1,0:T(8,128)S(1)} %get-tuple-element.57), channel_id=1, source_target_pairs={{0,32},{1,2},{2,1},{3,35},{4,36},{5,6},{6,5},{7,39},{8,40},{9,10},... | collective-permute-start | bytes 61448 | tf_op jit(solution)/shard_map/ppermute | solution.py:353
  8.9 2.5 %collective-permute-start.5 = (f32[40,128]{1,0:T(8,128)S(1)}, f32[40,128]{1,0:T(8,128)S(1)}, u32[]{:S(2)}, u32[]{:S(2)}) collective-permute-start(f32[40,128]{1,0:T(8,128)S(1)} %get-tuple-element.58), channel_id=1, source_target_pairs={{0,32},{1,33},{2,34},{3,35},{4,36},{5,37},{6,38},{7,39},{8,40},{9,... | collective-permute-start | bytes 61448 | tf_op jit(solution)/shard_map/ppermute | solution.py:353
  10.0 1.3 %copy-start.2 = (bf16[1,768,768]{2,1,0:T(8,128)(2,1)S(1)}, bf16[1,768,768]{2,1,0:T(8,128)(2,1)}, u32[]{:S(2)}) copy-start(bf16[1,768,768]{2,1,0:T(8,128)(2,1)} %source.2) | copy-start | bytes 3538948
  11.3 0.7 copy-start.5
  11.3 10.0 %copy-start = (bf16[1,768,768]{2,1,0:T(8,128)(2,1)S(1)}, bf16[1,768,768]{2,1,0:T(8,128)(2,1)}, u32[]{:S(2)}) copy-start(bf16[1,768,768]{2,1,0:T(8,128)(2,1)} %schur.5) | copy-start | bytes 3538948
  11.4 10.0 %copy-start.1 = (bf16[1,768,128]{2,1,0:T(8,128)(2,1)S(1)}, bf16[1,768,128]{2,1,0:T(8,128)(2,1)}, u32[]{:S(2)}) copy-start(bf16[1,768,128]{2,1,0:T(8,128)(2,1)} %coupling.7) | copy-start | bytes 589828
  11.4 10.0 %copy-start.6 = (s32[1,128]{1,0:T(1,128)S(1)}, s32[1,128]{1,0:T(1,128)}, u32[]{:S(2)}) copy-start(s32[1,128]{1,0:T(1,128)} %corner_map.7) | copy-start | bytes 1540
  12.4 6.3 %collective-permute-start.6 = (f32[32,128]{1,0:T(8,128)S(1)}, f32[32,128]{1,0:T(8,128)S(1)}, u32[]{:S(2)}, u32[]{:S(2)}) collective-permute-start(f32[32,128]{1,0:T(8,128)S(1)} %get-tuple-element.63), channel_id=1, source_target_pairs={{0,32},{1,33},{2,34},{3,35},{4,8},{5,9},{6,10},{7,11},{8,4},{9,5},... | collective-permute-start | bytes 49160 | tf_op jit(solution)/shard_map/ppermute | solution.py:353
  12.5 7.3 %collective-permute-start.7 = (f32[32,128]{1,0:T(8,128)S(1)}, f32[32,128]{1,0:T(8,128)S(1)}, u32[]{:S(2)}, u32[]{:S(2)}) collective-permute-start(f32[32,128]{1,0:T(8,128)S(1)} %get-tuple-element.64), channel_id=1, source_target_pairs={{0,4},{1,5},{2,6},{3,7},{4,0},{5,1},{6,2},{7,3},{8,12},{9,13},{10,... | collective-permute-start | bytes 49160 | tf_op jit(solution)/shard_map/ppermute | solution.py:353
  17.6 3.7 %collective-permute-start.8 = (f32[32,128]{1,0:T(8,128)S(1)}, f32[32,128]{1,0:T(8,128)S(1)}, u32[]{:S(2)}, u32[]{:S(2)}) collective-permute-start(f32[32,128]{1,0:T(8,128)S(1)} %get-tuple-element.65), channel_id=1, source_target_pairs={{0,4},{1,5},{2,6},{3,7},{4,0},{5,1},{6,2},{7,3},{8,12},{9,13},{10,... | collective-permute-start | bytes 49160 | tf_op jit(solution)/shard_map/ppermute | solution.py:353
  17.6 3.7 %collective-permute-start.9 = (f32[32,128]{1,0:T(8,128)S(1)}, f32[32,128]{1,0:T(8,128)S(1)}, u32[]{:S(2)}, u32[]{:S(2)}) collective-permute-start(f32[32,128]{1,0:T(8,128)S(1)} %get-tuple-element.66), channel_id=1, source_target_pairs={{0,1},{1,0},{2,3},{3,2},{4,5},{5,4},{6,7},{7,6},{8,9},{9,8},{10,11... | collective-permute-start | bytes 49160 | tf_op jit(solution)/shard_map/ppermute | solution.py:353
  17.6 3.7 %collective-permute-start.10 = (f32[32,128]{1,0:T(8,128)S(1)}, f32[32,128]{1,0:T(8,128)S(1)}, u32[]{:S(2)}, u32[]{:S(2)}) collective-permute-start(f32[32,128]{1,0:T(8,128)S(1)} %get-tuple-element.67), channel_id=1, source_target_pairs={{0,32},{1,2},{2,1},{3,35},{4,36},{5,6},{6,5},{7,39},{8,40},{9,10},... | collective-permute-start | bytes 49160 | tf_op jit(solution)/shard_map/ppermute | solution.py:353
  18.7 2.6 %collective-permute-start.11 = (f32[32,128]{1,0:T(8,128)S(1)}, f32[32,128]{1,0:T(8,128)S(1)}, u32[]{:S(2)}, u32[]{:S(2)}) collective-permute-start(f32[32,128]{1,0:T(8,128)S(1)} %get-tuple-element.68), channel_id=1, source_target_pairs={{0,32},{1,33},{2,34},{3,35},{4,36},{5,37},{6,38},{7,39},{8,40},{9,... | collective-permute-start | bytes 49160 | tf_op jit(solution)/shard_map/ppermute | solution.py:353
  21.4 25.1 %copy-start.3 = (f32[512,512]{1,0:T(8,128)S(1)}, f32[512,512]{1,0:T(8,128)}, u32[]{:S(2)}) copy-start(f32[512,512]{1,0:T(8,128)} %source.3) | copy-start | bytes 3145732
  46.4 1.3 %collective-permute-start.12 = (f32[32,384]{1,0:T(8,128)S(1)}, f32[32,384]{1,0:T(8,128)S(1)}, u32[]{:S(2)}, u32[]{:S(2)}) collective-permute-start(f32[32,384]{1,0:T(8,128)S(1)} %shard_map.101.mine), channel_id=1, source_target_pairs={{0,32},{1,33},{2,34},{3,35},{4,36},{5,37},{6,38},{7,39},{8,40},{9,... | collective-permute-start | bytes 147464 | tf_op jit(solution)/shard_map/ppermute | solution.py:363
  48.2 4.6 %collective-permute-start.13 = (f32[32,128]{1,0:T(8,128)S(1)}, f32[32,128]{1,0:T(8,128)S(1)}, u32[]{:S(2)}, u32[]{:S(2)}) collective-permute-start(f32[32,128]{1,0:T(8,128)S(1)} %get-tuple-element.73), channel_id=1, source_target_pairs={{0,32},{1,33},{2,34},{3,35},{4,8},{5,9},{6,10},{7,11},{8,4},{9,5},... | collective-permute-start | bytes 49160 | tf_op jit(solution)/shard_map/ppermute | solution.py:353
  48.5 4.3 %collective-permute-start.14 = (f32[32,128]{1,0:T(8,128)S(1)}, f32[32,128]{1,0:T(8,128)S(1)}, u32[]{:S(2)}, u32[]{:S(2)}) collective-permute-start(f32[32,128]{1,0:T(8,128)S(1)} %get-tuple-element.74), channel_id=1, source_target_pairs={{0,4},{1,5},{2,6},{3,7},{4,0},{5,1},{6,2},{7,3},{8,12},{9,13},{10,... | collective-permute-start | bytes 49160 | tf_op jit(solution)/shard_map/ppermute | solution.py:353
  50.2 3.7 %collective-permute-start.15 = (f32[32,128]{1,0:T(8,128)S(1)}, f32[32,128]{1,0:T(8,128)S(1)}, u32[]{:S(2)}, u32[]{:S(2)}) collective-permute-start(f32[32,128]{1,0:T(8,128)S(1)} %get-tuple-element.75), channel_id=1, source_target_pairs={{0,4},{1,5},{2,6},{3,7},{4,0},{5,1},{6,2},{7,3},{8,12},{9,13},{10,... | collective-permute-start | bytes 49160 | tf_op jit(solution)/shard_map/ppermute | solution.py:353
  50.5 3.7 %collective-permute-start.16 = (f32[32,128]{1,0:T(8,128)S(1)}, f32[32,128]{1,0:T(8,128)S(1)}, u32[]{:S(2)}, u32[]{:S(2)}) collective-permute-start(f32[32,128]{1,0:T(8,128)S(1)} %get-tuple-element.76), channel_id=1, source_target_pairs={{0,1},{1,0},{2,3},{3,2},{4,5},{5,4},{6,7},{7,6},{8,9},{9,8},{10,11... | collective-permute-start | bytes 49160 | tf_op jit(solution)/shard_map/ppermute | solution.py:353
  52.0 3.7 %collective-permute-start.17 = (f32[32,128]{1,0:T(8,128)S(1)}, f32[32,128]{1,0:T(8,128)S(1)}, u32[]{:S(2)}, u32[]{:S(2)}) collective-permute-start(f32[32,128]{1,0:T(8,128)S(1)} %get-tuple-element.77), channel_id=1, source_target_pairs={{0,32},{1,2},{2,1},{3,35},{4,36},{5,6},{6,5},{7,39},{8,40},{9,10},... | collective-permute-start | bytes 49160 | tf_op jit(solution)/shard_map/ppermute | solution.py:353
  52.8 2.9 %collective-permute-start.18 = (f32[32,128]{1,0:T(8,128)S(1)}, f32[32,128]{1,0:T(8,128)S(1)}, u32[]{:S(2)}, u32[]{:S(2)}) collective-permute-start(f32[32,128]{1,0:T(8,128)S(1)} %get-tuple-element.78), channel_id=1, source_target_pairs={{0,32},{1,33},{2,34},{3,35},{4,36},{5,37},{6,38},{7,39},{8,40},{9,... | collective-permute-start | bytes 49160 | tf_op jit(solution)/shard_map/ppermute | solution.py:353
  56.2 3.8 %collective-permute-start.19 = (f32[32,128]{1,0:T(8,128)S(1)}, f32[32,128]{1,0:T(8,128)S(1)}, u32[]{:S(2)}, u32[]{:S(2)}) collective-permute-start(f32[32,128]{1,0:T(8,128)S(1)} %get-tuple-element.82), channel_id=1, source_target_pairs={{0,32},{1,33},{2,34},{3,35},{4,8},{5,9},{6,10},{7,11},{8,4},{9,5},... | collective-permute-start | bytes 49160 | tf_op jit(solution)/shard_map/ppermute | solution.py:353
  56.3 4.6 %collective-permute-start.20 = (f32[32,128]{1,0:T(8,128)S(1)}, f32[32,128]{1,0:T(8,128)S(1)}, u32[]{:S(2)}, u32[]{:S(2)}) collective-permute-start(f32[32,128]{1,0:T(8,128)S(1)} %get-tuple-element.83), channel_id=1, source_target_pairs={{0,4},{1,5},{2,6},{3,7},{4,0},{5,1},{6,2},{7,3},{8,12},{9,13},{10,... | collective-permute-start | bytes 49160 | tf_op jit(solution)/shard_map/ppermute | solution.py:353
  59.2 3.7 %collective-permute-start.21 = (f32[32,128]{1,0:T(8,128)S(1)}, f32[32,128]{1,0:T(8,128)S(1)}, u32[]{:S(2)}, u32[]{:S(2)}) collective-permute-start(f32[32,128]{1,0:T(8,128)S(1)} %get-tuple-element.84), channel_id=1, source_target_pairs={{0,4},{1,5},{2,6},{3,7},{4,0},{5,1},{6,2},{7,3},{8,12},{9,13},{10,... | collective-permute-start | bytes 49160 | tf_op jit(solution)/shard_map/ppermute | solution.py:353
  59.2 3.7 %collective-permute-start.22 = (f32[32,128]{1,0:T(8,128)S(1)}, f32[32,128]{1,0:T(8,128)S(1)}, u32[]{:S(2)}, u32[]{:S(2)}) collective-permute-start(f32[32,128]{1,0:T(8,128)S(1)} %get-tuple-element.85), channel_id=1, source_target_pairs={{0,1},{1,0},{2,3},{3,2},{4,5},{5,4},{6,7},{7,6},{8,9},{9,8},{10,11... | collective-permute-start | bytes 49160 | tf_op jit(solution)/shard_map/ppermute | solution.py:353
  59.2 3.7 %collective-permute-start.23 = (f32[32,128]{1,0:T(8,128)S(1)}, f32[32,128]{1,0:T(8,128)S(1)}, u32[]{:S(2)}, u32[]{:S(2)}) collective-permute-start(f32[32,128]{1,0:T(8,128)S(1)} %get-tuple-element.86), channel_id=1, source_target_pairs={{0,32},{1,2},{2,1},{3,35},{4,36},{5,6},{6,5},{7,39},{8,40},{9,10},... | collective-permute-start | bytes 49160 | tf_op jit(solution)/shard_map/ppermute | solution.py:353
  60.0 3.0 %collective-permute-start.24 = (f32[32,128]{1,0:T(8,128)S(1)}, f32[32,128]{1,0:T(8,128)S(1)}, u32[]{:S(2)}, u32[]{:S(2)}) collective-permute-start(f32[32,128]{1,0:T(8,128)S(1)} %get-tuple-element.87), channel_id=1, source_target_pairs={{0,32},{1,33},{2,34},{3,35},{4,36},{5,37},{6,38},{7,39},{8,40},{9,... | collective-permute-start | bytes 49160 | tf_op jit(solution)/shard_map/ppermute | solution.py:353
  86.0 1.3 %collective-permute-start.25 = (f32[32,384]{1,0:T(8,128)S(1)}, f32[32,384]{1,0:T(8,128)S(1)}, u32[]{:S(2)}, u32[]{:S(2)}) collective-permute-start(f32[32,384]{1,0:T(8,128)S(1)} %shard_map.105.mine), channel_id=1, source_target_pairs={{0,32},{1,33},{2,34},{3,35},{4,36},{5,37},{6,38},{7,39},{8,40},{9,... | collective-permute-start | bytes 147464 | tf_op jit(solution)/shard_map/ppermute | solution.py:363
  88.2 4.5 %collective-permute-start.26 = (f32[32,128]{1,0:T(8,128)S(1)}, f32[32,128]{1,0:T(8,128)S(1)}, u32[]{:S(2)}, u32[]{:S(2)}) collective-permute-start(f32[32,128]{1,0:T(8,128)S(1)} %get-tuple-element.96), channel_id=1, source_target_pairs={{0,32},{1,33},{2,34},{3,35},{4,8},{5,9},{6,10},{7,11},{8,4},{9,5},... | collective-permute-start | bytes 49160 | tf_op jit(solution)/shard_map/ppermute | solution.py:353
  88.4 4.3 %collective-permute-start.27 = (f32[32,128]{1,0:T(8,128)S(1)}, f32[32,128]{1,0:T(8,128)S(1)}, u32[]{:S(2)}, u32[]{:S(2)}) collective-permute-start(f32[32,128]{1,0:T(8,128)S(1)} %get-tuple-element.97), channel_id=1, source_target_pairs={{0,4},{1,5},{2,6},{3,7},{4,0},{5,1},{6,2},{7,3},{8,12},{9,13},{10,... | collective-permute-start | bytes 49160 | tf_op jit(solution)/shard_map/ppermute | solution.py:353
  90.2 3.7 %collective-permute-start.28 = (f32[32,128]{1,0:T(8,128)S(1)}, f32[32,128]{1,0:T(8,128)S(1)}, u32[]{:S(2)}, u32[]{:S(2)}) collective-permute-start(f32[32,128]{1,0:T(8,128)S(1)} %get-tuple-element.98), channel_id=1, source_target_pairs={{0,4},{1,5},{2,6},{3,7},{4,0},{5,1},{6,2},{7,3},{8,12},{9,13},{10,... | collective-permute-start | bytes 49160 | tf_op jit(solution)/shard_map/ppermute | solution.py:353
  90.5 3.7 %collective-permute-start.29 = (f32[32,128]{1,0:T(8,128)S(1)}, f32[32,128]{1,0:T(8,128)S(1)}, u32[]{:S(2)}, u32[]{:S(2)}) collective-permute-start(f32[32,128]{1,0:T(8,128)S(1)} %get-tuple-element.99), channel_id=1, source_target_pairs={{0,1},{1,0},{2,3},{3,2},{4,5},{5,4},{6,7},{7,6},{8,9},{9,8},{10,11... | collective-permute-start | bytes 49160 | tf_op jit(solution)/shard_map/ppermute | solution.py:353
  91.9 3.7 %collective-permute-start.30 = (f32[32,128]{1,0:T(8,128)S(1)}, f32[32,128]{1,0:T(8,128)S(1)}, u32[]{:S(2)}, u32[]{:S(2)}) collective-permute-start(f32[32,128]{1,0:T(8,128)S(1)} %get-tuple-element.100), channel_id=1, source_target_pairs={{0,32},{1,2},{2,1},{3,35},{4,36},{5,6},{6,5},{7,39},{8,40},{9,10},... | collective-permute-start | bytes 49160 | tf_op jit(solution)/shard_map/ppermute | solution.py:353
  92.8 2.9 %collective-permute-start.31 = (f32[32,128]{1,0:T(8,128)S(1)}, f32[32,128]{1,0:T(8,128)S(1)}, u32[]{:S(2)}, u32[]{:S(2)}) collective-permute-start(f32[32,128]{1,0:T(8,128)S(1)} %get-tuple-element.101), channel_id=1, source_target_pairs={{0,32},{1,33},{2,34},{3,35},{4,36},{5,37},{6,38},{7,39},{8,40},{9,... | collective-permute-start | bytes 49160 | tf_op jit(solution)/shard_map/ppermute | solution.py:353
